TPU v7x, 768 devices: a whole 4x8x12 slice. The times are simulated.
768 devices in a mesh: dp: 128 (over y, x, z_hi, core), tensor: 6 (over z_lo).
Axes of the slice: x: 4, y: 8, z: 12 (z_hi: 2, z_lo: 6; z = z_hi * 6 + z_lo), core: 2. Of those that a mesh axis runs over, the one named last changes fastest.
Arguments:
- hidden: bfloat16 [49152, 3840], P('dp', 'tensor'), may hold values from -36 to 36
- targets: int32 [49152], P('dp'), may hold values from 0 to 31999
- padding: int32 [49152], P('dp'), may hold values 0 or 1
- gold_logit: float32 [49152], P('dp'), may hold values from 0 to 6
- vocab_lse: float32 [49152], P('dp'), may hold values from 6 to 10
- cotangent: float32 [49152], P('dp'), may hold values from -6 to 6
Outputs:
- grad_hidden: bfloat16 [49152, 3840], P('dp', 'tensor')
All inputs are finite; a program needn't handle non-finite values. No bound on the sum of `padding` on one device may be relied on, other than what follows from the above.
Results may differ from a plain program's by a relative error of at most 0.0075.
Values may be sent and summed in bfloat16 or wider, within the bound.
No kernel may reach another device: no remote copies, remote signals or barrier semaphores. Data moves between devices by JAX's collectives and lax.ppermute only.
A program may use at most 32 MiB of HBM per device.

v0:
```python
import math

import jax
import jax.numpy as jnp
from jax import lax
from jax.sharding import PartitionSpec as P

KW = 3840
SPAN = 4


def passed_along(value, axis, steps):
    count = lax.axis_size(axis)
    pairs = [(source, (source + steps) % count) for source in range(count)]
    return lax.ppermute(value, axis, pairs)


def normalizer(scores, allowed, outside):
    masked = jnp.where(allowed, scores, -1e30)
    peak_value = jnp.maximum(outside, jnp.max(masked, axis=(1, 2)))
    denominator = jnp.exp(outside - peak_value) + jnp.sum(
        jnp.where(allowed, jnp.exp(scores - peak_value[:, None, None]), 0.0), axis=(1, 2)
    )
    return peak_value + jnp.log(denominator)


def slope_tile(scores, usable, matches, total_lse, pos_lse, weight, score_scale):
    spread = jnp.where(usable, jnp.exp(scores - total_lse), 0.0) - jnp.where(
        matches, jnp.exp(scores - pos_lse), 0.0
    )
    return (weight * spread * score_scale).astype(jnp.bfloat16)


def per_device(hidden, targets, padding, gold_logit, vocab_lse, cotangent):
    score_scale = 1.0 / math.sqrt(KW)
    label_code = jnp.where(padding == 1, targets, -1)
    weight = cotangent * padding.astype(jnp.float32)

    def relay_keys(payload, unused):
        arrived = passed_along((payload[0], payload[1]), "dp", 1)
        return (arrived, arrived)

    final_keys, (keys_all, key_labels) = lax.scan(
        relay_keys, (hidden, label_code), None, length=SPAN
    )
    usable = (key_labels >= 0)[None]
    partial_scores = jnp.einsum("tc,sjc->tsj", hidden, keys_all, preferred_element_type=jnp.float32)
    scores = lax.psum(partial_scores, "tensor") * score_scale
    matches = usable & (key_labels[None] == targets[:, None, None])
    total_lse = normalizer(scores, usable, vocab_lse)
    pos_lse = normalizer(scores, matches, gold_logit)
    slopes = slope_tile(
        scores,
        usable,
        matches,
        total_lse[:, None, None],
        pos_lse[:, None, None],
        weight[:, None, None],
        score_scale,
    )
    query_grad = jnp.einsum("tsj,sjc->tc", slopes, keys_all, preferred_element_type=jnp.float32)
    key_terms = jnp.einsum("tsj,tc->sjc", slopes, hidden, preferred_element_type=jnp.float32)

    def carry_back(running, term):
        arrived = passed_along(running + term, "dp", -1)
        return (arrived, None)

    start_grad = jnp.zeros(hidden.shape, jnp.float32)
    key_grad, unused_out = lax.scan(carry_back, start_grad, key_terms[::-1])
    return (query_grad + key_grad).astype(jnp.bfloat16)


def solution(mesh):
    placed = (P("dp", "tensor"), P("dp"), P("dp"), P("dp"), P("dp"), P("dp"))
    return jax.shard_map(
        per_device, mesh=mesh, in_specs=placed, out_specs=P("dp", "tensor"), check_vma=False
    )
```

profile of v0, /device:TPU:78, one launch (start us, length us, event | category | flops | bytes accessed | tf_op | source)
XLA Modules:
  0.0 442.0 jit_solution(4631558633395729482)
XLA Ops:
  8.3 100.3 %while.28 = (s32[]{:T(128)}, bf16[384,640]{1,0:T(8,128)(2,1)S(1)}, s32[384]{0:T(512)S(1)}, bf16[4,384,640]{2,1,0:T(8,128)(2,1)S(1)}, s32[4,384]{1,0:T(4,128)S(1)}) while((s32[]{:T(128)}, bf16[384,640]{1,0:T(8,128)(2,1)S(1)}, s32[384]{0:T(512)S(1)}, bf16[4,384,640]{2,1,0:T(8,128)(2,1)S(1)}, s32[4,384]{1,0:T(4,128)S(1)}) %tuple.39), condition=%wide.region_1.2_spmd.clone, body=%wide.region_0.1_spmd.sunk.clone | while | flops 2 | bytes 3947677 | solution.py:43
  8.3 2.0 collective-permute-start
  10.3 14.3 %collective-permute-start.1 = (s32[384]{0:T(512)S(1)}, s32[384]{0:T(512)S(1)}, u32[]{:S(2)}, u32[]{:S(2)}) collective-permute-start(s32[384]{0:T(512)S(1)} %get-tuple-element.151), channel_id=1, source_target_pairs={{0,6},{6,12},{12,18},{18,24},{24,30},{30,36},{36,42},{42,48},{48,5... | collective-permute-start | bytes 4616 | tf_op jit(solution)/shard_map/while/body/eval_jaxpr/ppermute | solution.py:15
  24.7 15.0 %collective-permute-done.1 = s32[384]{0:T(512)S(1)} collective-permute-done((s32[384]{0:T(512)S(1)}, s32[384]{0:T(512)S(1)}, u32[]{:S(2)}, u32[]{:S(2)}) %collective-permute-start.1) | collective-permute-done | bytes 1568 | tf_op jit(solution)/shard_map/while/body/eval_jaxpr/ppermute | solution.py:15
  39.9 1.9 collective-permute-start
  41.8 7.0 %collective-permute-start.1 = (s32[384]{0:T(512)S(1)}, s32[384]{0:T(512)S(1)}, u32[]{:S(2)}, u32[]{:S(2)}) collective-permute-start(s32[384]{0:T(512)S(1)} %get-tuple-element.151), channel_id=1, source_target_pairs={{0,6},{6,12},{12,18},{18,24},{24,30},{30,36},{36,42},{42,48},{48,5... | collective-permute-start | bytes 4616 | tf_op jit(solution)/shard_map/while/body/eval_jaxpr/ppermute | solution.py:15
  48.9 15.0 %collective-permute-done.1 = s32[384]{0:T(512)S(1)} collective-permute-done((s32[384]{0:T(512)S(1)}, s32[384]{0:T(512)S(1)}, u32[]{:S(2)}, u32[]{:S(2)}) %collective-permute-start.1) | collective-permute-done | bytes 1568 | tf_op jit(solution)/shard_map/while/body/eval_jaxpr/ppermute | solution.py:15
  64.1 1.9 collective-permute-start
  66.0 3.2 collective-permute-start.1
  69.2 18.0 %collective-permute-done.1 = s32[384]{0:T(512)S(1)} collective-permute-done((s32[384]{0:T(512)S(1)}, s32[384]{0:T(512)S(1)}, u32[]{:S(2)}, u32[]{:S(2)}) %collective-permute-start.1) | collective-permute-done | bytes 1568 | tf_op jit(solution)/shard_map/while/body/eval_jaxpr/ppermute | solution.py:15
  87.4 1.9 collective-permute-start
  89.3 1.9 collective-permute-start.1
  91.2 17.2 %collective-permute-done.1 = s32[384]{0:T(512)S(1)} collective-permute-done((s32[384]{0:T(512)S(1)}, s32[384]{0:T(512)S(1)}, u32[]{:S(2)}, u32[]{:S(2)}) %collective-permute-start.1) | collective-permute-done | bytes 1568 | tf_op jit(solution)/shard_map/while/body/eval_jaxpr/ppermute | solution.py:15
  108.6 2.7 convolution_bitcast_fusion
  112.1 128.8 %all-reduce.2.cloned.1.call-done = f32[384,4,384]{0,2,1:T(8,128)} async-done(((f32[384,4,384]{0,2,1:T(8,128)}), f32[384,4,384]{0,2,1:T(8,128)}) %all-reduce.2.cloned.1.call-update) | async-done | bytes 2359312 | tf_op jit(solution)/shard_map/psum | solution.py:48
  240.9 2.2 select_reduce_fusion.3
  245.3 3.9 fusion.2
  249.2 4.2 rev.3
  253.5 176.6 %while.29 = (s32[]{:T(128)}, f32[384,640]{1,0:T(8,128)S(1)}, f32[4,384,640]{2,1,0:T(8,128)}) while((s32[]{:T(128)}, f32[384,640]{1,0:T(8,128)S(1)}, f32[4,384,640]{2,1,0:T(8,128)}) %tuple.42), condition=%wide.region_8.9_spmd.clone, body=%wide.region_7.8_spmd.sunk.clone | while | flops 245762 | bytes 6881369 | solution.py:69
  253.5 1.3 bitcast_add_fusion.3
  254.8 9.6 %collective-permute-start.2 = (f32[384,640]{1,0:T(8,128)S(1)}, f32[384,640]{1,0:T(8,128)S(1)}, u32[]{:S(2)}, u32[]{:S(2)}) collective-permute-start(f32[384,640]{1,0:T(8,128)S(1)} %bitcast_add_fusion.3), channel_id=1, source_target_pairs={{0,762},{6,0},{12,6},{18,12},{24,18},{30,24},{36,30},{42,36},{48,4... | collective-permute-start | bytes 2949128 | tf_op jit(solution)/shard_map/while/body/eval_jaxpr/ppermute | solution.py:15
  264.5 27.2 %collective-permute-done.2 = f32[384,640]{1,0:T(8,128)S(1)} collective-permute-done((f32[384,640]{1,0:T(8,128)S(1)}, f32[384,640]{1,0:T(8,128)S(1)}, u32[]{:S(2)}, u32[]{:S(2)}) %collective-permute-start.2) | collective-permute-done | bytes 983072 | tf_op jit(solution)/shard_map/while/body/eval_jaxpr/ppermute | solution.py:15
  291.7 1.3 bitcast_add_fusion.3
  293.0 16.6 %collective-permute-start.2 = (f32[384,640]{1,0:T(8,128)S(1)}, f32[384,640]{1,0:T(8,128)S(1)}, u32[]{:S(2)}, u32[]{:S(2)}) collective-permute-start(f32[384,640]{1,0:T(8,128)S(1)} %bitcast_add_fusion.3), channel_id=1, source_target_pairs={{0,762},{6,0},{12,6},{18,12},{24,18},{30,24},{36,30},{42,36},{48,4... | collective-permute-start | bytes 2949128 | tf_op jit(solution)/shard_map/while/body/eval_jaxpr/ppermute | solution.py:15
  309.6 51.9 %collective-permute-done.2 = f32[384,640]{1,0:T(8,128)S(1)} collective-permute-done((f32[384,640]{1,0:T(8,128)S(1)}, f32[384,640]{1,0:T(8,128)S(1)}, u32[]{:S(2)}, u32[]{:S(2)}) %collective-permute-start.2) | collective-permute-done | bytes 983072 | tf_op jit(solution)/shard_map/while/body/eval_jaxpr/ppermute | solution.py:15
  361.5 1.3 bitcast_add_fusion.3
  362.8 11.1 %collective-permute-start.2 = (f32[384,640]{1,0:T(8,128)S(1)}, f32[384,640]{1,0:T(8,128)S(1)}, u32[]{:S(2)}, u32[]{:S(2)}) collective-permute-start(f32[384,640]{1,0:T(8,128)S(1)} %bitcast_add_fusion.3), channel_id=1, source_target_pairs={{0,762},{6,0},{12,6},{18,12},{24,18},{30,24},{36,30},{42,36},{48,4... | collective-permute-start | bytes 2949128 | tf_op jit(solution)/shard_map/while/body/eval_jaxpr/ppermute | solution.py:15
  373.9 32.2 %collective-permute-done.2 = f32[384,640]{1,0:T(8,128)S(1)} collective-permute-done((f32[384,640]{1,0:T(8,128)S(1)}, f32[384,640]{1,0:T(8,128)S(1)}, u32[]{:S(2)}, u32[]{:S(2)}) %collective-permute-start.2) | collective-permute-done | bytes 983072 | tf_op jit(solution)/shard_map/while/body/eval_jaxpr/ppermute | solution.py:15
  406.1 1.3 bitcast_add_fusion.3
  407.4 11.1 %collective-permute-start.2 = (f32[384,640]{1,0:T(8,128)S(1)}, f32[384,640]{1,0:T(8,128)S(1)}, u32[]{:S(2)}, u32[]{:S(2)}) collective-permute-start(f32[384,640]{1,0:T(8,128)S(1)} %bitcast_add_fusion.3), channel_id=1, source_target_pairs={{0,762},{6,0},{12,6},{18,12},{24,18},{30,24},{36,30},{42,36},{48,4... | collective-permute-start | bytes 2949128 | tf_op jit(solution)/shard_map/while/body/eval_jaxpr/ppermute | solution.py:15
  418.5 11.6 %collective-permute-done.2 = f32[384,640]{1,0:T(8,128)S(1)} collective-permute-done((f32[384,640]{1,0:T(8,128)S(1)}, f32[384,640]{1,0:T(8,128)S(1)}, u32[]{:S(2)}, u32[]{:S(2)}) %collective-permute-start.2) | collective-permute-done | bytes 983072 | tf_op jit(solution)/shard_map/while/body/eval_jaxpr/ppermute | solution.py:15
  430.1 5.1 %fusion.1 = bf16[384,640]{1,0:T(8,128)(2,1)} fusion(f32[384,640]{1,0:T(8,128)S(1)} %get-tuple-element.52, bf16[4,384,640]{2,1,0:T(8,128)(2,1)} %copy-done.1, f32[384,4,384]{0,2,1:T(8,128)} %all-reduce.2.cloned.1.call-done, f32[384]{0:T(512)S(1)} %get-tuple-element.71, s32[384]{0:T(512)S(1)} %copy-done.3, s32[4,384]{1,0:T(4,128)S(1)} %get-tuple-element.50, ...), kind=kOutput, calls=%fused_computation.11 | convolution fusion | flops 761954304 | bytes 5813760 | tf_op jit(solution)/shard_map/tsj,sjc->tc/dot_general | solution.py:61
  (54 shorter events, 5.3 us)
Async XLA Ops:
  6.5 234.3 %all-reduce.2.cloned.1.call-start = ((), (), s32[]{:S(2)}) async-start(), calls=%async_computation | async-start | bytes 4718592 | tf_op jit(solution)/shard_map/psum | solution.py:48
  8.3 100.4 %copy-start.2 = (bf16[384,640]{1,0:T(8,128)(2,1)S(1)}, bf16[384,640]{1,0:T(8,128)(2,1)}, u32[]{:S(2)}) copy-start(bf16[384,640]{1,0:T(8,128)(2,1)} %param.10) | copy-start | bytes 1474564
  8.3 31.5 %collective-permute-start = (bf16[384,640]{1,0:T(8,128)(2,1)S(1)}, bf16[384,640]{1,0:T(8,128)(2,1)S(1)}, u32[]{:S(2)}, u32[]{:S(2)}) collective-permute-start(bf16[384,640]{1,0:T(8,128)(2,1)S(1)} %get-tuple-element.150), channel_id=1, source_target_pairs={{0,6},{6,12},{12,18},{18,24},{24,30},{30,36},{36,42},{42,48},{48,5... | collective-permute-start | bytes 1474568 | tf_op jit(solution)/shard_map/while/body/eval_jaxpr/ppermute | solution.py:15
  10.3 29.4 %collective-permute-start.1 = (s32[384]{0:T(512)S(1)}, s32[384]{0:T(512)S(1)}, u32[]{:S(2)}, u32[]{:S(2)}) collective-permute-start(s32[384]{0:T(512)S(1)} %get-tuple-element.151), channel_id=1, source_target_pairs={{0,6},{6,12},{12,18},{18,24},{24,30},{30,36},{36,42},{42,48},{48,5... | collective-permute-start | bytes 4616 | tf_op jit(solution)/shard_map/while/body/eval_jaxpr/ppermute | solution.py:15
  39.9 24.0 %collective-permute-start = (bf16[384,640]{1,0:T(8,128)(2,1)S(1)}, bf16[384,640]{1,0:T(8,128)(2,1)S(1)}, u32[]{:S(2)}, u32[]{:S(2)}) collective-permute-start(bf16[384,640]{1,0:T(8,128)(2,1)S(1)} %get-tuple-element.150), channel_id=1, source_target_pairs={{0,6},{6,12},{12,18},{18,24},{24,30},{30,36},{36,42},{42,48},{48,5... | collective-permute-start | bytes 1474568 | tf_op jit(solution)/shard_map/while/body/eval_jaxpr/ppermute | solution.py:15
  41.8 22.0 %collective-permute-start.1 = (s32[384]{0:T(512)S(1)}, s32[384]{0:T(512)S(1)}, u32[]{:S(2)}, u32[]{:S(2)}) collective-permute-start(s32[384]{0:T(512)S(1)} %get-tuple-element.151), channel_id=1, source_target_pairs={{0,6},{6,12},{12,18},{18,24},{24,30},{30,36},{36,42},{42,48},{48,5... | collective-permute-start | bytes 4616 | tf_op jit(solution)/shard_map/while/body/eval_jaxpr/ppermute | solution.py:15
  64.1 23.1 %collective-permute-start = (bf16[384,640]{1,0:T(8,128)(2,1)S(1)}, bf16[384,640]{1,0:T(8,128)(2,1)S(1)}, u32[]{:S(2)}, u32[]{:S(2)}) collective-permute-start(bf16[384,640]{1,0:T(8,128)(2,1)S(1)} %get-tuple-element.150), channel_id=1, source_target_pairs={{0,6},{6,12},{12,18},{18,24},{24,30},{30,36},{36,42},{42,48},{48,5... | collective-permute-start | bytes 1474568 | tf_op jit(solution)/shard_map/while/body/eval_jaxpr/ppermute | solution.py:15
  66.0 21.2 %collective-permute-start.1 = (s32[384]{0:T(512)S(1)}, s32[384]{0:T(512)S(1)}, u32[]{:S(2)}, u32[]{:S(2)}) collective-permute-start(s32[384]{0:T(512)S(1)} %get-tuple-element.151), channel_id=1, source_target_pairs={{0,6},{6,12},{12,18},{18,24},{24,30},{30,36},{36,42},{42,48},{48,5... | collective-permute-start | bytes 4616 | tf_op jit(solution)/shard_map/while/body/eval_jaxpr/ppermute | solution.py:15
  87.4 21.1 %collective-permute-start = (bf16[384,640]{1,0:T(8,128)(2,1)S(1)}, bf16[384,640]{1,0:T(8,128)(2,1)S(1)}, u32[]{:S(2)}, u32[]{:S(2)}) collective-permute-start(bf16[384,640]{1,0:T(8,128)(2,1)S(1)} %get-tuple-element.150), channel_id=1, source_target_pairs={{0,6},{6,12},{12,18},{18,24},{24,30},{30,36},{36,42},{42,48},{48,5... | collective-permute-start | bytes 1474568 | tf_op jit(solution)/shard_map/while/body/eval_jaxpr/ppermute | solution.py:15
  89.3 19.1 %collective-permute-start.1 = (s32[384]{0:T(512)S(1)}, s32[384]{0:T(512)S(1)}, u32[]{:S(2)}, u32[]{:S(2)}) collective-permute-start(s32[384]{0:T(512)S(1)} %get-tuple-element.151), channel_id=1, source_target_pairs={{0,6},{6,12},{12,18},{18,24},{24,30},{30,36},{36,42},{42,48},{48,5... | collective-permute-start | bytes 4616 | tf_op jit(solution)/shard_map/while/body/eval_jaxpr/ppermute | solution.py:15
  108.6 2.7 copy-start.1
  111.4 0.7 copy-start.4
  111.4 0.7 copy-start.7
  111.4 131.7 %copy-start.6 = (f32[384]{0:T(512)S(1)}, f32[384]{0:T(512)}, u32[]{:S(2)}) copy-start(f32[384]{0:T(512)} %param.14) | copy-start | bytes 4612
  111.4 131.7 %copy-start.3 = (s32[384]{0:T(512)S(1)}, s32[384]{0:T(512)}, u32[]{:S(2)}) copy-start(s32[384]{0:T(512)} %param.11) | copy-start | bytes 4612
  112.1 132.3 %copy-start.5 = (f32[384]{0:T(512)S(1)}, f32[384]{0:T(512)}, u32[]{:S(2)}) copy-start(f32[384]{0:T(512)} %param.13) | copy-start | bytes 4612
  240.9 2.4 copy-start
  254.8 36.8 %collective-permute-start.2 = (f32[384,640]{1,0:T(8,128)S(1)}, f32[384,640]{1,0:T(8,128)S(1)}, u32[]{:S(2)}, u32[]{:S(2)}) collective-permute-start(f32[384,640]{1,0:T(8,128)S(1)} %bitcast_add_fusion.3), channel_id=1, source_target_pairs={{0,762},{6,0},{12,6},{18,12},{24,18},{30,24},{36,30},{42,36},{48,4... | collective-permute-start | bytes 2949128 | tf_op jit(solution)/shard_map/while/body/eval_jaxpr/ppermute | solution.py:15
  293.0 68.6 %collective-permute-start.2 = (f32[384,640]{1,0:T(8,128)S(1)}, f32[384,640]{1,0:T(8,128)S(1)}, u32[]{:S(2)}, u32[]{:S(2)}) collective-permute-start(f32[384,640]{1,0:T(8,128)S(1)} %bitcast_add_fusion.3), channel_id=1, source_target_pairs={{0,762},{6,0},{12,6},{18,12},{24,18},{30,24},{36,30},{42,36},{48,4... | collective-permute-start | bytes 2949128 | tf_op jit(solution)/shard_map/while/body/eval_jaxpr/ppermute | solution.py:15
  362.8 43.3 %collective-permute-start.2 = (f32[384,640]{1,0:T(8,128)S(1)}, f32[384,640]{1,0:T(8,128)S(1)}, u32[]{:S(2)}, u32[]{:S(2)}) collective-permute-start(f32[384,640]{1,0:T(8,128)S(1)} %bitcast_add_fusion.3), channel_id=1, source_target_pairs={{0,762},{6,0},{12,6},{18,12},{24,18},{30,24},{36,30},{42,36},{48,4... | collective-permute-start | bytes 2949128 | tf_op jit(solution)/shard_map/while/body/eval_jaxpr/ppermute | solution.py:15
  407.4 22.7 %collective-permute-start.2 = (f32[384,640]{1,0:T(8,128)S(1)}, f32[384,640]{1,0:T(8,128)S(1)}, u32[]{:S(2)}, u32[]{:S(2)}) collective-permute-start(f32[384,640]{1,0:T(8,128)S(1)} %bitcast_add_fusion.3), channel_id=1, source_target_pairs={{0,762},{6,0},{12,6},{18,12},{24,18},{30,24},{36,30},{42,36},{48,4... | collective-permute-start | bytes 2949128 | tf_op jit(solution)/shard_map/while/body/eval_jaxpr/ppermute | solution.py:15
Sparse Core Ops, SparseCore 0:
  111.5 129.2 all-reduce.1
where the time goes:
time: 443 us; the launch traced here: 442 us
  waiting for transfers between devices  317 us (72%)
  starting transfers between devices  82.6 us (19%)
  between operations  13.5 us (3%)
  matrix products  11.7 us (3%)
  other arithmetic  10.1 us (2%)
  local copies, waits for them, and re-layouts  6.76 us (2%)
    ppermute x12, waiting for transfers between devices, passed_along(): return lax.ppermute(value, axis, pairs)  188 us
    psum x1, waiting for transfers between devices, per_device(): scores = lax.psum(partial_scores, 'tensor') * score_scale  129 us
    ppermute x12, starting transfers between devices, passed_along(): return lax.ppermute(value, axis, pairs)  82.6 us
  transfers between devices with their start and end apart: 13, of which 9 were waited for; matrix products, arithmetic and copies ran while one was open for 0% of the time, Pallas kernels for 0%

commit v1 on v0

v1 whole, which is shorter than its diff:
```python
import math

import jax
import jax.numpy as jnp
from jax import lax
from jax.sharding import PartitionSpec as P

KW = 3840
SEG = 384
BF = jnp.bfloat16
F32 = jnp.float32


def dp_shift(value, steps):
    count = lax.axis_size("dp")
    return lax.ppermute(value, "dp", [(i, (i + steps) % count) for i in range(count)])


def core_swap(value):
    count = lax.axis_size("dp")
    return lax.ppermute(value, "dp", [(i, i ^ 1) for i in range(count)])


def triple_shift(value, steps):
    pairs = [(3 * u + v, 3 * u + (v + steps) % 3) for u in range(2) for v in range(3)]
    return lax.ppermute(value, "tensor", pairs)


def triple_swap(value):
    return lax.ppermute(value, "tensor", [(r, (r + 3) % 6) for r in range(6)])


def rows_of(value, start, size):
    return lax.dynamic_slice_in_dim(value, start, size, 0)


def partial_of(queries, keys):
    return lax.dot_general(queries, keys, (((1,), (1,)), ((), ())), preferred_element_type=F32)


def reduced(hidden, keys, u, v):
    def group(steps):
        return partial_of(rows_of(hidden, ((v + steps) % 3) * 128, 128), keys)

    first = triple_shift(group(1), 1)
    second = triple_shift(group(2), 2)
    total = group(0) + first + second
    other = triple_swap(rows_of(total, (1 - u) * 64, 64))
    return rows_of(total, u * 64, 64) + other


def normalizer(parts, outside):
    peak = outside
    for scores, allowed in parts:
        peak = jnp.maximum(peak, jnp.max(jnp.where(allowed, scores, -1e30), axis=1))
    total = jnp.exp(outside - peak)
    for scores, allowed in parts:
        total = total + jnp.sum(jnp.where(allowed, jnp.exp(scores - peak[:, None]), 0.0), axis=1)
    return peak + jnp.log(total)


def gathered(mine, u, v):
    other = triple_swap(mine)
    low = jnp.where(u == 0, mine, other)
    high = jnp.where(u == 0, other, mine)
    group = jnp.concatenate([low, high], axis=0)
    first = triple_shift(group, 1)
    second = triple_shift(group, 2)
    full = jnp.zeros((SEG, mine.shape[1]), BF)
    full = lax.dynamic_update_slice_in_dim(full, group, v * 128, 0)
    full = lax.dynamic_update_slice_in_dim(full, first, ((v + 2) % 3) * 128, 0)
    return lax.dynamic_update_slice_in_dim(full, second, ((v + 1) % 3) * 128, 0)


def key_grad(slopes, hidden):
    return lax.dot_general(slopes, hidden, (((0,), (0,)), ((), ())), preferred_element_type=F32)


def per_device(hidden, targets, padding, gold_logit, vocab_lse, cotangent):
    score_scale = 1.0 / math.sqrt(KW)
    core = lax.axis_index("dp") % 2
    r = lax.axis_index("tensor")
    u, v = r // 3, r % 3
    label_code = jnp.where(padding == 1, targets, -1)
    weight = cotangent * padding.astype(F32)

    far = dp_shift(hidden, 2)
    near = dp_shift(hidden, 4)
    far_label = dp_shift(label_code, 2)
    near_label = dp_shift(label_code, 4)
    near_pair = core_swap(jnp.where(core == 0, hidden, near))
    far_pair = core_swap(far)
    pair_labels = core_swap(jnp.stack([jnp.where(core == 0, label_code, near_label), far_label]))

    near_keys = jnp.concatenate([near, near_pair], axis=0)
    far_keys = jnp.concatenate([far, far_pair], axis=0)
    near_labels = jnp.concatenate([near_label, pair_labels[0]])
    far_labels = jnp.concatenate([far_label, pair_labels[1]])

    near_scores = reduced(hidden, near_keys, u, v) * score_scale
    far_scores = reduced(hidden, far_keys, u, v) * score_scale

    base = v * 128 + u * 64
    row_targets = rows_of(targets, base, 64)
    parts = []
    for scores, labels in ((near_scores, near_labels), (far_scores, far_labels)):
        usable = jnp.broadcast_to((labels >= 0)[None], scores.shape)
        matches = usable & (labels[None] == row_targets[:, None])
        parts.append((scores, usable, matches))
    total_lse = normalizer([(s, a) for s, a, m in parts], rows_of(vocab_lse, base, 64))
    pos_lse = normalizer([(s, m) for s, a, m in parts], rows_of(gold_logit, base, 64))
    row_weight = rows_of(weight, base, 64)
    slopes = []
    for scores, usable, matches in parts:
        spread = jnp.where(usable, jnp.exp(scores - total_lse[:, None]), 0.0) - jnp.where(
            matches, jnp.exp(scores - pos_lse[:, None]), 0.0
        )
        slopes.append((row_weight[:, None] * spread * score_scale).astype(BF))
    full = gathered(jnp.concatenate(slopes, axis=1), u, v)

    far_back = core_swap(key_grad(full[:, 3 * SEG :], hidden).astype(BF))
    far_sum = key_grad(full[:, 2 * SEG : 3 * SEG], hidden) + far_back.astype(F32)
    far_home = dp_shift(far_sum.astype(BF), -2)
    near_back = core_swap(key_grad(full[:, SEG : 2 * SEG], hidden).astype(BF)).astype(F32)
    near_sum = key_grad(full[:, :SEG], hidden) + jnp.where(core == 1, near_back, 0.0)
    near_home = dp_shift(near_sum.astype(BF), -4)
    query_grad = jnp.dot(full[:, : 2 * SEG], near_keys, preferred_element_type=F32)
    query_grad = query_grad + jnp.dot(full[:, 2 * SEG :], far_keys, preferred_element_type=F32)
    query_grad = query_grad + jnp.where(core == 0, near_back, 0.0)
    return (query_grad + near_home.astype(F32) + far_home.astype(F32)).astype(BF)


def solution(mesh):
    placed = (P("dp", "tensor"), P("dp"), P("dp"), P("dp"), P("dp"), P("dp"))
    return jax.shard_map(
        per_device, mesh=mesh, in_specs=placed, out_specs=P("dp", "tensor"), check_vma=False
    )
```

time: 443 us -> 225 us (0.51)
  the two profiles are of different devices: /device:TPU:78 before, /device:TPU:1 now
where the time goes in v1:
time: 225 us; the launch traced here: 224 us
  starting transfers between devices  124 us (55%)
  waiting for transfers between devices  85.9 us (38%)
  matrix products  9.09 us (4%)
  other arithmetic  3.06 us (1%)
    ppermute x6, starting transfers between devices, triple_shift(): return lax.ppermute(value, 'tensor', pairs)  44.8 us
    ppermute x6, waiting for transfers between devices, dp_shift(): lax.ppermute(value, 'dp', [(i, (i + steps) % count) for i in range(count)])  41.9 us
    ppermute x6, starting transfers between devices, dp_shift(): lax.ppermute(value, 'dp', [(i, (i + steps) % count) for i in range(count)])  36.2 us
    ppermute x6, waiting for transfers between devices, triple_shift(): return lax.ppermute(value, 'tensor', pairs)  34.5 us
    ppermute x3, starting transfers between devices, triple_swap(): return lax.ppermute(value, 'tensor', [(r, (r + 3) % 6) for r in range(6)])  28.1 us
    ppermute x5, starting transfers between devices, core_swap(): return lax.ppermute(value, 'dp', [(i, i ^ 1) for i in range(count)])  14.9 us
    ppermute x3, waiting for transfers between devices, triple_swap(): return lax.ppermute(value, 'tensor', [(r, (r + 3) % 6) for r in range(6)])  9.47 us
    dot_general x4, matrix products, key_grad(): lax.dot_general(slopes, hidden, (((0,), (0,)), ((), ())), preferred_eleme...  4.53 us
  transfers between devices with their start and end apart: 20, of which 12 were waited for; matrix products, arithmetic and copies ran while one was open for 4% of the time, Pallas kernels for 0%

profile of v1, /device:TPU:1, one launch (start us, length us, event | category | flops | bytes accessed | tf_op | source)
XLA Modules:
  0.0 223.8 jit_solution(7888780845821991166)
XLA Ops:
  0.0 15.7 %collective-permute-start.8 = (bf16[384,640]{1,0:T(8,128)(2,1)}, bf16[384,640]{1,0:T(8,128)(2,1)S(1)}, u32[]{:S(2)}, u32[]{:S(2)}) collective-permute-start(bf16[384,640]{1,0:T(8,128)(2,1)} %param.6), channel_id=1, source_target_pairs={{0,12},{6,18},{12,24},{18,30},{24,36},{30,42},{36,48},{42,54},{48,... | collective-permute-start | bytes 1474568 | tf_op jit(solution)/shard_map/ppermute | solution.py:16
  16.4 1.9 collective-permute-start.1
  18.3 3.1 %collective-permute-start = (s32[384]{0:T(512)S(1)}, s32[384]{0:T(512)S(1)}, u32[]{:S(2)}, u32[]{:S(2)}) collective-permute-start(s32[384]{0:T(512)S(1)} %compare_select_fusion), channel_id=1, source_target_pairs={{0,24},{6,30},{12,36},{18,42},{24,48},{30,54},{36,60},{42,66},{48,... | collective-permute-start | bytes 4616 | tf_op jit(solution)/shard_map/ppermute | solution.py:16
  21.4 3.1 %collective-permute-start.3 = (bf16[384,640]{1,0:T(8,128)(2,1)}, bf16[384,640]{1,0:T(8,128)(2,1)S(1)}, u32[]{:S(2)}, u32[]{:S(2)}) collective-permute-start(bf16[384,640]{1,0:T(8,128)(2,1)} %param.6), channel_id=1, source_target_pairs={{0,24},{6,30},{12,36},{18,42},{24,48},{30,54},{36,60},{42,66},{48,... | collective-permute-start | bytes 1474568 | tf_op jit(solution)/shard_map/ppermute | solution.py:16
  27.1 4.5 %collective-permute-done.1 = s32[384]{0:T(512)S(1)} collective-permute-done((s32[384]{0:T(512)S(1)}, s32[384]{0:T(512)S(1)}, u32[]{:S(2)}, u32[]{:S(2)}) %collective-permute-start.1) | collective-permute-done | bytes 1568 | tf_op jit(solution)/shard_map/ppermute | solution.py:16
  31.6 4.5 %collective-permute-start.9 = (bf16[384,640]{1,0:T(8,128)(2,1)S(1)}, bf16[384,640]{1,0:T(8,128)(2,1)S(1)}, u32[]{:S(2)}, u32[]{:S(2)}) collective-permute-start(bf16[384,640]{1,0:T(8,128)(2,1)S(1)} %collective-permute-done.8), channel_id=1, source_target_pairs={{0,6},{6,0},{12,18},{18,12},{24,30},{30,24},{36,42},{42,36},{48,54... | collective-permute-start | bytes 1474568 | tf_op jit(solution)/shard_map/ppermute | solution.py:21
  36.2 1.9 collective-permute-start.2
  38.1 4.9 %collective-permute-done.3 = bf16[384,640]{1,0:T(8,128)(2,1)S(1)} collective-permute-done((bf16[384,640]{1,0:T(8,128)(2,1)}, bf16[384,640]{1,0:T(8,128)(2,1)S(1)}, u32[]{:S(2)}, u32[]{:S(2)}) %collective-permute-start.3) | collective-permute-done | bytes 491552 | tf_op jit(solution)/shard_map/ppermute | solution.py:16
  43.2 4.1 %collective-permute-start.4 = (bf16[384,640]{1,0:T(8,128)(2,1)S(1)}, bf16[384,640]{1,0:T(8,128)(2,1)S(1)}, u32[]{:S(2)}, u32[]{:S(2)}) collective-permute-start(bf16[384,640]{1,0:T(8,128)(2,1)S(1)} %get-tuple-element.19), channel_id=1, source_target_pairs={{0,6},{6,0},{12,18},{18,12},{24,30},{30,24},{36,42},{42,36},{48,54... | collective-permute-start | bytes 1474568 | tf_op jit(solution)/shard_map/ppermute | solution.py:21
  47.9 18.1 %collective-permute-start.10 = (f32[128,768]{1,0:T(8,128)S(1)}, f32[128,768]{1,0:T(8,128)S(1)}, u32[]{:S(2)}, u32[]{:S(2)}) collective-permute-start(f32[128,768]{1,0:T(8,128)S(1)} %fusion.18), channel_id=1, source_target_pairs={{0,1},{1,2},{2,0},{3,4},{4,5},{5,3},{6,7},{7,8},{8,6},{9,10},{10,1... | collective-permute-start | bytes 1179656 | tf_op jit(solution)/shard_map/ppermute | solution.py:26
  66.4 1.9 collective-permute-start.11
  69.3 3.4 %collective-permute-start.5 = (f32[128,768]{1,0:T(8,128)S(1)}, f32[128,768]{1,0:T(8,128)S(1)}, u32[]{:S(2)}, u32[]{:S(2)}) collective-permute-start(f32[128,768]{1,0:T(8,128)S(1)} %fusion.20), channel_id=1, source_target_pairs={{0,1},{1,2},{2,0},{3,4},{4,5},{5,3},{6,7},{7,8},{8,6},{9,10},{10,1... | collective-permute-start | bytes 1179656 | tf_op jit(solution)/shard_map/ppermute | solution.py:26
  72.6 2.8 %collective-permute-start.6 = (f32[128,768]{1,0:T(8,128)S(1)}, f32[128,768]{1,0:T(8,128)S(1)}, u32[]{:S(2)}, u32[]{:S(2)}) collective-permute-start(f32[128,768]{1,0:T(8,128)S(1)} %fusion.16), channel_id=1, source_target_pairs={{0,2},{1,0},{2,1},{3,5},{4,3},{5,4},{6,8},{7,6},{8,7},{9,11},{10,9... | collective-permute-start | bytes 1179656 | tf_op jit(solution)/shard_map/ppermute | solution.py:26
  76.0 7.0 %collective-permute-done.11 = f32[128,768]{1,0:T(8,128)S(1)} collective-permute-done((f32[128,768]{1,0:T(8,128)S(1)}, f32[128,768]{1,0:T(8,128)S(1)}, u32[]{:S(2)}, u32[]{:S(2)}) %collective-permute-start.11) | collective-permute-done | bytes 393248 | tf_op jit(solution)/shard_map/ppermute | solution.py:26
  83.1 5.4 %collective-permute-start.12 = (f32[64,768]{1,0:T(8,128)S(1)}, f32[64,768]{1,0:T(8,128)S(1)}, u32[]{:S(2)}, u32[]{:S(2)}) collective-permute-start(f32[64,768]{1,0:T(8,128)S(1)} %constant_dynamic-slice_fusion), channel_id=1, source_target_pairs={{0,3},{1,4},{2,5},{3,0},{4,1},{5,2},{6,9},{7,10},{8,11},{9,6},{10,... | collective-permute-start | bytes 589832 | tf_op jit(solution)/shard_map/ppermute | solution.py:30
  88.5 3.0 %collective-permute-done.5 = f32[128,768]{1,0:T(8,128)S(1)} collective-permute-done((f32[128,768]{1,0:T(8,128)S(1)}, f32[128,768]{1,0:T(8,128)S(1)}, u32[]{:S(2)}, u32[]{:S(2)}) %collective-permute-start.5) | collective-permute-done | bytes 393248 | tf_op jit(solution)/shard_map/ppermute | solution.py:26
  91.4 8.5 %collective-permute-done.6 = f32[128,768]{1,0:T(8,128)S(1)} collective-permute-done((f32[128,768]{1,0:T(8,128)S(1)}, f32[128,768]{1,0:T(8,128)S(1)}, u32[]{:S(2)}, u32[]{:S(2)}) %collective-permute-start.6) | collective-permute-done | bytes 393248 | tf_op jit(solution)/shard_map/ppermute | solution.py:26
  100.4 17.8 %collective-permute-start.7 = (f32[64,768]{1,0:T(8,128)S(1)}, f32[64,768]{1,0:T(8,128)S(1)}, u32[]{:S(2)}, u32[]{:S(2)}) collective-permute-start(f32[64,768]{1,0:T(8,128)S(1)} %constant_dynamic-slice_fusion.1), channel_id=1, source_target_pairs={{0,3},{1,4},{2,5},{3,0},{4,1},{5,2},{6,9},{7,10},{8,11},{9,6},{10,... | collective-permute-start | bytes 589832 | tf_op jit(solution)/shard_map/ppermute | solution.py:30
  118.3 4.3 %collective-permute-done.7 = f32[64,768]{1,0:T(8,128)S(1)} collective-permute-done((f32[64,768]{1,0:T(8,128)S(1)}, f32[64,768]{1,0:T(8,128)S(1)}, u32[]{:S(2)}, u32[]{:S(2)}) %collective-permute-start.7) | collective-permute-done | bytes 196640 | tf_op jit(solution)/shard_map/ppermute | solution.py:30
  123.9 4.8 %collective-permute-start.13 = (bf16[64,1536]{1,0:T(8,128)(2,1)S(1)}, bf16[64,1536]{1,0:T(8,128)(2,1)S(1)}, u32[]{:S(2)}, u32[]{:S(2)}) collective-permute-start(bf16[64,1536]{1,0:T(8,128)(2,1)S(1)} %pad_maximum_fusion.1), channel_id=1, source_target_pairs={{0,3},{1,4},{2,5},{3,0},{4,1},{5,2},{6,9},{7,10},{8,11},{9,6},{10,... | collective-permute-start | bytes 589832 | tf_op jit(solution)/shard_map/ppermute | solution.py:30
  128.7 5.2 %collective-permute-done.13 = bf16[64,1536]{1,0:T(8,128)(2,1)S(1)} collective-permute-done((bf16[64,1536]{1,0:T(8,128)(2,1)S(1)}, bf16[64,1536]{1,0:T(8,128)(2,1)S(1)}, u32[]{:S(2)}, u32[]{:S(2)}) %collective-permute-start.13) | collective-permute-done | bytes 196640 | tf_op jit(solution)/shard_map/ppermute | solution.py:30
  134.1 1.9 collective-permute-start.14
  136.0 16.7 %collective-permute-start.15 = (bf16[128,1536]{1,0:T(8,128)(2,1)S(1)}, bf16[128,1536]{1,0:T(8,128)(2,1)S(1)}, u32[]{:S(2)}, u32[]{:S(2)}) collective-permute-start(bf16[128,1536]{1,0:T(8,128)(2,1)S(1)} %get-tuple-element.21), channel_id=1, source_target_pairs={{0,2},{1,0},{2,1},{3,5},{4,3},{5,4},{6,8},{7,6},{8,7},{9,11},{10,9... | collective-permute-start | bytes 1179656 | tf_op jit(solution)/shard_map/ppermute | solution.py:26
  152.8 6.5 %collective-permute-done.14 = bf16[128,1536]{1,0:T(8,128)(2,1)S(1)} collective-permute-done((bf16[128,1536]{1,0:T(8,128)(2,1)S(1)}, bf16[128,1536]{1,0:T(8,128)(2,1)S(1)}, u32[]{:S(2)}, u32[]{:S(2)}) %collective-permute-start.14) | collective-permute-done | bytes 393248 | tf_op jit(solution)/shard_map/ppermute | solution.py:26
  159.3 9.5 %collective-permute-done.15 = bf16[128,1536]{1,0:T(8,128)(2,1)S(1)} collective-permute-done((bf16[128,1536]{1,0:T(8,128)(2,1)S(1)}, bf16[128,1536]{1,0:T(8,128)(2,1)S(1)}, u32[]{:S(2)}, u32[]{:S(2)}) %collective-permute-start.15) | collective-permute-done | bytes 393248 | tf_op jit(solution)/shard_map/ppermute | solution.py:26
  170.1 2.4 %collective-permute-start.16 = (bf16[384,640]{1,0:T(8,128)(2,1)}, bf16[384,640]{1,0:T(8,128)(2,1)S(1)}, u32[]{:S(2)}, u32[]{:S(2)}) collective-permute-start(bf16[384,640]{1,0:T(8,128)(2,1)} %convolution_convert_fusion.1), channel_id=1, source_target_pairs={{0,6},{6,0},{12,18},{18,12},{24,30},{30,24},{36,42},{42,36},{48,54... | collective-permute-start | bytes 1474568 | tf_op jit(solution)/shard_map/ppermute | solution.py:21
  173.8 1.9 collective-permute-start.18
  175.7 1.5 fusion.4
  177.3 1.9 collective-permute-start.17
  179.7 10.4 %collective-permute-start.19 = (bf16[384,640]{1,0:T(8,128)(2,1)S(1)}, bf16[384,640]{1,0:T(8,128)(2,1)S(1)}, u32[]{:S(2)}, u32[]{:S(2)}) collective-permute-start(bf16[384,640]{1,0:T(8,128)(2,1)S(1)} %fusion.5), channel_id=1, source_target_pairs={{0,756},{6,762},{12,0},{18,6},{24,12},{30,18},{36,24},{42,30},{48,... | collective-permute-start | bytes 1474568 | tf_op jit(solution)/shard_map/ppermute | solution.py:16
  191.5 30.9 %collective-permute-done.19 = bf16[384,640]{1,0:T(8,128)(2,1)S(1)} collective-permute-done((bf16[384,640]{1,0:T(8,128)(2,1)S(1)}, bf16[384,640]{1,0:T(8,128)(2,1)S(1)}, u32[]{:S(2)}, u32[]{:S(2)}) %collective-permute-start.19) | collective-permute-done | bytes 491552 | tf_op jit(solution)/shard_map/ppermute | solution.py:16
  222.4 1.4 fusion.3
  (61 shorter events, 12.0 us)
Async XLA Ops:
  0.0 31.6 %collective-permute-start.8 = (bf16[384,640]{1,0:T(8,128)(2,1)}, bf16[384,640]{1,0:T(8,128)(2,1)S(1)}, u32[]{:S(2)}, u32[]{:S(2)}) collective-permute-start(bf16[384,640]{1,0:T(8,128)(2,1)} %param.6), channel_id=1, source_target_pairs={{0,12},{6,18},{12,24},{18,30},{24,36},{30,42},{36,48},{42,54},{48,... | collective-permute-start | bytes 1474568 | tf_op jit(solution)/shard_map/ppermute | solution.py:16
  16.4 15.2 %collective-permute-start.1 = (s32[384]{0:T(512)S(1)}, s32[384]{0:T(512)S(1)}, u32[]{:S(2)}, u32[]{:S(2)}) collective-permute-start(s32[384]{0:T(512)S(1)} %compare_select_fusion), channel_id=1, source_target_pairs={{0,12},{6,18},{12,24},{18,30},{24,36},{30,42},{36,48},{42,54},{48,... | collective-permute-start | bytes 4616 | tf_op jit(solution)/shard_map/ppermute | solution.py:16
  18.3 8.8 %collective-permute-start = (s32[384]{0:T(512)S(1)}, s32[384]{0:T(512)S(1)}, u32[]{:S(2)}, u32[]{:S(2)}) collective-permute-start(s32[384]{0:T(512)S(1)} %compare_select_fusion), channel_id=1, source_target_pairs={{0,24},{6,30},{12,36},{18,42},{24,48},{30,54},{36,60},{42,66},{48,... | collective-permute-start | bytes 4616 | tf_op jit(solution)/shard_map/ppermute | solution.py:16
  21.4 21.6 %collective-permute-start.3 = (bf16[384,640]{1,0:T(8,128)(2,1)}, bf16[384,640]{1,0:T(8,128)(2,1)S(1)}, u32[]{:S(2)}, u32[]{:S(2)}) collective-permute-start(bf16[384,640]{1,0:T(8,128)(2,1)} %param.6), channel_id=1, source_target_pairs={{0,24},{6,30},{12,36},{18,42},{24,48},{30,54},{36,60},{42,66},{48,... | collective-permute-start | bytes 1474568 | tf_op jit(solution)/shard_map/ppermute | solution.py:16
  31.6 15.8 %collective-permute-start.9 = (bf16[384,640]{1,0:T(8,128)(2,1)S(1)}, bf16[384,640]{1,0:T(8,128)(2,1)S(1)}, u32[]{:S(2)}, u32[]{:S(2)}) collective-permute-start(bf16[384,640]{1,0:T(8,128)(2,1)S(1)} %collective-permute-done.8), channel_id=1, source_target_pairs={{0,6},{6,0},{12,18},{18,12},{24,30},{30,24},{36,42},{42,36},{48,54... | collective-permute-start | bytes 1474568 | tf_op jit(solution)/shard_map/ppermute | solution.py:21
  36.2 39.3 %collective-permute-start.2 = (s32[2,384]{1,0:T(2,128)S(1)}, s32[2,384]{1,0:T(2,128)S(1)}, u32[]{:S(2)}, u32[]{:S(2)}) collective-permute-start(s32[2,384]{1,0:T(2,128)S(1)} %pad_add_fusion.2), channel_id=1, source_target_pairs={{0,6},{6,0},{12,18},{18,12},{24,30},{30,24},{36,42},{42,36},{48,54... | collective-permute-start | bytes 9224 | tf_op jit(solution)/shard_map/ppermute | solution.py:21
  43.2 4.3 %copy-start = (bf16[384,640]{1,0:T(8,128)(2,1)S(1)}, bf16[384,640]{1,0:T(8,128)(2,1)}, u32[]{:S(2)}) copy-start(bf16[384,640]{1,0:T(8,128)(2,1)} %param.6) | copy-start | bytes 1474564
  43.2 25.2 %collective-permute-start.4 = (bf16[384,640]{1,0:T(8,128)(2,1)S(1)}, bf16[384,640]{1,0:T(8,128)(2,1)S(1)}, u32[]{:S(2)}, u32[]{:S(2)}) collective-permute-start(bf16[384,640]{1,0:T(8,128)(2,1)S(1)} %get-tuple-element.19), channel_id=1, source_target_pairs={{0,6},{6,0},{12,18},{18,12},{24,30},{30,24},{36,42},{42,36},{48,54... | collective-permute-start | bytes 1474568 | tf_op jit(solution)/shard_map/ppermute | solution.py:21
  47.9 27.6 %collective-permute-start.10 = (f32[128,768]{1,0:T(8,128)S(1)}, f32[128,768]{1,0:T(8,128)S(1)}, u32[]{:S(2)}, u32[]{:S(2)}) collective-permute-start(f32[128,768]{1,0:T(8,128)S(1)} %fusion.18), channel_id=1, source_target_pairs={{0,1},{1,2},{2,0},{3,4},{4,5},{5,3},{6,7},{7,8},{8,6},{9,10},{10,1... | collective-permute-start | bytes 1179656 | tf_op jit(solution)/shard_map/ppermute | solution.py:26
  66.4 16.6 %collective-permute-start.11 = (f32[128,768]{1,0:T(8,128)S(1)}, f32[128,768]{1,0:T(8,128)S(1)}, u32[]{:S(2)}, u32[]{:S(2)}) collective-permute-start(f32[128,768]{1,0:T(8,128)S(1)} %fusion.14), channel_id=1, source_target_pairs={{0,2},{1,0},{2,1},{3,5},{4,3},{5,4},{6,8},{7,6},{8,7},{9,11},{10,9... | collective-permute-start | bytes 1179656 | tf_op jit(solution)/shard_map/ppermute | solution.py:26
  69.3 22.1 %collective-permute-start.5 = (f32[128,768]{1,0:T(8,128)S(1)}, f32[128,768]{1,0:T(8,128)S(1)}, u32[]{:S(2)}, u32[]{:S(2)}) collective-permute-start(f32[128,768]{1,0:T(8,128)S(1)} %fusion.20), channel_id=1, source_target_pairs={{0,1},{1,2},{2,0},{3,4},{4,5},{5,3},{6,7},{7,8},{8,6},{9,10},{10,1... | collective-permute-start | bytes 1179656 | tf_op jit(solution)/shard_map/ppermute | solution.py:26
  72.6 27.2 %collective-permute-start.6 = (f32[128,768]{1,0:T(8,128)S(1)}, f32[128,768]{1,0:T(8,128)S(1)}, u32[]{:S(2)}, u32[]{:S(2)}) collective-permute-start(f32[128,768]{1,0:T(8,128)S(1)} %fusion.16), channel_id=1, source_target_pairs={{0,2},{1,0},{2,1},{3,5},{4,3},{5,4},{6,8},{7,6},{8,7},{9,11},{10,9... | collective-permute-start | bytes 1179656 | tf_op jit(solution)/shard_map/ppermute | solution.py:26
  83.1 35.2 %collective-permute-start.12 = (f32[64,768]{1,0:T(8,128)S(1)}, f32[64,768]{1,0:T(8,128)S(1)}, u32[]{:S(2)}, u32[]{:S(2)}) collective-permute-start(f32[64,768]{1,0:T(8,128)S(1)} %constant_dynamic-slice_fusion), channel_id=1, source_target_pairs={{0,3},{1,4},{2,5},{3,0},{4,1},{5,2},{6,9},{7,10},{8,11},{9,6},{10,... | collective-permute-start | bytes 589832 | tf_op jit(solution)/shard_map/ppermute | solution.py:30
  100.3 22.5 %copy-start.3 = (f32[384]{0:T(512)S(1)}, f32[384]{0:T(512)}, u32[]{:S(2)}) copy-start(f32[384]{0:T(512)} %param.10) | copy-start | bytes 4612
  100.3 22.6 %copy-start.4 = (f32[384]{0:T(512)S(1)}, f32[384]{0:T(512)}, u32[]{:S(2)}) copy-start(f32[384]{0:T(512)} %param.9) | copy-start | bytes 4612
  100.4 22.2 %collective-permute-start.7 = (f32[64,768]{1,0:T(8,128)S(1)}, f32[64,768]{1,0:T(8,128)S(1)}, u32[]{:S(2)}, u32[]{:S(2)}) collective-permute-start(f32[64,768]{1,0:T(8,128)S(1)} %constant_dynamic-slice_fusion.1), channel_id=1, source_target_pairs={{0,3},{1,4},{2,5},{3,0},{4,1},{5,2},{6,9},{7,10},{8,11},{9,6},{10,... | collective-permute-start | bytes 589832 | tf_op jit(solution)/shard_map/ppermute | solution.py:30
  123.9 10.0 %collective-permute-start.13 = (bf16[64,1536]{1,0:T(8,128)(2,1)S(1)}, bf16[64,1536]{1,0:T(8,128)(2,1)S(1)}, u32[]{:S(2)}, u32[]{:S(2)}) collective-permute-start(bf16[64,1536]{1,0:T(8,128)(2,1)S(1)} %pad_maximum_fusion.1), channel_id=1, source_target_pairs={{0,3},{1,4},{2,5},{3,0},{4,1},{5,2},{6,9},{7,10},{8,11},{9,6},{10,... | collective-permute-start | bytes 589832 | tf_op jit(solution)/shard_map/ppermute | solution.py:30
  134.1 25.2 %collective-permute-start.14 = (bf16[128,1536]{1,0:T(8,128)(2,1)S(1)}, bf16[128,1536]{1,0:T(8,128)(2,1)S(1)}, u32[]{:S(2)}, u32[]{:S(2)}) collective-permute-start(bf16[128,1536]{1,0:T(8,128)(2,1)S(1)} %get-tuple-element.21), channel_id=1, source_target_pairs={{0,1},{1,2},{2,0},{3,4},{4,5},{5,3},{6,7},{7,8},{8,6},{9,10},{10,1... | collective-permute-start | bytes 1179656 | tf_op jit(solution)/shard_map/ppermute | solution.py:26
  136.0 32.8 %collective-permute-start.15 = (bf16[128,1536]{1,0:T(8,128)(2,1)S(1)}, bf16[128,1536]{1,0:T(8,128)(2,1)S(1)}, u32[]{:S(2)}, u32[]{:S(2)}) collective-permute-start(bf16[128,1536]{1,0:T(8,128)(2,1)S(1)} %get-tuple-element.21), channel_id=1, source_target_pairs={{0,2},{1,0},{2,1},{3,5},{4,3},{5,4},{6,8},{7,6},{8,7},{9,11},{10,9... | collective-permute-start | bytes 1179656 | tf_op jit(solution)/shard_map/ppermute | solution.py:26
  168.9 4.9 %copy-start.1 = (bf16[384,1536]{1,0:T(8,128)(2,1)}, bf16[384,1536]{1,0:T(8,128)(2,1)S(1)}, u32[]{:S(2)}) copy-start(bf16[384,1536]{1,0:T(8,128)(2,1)S(1)} %constant_dynamic-update-slice_fusion.4) | copy-start | bytes 3538948
  170.1 5.6 %collective-permute-start.16 = (bf16[384,640]{1,0:T(8,128)(2,1)}, bf16[384,640]{1,0:T(8,128)(2,1)S(1)}, u32[]{:S(2)}, u32[]{:S(2)}) collective-permute-start(bf16[384,640]{1,0:T(8,128)(2,1)} %convolution_convert_fusion.1), channel_id=1, source_target_pairs={{0,6},{6,0},{12,18},{18,12},{24,30},{30,24},{36,42},{42,36},{48,54... | collective-permute-start | bytes 1474568 | tf_op jit(solution)/shard_map/ppermute | solution.py:21
  173.8 5.4 %collective-permute-start.18 = (bf16[384,640]{1,0:T(8,128)(2,1)}, bf16[384,640]{1,0:T(8,128)(2,1)S(1)}, u32[]{:S(2)}, u32[]{:S(2)}) collective-permute-start(bf16[384,640]{1,0:T(8,128)(2,1)} %convolution_convert_fusion), channel_id=1, source_target_pairs={{0,6},{6,0},{12,18},{18,12},{24,30},{30,24},{36,42},{42,36},{48,54... | collective-permute-start | bytes 1474568 | tf_op jit(solution)/shard_map/ppermute | solution.py:21
  175.7 3.5 %copy-start.2 = (bf16[384,1536]{1,0:T(8,128)(2,1)S(1)}, bf16[384,1536]{1,0:T(8,128)(2,1)}, u32[]{:S(2)}) copy-start(bf16[384,1536]{1,0:T(8,128)(2,1)} %copy-done.1) | copy-start | bytes 3538948
  177.3 14.2 %collective-permute-start.17 = (bf16[384,640]{1,0:T(8,128)(2,1)S(1)}, bf16[384,640]{1,0:T(8,128)(2,1)S(1)}, u32[]{:S(2)}, u32[]{:S(2)}) collective-permute-start(bf16[384,640]{1,0:T(8,128)(2,1)S(1)} %fusion.4), channel_id=1, source_target_pairs={{0,744},{6,750},{12,756},{18,762},{24,0},{30,6},{36,12},{42,18},{4... | collective-permute-start | bytes 1474568 | tf_op jit(solution)/shard_map/ppermute | solution.py:16
  179.7 42.6 %collective-permute-start.19 = (bf16[384,640]{1,0:T(8,128)(2,1)S(1)}, bf16[384,640]{1,0:T(8,128)(2,1)S(1)}, u32[]{:S(2)}, u32[]{:S(2)}) collective-permute-start(bf16[384,640]{1,0:T(8,128)(2,1)S(1)} %fusion.5), channel_id=1, source_target_pairs={{0,756},{6,762},{12,0},{18,6},{24,12},{30,18},{36,24},{42,30},{48,... | collective-permute-start | bytes 1474568 | tf_op jit(solution)/shard_map/ppermute | solution.py:16

commit v2 on v1

v2 whole, which is shorter than its diff:
```python
import math

import jax
import jax.numpy as jnp
from jax import lax
from jax.sharding import PartitionSpec as P

KW = 3840
SEG = 384
BF = jnp.bfloat16
F32 = jnp.float32


def dp_shift(value, steps):
    count = lax.axis_size("dp")
    return lax.ppermute(value, "dp", [(i, (i + steps) % count) for i in range(count)])


def core_swap(value):
    count = lax.axis_size("dp")
    return lax.ppermute(value, "dp", [(i, i ^ 1) for i in range(count)])


def odd_keys(value):
    count = lax.axis_size("dp")
    return lax.ppermute(value, "dp", [(i, (i + (1 if i % 2 == 0 else 3)) % count) for i in range(count)])


def odd_home(value):
    count = lax.axis_size("dp")
    return lax.ppermute(value, "dp", [((i + (1 if i % 2 == 0 else 3)) % count, i) for i in range(count)])


def triple_shift(value, steps):
    pairs = [(3 * u + v, 3 * u + (v + steps) % 3) for u in range(2) for v in range(3)]
    return lax.ppermute(value, "tensor", pairs)


def triple_swap(value):
    return lax.ppermute(value, "tensor", [(r, (r + 3) % 6) for r in range(6)])


def rows_of(value, start, size):
    return lax.dynamic_slice_in_dim(value, start, size, 0)


def partial_of(queries, keys):
    return lax.dot_general(queries, keys, (((1,), (1,)), ((), ())), preferred_element_type=F32)


def after(value, *others):
    return lax.optimization_barrier((value,) + others)[0]


def outgoing(hidden, keys, v):
    return tuple(
        partial_of(rows_of(hidden, ((v + steps) % 3) * 128, 128), keys) for steps in (1, 2)
    )


def normalizer(parts, outside):
    peak = outside
    for scores, allowed in parts:
        peak = jnp.maximum(peak, jnp.max(jnp.where(allowed, scores, -1e30), axis=1))
    total = jnp.exp(outside - peak)
    for scores, allowed in parts:
        total = total + jnp.sum(jnp.where(allowed, jnp.exp(scores - peak[:, None]), 0.0), axis=1)
    return peak + jnp.log(total)


def row_group(mine, other, u):
    low = jnp.where(u == 0, mine, other)
    high = jnp.where(u == 0, other, mine)
    return jnp.concatenate([low, high], axis=0)


def all_rows(group, first, second, v):
    full = jnp.zeros((SEG, group.shape[1]), BF)
    full = lax.dynamic_update_slice_in_dim(full, group, v * 128, 0)
    full = lax.dynamic_update_slice_in_dim(full, first, ((v + 2) % 3) * 128, 0)
    return lax.dynamic_update_slice_in_dim(full, second, ((v + 1) % 3) * 128, 0)


def key_grad(slopes, hidden):
    return lax.dot_general(slopes, hidden, (((0,), (0,)), ((), ())), preferred_element_type=F32)


def per_device(hidden, targets, padding, gold_logit, vocab_lse, cotangent):
    score_scale = 1.0 / math.sqrt(KW)
    core = lax.axis_index("dp") % 2
    r = lax.axis_index("tensor")
    u, v = r // 3, r % 3
    label_code = jnp.where(padding == 1, targets, -1)
    weight = cotangent * padding.astype(F32)

    far = dp_shift(hidden, 2)
    near = dp_shift(hidden, 4)
    odd = odd_keys(hidden)
    late_code = after(label_code, near)
    far_label = dp_shift(late_code, 2)
    near_labels = jnp.concatenate([dp_shift(late_code, 4), odd_keys(late_code)])
    far_labels = jnp.concatenate([far_label, core_swap(far_label)])
    own_rows = rows_of(hidden, v * 128, 128)

    near_keys = jnp.concatenate([near, odd], axis=0)
    near_out = outgoing(hidden, near_keys, v)
    near_group = partial_of(own_rows, near_keys)
    near_group = near_group + triple_shift(near_out[0], 1) + triple_shift(near_out[1], 2)
    near_send = rows_of(near_group, (1 - u) * 64, 64)
    near_other = triple_swap(near_send)

    far_keys = jnp.concatenate([far, core_swap(far)], axis=0)
    far_out = outgoing(hidden, far_keys, v)
    far_out = lax.optimization_barrier(far_out + (near_send,))
    far_group = partial_of(own_rows, far_keys)
    far_group = far_group + triple_shift(far_out[0], 1) + triple_shift(far_out[1], 2)
    far_other = triple_swap(rows_of(far_group, (1 - u) * 64, 64))
    near_scores = (rows_of(near_group, u * 64, 64) + near_other) * score_scale
    far_scores = (rows_of(far_group, u * 64, 64) + far_other) * score_scale

    base = v * 128 + u * 64
    row_targets = rows_of(targets, base, 64)
    parts = []
    for scores, labels in ((near_scores, near_labels), (far_scores, far_labels)):
        usable = jnp.broadcast_to((labels >= 0)[None], scores.shape)
        matches = usable & (labels[None] == row_targets[:, None])
        parts.append((scores, usable, matches))
    total_lse = normalizer([(s, a) for s, a, m in parts], rows_of(vocab_lse, base, 64))
    pos_lse = normalizer([(s, m) for s, a, m in parts], rows_of(gold_logit, base, 64))
    row_weight = rows_of(weight, base, 64)
    slopes = []
    for scores, usable, matches in parts:
        spread = jnp.where(usable, jnp.exp(scores - total_lse[:, None]), 0.0) - jnp.where(
            matches, jnp.exp(scores - pos_lse[:, None]), 0.0
        )
        slopes.append((row_weight[:, None] * spread * score_scale).astype(BF))
    near_mine, far_mine = slopes
    far_rows = row_group(far_mine, triple_swap(far_mine), u)
    near_other_rows = triple_swap(near_mine)
    far_one = triple_shift(far_rows, 1)
    far_two = triple_shift(far_rows, 2)
    near_rows = row_group(near_mine, after(near_other_rows, far_rows), u)
    near_one = triple_shift(near_rows, 1)
    near_two = triple_shift(near_rows, 2)

    far_full = all_rows(far_rows, far_one, far_two, v)
    far_back = core_swap(key_grad(far_full[:, SEG:], hidden).astype(BF))
    far_sum = key_grad(far_full[:, :SEG], hidden) + far_back.astype(F32)
    far_sum = far_sum.astype(BF)
    far_home = dp_shift(far_sum, -2)

    near_full = all_rows(near_rows, after(near_one, far_sum), near_two, v)
    near_home = dp_shift(key_grad(near_full[:, :SEG], hidden).astype(BF), -4)
    odd_back = odd_home(key_grad(near_full[:, SEG:], hidden).astype(BF))
    query_grad = jnp.dot(near_full, near_keys, preferred_element_type=F32)
    query_grad = query_grad + jnp.dot(far_full, far_keys, preferred_element_type=F32)
    home = near_home.astype(F32) + odd_back.astype(F32) + far_home.astype(F32)
    return (query_grad + home).astype(BF)


def solution(mesh):
    placed = (P("dp", "tensor"), P("dp"), P("dp"), P("dp"), P("dp"), P("dp"))
    return jax.shard_map(
        per_device, mesh=mesh, in_specs=placed, out_specs=P("dp", "tensor"), check_vma=False
    )
```

time: 225 us -> 239 us (1.062)
  the two profiles are of different devices: /device:TPU:1 before, /device:TPU:94 now
where the time goes in v2:
time: 239 us; the launch traced here: 238 us
  starting transfers between devices  139 us (58%)
  waiting for transfers between devices  84.2 us (35%)
  matrix products  8.9 us (4%)
  local copies, waits for them, and re-layouts  3.57 us (1%)
    ppermute x6, starting transfers between devices, dp_shift(): lax.ppermute(value, 'dp', [(i, (i + steps) % count) for i in range(count)])  66.7 us
    ppermute x8, starting transfers between devices, triple_shift(): return lax.ppermute(value, 'tensor', pairs)  35.4 us
    ppermute x6, waiting for transfers between devices, dp_shift(): lax.ppermute(value, 'dp', [(i, (i + steps) % count) for i in range(count)])  32.7 us
    ppermute x8, waiting for transfers between devices, triple_shift(): return lax.ppermute(value, 'tensor', pairs)  28.7 us
    ppermute x4, waiting for transfers between devices, triple_swap(): return lax.ppermute(value, 'tensor', [(r, (r + 3) % 6) for r in range(6)])  22.8 us
    ppermute x4, starting transfers between devices, triple_swap(): return lax.ppermute(value, 'tensor', [(r, (r + 3) % 6) for r in range(6)])  17.6 us
    ppermute x1, starting transfers between devices, odd_home(): lax.ppermute(value, 'dp', [((i + (1 if i % 2 == 0 else 3)) % count, i) fo...  7.13 us
    ppermute x3, starting transfers between devices, core_swap(): return lax.ppermute(value, 'dp', [(i, i ^ 1) for i in range(count)])  6.48 us
  transfers between devices with their start and end apart: 24, of which 11 were waited for; matrix products, arithmetic and copies ran while one was open for 3% of the time, Pallas kernels for 0%

profile of v2, /device:TPU:94, one launch (start us, length us, event | category | flops | bytes accessed | tf_op | source)
XLA Modules:
  0.0 237.8 jit_solution(3935090173520492055)
XLA Ops:
  0.0 4.6 %collective-permute-start = (bf16[384,640]{1,0:T(8,128)(2,1)}, bf16[384,640]{1,0:T(8,128)(2,1)S(1)}, u32[]{:S(2)}, u32[]{:S(2)}) collective-permute-start(bf16[384,640]{1,0:T(8,128)(2,1)} %param.6), channel_id=1, source_target_pairs={{0,24},{6,30},{12,36},{18,42},{24,48},{30,54},{36,60},{42,66},{48,... | collective-permute-start | bytes 1474568 | tf_op jit(solution)/shard_map/ppermute | solution.py:16
  4.6 1.9 collective-permute-start.3
  6.5 14.2 %collective-permute-start.9 = (bf16[384,640]{1,0:T(8,128)(2,1)}, bf16[384,640]{1,0:T(8,128)(2,1)S(1)}, u32[]{:S(2)}, u32[]{:S(2)}) collective-permute-start(bf16[384,640]{1,0:T(8,128)(2,1)} %param.6), channel_id=1, source_target_pairs={{0,12},{6,18},{12,24},{18,30},{24,36},{30,42},{36,48},{42,54},{48,... | collective-permute-start | bytes 1474568 | tf_op jit(solution)/shard_map/ppermute | solution.py:16
  23.8 2.6 %collective-permute-start.5 = (f32[128,768]{1,0:T(8,128)}, f32[128,768]{1,0:T(8,128)S(1)}, u32[]{:S(2)}, u32[]{:S(2)}) collective-permute-start(f32[128,768]{1,0:T(8,128)} %fusion.11), channel_id=1, source_target_pairs={{0,2},{1,0},{2,1},{3,5},{4,3},{5,4},{6,8},{7,6},{8,7},{9,11},{10,9... | collective-permute-start | bytes 1179656 | tf_op jit(solution)/shard_map/ppermute | solution.py:36
  27.6 3.4 %collective-permute-start.4 = (f32[128,768]{1,0:T(8,128)}, f32[128,768]{1,0:T(8,128)}, u32[]{:S(2)}, u32[]{:S(2)}) collective-permute-start(f32[128,768]{1,0:T(8,128)} %fusion.15), channel_id=1, source_target_pairs={{0,1},{1,2},{2,0},{3,4},{4,5},{5,3},{6,7},{7,8},{8,6},{9,10},{10,1... | collective-permute-start | bytes 1179656 | tf_op jit(solution)/shard_map/ppermute | solution.py:36
  31.2 13.2 %collective-permute-start.7 = (s32[384]{0:T(512)S(1)}, s32[384]{0:T(512)S(1)}, u32[]{:S(2)}, u32[]{:S(2)}) collective-permute-start(s32[384]{0:T(512)S(1)} %compare_select_fusion), channel_id=1, source_target_pairs={{0,12},{6,18},{12,24},{18,30},{24,36},{30,42},{36,48},{42,54},{48,... | collective-permute-start | bytes 4616 | tf_op jit(solution)/shard_map/ppermute | solution.py:16
  44.4 7.9 %collective-permute-start.1 = (s32[384]{0:T(512)S(1)}, s32[384]{0:T(512)S(1)}, u32[]{:S(2)}, u32[]{:S(2)}) collective-permute-start(s32[384]{0:T(512)S(1)} %compare_select_fusion), channel_id=1, source_target_pairs={{0,24},{6,30},{12,36},{18,42},{24,48},{30,54},{36,60},{42,66},{48,... | collective-permute-start | bytes 4616 | tf_op jit(solution)/shard_map/ppermute | solution.py:16
  52.3 3.9 %collective-permute-start.2 = (s32[384]{0:T(512)S(1)}, s32[384]{0:T(512)S(1)}, u32[]{:S(2)}, u32[]{:S(2)}) collective-permute-start(s32[384]{0:T(512)S(1)} %compare_select_fusion), channel_id=1, source_target_pairs={{0,6},{6,24},{12,18},{18,36},{24,30},{30,48},{36,42},{42,60},{48,5... | collective-permute-start | bytes 4616 | tf_op jit(solution)/shard_map/ppermute | solution.py:26
  56.3 5.4 %collective-permute-done.7 = s32[384]{0:T(512)S(1)} collective-permute-done((s32[384]{0:T(512)S(1)}, s32[384]{0:T(512)S(1)}, u32[]{:S(2)}, u32[]{:S(2)}) %collective-permute-start.7) | collective-permute-done | bytes 1568 | tf_op jit(solution)/shard_map/ppermute | solution.py:16
  61.7 2.6 %collective-permute-start.10 = (bf16[384,640]{1,0:T(8,128)(2,1)S(1)}, bf16[384,640]{1,0:T(8,128)(2,1)S(1)}, u32[]{:S(2)}, u32[]{:S(2)}) collective-permute-start(bf16[384,640]{1,0:T(8,128)(2,1)S(1)} %collective-permute-done.9), channel_id=1, source_target_pairs={{0,6},{6,0},{12,18},{18,12},{24,30},{30,24},{36,42},{42,36},{48,54... | collective-permute-start | bytes 1474568 | tf_op jit(solution)/shard_map/ppermute | solution.py:21
  64.3 1.9 collective-permute-start.8
  66.3 4.2 %collective-permute-done.4 = f32[128,768]{1,0:T(8,128)} collective-permute-done((f32[128,768]{1,0:T(8,128)}, f32[128,768]{1,0:T(8,128)}, u32[]{:S(2)}, u32[]{:S(2)}) %collective-permute-start.4) | collective-permute-done | bytes 393248 | tf_op jit(solution)/shard_map/ppermute | solution.py:36
  72.8 11.8 %collective-permute-start.12 = (f32[128,768]{1,0:T(8,128)S(1)}, f32[128,768]{1,0:T(8,128)S(1)}, u32[]{:S(2)}, u32[]{:S(2)}) collective-permute-start(f32[128,768]{1,0:T(8,128)S(1)} %fusion.9), channel_id=1, source_target_pairs={{0,2},{1,0},{2,1},{3,5},{4,3},{5,4},{6,8},{7,6},{8,7},{9,11},{10,9... | collective-permute-start | bytes 1179656 | tf_op jit(solution)/shard_map/ppermute | solution.py:36
  84.6 1.9 collective-permute-start.11
  86.6 3.1 %collective-permute-start.6 = (f32[64,768]{1,0:T(8,128)S(1)}, f32[64,768]{1,0:T(8,128)S(1)}, u32[]{:S(2)}, u32[]{:S(2)}) collective-permute-start(f32[64,768]{1,0:T(8,128)S(1)} %constant_dynamic-slice_fusion.1), channel_id=1, source_target_pairs={{0,3},{1,4},{2,5},{3,0},{4,1},{5,2},{6,9},{7,10},{8,11},{9,6},{10,... | collective-permute-start | bytes 589832 | tf_op jit(solution)/shard_map/ppermute | solution.py:40
  89.7 16.1 %collective-permute-done.12 = f32[128,768]{1,0:T(8,128)S(1)} collective-permute-done((f32[128,768]{1,0:T(8,128)S(1)}, f32[128,768]{1,0:T(8,128)S(1)}, u32[]{:S(2)}, u32[]{:S(2)}) %collective-permute-start.12) | collective-permute-done | bytes 393248 | tf_op jit(solution)/shard_map/ppermute | solution.py:36
  106.3 6.8 %collective-permute-start.13 = (f32[64,768]{1,0:T(8,128)S(1)}, f32[64,768]{1,0:T(8,128)S(1)}, u32[]{:S(2)}, u32[]{:S(2)}) collective-permute-start(f32[64,768]{1,0:T(8,128)S(1)} %constant_dynamic-slice_fusion), channel_id=1, source_target_pairs={{0,3},{1,4},{2,5},{3,0},{4,1},{5,2},{6,9},{7,10},{8,11},{9,6},{10,... | collective-permute-start | bytes 589832 | tf_op jit(solution)/shard_map/ppermute | solution.py:40
  113.0 8.9 %collective-permute-done.13 = f32[64,768]{1,0:T(8,128)S(1)} collective-permute-done((f32[64,768]{1,0:T(8,128)S(1)}, f32[64,768]{1,0:T(8,128)S(1)}, u32[]{:S(2)}, u32[]{:S(2)}) %collective-permute-start.13) | collective-permute-done | bytes 196640 | tf_op jit(solution)/shard_map/ppermute | solution.py:40
  124.5 4.4 %collective-permute-start.15 = (bf16[64,768]{1,0:T(8,128)(2,1)S(1)}, bf16[64,768]{1,0:T(8,128)(2,1)S(1)}, u32[]{:S(2)}, u32[]{:S(2)}) collective-permute-start(bf16[64,768]{1,0:T(8,128)(2,1)S(1)} %get-tuple-element.35), channel_id=1, source_target_pairs={{0,3},{1,4},{2,5},{3,0},{4,1},{5,2},{6,9},{7,10},{8,11},{9,6},{10,... | collective-permute-start | bytes 294920 | tf_op jit(solution)/shard_map/ppermute | solution.py:40
  128.9 5.1 %collective-permute-done.15 = bf16[64,768]{1,0:T(8,128)(2,1)S(1)} collective-permute-done((bf16[64,768]{1,0:T(8,128)(2,1)S(1)}, bf16[64,768]{1,0:T(8,128)(2,1)S(1)}, u32[]{:S(2)}, u32[]{:S(2)}) %collective-permute-start.15) | collective-permute-done | bytes 98336 | tf_op jit(solution)/shard_map/ppermute | solution.py:40
  134.2 5.4 %collective-permute-start.17 = (bf16[128,768]{1,0:T(8,128)(2,1)S(1)}, bf16[128,768]{1,0:T(8,128)(2,1)S(1)}, u32[]{:S(2)}, u32[]{:S(2)}) collective-permute-start(bf16[128,768]{1,0:T(8,128)(2,1)S(1)} %get-tuple-element.28), channel_id=1, source_target_pairs={{0,1},{1,2},{2,0},{3,4},{4,5},{5,3},{6,7},{7,8},{8,6},{9,10},{10,1... | collective-permute-start | bytes 589832 | tf_op jit(solution)/shard_map/ppermute | solution.py:36
  139.6 4.0 %collective-permute-start.18 = (bf16[128,768]{1,0:T(8,128)(2,1)S(1)}, bf16[128,768]{1,0:T(8,128)(2,1)S(1)}, u32[]{:S(2)}, u32[]{:S(2)}) collective-permute-start(bf16[128,768]{1,0:T(8,128)(2,1)S(1)} %get-tuple-element.28), channel_id=1, source_target_pairs={{0,2},{1,0},{2,1},{3,5},{4,3},{5,4},{6,8},{7,6},{8,7},{9,11},{10,9... | collective-permute-start | bytes 589832 | tf_op jit(solution)/shard_map/ppermute | solution.py:36
  143.7 2.3 collective-permute-done.17
  146.0 5.4 %collective-permute-done.18 = bf16[128,768]{1,0:T(8,128)(2,1)S(1)} collective-permute-done((bf16[128,768]{1,0:T(8,128)(2,1)S(1)}, bf16[128,768]{1,0:T(8,128)(2,1)S(1)}, u32[]{:S(2)}, u32[]{:S(2)}) %collective-permute-start.18) | collective-permute-done | bytes 196640 | tf_op jit(solution)/shard_map/ppermute | solution.py:36
  153.8 3.3 %collective-permute-start.14 = (bf16[64,768]{1,0:T(8,128)(2,1)S(1)}, bf16[64,768]{1,0:T(8,128)(2,1)S(1)}, u32[]{:S(2)}, u32[]{:S(2)}) collective-permute-start(bf16[64,768]{1,0:T(8,128)(2,1)S(1)} %get-tuple-element.36), channel_id=1, source_target_pairs={{0,3},{1,4},{2,5},{3,0},{4,1},{5,2},{6,9},{7,10},{8,11},{9,6},{10,... | collective-permute-start | bytes 294920 | tf_op jit(solution)/shard_map/ppermute | solution.py:40
  157.1 8.7 %collective-permute-done.14 = bf16[64,768]{1,0:T(8,128)(2,1)S(1)} collective-permute-done((bf16[64,768]{1,0:T(8,128)(2,1)S(1)}, bf16[64,768]{1,0:T(8,128)(2,1)S(1)}, u32[]{:S(2)}, u32[]{:S(2)}) %collective-permute-start.14) | collective-permute-done | bytes 98336 | tf_op jit(solution)/shard_map/ppermute | solution.py:40
  167.9 4.4 %collective-permute-start.20 = (bf16[128,768]{1,0:T(8,128)(2,1)S(1)}, bf16[128,768]{1,0:T(8,128)(2,1)S(1)}, u32[]{:S(2)}, u32[]{:S(2)}) collective-permute-start(bf16[128,768]{1,0:T(8,128)(2,1)S(1)} %get-tuple-element.29), channel_id=1, source_target_pairs={{0,2},{1,0},{2,1},{3,5},{4,3},{5,4},{6,8},{7,6},{8,7},{9,11},{10,9... | collective-permute-start | bytes 589832 | tf_op jit(solution)/shard_map/ppermute | solution.py:36
  172.8 7.0 %collective-permute-start.23 = (bf16[384,640]{1,0:T(8,128)(2,1)S(1)}, bf16[384,640]{1,0:T(8,128)(2,1)S(1)}, u32[]{:S(2)}, u32[]{:S(2)}) collective-permute-start(bf16[384,640]{1,0:T(8,128)(2,1)S(1)} %fusion.2), channel_id=1, source_target_pairs={{0,756},{6,762},{12,0},{18,6},{24,12},{30,18},{36,24},{42,30},{48,... | collective-permute-start | bytes 1474568 | tf_op jit(solution)/shard_map/ppermute | solution.py:16
  181.5 7.1 %collective-permute-start.22 = (bf16[384,640]{1,0:T(8,128)(2,1)S(1)}, bf16[384,640]{1,0:T(8,128)(2,1)S(1)}, u32[]{:S(2)}, u32[]{:S(2)}) collective-permute-start(bf16[384,640]{1,0:T(8,128)(2,1)S(1)} %convolution_convert_fusion), channel_id=1, source_target_pairs={{6,0},{24,6},{18,12},{36,18},{30,24},{48,30},{42,36},{60,42},{54,4... | collective-permute-start | bytes 1474568 | tf_op jit(solution)/shard_map/ppermute | solution.py:31
  188.7 19.7 %collective-permute-start.21 = (bf16[384,640]{1,0:T(8,128)(2,1)S(1)}, bf16[384,640]{1,0:T(8,128)(2,1)S(1)}, u32[]{:S(2)}, u32[]{:S(2)}) collective-permute-start(bf16[384,640]{1,0:T(8,128)(2,1)S(1)} %convolution_convert_fusion.1), channel_id=1, source_target_pairs={{0,744},{6,750},{12,756},{18,762},{24,0},{30,6},{36,12},{42,18},{4... | collective-permute-start | bytes 1474568 | tf_op jit(solution)/shard_map/ppermute | solution.py:16
  209.0 10.3 %collective-permute-done.23 = bf16[384,640]{1,0:T(8,128)(2,1)S(1)} collective-permute-done((bf16[384,640]{1,0:T(8,128)(2,1)S(1)}, bf16[384,640]{1,0:T(8,128)(2,1)S(1)}, u32[]{:S(2)}, u32[]{:S(2)}) %collective-permute-start.23) | collective-permute-done | bytes 491552 | tf_op jit(solution)/shard_map/ppermute | solution.py:16
  219.3 17.1 %collective-permute-done.21 = bf16[384,640]{1,0:T(8,128)(2,1)S(1)} collective-permute-done((bf16[384,640]{1,0:T(8,128)(2,1)S(1)}, bf16[384,640]{1,0:T(8,128)(2,1)S(1)}, u32[]{:S(2)}, u32[]{:S(2)}) %collective-permute-start.21) | collective-permute-done | bytes 491552 | tf_op jit(solution)/shard_map/ppermute | solution.py:16
  (74 shorter events, 18.4 us)
Async XLA Ops:
  0.0 21.6 %collective-permute-start = (bf16[384,640]{1,0:T(8,128)(2,1)}, bf16[384,640]{1,0:T(8,128)(2,1)S(1)}, u32[]{:S(2)}, u32[]{:S(2)}) collective-permute-start(bf16[384,640]{1,0:T(8,128)(2,1)} %param.6), channel_id=1, source_target_pairs={{0,24},{6,30},{12,36},{18,42},{24,48},{30,54},{36,60},{42,66},{48,... | collective-permute-start | bytes 1474568 | tf_op jit(solution)/shard_map/ppermute | solution.py:16
  4.6 17.0 %collective-permute-start.3 = (bf16[384,640]{1,0:T(8,128)(2,1)}, bf16[384,640]{1,0:T(8,128)(2,1)S(1)}, u32[]{:S(2)}, u32[]{:S(2)}) collective-permute-start(bf16[384,640]{1,0:T(8,128)(2,1)} %param.6), channel_id=1, source_target_pairs={{0,6},{6,24},{12,18},{18,36},{24,30},{30,48},{36,42},{42,60},{48,5... | collective-permute-start | bytes 1474568 | tf_op jit(solution)/shard_map/ppermute | solution.py:26
  6.5 45.8 %collective-permute-start.9 = (bf16[384,640]{1,0:T(8,128)(2,1)}, bf16[384,640]{1,0:T(8,128)(2,1)S(1)}, u32[]{:S(2)}, u32[]{:S(2)}) collective-permute-start(bf16[384,640]{1,0:T(8,128)(2,1)} %param.6), channel_id=1, source_target_pairs={{0,12},{6,18},{12,24},{18,30},{24,36},{30,42},{36,48},{42,54},{48,... | collective-permute-start | bytes 1474568 | tf_op jit(solution)/shard_map/ppermute | solution.py:16
  20.9 0.7 copy-start.1
  20.9 0.7 copy-start.3
  21.6 1.0 copy-start
  23.8 7.1 %copy-start.2 = (f32[384]{0:T(512)S(1)}, f32[384]{0:T(512)}, u32[]{:S(2)}) copy-start(f32[384]{0:T(512)} %param.11) | copy-start | bytes 4612
  23.8 42.5 %collective-permute-start.5 = (f32[128,768]{1,0:T(8,128)}, f32[128,768]{1,0:T(8,128)S(1)}, u32[]{:S(2)}, u32[]{:S(2)}) collective-permute-start(f32[128,768]{1,0:T(8,128)} %fusion.11), channel_id=1, source_target_pairs={{0,2},{1,0},{2,1},{3,5},{4,3},{5,4},{6,8},{7,6},{8,7},{9,11},{10,9... | collective-permute-start | bytes 1179656 | tf_op jit(solution)/shard_map/ppermute | solution.py:36
  27.6 42.9 %collective-permute-start.4 = (f32[128,768]{1,0:T(8,128)}, f32[128,768]{1,0:T(8,128)}, u32[]{:S(2)}, u32[]{:S(2)}) collective-permute-start(f32[128,768]{1,0:T(8,128)} %fusion.15), channel_id=1, source_target_pairs={{0,1},{1,2},{2,0},{3,4},{4,5},{5,3},{6,7},{7,8},{8,6},{9,10},{10,1... | collective-permute-start | bytes 1179656 | tf_op jit(solution)/shard_map/ppermute | solution.py:36
  31.2 30.5 %collective-permute-start.7 = (s32[384]{0:T(512)S(1)}, s32[384]{0:T(512)S(1)}, u32[]{:S(2)}, u32[]{:S(2)}) collective-permute-start(s32[384]{0:T(512)S(1)} %compare_select_fusion), channel_id=1, source_target_pairs={{0,12},{6,18},{12,24},{18,30},{24,36},{30,42},{36,48},{42,54},{48,... | collective-permute-start | bytes 4616 | tf_op jit(solution)/shard_map/ppermute | solution.py:16
  44.4 19.9 %collective-permute-start.1 = (s32[384]{0:T(512)S(1)}, s32[384]{0:T(512)S(1)}, u32[]{:S(2)}, u32[]{:S(2)}) collective-permute-start(s32[384]{0:T(512)S(1)} %compare_select_fusion), channel_id=1, source_target_pairs={{0,24},{6,30},{12,36},{18,42},{24,48},{30,54},{36,60},{42,66},{48,... | collective-permute-start | bytes 4616 | tf_op jit(solution)/shard_map/ppermute | solution.py:16
  52.3 13.9 %collective-permute-start.2 = (s32[384]{0:T(512)S(1)}, s32[384]{0:T(512)S(1)}, u32[]{:S(2)}, u32[]{:S(2)}) collective-permute-start(s32[384]{0:T(512)S(1)} %compare_select_fusion), channel_id=1, source_target_pairs={{0,6},{6,24},{12,18},{18,36},{24,30},{30,48},{36,42},{42,60},{48,5... | collective-permute-start | bytes 4616 | tf_op jit(solution)/shard_map/ppermute | solution.py:26
  61.7 10.3 %collective-permute-start.10 = (bf16[384,640]{1,0:T(8,128)(2,1)S(1)}, bf16[384,640]{1,0:T(8,128)(2,1)S(1)}, u32[]{:S(2)}, u32[]{:S(2)}) collective-permute-start(bf16[384,640]{1,0:T(8,128)(2,1)S(1)} %collective-permute-done.9), channel_id=1, source_target_pairs={{0,6},{6,0},{12,18},{18,12},{24,30},{30,24},{36,42},{42,36},{48,54... | collective-permute-start | bytes 1474568 | tf_op jit(solution)/shard_map/ppermute | solution.py:21
  64.3 22.3 %collective-permute-start.8 = (s32[384]{0:T(512)S(1)}, s32[384]{0:T(512)S(1)}, u32[]{:S(2)}, u32[]{:S(2)}) collective-permute-start(s32[384]{0:T(512)S(1)} %collective-permute-done.7), channel_id=1, source_target_pairs={{0,6},{6,0},{12,18},{18,12},{24,30},{30,24},{36,42},{42,36},{48,54... | collective-permute-start | bytes 4616 | tf_op jit(solution)/shard_map/ppermute | solution.py:21
  72.8 33.0 %collective-permute-start.12 = (f32[128,768]{1,0:T(8,128)S(1)}, f32[128,768]{1,0:T(8,128)S(1)}, u32[]{:S(2)}, u32[]{:S(2)}) collective-permute-start(f32[128,768]{1,0:T(8,128)S(1)} %fusion.9), channel_id=1, source_target_pairs={{0,2},{1,0},{2,1},{3,5},{4,3},{5,4},{6,8},{7,6},{8,7},{9,11},{10,9... | collective-permute-start | bytes 1179656 | tf_op jit(solution)/shard_map/ppermute | solution.py:36
  84.6 21.2 %collective-permute-start.11 = (f32[128,768]{1,0:T(8,128)S(1)}, f32[128,768]{1,0:T(8,128)S(1)}, u32[]{:S(2)}, u32[]{:S(2)}) collective-permute-start(f32[128,768]{1,0:T(8,128)S(1)} %fusion.13), channel_id=1, source_target_pairs={{0,1},{1,2},{2,0},{3,4},{4,5},{5,3},{6,7},{7,8},{8,6},{9,10},{10,1... | collective-permute-start | bytes 1179656 | tf_op jit(solution)/shard_map/ppermute | solution.py:36
  86.6 26.4 %collective-permute-start.6 = (f32[64,768]{1,0:T(8,128)S(1)}, f32[64,768]{1,0:T(8,128)S(1)}, u32[]{:S(2)}, u32[]{:S(2)}) collective-permute-start(f32[64,768]{1,0:T(8,128)S(1)} %constant_dynamic-slice_fusion.1), channel_id=1, source_target_pairs={{0,3},{1,4},{2,5},{3,0},{4,1},{5,2},{6,9},{7,10},{8,11},{9,6},{10,... | collective-permute-start | bytes 589832 | tf_op jit(solution)/shard_map/ppermute | solution.py:40
  106.3 15.7 %collective-permute-start.13 = (f32[64,768]{1,0:T(8,128)S(1)}, f32[64,768]{1,0:T(8,128)S(1)}, u32[]{:S(2)}, u32[]{:S(2)}) collective-permute-start(f32[64,768]{1,0:T(8,128)S(1)} %constant_dynamic-slice_fusion), channel_id=1, source_target_pairs={{0,3},{1,4},{2,5},{3,0},{4,1},{5,2},{6,9},{7,10},{8,11},{9,6},{10,... | collective-permute-start | bytes 589832 | tf_op jit(solution)/shard_map/ppermute | solution.py:40
  122.2 0.7 copy-start.4
  123.0 0.7 copy-start.5
  124.5 9.6 %collective-permute-start.15 = (bf16[64,768]{1,0:T(8,128)(2,1)S(1)}, bf16[64,768]{1,0:T(8,128)(2,1)S(1)}, u32[]{:S(2)}, u32[]{:S(2)}) collective-permute-start(bf16[64,768]{1,0:T(8,128)(2,1)S(1)} %get-tuple-element.35), channel_id=1, source_target_pairs={{0,3},{1,4},{2,5},{3,0},{4,1},{5,2},{6,9},{7,10},{8,11},{9,6},{10,... | collective-permute-start | bytes 294920 | tf_op jit(solution)/shard_map/ppermute | solution.py:40
  134.2 11.8 %collective-permute-start.17 = (bf16[128,768]{1,0:T(8,128)(2,1)S(1)}, bf16[128,768]{1,0:T(8,128)(2,1)S(1)}, u32[]{:S(2)}, u32[]{:S(2)}) collective-permute-start(bf16[128,768]{1,0:T(8,128)(2,1)S(1)} %get-tuple-element.28), channel_id=1, source_target_pairs={{0,1},{1,2},{2,0},{3,4},{4,5},{5,3},{6,7},{7,8},{8,6},{9,10},{10,1... | collective-permute-start | bytes 589832 | tf_op jit(solution)/shard_map/ppermute | solution.py:36
  139.6 11.7 %collective-permute-start.18 = (bf16[128,768]{1,0:T(8,128)(2,1)S(1)}, bf16[128,768]{1,0:T(8,128)(2,1)S(1)}, u32[]{:S(2)}, u32[]{:S(2)}) collective-permute-start(bf16[128,768]{1,0:T(8,128)(2,1)S(1)} %get-tuple-element.28), channel_id=1, source_target_pairs={{0,2},{1,0},{2,1},{3,5},{4,3},{5,4},{6,8},{7,6},{8,7},{9,11},{10,9... | collective-permute-start | bytes 589832 | tf_op jit(solution)/shard_map/ppermute | solution.py:36
  151.8 20.5 %collective-permute-start.19 = (bf16[384,640]{1,0:T(8,128)(2,1)S(1)}, bf16[384,640]{1,0:T(8,128)(2,1)S(1)}, u32[]{:S(2)}, u32[]{:S(2)}) collective-permute-start(bf16[384,640]{1,0:T(8,128)(2,1)S(1)} %convolution_convert_fusion.2), channel_id=1, source_target_pairs={{0,6},{6,0},{12,18},{18,12},{24,30},{30,24},{36,42},{42,36},{48,54... | collective-permute-start | bytes 1474568 | tf_op jit(solution)/shard_map/ppermute | solution.py:21
  153.8 12.1 %collective-permute-start.14 = (bf16[64,768]{1,0:T(8,128)(2,1)S(1)}, bf16[64,768]{1,0:T(8,128)(2,1)S(1)}, u32[]{:S(2)}, u32[]{:S(2)}) collective-permute-start(bf16[64,768]{1,0:T(8,128)(2,1)S(1)} %get-tuple-element.36), channel_id=1, source_target_pairs={{0,3},{1,4},{2,5},{3,0},{4,1},{5,2},{6,9},{7,10},{8,11},{9,6},{10,... | collective-permute-start | bytes 294920 | tf_op jit(solution)/shard_map/ppermute | solution.py:40
  166.0 13.8 %collective-permute-start.16 = (bf16[128,768]{1,0:T(8,128)(2,1)S(1)}, bf16[128,768]{1,0:T(8,128)(2,1)S(1)}, u32[]{:S(2)}, u32[]{:S(2)}) collective-permute-start(bf16[128,768]{1,0:T(8,128)(2,1)S(1)} %get-tuple-element.29), channel_id=1, source_target_pairs={{0,1},{1,2},{2,0},{3,4},{4,5},{5,3},{6,7},{7,8},{8,6},{9,10},{10,1... | collective-permute-start | bytes 589832 | tf_op jit(solution)/shard_map/ppermute | solution.py:36
  167.9 12.7 %collective-permute-start.20 = (bf16[128,768]{1,0:T(8,128)(2,1)S(1)}, bf16[128,768]{1,0:T(8,128)(2,1)S(1)}, u32[]{:S(2)}, u32[]{:S(2)}) collective-permute-start(bf16[128,768]{1,0:T(8,128)(2,1)S(1)} %get-tuple-element.29), channel_id=1, source_target_pairs={{0,2},{1,0},{2,1},{3,5},{4,3},{5,4},{6,8},{7,6},{8,7},{9,11},{10,9... | collective-permute-start | bytes 589832 | tf_op jit(solution)/shard_map/ppermute | solution.py:36
  172.8 46.5 %collective-permute-start.23 = (bf16[384,640]{1,0:T(8,128)(2,1)S(1)}, bf16[384,640]{1,0:T(8,128)(2,1)S(1)}, u32[]{:S(2)}, u32[]{:S(2)}) collective-permute-start(bf16[384,640]{1,0:T(8,128)(2,1)S(1)} %fusion.2), channel_id=1, source_target_pairs={{0,756},{6,762},{12,0},{18,6},{24,12},{30,18},{36,24},{42,30},{48,... | collective-permute-start | bytes 1474568 | tf_op jit(solution)/shard_map/ppermute | solution.py:16
  181.5 37.8 %collective-permute-start.22 = (bf16[384,640]{1,0:T(8,128)(2,1)S(1)}, bf16[384,640]{1,0:T(8,128)(2,1)S(1)}, u32[]{:S(2)}, u32[]{:S(2)}) collective-permute-start(bf16[384,640]{1,0:T(8,128)(2,1)S(1)} %convolution_convert_fusion), channel_id=1, source_target_pairs={{6,0},{24,6},{18,12},{36,18},{30,24},{48,30},{42,36},{60,42},{54,4... | collective-permute-start | bytes 1474568 | tf_op jit(solution)/shard_map/ppermute | solution.py:31
  188.7 47.7 %collective-permute-start.21 = (bf16[384,640]{1,0:T(8,128)(2,1)S(1)}, bf16[384,640]{1,0:T(8,128)(2,1)S(1)}, u32[]{:S(2)}, u32[]{:S(2)}) collective-permute-start(bf16[384,640]{1,0:T(8,128)(2,1)S(1)} %convolution_convert_fusion.1), channel_id=1, source_target_pairs={{0,744},{6,750},{12,756},{18,762},{24,0},{30,6},{36,12},{42,18},{4... | collective-permute-start | bytes 1474568 | tf_op jit(solution)/shard_map/ppermute | solution.py:16

commit v3 on v2

--- a/solution.py
+++ b/solution.py
@@ -48,6 +48,18 @@
     return lax.dot_general(queries, keys, (((1,), (1,)), ((), ())), preferred_element_type=F32)
 
 
+def with_codes(hidden, targets, padding):
+    code = jnp.where(padding == 1, targets + 1, 0)
+    digits = jnp.stack([code >> 8, code & 255]).astype(BF)
+    tail = jnp.pad(digits, ((0, 14), (0, hidden.shape[1] - SEG)))
+    return jnp.concatenate([hidden, tail], axis=0)
+
+
+def codes_of(payload):
+    digits = lax.optimization_barrier(payload[SEG:])[:2, :SEG].astype(F32)
+    return digits[0] * 256.0 + digits[1]
+
+
 def after(value, *others):
     return lax.optimization_barrier((value,) + others)[0]
 
@@ -90,26 +102,25 @@
     core = lax.axis_index("dp") % 2
     r = lax.axis_index("tensor")
     u, v = r // 3, r % 3
-    label_code = jnp.where(padding == 1, targets, -1)
     weight = cotangent * padding.astype(F32)
+    payload = with_codes(hidden, targets, padding)
 
-    far = dp_shift(hidden, 2)
-    near = dp_shift(hidden, 4)
-    odd = odd_keys(hidden)
-    late_code = after(label_code, near)
-    far_label = dp_shift(late_code, 2)
-    near_labels = jnp.concatenate([dp_shift(late_code, 4), odd_keys(late_code)])
-    far_labels = jnp.concatenate([far_label, core_swap(far_label)])
+    far = dp_shift(payload, 2)
+    near = dp_shift(payload, 4)
+    odd = odd_keys(payload)
     own_rows = rows_of(hidden, v * 128, 128)
 
-    near_keys = jnp.concatenate([near, odd], axis=0)
+    near_keys = jnp.concatenate([near[:SEG], odd[:SEG]], axis=0)
+    near_codes = jnp.concatenate([codes_of(near), codes_of(odd)])
     near_out = outgoing(hidden, near_keys, v)
     near_group = partial_of(own_rows, near_keys)
     near_group = near_group + triple_shift(near_out[0], 1) + triple_shift(near_out[1], 2)
     near_send = rows_of(near_group, (1 - u) * 64, 64)
     near_other = triple_swap(near_send)
 
-    far_keys = jnp.concatenate([far, core_swap(far)], axis=0)
+    far_pair = core_swap(far)
+    far_keys = jnp.concatenate([far[:SEG], far_pair[:SEG]], axis=0)
+    far_codes = jnp.concatenate([codes_of(far), codes_of(far_pair)])
     far_out = outgoing(hidden, far_keys, v)
     far_out = lax.optimization_barrier(far_out + (near_send,))
     far_group = partial_of(own_rows, far_keys)
@@ -119,11 +130,11 @@
     far_scores = (rows_of(far_group, u * 64, 64) + far_other) * score_scale
 
     base = v * 128 + u * 64
-    row_targets = rows_of(targets, base, 64)
+    row_codes = rows_of(targets, base, 64).astype(F32) + 1.0
     parts = []
-    for scores, labels in ((near_scores, near_labels), (far_scores, far_labels)):
-        usable = jnp.broadcast_to((labels >= 0)[None], scores.shape)
-        matches = usable & (labels[None] == row_targets[:, None])
+    for scores, codes in ((near_scores, near_codes), (far_scores, far_codes)):
+        usable = jnp.broadcast_to((codes > 0.0)[None], scores.shape)
+        matches = usable & (codes[None] == row_codes[:, None])
         parts.append((scores, usable, matches))
     total_lse = normalizer([(s, a) for s, a, m in parts], rows_of(vocab_lse, base, 64))
     pos_lse = normalizer([(s, m) for s, a, m in parts], rows_of(gold_logit, base, 64))
@@ -136,10 +147,10 @@
         slopes.append((row_weight[:, None] * spread * score_scale).astype(BF))
     near_mine, far_mine = slopes
     far_rows = row_group(far_mine, triple_swap(far_mine), u)
-    near_other_rows = triple_swap(near_mine)
+    near_rows = row_group(near_mine, triple_swap(near_mine), u)
+    far_rows, near_rows = lax.optimization_barrier((far_rows, near_rows))
     far_one = triple_shift(far_rows, 1)
     far_two = triple_shift(far_rows, 2)
-    near_rows = row_group(near_mine, after(near_other_rows, far_rows), u)
     near_one = triple_shift(near_rows, 1)
     near_two = triple_shift(near_rows, 2)
 

time: 239 us -> 224 us (0.937)
  the two profiles are of different devices: /device:TPU:94 before, /device:TPU:447 now
where the time goes in v3:
time: 224 us; the launch traced here: 223 us
  waiting for transfers between devices  153 us (68%)
  starting transfers between devices  57.3 us (26%)
  matrix products  6.44 us (3%)
  other arithmetic  4.06 us (2%)
    ppermute x8, waiting for transfers between devices, triple_shift(): return lax.ppermute(value, 'tensor', pairs)  94.7 us
    ppermute x8, starting transfers between devices, triple_shift(): return lax.ppermute(value, 'tensor', pairs)  27.2 us
    ppermute x4, waiting for transfers between devices, triple_swap(): return lax.ppermute(value, 'tensor', [(r, (r + 3) % 6) for r in range(6)])  26.6 us
    ppermute x4, waiting for transfers between devices, dp_shift(): lax.ppermute(value, 'dp', [(i, (i + steps) % count) for i in range(count)])  23 us
    ppermute x4, starting transfers between devices, triple_swap(): return lax.ppermute(value, 'tensor', [(r, (r + 3) % 6) for r in range(6)])  12.1 us
    ppermute x4, starting transfers between devices, dp_shift(): lax.ppermute(value, 'dp', [(i, (i + steps) % count) for i in range(count)])  8.83 us
    ppermute x1, waiting for transfers between devices, odd_home(): lax.ppermute(value, 'dp', [((i + (1 if i % 2 == 0 else 3)) % count, i) fo...  6.26 us
    ppermute x2, starting transfers between devices, core_swap(): return lax.ppermute(value, 'dp', [(i, i ^ 1) for i in range(count)])  4.51 us
  transfers between devices with their start and end apart: 20, of which 14 were waited for; matrix products, arithmetic and copies ran while one was open for 2% of the time, Pallas kernels for 0%

profile of v3, /device:TPU:447, one launch (start us, length us, event | category | flops | bytes accessed | tf_op | source)
XLA Modules:
  0.0 223.4 jit_solution(17447492866877933848)
XLA Ops:
  1.9 1.9 collective-permute-start.3
  3.8 3.1 %collective-permute-start.2 = (bf16[400,640]{1,0:T(8,128)(2,1)S(1)}, bf16[400,640]{1,0:T(8,128)(2,1)S(1)}, u32[]{:S(2)}, u32[]{:S(2)}) collective-permute-start(bf16[400,640]{1,0:T(8,128)(2,1)S(1)} %pad_maximum_fusion.2), channel_id=1, source_target_pairs={{0,24},{6,30},{12,36},{18,42},{24,48},{30,54},{36,60},{42,66},{48,... | collective-permute-start | bytes 1536008 | tf_op jit(solution)/shard_map/ppermute | solution.py:16
  6.9 1.9 collective-permute-start
  9.8 2.6 %collective-permute-done.3 = bf16[400,640]{1,0:T(8,128)(2,1)S(1)} collective-permute-done((bf16[400,640]{1,0:T(8,128)(2,1)S(1)}, bf16[400,640]{1,0:T(8,128)(2,1)S(1)}, u32[]{:S(2)}, u32[]{:S(2)}) %collective-permute-start.3) | collective-permute-done | bytes 512032 | tf_op jit(solution)/shard_map/ppermute | solution.py:26
  12.4 11.1 %collective-permute-done.2 = bf16[400,640]{1,0:T(8,128)(2,1)S(1)} collective-permute-done((bf16[400,640]{1,0:T(8,128)(2,1)S(1)}, bf16[400,640]{1,0:T(8,128)(2,1)S(1)}, u32[]{:S(2)}, u32[]{:S(2)}) %collective-permute-start.2) | collective-permute-done | bytes 512032 | tf_op jit(solution)/shard_map/ppermute | solution.py:16
  25.2 4.6 %collective-permute-start.5 = (f32[128,768]{1,0:T(8,128)S(1)}, f32[128,768]{1,0:T(8,128)S(1)}, u32[]{:S(2)}, u32[]{:S(2)}) collective-permute-start(f32[128,768]{1,0:T(8,128)S(1)} %fusion.9), channel_id=1, source_target_pairs={{0,2},{1,0},{2,1},{3,5},{4,3},{5,4},{6,8},{7,6},{8,7},{9,11},{10,9... | collective-permute-start | bytes 1179656 | tf_op jit(solution)/shard_map/ppermute | solution.py:36
  30.2 1.9 collective-permute-start.4
  32.2 1.9 collective-permute-start.1
  34.2 23.4 %collective-permute-done.5 = f32[128,768]{1,0:T(8,128)S(1)} collective-permute-done((f32[128,768]{1,0:T(8,128)S(1)}, f32[128,768]{1,0:T(8,128)S(1)}, u32[]{:S(2)}, u32[]{:S(2)}) %collective-permute-start.5) | collective-permute-done | bytes 393248 | tf_op jit(solution)/shard_map/ppermute | solution.py:36
  57.6 8.0 %collective-permute-done.4 = f32[128,768]{1,0:T(8,128)S(1)} collective-permute-done((f32[128,768]{1,0:T(8,128)S(1)}, f32[128,768]{1,0:T(8,128)S(1)}, u32[]{:S(2)}, u32[]{:S(2)}) %collective-permute-start.4) | collective-permute-done | bytes 393248 | tf_op jit(solution)/shard_map/ppermute | solution.py:36
  66.9 3.8 %collective-permute-start.6 = (f32[128,768]{1,0:T(8,128)S(1)}, f32[128,768]{1,0:T(8,128)S(1)}, u32[]{:S(2)}, u32[]{:S(2)}) collective-permute-start(f32[128,768]{1,0:T(8,128)S(1)} %fusion.15), channel_id=1, source_target_pairs={{0,1},{1,2},{2,0},{3,4},{4,5},{5,3},{6,7},{7,8},{8,6},{9,10},{10,1... | collective-permute-start | bytes 1179656 | tf_op jit(solution)/shard_map/ppermute | solution.py:36
  70.8 4.2 %collective-permute-start.7 = (f32[128,768]{1,0:T(8,128)S(1)}, f32[128,768]{1,0:T(8,128)S(1)}, u32[]{:S(2)}, u32[]{:S(2)}) collective-permute-start(f32[128,768]{1,0:T(8,128)S(1)} %fusion.11), channel_id=1, source_target_pairs={{0,2},{1,0},{2,1},{3,5},{4,3},{5,4},{6,8},{7,6},{8,7},{9,11},{10,9... | collective-permute-start | bytes 1179656 | tf_op jit(solution)/shard_map/ppermute | solution.py:36
  75.0 1.9 collective-permute-start.9
  77.0 5.3 %collective-permute-done.6 = f32[128,768]{1,0:T(8,128)S(1)} collective-permute-done((f32[128,768]{1,0:T(8,128)S(1)}, f32[128,768]{1,0:T(8,128)S(1)}, u32[]{:S(2)}, u32[]{:S(2)}) %collective-permute-start.6) | collective-permute-done | bytes 393248 | tf_op jit(solution)/shard_map/ppermute | solution.py:36
  82.2 13.0 %collective-permute-done.7 = f32[128,768]{1,0:T(8,128)S(1)} collective-permute-done((f32[128,768]{1,0:T(8,128)S(1)}, f32[128,768]{1,0:T(8,128)S(1)}, u32[]{:S(2)}, u32[]{:S(2)}) %collective-permute-start.7) | collective-permute-done | bytes 393248 | tf_op jit(solution)/shard_map/ppermute | solution.py:36
  95.7 1.9 collective-permute-start.8
  97.7 17.8 %collective-permute-done.8 = f32[64,768]{1,0:T(8,128)S(1)} collective-permute-done((f32[64,768]{1,0:T(8,128)S(1)}, f32[64,768]{1,0:T(8,128)S(1)}, u32[]{:S(2)}, u32[]{:S(2)}) %collective-permute-start.8) | collective-permute-done | bytes 196640 | tf_op jit(solution)/shard_map/ppermute | solution.py:40
  116.8 1.9 collective-permute-start.11
  118.7 6.4 %collective-permute-start.10 = (bf16[64,768]{1,0:T(8,128)(2,1)S(1)}, bf16[64,768]{1,0:T(8,128)(2,1)S(1)}, u32[]{:S(2)}, u32[]{:S(2)}) collective-permute-start(bf16[64,768]{1,0:T(8,128)(2,1)S(1)} %get-tuple-element.34), channel_id=1, source_target_pairs={{0,3},{1,4},{2,5},{3,0},{4,1},{5,2},{6,9},{7,10},{8,11},{9,6},{10,... | collective-permute-start | bytes 294920 | tf_op jit(solution)/shard_map/ppermute | solution.py:40
  125.1 6.8 %collective-permute-done.11 = bf16[64,768]{1,0:T(8,128)(2,1)S(1)} collective-permute-done((bf16[64,768]{1,0:T(8,128)(2,1)S(1)}, bf16[64,768]{1,0:T(8,128)(2,1)S(1)}, u32[]{:S(2)}, u32[]{:S(2)}) %collective-permute-start.11) | collective-permute-done | bytes 98336 | tf_op jit(solution)/shard_map/ppermute | solution.py:40
  132.0 2.1 collective-permute-done.10
  134.1 1.9 collective-permute-start.13
  136.0 5.5 %collective-permute-start.14 = (bf16[128,768]{1,0:T(8,128)(2,1)S(1)}, bf16[128,768]{1,0:T(8,128)(2,1)S(1)}, u32[]{:S(2)}, u32[]{:S(2)}) collective-permute-start(bf16[128,768]{1,0:T(8,128)(2,1)S(1)} %pad_maximum_fusion.3), channel_id=1, source_target_pairs={{0,2},{1,0},{2,1},{3,5},{4,3},{5,4},{6,8},{7,6},{8,7},{9,11},{10,9... | collective-permute-start | bytes 589832 | tf_op jit(solution)/shard_map/ppermute | solution.py:36
  141.5 2.5 %collective-permute-done.13 = bf16[128,768]{1,0:T(8,128)(2,1)S(1)} collective-permute-done((bf16[128,768]{1,0:T(8,128)(2,1)S(1)}, bf16[128,768]{1,0:T(8,128)(2,1)S(1)}, u32[]{:S(2)}, u32[]{:S(2)}) %collective-permute-start.13) | collective-permute-done | bytes 196640 | tf_op jit(solution)/shard_map/ppermute | solution.py:36
  144.1 4.6 %collective-permute-done.14 = bf16[128,768]{1,0:T(8,128)(2,1)S(1)} collective-permute-done((bf16[128,768]{1,0:T(8,128)(2,1)S(1)}, bf16[128,768]{1,0:T(8,128)(2,1)S(1)}, u32[]{:S(2)}, u32[]{:S(2)}) %collective-permute-start.14) | collective-permute-done | bytes 196640 | tf_op jit(solution)/shard_map/ppermute | solution.py:36
  149.2 2.6 %collective-permute-start.15 = (bf16[384,640]{1,0:T(8,128)(2,1)S(1)}, bf16[384,640]{1,0:T(8,128)(2,1)S(1)}, u32[]{:S(2)}, u32[]{:S(2)}) collective-permute-start(bf16[384,640]{1,0:T(8,128)(2,1)S(1)} %convolution_convert_fusion.2), channel_id=1, source_target_pairs={{0,6},{6,0},{12,18},{18,12},{24,30},{30,24},{36,42},{42,36},{48,54... | collective-permute-start | bytes 1474568 | tf_op jit(solution)/shard_map/ppermute | solution.py:21
  151.8 3.4 %collective-permute-start.16 = (bf16[128,768]{1,0:T(8,128)(2,1)S(1)}, bf16[128,768]{1,0:T(8,128)(2,1)S(1)}, u32[]{:S(2)}, u32[]{:S(2)}) collective-permute-start(bf16[128,768]{1,0:T(8,128)(2,1)S(1)} %pad_maximum_fusion.4), channel_id=1, source_target_pairs={{0,2},{1,0},{2,1},{3,5},{4,3},{5,4},{6,8},{7,6},{8,7},{9,11},{10,9... | collective-permute-start | bytes 589832 | tf_op jit(solution)/shard_map/ppermute | solution.py:36
  157.7 1.9 collective-permute-start.19
  159.6 37.9 %collective-permute-done.12 = bf16[128,768]{1,0:T(8,128)(2,1)S(1)} collective-permute-done((bf16[128,768]{1,0:T(8,128)(2,1)S(1)}, bf16[128,768]{1,0:T(8,128)(2,1)S(1)}, u32[]{:S(2)}, u32[]{:S(2)}) %collective-permute-start.12) | collective-permute-done | bytes 196640 | tf_op jit(solution)/shard_map/ppermute | solution.py:36
  200.4 2.7 %collective-permute-start.18 = (bf16[384,640]{1,0:T(8,128)(2,1)S(1)}, bf16[384,640]{1,0:T(8,128)(2,1)S(1)}, u32[]{:S(2)}, u32[]{:S(2)}) collective-permute-start(bf16[384,640]{1,0:T(8,128)(2,1)S(1)} %convolution_convert_fusion), channel_id=1, source_target_pairs={{6,0},{24,6},{18,12},{36,18},{30,24},{48,30},{42,36},{60,42},{54,4... | collective-permute-start | bytes 1474568 | tf_op jit(solution)/shard_map/ppermute | solution.py:31
  203.8 11.9 %collective-permute-done.17 = bf16[384,640]{1,0:T(8,128)(2,1)S(1)} collective-permute-done((bf16[384,640]{1,0:T(8,128)(2,1)S(1)}, bf16[384,640]{1,0:T(8,128)(2,1)S(1)}, u32[]{:S(2)}, u32[]{:S(2)}) %collective-permute-start.17) | collective-permute-done | bytes 491552 | tf_op jit(solution)/shard_map/ppermute | solution.py:16
  215.7 6.3 %collective-permute-done.18 = bf16[384,640]{1,0:T(8,128)(2,1)S(1)} collective-permute-done((bf16[384,640]{1,0:T(8,128)(2,1)S(1)}, bf16[384,640]{1,0:T(8,128)(2,1)S(1)}, u32[]{:S(2)}, u32[]{:S(2)}) %collective-permute-start.18) | collective-permute-done | bytes 491552 | tf_op jit(solution)/shard_map/ppermute | solution.py:31
  (83 shorter events, 16.0 us)
Async XLA Ops:
  0.0 8.9 %copy-start.3 = (s32[384]{0:T(512)S(1)}, s32[384]{0:T(512)}, u32[]{:S(2)}) copy-start(s32[384]{0:T(512)} %param.8) | copy-start | bytes 4612
  0.0 8.9 %copy-start.4 = (f32[384]{0:T(512)S(1)}, f32[384]{0:T(512)}, u32[]{:S(2)}) copy-start(f32[384]{0:T(512)} %param.11) | copy-start | bytes 4612
  1.9 10.5 %collective-permute-start.3 = (bf16[400,640]{1,0:T(8,128)(2,1)S(1)}, bf16[400,640]{1,0:T(8,128)(2,1)S(1)}, u32[]{:S(2)}, u32[]{:S(2)}) collective-permute-start(bf16[400,640]{1,0:T(8,128)(2,1)S(1)} %pad_maximum_fusion.2), channel_id=1, source_target_pairs={{0,6},{6,24},{12,18},{18,36},{24,30},{30,48},{36,42},{42,60},{48,5... | collective-permute-start | bytes 1536008 | tf_op jit(solution)/shard_map/ppermute | solution.py:26
  3.8 19.7 %collective-permute-start.2 = (bf16[400,640]{1,0:T(8,128)(2,1)S(1)}, bf16[400,640]{1,0:T(8,128)(2,1)S(1)}, u32[]{:S(2)}, u32[]{:S(2)}) collective-permute-start(bf16[400,640]{1,0:T(8,128)(2,1)S(1)} %pad_maximum_fusion.2), channel_id=1, source_target_pairs={{0,24},{6,30},{12,36},{18,42},{24,48},{30,54},{36,60},{42,66},{48,... | collective-permute-start | bytes 1536008 | tf_op jit(solution)/shard_map/ppermute | solution.py:16
  6.9 25.3 %collective-permute-start = (bf16[400,640]{1,0:T(8,128)(2,1)S(1)}, bf16[400,640]{1,0:T(8,128)(2,1)S(1)}, u32[]{:S(2)}, u32[]{:S(2)}) collective-permute-start(bf16[400,640]{1,0:T(8,128)(2,1)S(1)} %pad_maximum_fusion.2), channel_id=1, source_target_pairs={{0,12},{6,18},{12,24},{18,30},{24,36},{30,42},{36,48},{42,54},{48,... | collective-permute-start | bytes 1536008 | tf_op jit(solution)/shard_map/ppermute | solution.py:16
  12.4 11.2 %copy-start.1 = (bf16[400,640]{1,0:T(8,128)(2,1)}, bf16[400,640]{1,0:T(8,128)(2,1)S(1)}, u32[]{:S(2)}) copy-start(bf16[400,640]{1,0:T(8,128)(2,1)S(1)} %collective-permute-done.3) | copy-start | bytes 1536004
  23.5 0.8 copy-start.2
  23.5 1.2 copy-start
  25.1 7.0 %slice-start = ((bf16[400,640]{1,0:T(8,128)(2,1)}), bf16[16,640]{1,0:T(8,128)(2,1)S(1)}, s32[]{:S(2)}) async-start(bf16[400,640]{1,0:T(8,128)(2,1)} %copy-done.1), calls=%async_computation | async-start | bytes 40960 | tf_op jit(solution)/shard_map/slice | solution.py:59
  25.1 7.0 %slice-start.1 = ((bf16[400,640]{1,0:T(8,128)(2,1)}), bf16[16,640]{1,0:T(8,128)(2,1)S(1)}, s32[]{:S(2)}) async-start(bf16[400,640]{1,0:T(8,128)(2,1)} %copy-done.2), calls=%async_computation.1 | async-start | bytes 40960 | tf_op jit(solution)/shard_map/slice | solution.py:59
  25.2 32.4 %collective-permute-start.5 = (f32[128,768]{1,0:T(8,128)S(1)}, f32[128,768]{1,0:T(8,128)S(1)}, u32[]{:S(2)}, u32[]{:S(2)}) collective-permute-start(f32[128,768]{1,0:T(8,128)S(1)} %fusion.9), channel_id=1, source_target_pairs={{0,2},{1,0},{2,1},{3,5},{4,3},{5,4},{6,8},{7,6},{8,7},{9,11},{10,9... | collective-permute-start | bytes 1179656 | tf_op jit(solution)/shard_map/ppermute | solution.py:36
  30.2 35.4 %collective-permute-start.4 = (f32[128,768]{1,0:T(8,128)S(1)}, f32[128,768]{1,0:T(8,128)S(1)}, u32[]{:S(2)}, u32[]{:S(2)}) collective-permute-start(f32[128,768]{1,0:T(8,128)S(1)} %fusion.13), channel_id=1, source_target_pairs={{0,1},{1,2},{2,0},{3,4},{4,5},{5,3},{6,7},{7,8},{8,6},{9,10},{10,1... | collective-permute-start | bytes 1179656 | tf_op jit(solution)/shard_map/ppermute | solution.py:36
  32.2 33.8 %collective-permute-start.1 = (bf16[400,640]{1,0:T(8,128)(2,1)S(1)}, bf16[400,640]{1,0:T(8,128)(2,1)S(1)}, u32[]{:S(2)}, u32[]{:S(2)}) collective-permute-start(bf16[400,640]{1,0:T(8,128)(2,1)S(1)} %collective-permute-done), channel_id=1, source_target_pairs={{0,6},{6,0},{12,18},{18,12},{24,30},{30,24},{36,42},{42,36},{48,54... | collective-permute-start | bytes 1536008 | tf_op jit(solution)/shard_map/ppermute | solution.py:21
  66.9 15.3 %collective-permute-start.6 = (f32[128,768]{1,0:T(8,128)S(1)}, f32[128,768]{1,0:T(8,128)S(1)}, u32[]{:S(2)}, u32[]{:S(2)}) collective-permute-start(f32[128,768]{1,0:T(8,128)S(1)} %fusion.15), channel_id=1, source_target_pairs={{0,1},{1,2},{2,0},{3,4},{4,5},{5,3},{6,7},{7,8},{8,6},{9,10},{10,1... | collective-permute-start | bytes 1179656 | tf_op jit(solution)/shard_map/ppermute | solution.py:36
  70.8 24.4 %collective-permute-start.7 = (f32[128,768]{1,0:T(8,128)S(1)}, f32[128,768]{1,0:T(8,128)S(1)}, u32[]{:S(2)}, u32[]{:S(2)}) collective-permute-start(f32[128,768]{1,0:T(8,128)S(1)} %fusion.11), channel_id=1, source_target_pairs={{0,2},{1,0},{2,1},{3,5},{4,3},{5,4},{6,8},{7,6},{8,7},{9,11},{10,9... | collective-permute-start | bytes 1179656 | tf_op jit(solution)/shard_map/ppermute | solution.py:36
  75.0 22.7 %collective-permute-start.9 = (f32[64,768]{1,0:T(8,128)S(1)}, f32[64,768]{1,0:T(8,128)S(1)}, u32[]{:S(2)}, u32[]{:S(2)}) collective-permute-start(f32[64,768]{1,0:T(8,128)S(1)} %constant_dynamic-slice_fusion.1), channel_id=1, source_target_pairs={{0,3},{1,4},{2,5},{3,0},{4,1},{5,2},{6,9},{7,10},{8,11},{9,6},{10,... | collective-permute-start | bytes 589832 | tf_op jit(solution)/shard_map/ppermute | solution.py:40
  95.7 20.1 %copy-start.5 = (f32[384]{0:T(512)S(1)}, f32[384]{0:T(512)}, u32[]{:S(2)}) copy-start(f32[384]{0:T(512)} %param.10) | copy-start | bytes 4612
  95.7 20.2 %copy-start.6 = (f32[384]{0:T(512)S(1)}, f32[384]{0:T(512)}, u32[]{:S(2)}) copy-start(f32[384]{0:T(512)} %param.9) | copy-start | bytes 4612
  95.7 19.7 %collective-permute-start.8 = (f32[64,768]{1,0:T(8,128)S(1)}, f32[64,768]{1,0:T(8,128)S(1)}, u32[]{:S(2)}, u32[]{:S(2)}) collective-permute-start(f32[64,768]{1,0:T(8,128)S(1)} %constant_dynamic-slice_fusion), channel_id=1, source_target_pairs={{0,3},{1,4},{2,5},{3,0},{4,1},{5,2},{6,9},{7,10},{8,11},{9,6},{10,... | collective-permute-start | bytes 589832 | tf_op jit(solution)/shard_map/ppermute | solution.py:40
  116.8 15.1 %collective-permute-start.11 = (bf16[64,768]{1,0:T(8,128)(2,1)S(1)}, bf16[64,768]{1,0:T(8,128)(2,1)S(1)}, u32[]{:S(2)}, u32[]{:S(2)}) collective-permute-start(bf16[64,768]{1,0:T(8,128)(2,1)S(1)} %get-tuple-element.33), channel_id=1, source_target_pairs={{0,3},{1,4},{2,5},{3,0},{4,1},{5,2},{6,9},{7,10},{8,11},{9,6},{10,... | collective-permute-start | bytes 294920 | tf_op jit(solution)/shard_map/ppermute | solution.py:40
  118.7 15.3 %collective-permute-start.10 = (bf16[64,768]{1,0:T(8,128)(2,1)S(1)}, bf16[64,768]{1,0:T(8,128)(2,1)S(1)}, u32[]{:S(2)}, u32[]{:S(2)}) collective-permute-start(bf16[64,768]{1,0:T(8,128)(2,1)S(1)} %get-tuple-element.34), channel_id=1, source_target_pairs={{0,3},{1,4},{2,5},{3,0},{4,1},{5,2},{6,9},{7,10},{8,11},{9,6},{10,... | collective-permute-start | bytes 294920 | tf_op jit(solution)/shard_map/ppermute | solution.py:40
  134.1 10.0 %collective-permute-start.13 = (bf16[128,768]{1,0:T(8,128)(2,1)S(1)}, bf16[128,768]{1,0:T(8,128)(2,1)S(1)}, u32[]{:S(2)}, u32[]{:S(2)}) collective-permute-start(bf16[128,768]{1,0:T(8,128)(2,1)S(1)} %pad_maximum_fusion.3), channel_id=1, source_target_pairs={{0,1},{1,2},{2,0},{3,4},{4,5},{5,3},{6,7},{7,8},{8,6},{9,10},{10,1... | collective-permute-start | bytes 589832 | tf_op jit(solution)/shard_map/ppermute | solution.py:36
  136.0 12.7 %collective-permute-start.14 = (bf16[128,768]{1,0:T(8,128)(2,1)S(1)}, bf16[128,768]{1,0:T(8,128)(2,1)S(1)}, u32[]{:S(2)}, u32[]{:S(2)}) collective-permute-start(bf16[128,768]{1,0:T(8,128)(2,1)S(1)} %pad_maximum_fusion.3), channel_id=1, source_target_pairs={{0,2},{1,0},{2,1},{3,5},{4,3},{5,4},{6,8},{7,6},{8,7},{9,11},{10,9... | collective-permute-start | bytes 589832 | tf_op jit(solution)/shard_map/ppermute | solution.py:36
  149.2 8.0 %collective-permute-start.15 = (bf16[384,640]{1,0:T(8,128)(2,1)S(1)}, bf16[384,640]{1,0:T(8,128)(2,1)S(1)}, u32[]{:S(2)}, u32[]{:S(2)}) collective-permute-start(bf16[384,640]{1,0:T(8,128)(2,1)S(1)} %convolution_convert_fusion.2), channel_id=1, source_target_pairs={{0,6},{6,0},{12,18},{18,12},{24,30},{30,24},{36,42},{42,36},{48,54... | collective-permute-start | bytes 1474568 | tf_op jit(solution)/shard_map/ppermute | solution.py:21
  151.8 45.7 %collective-permute-start.16 = (bf16[128,768]{1,0:T(8,128)(2,1)S(1)}, bf16[128,768]{1,0:T(8,128)(2,1)S(1)}, u32[]{:S(2)}, u32[]{:S(2)}) collective-permute-start(bf16[128,768]{1,0:T(8,128)(2,1)S(1)} %pad_maximum_fusion.4), channel_id=1, source_target_pairs={{0,2},{1,0},{2,1},{3,5},{4,3},{5,4},{6,8},{7,6},{8,7},{9,11},{10,9... | collective-permute-start | bytes 589832 | tf_op jit(solution)/shard_map/ppermute | solution.py:36
  155.2 42.3 %collective-permute-start.12 = (bf16[128,768]{1,0:T(8,128)(2,1)S(1)}, bf16[128,768]{1,0:T(8,128)(2,1)S(1)}, u32[]{:S(2)}, u32[]{:S(2)}) collective-permute-start(bf16[128,768]{1,0:T(8,128)(2,1)S(1)} %pad_maximum_fusion.4), channel_id=1, source_target_pairs={{0,1},{1,2},{2,0},{3,4},{4,5},{5,3},{6,7},{7,8},{8,6},{9,10},{10,1... | collective-permute-start | bytes 589832 | tf_op jit(solution)/shard_map/ppermute | solution.py:36
  157.7 46.1 %collective-permute-start.19 = (bf16[384,640]{1,0:T(8,128)(2,1)S(1)}, bf16[384,640]{1,0:T(8,128)(2,1)S(1)}, u32[]{:S(2)}, u32[]{:S(2)}) collective-permute-start(bf16[384,640]{1,0:T(8,128)(2,1)S(1)} %fusion.2), channel_id=1, source_target_pairs={{0,756},{6,762},{12,0},{18,6},{24,12},{30,18},{36,24},{42,30},{48,... | collective-permute-start | bytes 1474568 | tf_op jit(solution)/shard_map/ppermute | solution.py:16
  198.5 17.2 %collective-permute-start.17 = (bf16[384,640]{1,0:T(8,128)(2,1)S(1)}, bf16[384,640]{1,0:T(8,128)(2,1)S(1)}, u32[]{:S(2)}, u32[]{:S(2)}) collective-permute-start(bf16[384,640]{1,0:T(8,128)(2,1)S(1)} %convolution_convert_fusion.1), channel_id=1, source_target_pairs={{0,744},{6,750},{12,756},{18,762},{24,0},{30,6},{36,12},{42,18},{4... | collective-permute-start | bytes 1474568 | tf_op jit(solution)/shard_map/ppermute | solution.py:16
  200.4 21.5 %collective-permute-start.18 = (bf16[384,640]{1,0:T(8,128)(2,1)S(1)}, bf16[384,640]{1,0:T(8,128)(2,1)S(1)}, u32[]{:S(2)}, u32[]{:S(2)}) collective-permute-start(bf16[384,640]{1,0:T(8,128)(2,1)S(1)} %convolution_convert_fusion), channel_id=1, source_target_pairs={{6,0},{24,6},{18,12},{36,18},{30,24},{48,30},{42,36},{60,42},{54,4... | collective-permute-start | bytes 1474568 | tf_op jit(solution)/shard_map/ppermute | solution.py:31

commit v4 on v3

--- a/solution.py
+++ b/solution.py
@@ -113,16 +113,16 @@
     near_keys = jnp.concatenate([near[:SEG], odd[:SEG]], axis=0)
     near_codes = jnp.concatenate([codes_of(near), codes_of(odd)])
     near_out = outgoing(hidden, near_keys, v)
+    near_out = lax.optimization_barrier(near_out + (far,))[:2]
     near_group = partial_of(own_rows, near_keys)
-    near_group = near_group + triple_shift(near_out[0], 1) + triple_shift(near_out[1], 2)
-    near_send = rows_of(near_group, (1 - u) * 64, 64)
-    near_other = triple_swap(near_send)
+    near_in = (triple_shift(near_out[0], 1), triple_shift(near_out[1], 2))
 
     far_pair = core_swap(far)
     far_keys = jnp.concatenate([far[:SEG], far_pair[:SEG]], axis=0)
     far_codes = jnp.concatenate([codes_of(far), codes_of(far_pair)])
     far_out = outgoing(hidden, far_keys, v)
-    far_out = lax.optimization_barrier(far_out + (near_send,))
+    near_group = near_group + after(near_in[0], *far_out) + near_in[1]
+    near_other = triple_swap(rows_of(near_group, (1 - u) * 64, 64))
     far_group = partial_of(own_rows, far_keys)
     far_group = far_group + triple_shift(far_out[0], 1) + triple_shift(far_out[1], 2)
     far_other = triple_swap(rows_of(far_group, (1 - u) * 64, 64))
@@ -145,24 +145,21 @@
             matches, jnp.exp(scores - pos_lse[:, None]), 0.0
         )
         slopes.append((row_weight[:, None] * spread * score_scale).astype(BF))
-    near_mine, far_mine = slopes
-    far_rows = row_group(far_mine, triple_swap(far_mine), u)
-    near_rows = row_group(near_mine, triple_swap(near_mine), u)
-    far_rows, near_rows = lax.optimization_barrier((far_rows, near_rows))
-    far_one = triple_shift(far_rows, 1)
-    far_two = triple_shift(far_rows, 2)
-    near_one = triple_shift(near_rows, 1)
-    near_two = triple_shift(near_rows, 2)
+    mine = jnp.concatenate(slopes, axis=1)
+    rows = row_group(mine, triple_swap(mine), u)
+    full = all_rows(rows, triple_shift(rows, 1), triple_shift(rows, 2), v)
+    near_full, far_full = full[:, : 2 * SEG], full[:, 2 * SEG :]
 
-    far_full = all_rows(far_rows, far_one, far_two, v)
     far_back = core_swap(key_grad(far_full[:, SEG:], hidden).astype(BF))
     far_sum = key_grad(far_full[:, :SEG], hidden) + far_back.astype(F32)
     far_sum = far_sum.astype(BF)
     far_home = dp_shift(far_sum, -2)
 
-    near_full = all_rows(near_rows, after(near_one, far_sum), near_two, v)
-    near_home = dp_shift(key_grad(near_full[:, :SEG], hidden).astype(BF), -4)
-    odd_back = odd_home(key_grad(near_full[:, SEG:], hidden).astype(BF))
+    near_sum = after(key_grad(near_full[:, :SEG], hidden).astype(BF), far_sum)
+    odd_sum = after(key_grad(near_full[:, SEG:], hidden).astype(BF), far_sum)
+    near_home = dp_shift(near_sum, -4)
+    odd_back = odd_home(odd_sum)
+    near_full = after(near_full, far_home)
     query_grad = jnp.dot(near_full, near_keys, preferred_element_type=F32)
     query_grad = query_grad + jnp.dot(far_full, far_keys, preferred_element_type=F32)
     home = near_home.astype(F32) + odd_back.astype(F32) + far_home.astype(F32)

time: 224 us -> 210 us (0.938)
  the two profiles are of different devices: /device:TPU:447 before, /device:TPU:1 now
where the time goes in v4:
time: 210 us; the launch traced here: 207 us
  waiting for transfers between devices  99.2 us (47%)
  starting transfers between devices  95 us (45%)
  matrix products  6.45 us (3%)
  other arithmetic  4.83 us (2%)
    ppermute x4, waiting for transfers between devices, dp_shift(): lax.ppermute(value, 'dp', [(i, (i + steps) % count) for i in range(count)])  42.3 us
    ppermute x6, starting transfers between devices, triple_shift(): return lax.ppermute(value, 'tensor', pairs)  34.7 us
    ppermute x4, starting transfers between devices, dp_shift(): lax.ppermute(value, 'dp', [(i, (i + steps) % count) for i in range(count)])  27 us
    ppermute x6, waiting for transfers between devices, triple_shift(): return lax.ppermute(value, 'tensor', pairs)  25.7 us
    ppermute x3, starting transfers between devices, triple_swap(): return lax.ppermute(value, 'tensor', [(r, (r + 3) % 6) for r in range(6)])  20.4 us
    ppermute x3, waiting for transfers between devices, triple_swap(): return lax.ppermute(value, 'tensor', [(r, (r + 3) % 6) for r in range(6)])  20.2 us
    ppermute x1, waiting for transfers between devices, odd_keys(): lax.ppermute(value, 'dp', [(i, (i + (1 if i % 2 == 0 else 3)) % count) fo...  9.1 us
    ppermute x2, starting transfers between devices, core_swap(): return lax.ppermute(value, 'dp', [(i, i ^ 1) for i in range(count)])  6.09 us
  transfers between devices with their start and end apart: 17, of which 13 were waited for; matrix products, arithmetic and copies ran while one was open for 2% of the time, Pallas kernels for 0%

profile of v4, /device:TPU:1, one launch (start us, length us, event | category | flops | bytes accessed | tf_op | source)
XLA Modules:
  0.0 206.8 jit_solution(11667132790351931424)
XLA Ops:
  0.7 1.1 pad_maximum_fusion.2
  1.8 15.8 %collective-permute-start.2 = (bf16[400,640]{1,0:T(8,128)(2,1)S(1)}, bf16[400,640]{1,0:T(8,128)(2,1)S(1)}, u32[]{:S(2)}, u32[]{:S(2)}) collective-permute-start(bf16[400,640]{1,0:T(8,128)(2,1)S(1)} %pad_maximum_fusion.2), channel_id=1, source_target_pairs={{0,12},{6,18},{12,24},{18,30},{24,36},{30,42},{36,48},{42,54},{48,... | collective-permute-start | bytes 1536008 | tf_op jit(solution)/shard_map/ppermute | solution.py:16
  17.7 4.0 %collective-permute-start.1 = (bf16[400,640]{1,0:T(8,128)(2,1)S(1)}, bf16[400,640]{1,0:T(8,128)(2,1)S(1)}, u32[]{:S(2)}, u32[]{:S(2)}) collective-permute-start(bf16[400,640]{1,0:T(8,128)(2,1)S(1)} %pad_maximum_fusion.2), channel_id=1, source_target_pairs={{0,6},{6,24},{12,18},{18,36},{24,30},{30,48},{36,42},{42,60},{48,5... | collective-permute-start | bytes 1536008 | tf_op jit(solution)/shard_map/ppermute | solution.py:26
  21.6 3.1 %collective-permute-start = (bf16[400,640]{1,0:T(8,128)(2,1)S(1)}, bf16[400,640]{1,0:T(8,128)(2,1)S(1)}, u32[]{:S(2)}, u32[]{:S(2)}) collective-permute-start(bf16[400,640]{1,0:T(8,128)(2,1)S(1)} %pad_maximum_fusion.2), channel_id=1, source_target_pairs={{0,24},{6,30},{12,36},{18,42},{24,48},{30,54},{36,60},{42,66},{48,... | collective-permute-start | bytes 1536008 | tf_op jit(solution)/shard_map/ppermute | solution.py:16
  25.6 0.8 convert_add_fusion
  26.4 4.4 %collective-permute-done.2 = bf16[400,640]{1,0:T(8,128)(2,1)S(1)} collective-permute-done((bf16[400,640]{1,0:T(8,128)(2,1)S(1)}, bf16[400,640]{1,0:T(8,128)(2,1)S(1)}, u32[]{:S(2)}, u32[]{:S(2)}) %collective-permute-start.2) | collective-permute-done | bytes 512032 | tf_op jit(solution)/shard_map/ppermute | solution.py:16
  30.8 9.1 %collective-permute-done.1 = bf16[400,640]{1,0:T(8,128)(2,1)S(1)} collective-permute-done((bf16[400,640]{1,0:T(8,128)(2,1)S(1)}, bf16[400,640]{1,0:T(8,128)(2,1)S(1)}, u32[]{:S(2)}, u32[]{:S(2)}) %collective-permute-start.1) | collective-permute-done | bytes 512032 | tf_op jit(solution)/shard_map/ppermute | solution.py:26
  39.9 11.4 %collective-permute-done = bf16[400,640]{1,0:T(8,128)(2,1)S(1)} collective-permute-done((bf16[400,640]{1,0:T(8,128)(2,1)S(1)}, bf16[400,640]{1,0:T(8,128)(2,1)S(1)}, u32[]{:S(2)}, u32[]{:S(2)}) %collective-permute-start) | collective-permute-done | bytes 512032 | tf_op jit(solution)/shard_map/ppermute | solution.py:16
  52.3 8.0 %collective-permute-start.3 = (f32[128,768]{1,0:T(8,128)S(1)}, f32[128,768]{1,0:T(8,128)S(1)}, u32[]{:S(2)}, u32[]{:S(2)}) collective-permute-start(f32[128,768]{1,0:T(8,128)S(1)} %fusion.16), channel_id=1, source_target_pairs={{0,1},{1,2},{2,0},{3,4},{4,5},{5,3},{6,7},{7,8},{8,6},{9,10},{10,1... | collective-permute-start | bytes 1179656 | tf_op jit(solution)/shard_map/ppermute | solution.py:36
  60.3 1.9 collective-permute-start.5
  62.2 3.7 %collective-permute-start.4 = (bf16[400,640]{1,0:T(8,128)(2,1)S(1)}, bf16[400,640]{1,0:T(8,128)(2,1)S(1)}, u32[]{:S(2)}, u32[]{:S(2)}) collective-permute-start(bf16[400,640]{1,0:T(8,128)(2,1)S(1)} %collective-permute-done.2), channel_id=1, source_target_pairs={{0,6},{6,0},{12,18},{18,12},{24,30},{30,24},{36,42},{42,36},{48,54... | collective-permute-start | bytes 1536008 | tf_op jit(solution)/shard_map/ppermute | solution.py:21
  66.0 1.4 collective-permute-done.4
  68.2 3.6 %collective-permute-start.7 = (f32[128,768]{1,0:T(8,128)S(1)}, f32[128,768]{1,0:T(8,128)S(1)}, u32[]{:S(2)}, u32[]{:S(2)}) collective-permute-start(f32[128,768]{1,0:T(8,128)S(1)} %fusion.14), channel_id=1, source_target_pairs={{0,1},{1,2},{2,0},{3,4},{4,5},{5,3},{6,7},{7,8},{8,6},{9,10},{10,1... | collective-permute-start | bytes 1179656 | tf_op jit(solution)/shard_map/ppermute | solution.py:36
  72.2 2.5 %collective-permute-start.8 = (f32[128,768]{1,0:T(8,128)S(1)}, f32[128,768]{1,0:T(8,128)S(1)}, u32[]{:S(2)}, u32[]{:S(2)}) collective-permute-start(f32[128,768]{1,0:T(8,128)S(1)} %fusion.10), channel_id=1, source_target_pairs={{0,2},{1,0},{2,1},{3,5},{4,3},{5,4},{6,8},{7,6},{8,7},{9,11},{10,9... | collective-permute-start | bytes 1179656 | tf_op jit(solution)/shard_map/ppermute | solution.py:36
  74.8 0.8 collective-permute-done.5
  76.1 7.1 %collective-permute-start.6 = (f32[64,768]{1,0:T(8,128)S(1)}, f32[64,768]{1,0:T(8,128)S(1)}, u32[]{:S(2)}, u32[]{:S(2)}) collective-permute-start(f32[64,768]{1,0:T(8,128)S(1)} %constant_dynamic-slice_fusion.1), channel_id=1, source_target_pairs={{0,3},{1,4},{2,5},{3,0},{4,1},{5,2},{6,9},{7,10},{8,11},{9,6},{10,... | collective-permute-start | bytes 589832 | tf_op jit(solution)/shard_map/ppermute | solution.py:40
  83.2 0.9 collective-permute-done.7
  84.5 8.0 %collective-permute-done.8 = f32[128,768]{1,0:T(8,128)S(1)} collective-permute-done((f32[128,768]{1,0:T(8,128)S(1)}, f32[128,768]{1,0:T(8,128)S(1)}, u32[]{:S(2)}, u32[]{:S(2)}) %collective-permute-start.8) | collective-permute-done | bytes 393248 | tf_op jit(solution)/shard_map/ppermute | solution.py:36
  92.6 11.4 %collective-permute-start.9 = (f32[64,768]{1,0:T(8,128)S(1)}, f32[64,768]{1,0:T(8,128)S(1)}, u32[]{:S(2)}, u32[]{:S(2)}) collective-permute-start(f32[64,768]{1,0:T(8,128)S(1)} %constant_dynamic-slice_fusion), channel_id=1, source_target_pairs={{0,3},{1,4},{2,5},{3,0},{4,1},{5,2},{6,9},{7,10},{8,11},{9,6},{10,... | collective-permute-start | bytes 589832 | tf_op jit(solution)/shard_map/ppermute | solution.py:40
  104.0 6.7 %collective-permute-done.9 = f32[64,768]{1,0:T(8,128)S(1)} collective-permute-done((f32[64,768]{1,0:T(8,128)S(1)}, f32[64,768]{1,0:T(8,128)S(1)}, u32[]{:S(2)}, u32[]{:S(2)}) %collective-permute-start.9) | collective-permute-done | bytes 196640 | tf_op jit(solution)/shard_map/ppermute | solution.py:40
  112.1 1.9 collective-permute-start.10
  114.0 13.4 %collective-permute-done.10 = bf16[64,1536]{1,0:T(8,128)(2,1)S(1)} collective-permute-done((bf16[64,1536]{1,0:T(8,128)(2,1)S(1)}, bf16[64,1536]{1,0:T(8,128)(2,1)S(1)}, u32[]{:S(2)}, u32[]{:S(2)}) %collective-permute-start.10) | collective-permute-done | bytes 196640 | tf_op jit(solution)/shard_map/ppermute | solution.py:40
  127.7 1.9 collective-permute-start.11
  129.6 16.8 %collective-permute-start.12 = (bf16[128,1536]{1,0:T(8,128)(2,1)S(1)}, bf16[128,1536]{1,0:T(8,128)(2,1)S(1)}, u32[]{:S(2)}, u32[]{:S(2)}) collective-permute-start(bf16[128,1536]{1,0:T(8,128)(2,1)S(1)} %get-tuple-element.29), channel_id=1, source_target_pairs={{0,2},{1,0},{2,1},{3,5},{4,3},{5,4},{6,8},{7,6},{8,7},{9,11},{10,9... | collective-permute-start | bytes 1179656 | tf_op jit(solution)/shard_map/ppermute | solution.py:36
  146.4 6.5 %collective-permute-done.11 = bf16[128,1536]{1,0:T(8,128)(2,1)S(1)} collective-permute-done((bf16[128,1536]{1,0:T(8,128)(2,1)S(1)}, bf16[128,1536]{1,0:T(8,128)(2,1)S(1)}, u32[]{:S(2)}, u32[]{:S(2)}) %collective-permute-start.11) | collective-permute-done | bytes 393248 | tf_op jit(solution)/shard_map/ppermute | solution.py:36
  153.0 9.5 %collective-permute-done.12 = bf16[128,1536]{1,0:T(8,128)(2,1)S(1)} collective-permute-done((bf16[128,1536]{1,0:T(8,128)(2,1)S(1)}, bf16[128,1536]{1,0:T(8,128)(2,1)S(1)}, u32[]{:S(2)}, u32[]{:S(2)}) %collective-permute-start.12) | collective-permute-done | bytes 393248 | tf_op jit(solution)/shard_map/ppermute | solution.py:36
  163.0 2.4 %collective-permute-start.13 = (bf16[384,640]{1,0:T(8,128)(2,1)S(1)}, bf16[384,640]{1,0:T(8,128)(2,1)S(1)}, u32[]{:S(2)}, u32[]{:S(2)}) collective-permute-start(bf16[384,640]{1,0:T(8,128)(2,1)S(1)} %convolution_convert_fusion.2), channel_id=1, source_target_pairs={{0,6},{6,0},{12,18},{18,12},{24,30},{30,24},{36,42},{42,36},{48,54... | collective-permute-start | bytes 1474568 | tf_op jit(solution)/shard_map/ppermute | solution.py:21
  167.3 5.4 %collective-permute-start.14 = (bf16[384,640]{1,0:T(8,128)(2,1)S(1)}, bf16[384,640]{1,0:T(8,128)(2,1)S(1)}, u32[]{:S(2)}, u32[]{:S(2)}) collective-permute-start(bf16[384,640]{1,0:T(8,128)(2,1)S(1)} %fusion.2), channel_id=1, source_target_pairs={{0,756},{6,762},{12,0},{18,6},{24,12},{30,18},{36,24},{42,30},{48,... | collective-permute-start | bytes 1474568 | tf_op jit(solution)/shard_map/ppermute | solution.py:16
  172.7 2.6 %collective-permute-start.15 = (bf16[384,640]{1,0:T(8,128)(2,1)S(1)}, bf16[384,640]{1,0:T(8,128)(2,1)S(1)}, u32[]{:S(2)}, u32[]{:S(2)}) collective-permute-start(bf16[384,640]{1,0:T(8,128)(2,1)S(1)} %convolution_convert_fusion.1), channel_id=1, source_target_pairs={{0,744},{6,750},{12,756},{18,762},{24,0},{30,6},{36,12},{42,18},{4... | collective-permute-start | bytes 1474568 | tf_op jit(solution)/shard_map/ppermute | solution.py:16
  175.4 2.8 %collective-permute-start.16 = (bf16[384,640]{1,0:T(8,128)(2,1)S(1)}, bf16[384,640]{1,0:T(8,128)(2,1)S(1)}, u32[]{:S(2)}, u32[]{:S(2)}) collective-permute-start(bf16[384,640]{1,0:T(8,128)(2,1)S(1)} %convolution_convert_fusion), channel_id=1, source_target_pairs={{6,0},{24,6},{18,12},{36,18},{30,24},{48,30},{42,36},{60,42},{54,4... | collective-permute-start | bytes 1474568 | tf_op jit(solution)/shard_map/ppermute | solution.py:31
  178.9 26.5 %collective-permute-done.14 = bf16[384,640]{1,0:T(8,128)(2,1)S(1)} collective-permute-done((bf16[384,640]{1,0:T(8,128)(2,1)S(1)}, bf16[384,640]{1,0:T(8,128)(2,1)S(1)}, u32[]{:S(2)}, u32[]{:S(2)}) %collective-permute-start.14) | collective-permute-done | bytes 491552 | tf_op jit(solution)/shard_map/ppermute | solution.py:16
  205.4 1.4 fusion.1
  (66 shorter events, 9.4 us)
Async XLA Ops:
  1.8 49.6 %copy-start = (bf16[384,640]{1,0:T(8,128)(2,1)S(1)}, bf16[384,640]{1,0:T(8,128)(2,1)}, u32[]{:S(2)}) copy-start(bf16[384,640]{1,0:T(8,128)(2,1)} %param.6) | copy-start | bytes 1474564
  1.8 29.0 %collective-permute-start.2 = (bf16[400,640]{1,0:T(8,128)(2,1)S(1)}, bf16[400,640]{1,0:T(8,128)(2,1)S(1)}, u32[]{:S(2)}, u32[]{:S(2)}) collective-permute-start(bf16[400,640]{1,0:T(8,128)(2,1)S(1)} %pad_maximum_fusion.2), channel_id=1, source_target_pairs={{0,12},{6,18},{12,24},{18,30},{24,36},{30,42},{36,48},{42,54},{48,... | collective-permute-start | bytes 1536008 | tf_op jit(solution)/shard_map/ppermute | solution.py:16
  17.7 22.3 %collective-permute-start.1 = (bf16[400,640]{1,0:T(8,128)(2,1)S(1)}, bf16[400,640]{1,0:T(8,128)(2,1)S(1)}, u32[]{:S(2)}, u32[]{:S(2)}) collective-permute-start(bf16[400,640]{1,0:T(8,128)(2,1)S(1)} %pad_maximum_fusion.2), channel_id=1, source_target_pairs={{0,6},{6,24},{12,18},{18,36},{24,30},{30,48},{36,42},{42,60},{48,5... | collective-permute-start | bytes 1536008 | tf_op jit(solution)/shard_map/ppermute | solution.py:26
  21.6 29.7 %collective-permute-start = (bf16[400,640]{1,0:T(8,128)(2,1)S(1)}, bf16[400,640]{1,0:T(8,128)(2,1)S(1)}, u32[]{:S(2)}, u32[]{:S(2)}) collective-permute-start(bf16[400,640]{1,0:T(8,128)(2,1)S(1)} %pad_maximum_fusion.2), channel_id=1, source_target_pairs={{0,24},{6,30},{12,36},{18,42},{24,48},{30,54},{36,60},{42,66},{48,... | collective-permute-start | bytes 1536008 | tf_op jit(solution)/shard_map/ppermute | solution.py:16
  52.3 22.5 %collective-permute-start.3 = (f32[128,768]{1,0:T(8,128)S(1)}, f32[128,768]{1,0:T(8,128)S(1)}, u32[]{:S(2)}, u32[]{:S(2)}) collective-permute-start(f32[128,768]{1,0:T(8,128)S(1)} %fusion.16), channel_id=1, source_target_pairs={{0,1},{1,2},{2,0},{3,4},{4,5},{5,3},{6,7},{7,8},{8,6},{9,10},{10,1... | collective-permute-start | bytes 1179656 | tf_op jit(solution)/shard_map/ppermute | solution.py:36
  60.3 15.4 %collective-permute-start.5 = (f32[128,768]{1,0:T(8,128)S(1)}, f32[128,768]{1,0:T(8,128)S(1)}, u32[]{:S(2)}, u32[]{:S(2)}) collective-permute-start(f32[128,768]{1,0:T(8,128)S(1)} %fusion.12), channel_id=1, source_target_pairs={{0,2},{1,0},{2,1},{3,5},{4,3},{5,4},{6,8},{7,6},{8,7},{9,11},{10,9... | collective-permute-start | bytes 1179656 | tf_op jit(solution)/shard_map/ppermute | solution.py:36
  62.2 5.2 %collective-permute-start.4 = (bf16[400,640]{1,0:T(8,128)(2,1)S(1)}, bf16[400,640]{1,0:T(8,128)(2,1)S(1)}, u32[]{:S(2)}, u32[]{:S(2)}) collective-permute-start(bf16[400,640]{1,0:T(8,128)(2,1)S(1)} %collective-permute-done.2), channel_id=1, source_target_pairs={{0,6},{6,0},{12,18},{18,12},{24,30},{30,24},{36,42},{42,36},{48,54... | collective-permute-start | bytes 1536008 | tf_op jit(solution)/shard_map/ppermute | solution.py:21
  67.4 0.8 copy-start.1
  68.2 15.9 %collective-permute-start.7 = (f32[128,768]{1,0:T(8,128)S(1)}, f32[128,768]{1,0:T(8,128)S(1)}, u32[]{:S(2)}, u32[]{:S(2)}) collective-permute-start(f32[128,768]{1,0:T(8,128)S(1)} %fusion.14), channel_id=1, source_target_pairs={{0,1},{1,2},{2,0},{3,4},{4,5},{5,3},{6,7},{7,8},{8,6},{9,10},{10,1... | collective-permute-start | bytes 1179656 | tf_op jit(solution)/shard_map/ppermute | solution.py:36
  72.2 3.8 %slice-start = ((bf16[400,640]{1,0:T(8,128)(2,1)}), bf16[16,640]{1,0:T(8,128)(2,1)S(1)}, s32[]{:S(2)}) async-start(bf16[400,640]{1,0:T(8,128)(2,1)} %copy-done.1), calls=%async_computation | async-start | bytes 40960 | tf_op jit(solution)/shard_map/slice | solution.py:59
  72.2 20.3 %collective-permute-start.8 = (f32[128,768]{1,0:T(8,128)S(1)}, f32[128,768]{1,0:T(8,128)S(1)}, u32[]{:S(2)}, u32[]{:S(2)}) collective-permute-start(f32[128,768]{1,0:T(8,128)S(1)} %fusion.10), channel_id=1, source_target_pairs={{0,2},{1,0},{2,1},{3,5},{4,3},{5,4},{6,8},{7,6},{8,7},{9,11},{10,9... | collective-permute-start | bytes 1179656 | tf_op jit(solution)/shard_map/ppermute | solution.py:36
  76.1 27.9 %collective-permute-start.6 = (f32[64,768]{1,0:T(8,128)S(1)}, f32[64,768]{1,0:T(8,128)S(1)}, u32[]{:S(2)}, u32[]{:S(2)}) collective-permute-start(f32[64,768]{1,0:T(8,128)S(1)} %constant_dynamic-slice_fusion.1), channel_id=1, source_target_pairs={{0,3},{1,4},{2,5},{3,0},{4,1},{5,2},{6,9},{7,10},{8,11},{9,6},{10,... | collective-permute-start | bytes 589832 | tf_op jit(solution)/shard_map/ppermute | solution.py:40
  84.5 26.6 %copy-start.2 = (f32[384]{0:T(512)S(1)}, f32[384]{0:T(512)}, u32[]{:S(2)}) copy-start(f32[384]{0:T(512)} %param.10) | copy-start | bytes 4612
  84.5 26.7 %copy-start.3 = (f32[384]{0:T(512)S(1)}, f32[384]{0:T(512)}, u32[]{:S(2)}) copy-start(f32[384]{0:T(512)} %param.9) | copy-start | bytes 4612
  92.6 18.2 %collective-permute-start.9 = (f32[64,768]{1,0:T(8,128)S(1)}, f32[64,768]{1,0:T(8,128)S(1)}, u32[]{:S(2)}, u32[]{:S(2)}) collective-permute-start(f32[64,768]{1,0:T(8,128)S(1)} %constant_dynamic-slice_fusion), channel_id=1, source_target_pairs={{0,3},{1,4},{2,5},{3,0},{4,1},{5,2},{6,9},{7,10},{8,11},{9,6},{10,... | collective-permute-start | bytes 589832 | tf_op jit(solution)/shard_map/ppermute | solution.py:40
  112.1 15.4 %collective-permute-start.10 = (bf16[64,1536]{1,0:T(8,128)(2,1)S(1)}, bf16[64,1536]{1,0:T(8,128)(2,1)S(1)}, u32[]{:S(2)}, u32[]{:S(2)}) collective-permute-start(bf16[64,1536]{1,0:T(8,128)(2,1)S(1)} %pad_maximum_fusion.4), channel_id=1, source_target_pairs={{0,3},{1,4},{2,5},{3,0},{4,1},{5,2},{6,9},{7,10},{8,11},{9,6},{10,... | collective-permute-start | bytes 589832 | tf_op jit(solution)/shard_map/ppermute | solution.py:40
  127.7 25.2 %collective-permute-start.11 = (bf16[128,1536]{1,0:T(8,128)(2,1)S(1)}, bf16[128,1536]{1,0:T(8,128)(2,1)S(1)}, u32[]{:S(2)}, u32[]{:S(2)}) collective-permute-start(bf16[128,1536]{1,0:T(8,128)(2,1)S(1)} %get-tuple-element.29), channel_id=1, source_target_pairs={{0,1},{1,2},{2,0},{3,4},{4,5},{5,3},{6,7},{7,8},{8,6},{9,10},{10,1... | collective-permute-start | bytes 1179656 | tf_op jit(solution)/shard_map/ppermute | solution.py:36
  129.6 32.8 %collective-permute-start.12 = (bf16[128,1536]{1,0:T(8,128)(2,1)S(1)}, bf16[128,1536]{1,0:T(8,128)(2,1)S(1)}, u32[]{:S(2)}, u32[]{:S(2)}) collective-permute-start(bf16[128,1536]{1,0:T(8,128)(2,1)S(1)} %get-tuple-element.29), channel_id=1, source_target_pairs={{0,2},{1,0},{2,1},{3,5},{4,3},{5,4},{6,8},{7,6},{8,7},{9,11},{10,9... | collective-permute-start | bytes 1179656 | tf_op jit(solution)/shard_map/ppermute | solution.py:36
  163.0 3.9 %collective-permute-start.13 = (bf16[384,640]{1,0:T(8,128)(2,1)S(1)}, bf16[384,640]{1,0:T(8,128)(2,1)S(1)}, u32[]{:S(2)}, u32[]{:S(2)}) collective-permute-start(bf16[384,640]{1,0:T(8,128)(2,1)S(1)} %convolution_convert_fusion.2), channel_id=1, source_target_pairs={{0,6},{6,0},{12,18},{18,12},{24,30},{30,24},{36,42},{42,36},{48,54... | collective-permute-start | bytes 1474568 | tf_op jit(solution)/shard_map/ppermute | solution.py:21
  167.3 38.1 %collective-permute-start.14 = (bf16[384,640]{1,0:T(8,128)(2,1)S(1)}, bf16[384,640]{1,0:T(8,128)(2,1)S(1)}, u32[]{:S(2)}, u32[]{:S(2)}) collective-permute-start(bf16[384,640]{1,0:T(8,128)(2,1)S(1)} %fusion.2), channel_id=1, source_target_pairs={{0,756},{6,762},{12,0},{18,6},{24,12},{30,18},{36,24},{42,30},{48,... | collective-permute-start | bytes 1474568 | tf_op jit(solution)/shard_map/ppermute | solution.py:16
  172.7 32.7 %collective-permute-start.15 = (bf16[384,640]{1,0:T(8,128)(2,1)S(1)}, bf16[384,640]{1,0:T(8,128)(2,1)S(1)}, u32[]{:S(2)}, u32[]{:S(2)}) collective-permute-start(bf16[384,640]{1,0:T(8,128)(2,1)S(1)} %convolution_convert_fusion.1), channel_id=1, source_target_pairs={{0,744},{6,750},{12,756},{18,762},{24,0},{30,6},{36,12},{42,18},{4... | collective-permute-start | bytes 1474568 | tf_op jit(solution)/shard_map/ppermute | solution.py:16
  175.4 30.0 %collective-permute-start.16 = (bf16[384,640]{1,0:T(8,128)(2,1)S(1)}, bf16[384,640]{1,0:T(8,128)(2,1)S(1)}, u32[]{:S(2)}, u32[]{:S(2)}) collective-permute-start(bf16[384,640]{1,0:T(8,128)(2,1)S(1)} %convolution_convert_fusion), channel_id=1, source_target_pairs={{6,0},{24,6},{18,12},{36,18},{30,24},{48,30},{42,36},{60,42},{54,4... | collective-permute-start | bytes 1474568 | tf_op jit(solution)/shard_map/ppermute | solution.py:31

commit v5 on v4

--- a/solution.py
+++ b/solution.py
@@ -80,17 +80,17 @@
     return peak + jnp.log(total)
 
 
-def row_group(mine, other, u):
-    low = jnp.where(u == 0, mine, other)
-    high = jnp.where(u == 0, other, mine)
-    return jnp.concatenate([low, high], axis=0)
-
-
-def all_rows(group, first, second, v):
-    full = jnp.zeros((SEG, group.shape[1]), BF)
-    full = lax.dynamic_update_slice_in_dim(full, group, v * 128, 0)
-    full = lax.dynamic_update_slice_in_dim(full, first, ((v + 2) % 3) * 128, 0)
-    return lax.dynamic_update_slice_in_dim(full, second, ((v + 1) % 3) * 128, 0)
+def gathered(mine, u, v):
+    partner = triple_swap(mine)
+    own = (triple_shift(mine, 1), triple_shift(mine, 2))
+    partner, *own = lax.optimization_barrier((partner,) + own)
+    passed = (triple_shift(partner, 1), triple_shift(partner, 2))
+    full = jnp.zeros((SEG, mine.shape[1]), BF)
+    for half, pieces in ((u, (mine, *own)), (1 - u, (partner, *passed))):
+        for steps, piece in enumerate(pieces):
+            start = ((v + 3 - steps) % 3) * 128 + half * 64
+            full = lax.dynamic_update_slice_in_dim(full, piece, start, 0)
+    return full
 
 
 def key_grad(slopes, hidden):
@@ -108,6 +108,7 @@
     far = dp_shift(payload, 2)
     near = dp_shift(payload, 4)
     odd = odd_keys(payload)
+    pair_hidden = core_swap(after(hidden, odd))
     own_rows = rows_of(hidden, v * 128, 128)
 
     near_keys = jnp.concatenate([near[:SEG], odd[:SEG]], axis=0)
@@ -146,12 +147,12 @@
         )
         slopes.append((row_weight[:, None] * spread * score_scale).astype(BF))
     mine = jnp.concatenate(slopes, axis=1)
-    rows = row_group(mine, triple_swap(mine), u)
-    full = all_rows(rows, triple_shift(rows, 1), triple_shift(rows, 2), v)
+    full = gathered(mine, u, v)
     near_full, far_full = full[:, : 2 * SEG], full[:, 2 * SEG :]
 
-    far_back = core_swap(key_grad(far_full[:, SEG:], hidden).astype(BF))
-    far_sum = key_grad(far_full[:, :SEG], hidden) + far_back.astype(F32)
+    pair_slopes = core_swap(far_full[:, SEG:])
+    own_sum = lax.optimization_barrier(key_grad(far_full[:, :SEG], hidden))
+    far_sum = own_sum + key_grad(pair_slopes, pair_hidden)
     far_sum = far_sum.astype(BF)
     far_home = dp_shift(far_sum, -2)
 

time: 210 us -> 215 us (1.024)
  the two profiles are of different devices: /device:TPU:1 before, /device:TPU:224 now
where the time goes in v5:
time: 215 us; the launch traced here: 214 us
  waiting for transfers between devices  115 us (53%)
  starting transfers between devices  85.2 us (40%)
  matrix products  6.41 us (3%)
  other arithmetic  4.84 us (2%)
    ppermute x4, waiting for transfers between devices, dp_shift(): lax.ppermute(value, 'dp', [(i, (i + steps) % count) for i in range(count)])  61.8 us
    ppermute x8, waiting for transfers between devices, triple_shift(): return lax.ppermute(value, 'tensor', pairs)  43.2 us
    ppermute x8, starting transfers between devices, triple_shift(): return lax.ppermute(value, 'tensor', pairs)  40.3 us
    ppermute x4, starting transfers between devices, dp_shift(): lax.ppermute(value, 'dp', [(i, (i + steps) % count) for i in range(count)])  20.1 us
    ppermute x3, starting transfers between devices, triple_swap(): return lax.ppermute(value, 'tensor', [(r, (r + 3) % 6) for r in range(6)])  14.3 us
    ppermute x3, waiting for transfers between devices, triple_swap(): return lax.ppermute(value, 'tensor', [(r, (r + 3) % 6) for r in range(6)])  8.07 us
    ppermute x3, starting transfers between devices, core_swap(): return lax.ppermute(value, 'dp', [(i, i ^ 1) for i in range(count)])  5.76 us
  transfers between devices with their start and end apart: 20, of which 13 were waited for; matrix products, arithmetic and copies ran while one was open for 3% of the time, Pallas kernels for 0%

profile of v5, /device:TPU:224, one launch (start us, length us, event | category | flops | bytes accessed | tf_op | source)
XLA Modules:
  0.0 214.1 jit_solution(14895456482370429455)
XLA Ops:
  1.9 2.1 collective-permute-start.1
  3.9 3.4 %collective-permute-start = (bf16[400,640]{1,0:T(8,128)(2,1)S(1)}, bf16[400,640]{1,0:T(8,128)(2,1)S(1)}, u32[]{:S(2)}, u32[]{:S(2)}) collective-permute-start(bf16[400,640]{1,0:T(8,128)(2,1)S(1)} %pad_maximum_fusion.2), channel_id=1, source_target_pairs={{0,24},{6,30},{12,36},{18,42},{24,48},{30,54},{36,60},{42,66},{48,... | collective-permute-start | bytes 1536008 | tf_op jit(solution)/shard_map/ppermute | solution.py:16
  7.4 12.4 %collective-permute-start.2 = (bf16[400,640]{1,0:T(8,128)(2,1)S(1)}, bf16[400,640]{1,0:T(8,128)(2,1)S(1)}, u32[]{:S(2)}, u32[]{:S(2)}) collective-permute-start(bf16[400,640]{1,0:T(8,128)(2,1)S(1)} %pad_maximum_fusion.2), channel_id=1, source_target_pairs={{0,12},{6,18},{12,24},{18,30},{24,36},{30,42},{36,48},{42,54},{48,... | collective-permute-start | bytes 1536008 | tf_op jit(solution)/shard_map/ppermute | solution.py:16
  20.8 3.0 %collective-permute-done = bf16[400,640]{1,0:T(8,128)(2,1)S(1)} collective-permute-done((bf16[400,640]{1,0:T(8,128)(2,1)S(1)}, bf16[400,640]{1,0:T(8,128)(2,1)S(1)}, u32[]{:S(2)}, u32[]{:S(2)}) %collective-permute-start) | collective-permute-done | bytes 512032 | tf_op jit(solution)/shard_map/ppermute | solution.py:16
  24.7 24.6 %collective-permute-done.2 = bf16[400,640]{1,0:T(8,128)(2,1)S(1)} collective-permute-done((bf16[400,640]{1,0:T(8,128)(2,1)S(1)}, bf16[400,640]{1,0:T(8,128)(2,1)S(1)}, u32[]{:S(2)}, u32[]{:S(2)}) %collective-permute-start.2) | collective-permute-done | bytes 512032 | tf_op jit(solution)/shard_map/ppermute | solution.py:16
  49.3 13.3 %collective-permute-start.5 = (f32[128,768]{1,0:T(8,128)S(1)}, f32[128,768]{1,0:T(8,128)S(1)}, u32[]{:S(2)}, u32[]{:S(2)}) collective-permute-start(f32[128,768]{1,0:T(8,128)S(1)} %fusion.11), channel_id=1, source_target_pairs={{0,2},{1,0},{2,1},{3,5},{4,3},{5,4},{6,8},{7,6},{8,7},{9,11},{10,9... | collective-permute-start | bytes 1179656 | tf_op jit(solution)/shard_map/ppermute | solution.py:36
  62.6 1.9 collective-permute-start.3
  64.6 1.9 collective-permute-start.4
  66.6 1.7 collective-permute-done.4
  68.8 3.0 %collective-permute-start.7 = (f32[128,768]{1,0:T(8,128)S(1)}, f32[128,768]{1,0:T(8,128)S(1)}, u32[]{:S(2)}, u32[]{:S(2)}) collective-permute-start(f32[128,768]{1,0:T(8,128)S(1)} %fusion.13), channel_id=1, source_target_pairs={{0,1},{1,2},{2,0},{3,4},{4,5},{5,3},{6,7},{7,8},{8,6},{9,10},{10,1... | collective-permute-start | bytes 1179656 | tf_op jit(solution)/shard_map/ppermute | solution.py:36
  72.3 5.0 %collective-permute-start.8 = (f32[128,768]{1,0:T(8,128)S(1)}, f32[128,768]{1,0:T(8,128)S(1)}, u32[]{:S(2)}, u32[]{:S(2)}) collective-permute-start(f32[128,768]{1,0:T(8,128)S(1)} %fusion.9), channel_id=1, source_target_pairs={{0,2},{1,0},{2,1},{3,5},{4,3},{5,4},{6,8},{7,6},{8,7},{9,11},{10,9... | collective-permute-start | bytes 1179656 | tf_op jit(solution)/shard_map/ppermute | solution.py:36
  77.2 4.4 %collective-permute-done.3 = f32[128,768]{1,0:T(8,128)S(1)} collective-permute-done((f32[128,768]{1,0:T(8,128)S(1)}, f32[128,768]{1,0:T(8,128)S(1)}, u32[]{:S(2)}, u32[]{:S(2)}) %collective-permute-start.3) | collective-permute-done | bytes 393248 | tf_op jit(solution)/shard_map/ppermute | solution.py:36
  82.1 1.9 collective-permute-start.6
  84.1 5.9 %collective-permute-done.7 = f32[128,768]{1,0:T(8,128)S(1)} collective-permute-done((f32[128,768]{1,0:T(8,128)S(1)}, f32[128,768]{1,0:T(8,128)S(1)}, u32[]{:S(2)}, u32[]{:S(2)}) %collective-permute-start.7) | collective-permute-done | bytes 393248 | tf_op jit(solution)/shard_map/ppermute | solution.py:36
  90.4 18.8 %collective-permute-done.8 = f32[128,768]{1,0:T(8,128)S(1)} collective-permute-done((f32[128,768]{1,0:T(8,128)S(1)}, f32[128,768]{1,0:T(8,128)S(1)}, u32[]{:S(2)}, u32[]{:S(2)}) %collective-permute-start.8) | collective-permute-done | bytes 393248 | tf_op jit(solution)/shard_map/ppermute | solution.py:36
  109.4 1.9 collective-permute-start.9
  111.3 8.1 %collective-permute-done.9 = f32[64,768]{1,0:T(8,128)S(1)} collective-permute-done((f32[64,768]{1,0:T(8,128)S(1)}, f32[64,768]{1,0:T(8,128)S(1)}, u32[]{:S(2)}, u32[]{:S(2)}) %collective-permute-start.9) | collective-permute-done | bytes 196640 | tf_op jit(solution)/shard_map/ppermute | solution.py:40
  121.5 10.4 %collective-permute-start.10 = (bf16[64,1536]{1,0:T(8,128)(2,1)}, bf16[64,1536]{1,0:T(8,128)(2,1)S(1)}, u32[]{:S(2)}, u32[]{:S(2)}) collective-permute-start(bf16[64,1536]{1,0:T(8,128)(2,1)} %get-tuple-element.37), channel_id=1, source_target_pairs={{0,3},{1,4},{2,5},{3,0},{4,1},{5,2},{6,9},{7,10},{8,11},{9,6},{10,... | collective-permute-start | bytes 589832 | tf_op jit(solution)/shard_map/ppermute | solution.py:40
  131.9 1.9 collective-permute-start.11
  133.9 7.3 %collective-permute-start.12 = (bf16[64,1536]{1,0:T(8,128)(2,1)}, bf16[64,1536]{1,0:T(8,128)(2,1)}, u32[]{:S(2)}, u32[]{:S(2)}) collective-permute-start(bf16[64,1536]{1,0:T(8,128)(2,1)} %get-tuple-element.37), channel_id=1, source_target_pairs={{0,2},{1,0},{2,1},{3,5},{4,3},{5,4},{6,8},{7,6},{8,7},{9,11},{10,9... | collective-permute-start | bytes 589832 | tf_op jit(solution)/shard_map/ppermute | solution.py:36
  141.2 1.9 collective-permute-start.16
  143.1 4.3 %collective-permute-done.11 = bf16[64,1536]{1,0:T(8,128)(2,1)S(1)} collective-permute-done((bf16[64,1536]{1,0:T(8,128)(2,1)}, bf16[64,1536]{1,0:T(8,128)(2,1)S(1)}, u32[]{:S(2)}, u32[]{:S(2)}) %collective-permute-start.11) | collective-permute-done | bytes 196640 | tf_op jit(solution)/shard_map/ppermute | solution.py:36
  147.4 3.7 %collective-permute-done.12 = bf16[64,1536]{1,0:T(8,128)(2,1)} collective-permute-done((bf16[64,1536]{1,0:T(8,128)(2,1)}, bf16[64,1536]{1,0:T(8,128)(2,1)}, u32[]{:S(2)}, u32[]{:S(2)}) %collective-permute-start.12) | collective-permute-done | bytes 196640 | tf_op jit(solution)/shard_map/ppermute | solution.py:36
  151.1 3.6 %collective-permute-start.13 = (bf16[64,1536]{1,0:T(8,128)(2,1)S(1)}, bf16[64,1536]{1,0:T(8,128)(2,1)S(1)}, u32[]{:S(2)}, u32[]{:S(2)}) collective-permute-start(bf16[64,1536]{1,0:T(8,128)(2,1)S(1)} %collective-permute-done.10), channel_id=1, source_target_pairs={{0,1},{1,2},{2,0},{3,4},{4,5},{5,3},{6,7},{7,8},{8,6},{9,10},{10,1... | collective-permute-start | bytes 589832 | tf_op jit(solution)/shard_map/ppermute | solution.py:36
  154.8 4.3 %collective-permute-start.14 = (bf16[64,1536]{1,0:T(8,128)(2,1)S(1)}, bf16[64,1536]{1,0:T(8,128)(2,1)S(1)}, u32[]{:S(2)}, u32[]{:S(2)}) collective-permute-start(bf16[64,1536]{1,0:T(8,128)(2,1)S(1)} %collective-permute-done.10), channel_id=1, source_target_pairs={{0,2},{1,0},{2,1},{3,5},{4,3},{5,4},{6,8},{7,6},{8,7},{9,11},{10,9... | collective-permute-start | bytes 589832 | tf_op jit(solution)/shard_map/ppermute | solution.py:36
  160.1 2.8 %collective-permute-done.13 = bf16[64,1536]{1,0:T(8,128)(2,1)S(1)} collective-permute-done((bf16[64,1536]{1,0:T(8,128)(2,1)S(1)}, bf16[64,1536]{1,0:T(8,128)(2,1)S(1)}, u32[]{:S(2)}, u32[]{:S(2)}) %collective-permute-start.13) | collective-permute-done | bytes 196640 | tf_op jit(solution)/shard_map/ppermute | solution.py:36
  162.9 3.2 %collective-permute-done.14 = bf16[64,1536]{1,0:T(8,128)(2,1)S(1)} collective-permute-done((bf16[64,1536]{1,0:T(8,128)(2,1)S(1)}, bf16[64,1536]{1,0:T(8,128)(2,1)S(1)}, u32[]{:S(2)}, u32[]{:S(2)}) %collective-permute-start.14) | collective-permute-done | bytes 196640 | tf_op jit(solution)/shard_map/ppermute | solution.py:36
  166.7 1.9 collective-permute-start.15
  170.7 2.1 collective-permute-start.17
  172.8 2.7 %collective-permute-start.19 = (bf16[384,640]{1,0:T(8,128)(2,1)S(1)}, bf16[384,640]{1,0:T(8,128)(2,1)S(1)}, u32[]{:S(2)}, u32[]{:S(2)}) collective-permute-start(bf16[384,640]{1,0:T(8,128)(2,1)S(1)} %convolution_convert_fusion), channel_id=1, source_target_pairs={{6,0},{24,6},{18,12},{36,18},{30,24},{48,30},{42,36},{60,42},{54,4... | collective-permute-start | bytes 1474568 | tf_op jit(solution)/shard_map/ppermute | solution.py:31
  175.5 2.2 %collective-permute-start.18 = (bf16[384,640]{1,0:T(8,128)(2,1)S(1)}, bf16[384,640]{1,0:T(8,128)(2,1)S(1)}, u32[]{:S(2)}, u32[]{:S(2)}) collective-permute-start(bf16[384,640]{1,0:T(8,128)(2,1)S(1)} %convolution_convert_fusion.1), channel_id=1, source_target_pairs={{0,744},{6,750},{12,756},{18,762},{24,0},{30,6},{36,12},{42,18},{4... | collective-permute-start | bytes 1474568 | tf_op jit(solution)/shard_map/ppermute | solution.py:16
  178.4 34.3 %collective-permute-done.17 = bf16[384,640]{1,0:T(8,128)(2,1)S(1)} collective-permute-done((bf16[384,640]{1,0:T(8,128)(2,1)S(1)}, bf16[384,640]{1,0:T(8,128)(2,1)S(1)}, u32[]{:S(2)}, u32[]{:S(2)}) %collective-permute-start.17) | collective-permute-done | bytes 491552 | tf_op jit(solution)/shard_map/ppermute | solution.py:16
  (80 shorter events, 13.4 us)
Async XLA Ops:
  0.0 19.9 %copy-start.3 = (s32[384]{0:T(512)S(1)}, s32[384]{0:T(512)}, u32[]{:S(2)}) copy-start(s32[384]{0:T(512)} %param.8) | copy-start | bytes 4612
  0.0 19.9 %copy-start.4 = (f32[384]{0:T(512)S(1)}, f32[384]{0:T(512)}, u32[]{:S(2)}) copy-start(f32[384]{0:T(512)} %param.11) | copy-start | bytes 4612
  1.9 22.0 %copy-start = (bf16[384,640]{1,0:T(8,128)(2,1)S(1)}, bf16[384,640]{1,0:T(8,128)(2,1)}, u32[]{:S(2)}) copy-start(bf16[384,640]{1,0:T(8,128)(2,1)} %param.6) | copy-start | bytes 1474564
  1.9 18.9 %collective-permute-start.1 = (bf16[400,640]{1,0:T(8,128)(2,1)S(1)}, bf16[400,640]{1,0:T(8,128)(2,1)S(1)}, u32[]{:S(2)}, u32[]{:S(2)}) collective-permute-start(bf16[400,640]{1,0:T(8,128)(2,1)S(1)} %pad_maximum_fusion.2), channel_id=1, source_target_pairs={{0,6},{6,24},{12,18},{18,36},{24,30},{30,48},{36,42},{42,60},{48,5... | collective-permute-start | bytes 1536008 | tf_op jit(solution)/shard_map/ppermute | solution.py:26
  3.9 19.8 %collective-permute-start = (bf16[400,640]{1,0:T(8,128)(2,1)S(1)}, bf16[400,640]{1,0:T(8,128)(2,1)S(1)}, u32[]{:S(2)}, u32[]{:S(2)}) collective-permute-start(bf16[400,640]{1,0:T(8,128)(2,1)S(1)} %pad_maximum_fusion.2), channel_id=1, source_target_pairs={{0,24},{6,30},{12,36},{18,42},{24,48},{30,54},{36,60},{42,66},{48,... | collective-permute-start | bytes 1536008 | tf_op jit(solution)/shard_map/ppermute | solution.py:16
  7.4 42.0 %collective-permute-start.2 = (bf16[400,640]{1,0:T(8,128)(2,1)S(1)}, bf16[400,640]{1,0:T(8,128)(2,1)S(1)}, u32[]{:S(2)}, u32[]{:S(2)}) collective-permute-start(bf16[400,640]{1,0:T(8,128)(2,1)S(1)} %pad_maximum_fusion.2), channel_id=1, source_target_pairs={{0,12},{6,18},{12,24},{18,30},{24,36},{30,42},{36,48},{42,54},{48,... | collective-permute-start | bytes 1536008 | tf_op jit(solution)/shard_map/ppermute | solution.py:16
  49.3 32.3 %collective-permute-start.5 = (f32[128,768]{1,0:T(8,128)S(1)}, f32[128,768]{1,0:T(8,128)S(1)}, u32[]{:S(2)}, u32[]{:S(2)}) collective-permute-start(f32[128,768]{1,0:T(8,128)S(1)} %fusion.11), channel_id=1, source_target_pairs={{0,2},{1,0},{2,1},{3,5},{4,3},{5,4},{6,8},{7,6},{8,7},{9,11},{10,9... | collective-permute-start | bytes 1179656 | tf_op jit(solution)/shard_map/ppermute | solution.py:36
  62.6 19.0 %collective-permute-start.3 = (f32[128,768]{1,0:T(8,128)S(1)}, f32[128,768]{1,0:T(8,128)S(1)}, u32[]{:S(2)}, u32[]{:S(2)}) collective-permute-start(f32[128,768]{1,0:T(8,128)S(1)} %fusion.15), channel_id=1, source_target_pairs={{0,1},{1,2},{2,0},{3,4},{4,5},{5,3},{6,7},{7,8},{8,6},{9,10},{10,1... | collective-permute-start | bytes 1179656 | tf_op jit(solution)/shard_map/ppermute | solution.py:36
  64.6 3.8 %collective-permute-start.4 = (bf16[400,640]{1,0:T(8,128)(2,1)S(1)}, bf16[400,640]{1,0:T(8,128)(2,1)S(1)}, u32[]{:S(2)}, u32[]{:S(2)}) collective-permute-start(bf16[400,640]{1,0:T(8,128)(2,1)S(1)} %collective-permute-done.2), channel_id=1, source_target_pairs={{0,6},{6,0},{12,18},{18,12},{24,30},{30,24},{36,42},{42,36},{48,54... | collective-permute-start | bytes 1536008 | tf_op jit(solution)/shard_map/ppermute | solution.py:21
  68.4 21.6 %copy-start.1 = (bf16[384,640]{1,0:T(8,128)(2,1)}, bf16[384,640]{1,0:T(8,128)(2,1)S(1)}, u32[]{:S(2)}) copy-start(bf16[384,640]{1,0:T(8,128)(2,1)S(1)} %slice.119) | copy-start | bytes 1474564
  68.8 21.2 %collective-permute-start.7 = (f32[128,768]{1,0:T(8,128)S(1)}, f32[128,768]{1,0:T(8,128)S(1)}, u32[]{:S(2)}, u32[]{:S(2)}) collective-permute-start(f32[128,768]{1,0:T(8,128)S(1)} %fusion.13), channel_id=1, source_target_pairs={{0,1},{1,2},{2,0},{3,4},{4,5},{5,3},{6,7},{7,8},{8,6},{9,10},{10,1... | collective-permute-start | bytes 1179656 | tf_op jit(solution)/shard_map/ppermute | solution.py:36
  72.3 37.0 %collective-permute-start.8 = (f32[128,768]{1,0:T(8,128)S(1)}, f32[128,768]{1,0:T(8,128)S(1)}, u32[]{:S(2)}, u32[]{:S(2)}) collective-permute-start(f32[128,768]{1,0:T(8,128)S(1)} %fusion.9), channel_id=1, source_target_pairs={{0,2},{1,0},{2,1},{3,5},{4,3},{5,4},{6,8},{7,6},{8,7},{9,11},{10,9... | collective-permute-start | bytes 1179656 | tf_op jit(solution)/shard_map/ppermute | solution.py:36
  82.1 29.2 %collective-permute-start.6 = (f32[64,768]{1,0:T(8,128)S(1)}, f32[64,768]{1,0:T(8,128)S(1)}, u32[]{:S(2)}, u32[]{:S(2)}) collective-permute-start(f32[64,768]{1,0:T(8,128)S(1)} %constant_dynamic-slice_fusion.1), channel_id=1, source_target_pairs={{0,3},{1,4},{2,5},{3,0},{4,1},{5,2},{6,9},{7,10},{8,11},{9,6},{10,... | collective-permute-start | bytes 589832 | tf_op jit(solution)/shard_map/ppermute | solution.py:40
  90.4 29.2 %copy-start.5 = (f32[384]{0:T(512)S(1)}, f32[384]{0:T(512)}, u32[]{:S(2)}) copy-start(f32[384]{0:T(512)} %param.9) | copy-start | bytes 4612
  90.4 29.3 %copy-start.6 = (f32[384]{0:T(512)S(1)}, f32[384]{0:T(512)}, u32[]{:S(2)}) copy-start(f32[384]{0:T(512)} %param.10) | copy-start | bytes 4612
  109.4 10.0 %collective-permute-start.9 = (f32[64,768]{1,0:T(8,128)S(1)}, f32[64,768]{1,0:T(8,128)S(1)}, u32[]{:S(2)}, u32[]{:S(2)}) collective-permute-start(f32[64,768]{1,0:T(8,128)S(1)} %constant_dynamic-slice_fusion), channel_id=1, source_target_pairs={{0,3},{1,4},{2,5},{3,0},{4,1},{5,2},{6,9},{7,10},{8,11},{9,6},{10,... | collective-permute-start | bytes 589832 | tf_op jit(solution)/shard_map/ppermute | solution.py:40
  121.5 21.6 %collective-permute-start.10 = (bf16[64,1536]{1,0:T(8,128)(2,1)}, bf16[64,1536]{1,0:T(8,128)(2,1)S(1)}, u32[]{:S(2)}, u32[]{:S(2)}) collective-permute-start(bf16[64,1536]{1,0:T(8,128)(2,1)} %get-tuple-element.37), channel_id=1, source_target_pairs={{0,3},{1,4},{2,5},{3,0},{4,1},{5,2},{6,9},{7,10},{8,11},{9,6},{10,... | collective-permute-start | bytes 589832 | tf_op jit(solution)/shard_map/ppermute | solution.py:40
  131.9 15.5 %collective-permute-start.11 = (bf16[64,1536]{1,0:T(8,128)(2,1)}, bf16[64,1536]{1,0:T(8,128)(2,1)S(1)}, u32[]{:S(2)}, u32[]{:S(2)}) collective-permute-start(bf16[64,1536]{1,0:T(8,128)(2,1)} %get-tuple-element.37), channel_id=1, source_target_pairs={{0,1},{1,2},{2,0},{3,4},{4,5},{5,3},{6,7},{7,8},{8,6},{9,10},{10,1... | collective-permute-start | bytes 589832 | tf_op jit(solution)/shard_map/ppermute | solution.py:36
  133.9 17.2 %collective-permute-start.12 = (bf16[64,1536]{1,0:T(8,128)(2,1)}, bf16[64,1536]{1,0:T(8,128)(2,1)}, u32[]{:S(2)}, u32[]{:S(2)}) collective-permute-start(bf16[64,1536]{1,0:T(8,128)(2,1)} %get-tuple-element.37), channel_id=1, source_target_pairs={{0,2},{1,0},{2,1},{3,5},{4,3},{5,4},{6,8},{7,6},{8,7},{9,11},{10,9... | collective-permute-start | bytes 589832 | tf_op jit(solution)/shard_map/ppermute | solution.py:36
  141.2 28.4 %collective-permute-start.16 = (bf16[384,640]{1,0:T(8,128)(2,1)S(1)}, bf16[384,640]{1,0:T(8,128)(2,1)S(1)}, u32[]{:S(2)}, u32[]{:S(2)}) collective-permute-start(bf16[384,640]{1,0:T(8,128)(2,1)S(1)} %copy-done), channel_id=1, source_target_pairs={{0,6},{6,0},{12,18},{18,12},{24,30},{30,24},{36,42},{42,36},{48,54... | collective-permute-start | bytes 1474568 | tf_op jit(solution)/shard_map/ppermute | solution.py:21
  151.1 11.8 %collective-permute-start.13 = (bf16[64,1536]{1,0:T(8,128)(2,1)S(1)}, bf16[64,1536]{1,0:T(8,128)(2,1)S(1)}, u32[]{:S(2)}, u32[]{:S(2)}) collective-permute-start(bf16[64,1536]{1,0:T(8,128)(2,1)S(1)} %collective-permute-done.10), channel_id=1, source_target_pairs={{0,1},{1,2},{2,0},{3,4},{4,5},{5,3},{6,7},{7,8},{8,6},{9,10},{10,1... | collective-permute-start | bytes 589832 | tf_op jit(solution)/shard_map/ppermute | solution.py:36
  154.8 11.4 %collective-permute-start.14 = (bf16[64,1536]{1,0:T(8,128)(2,1)S(1)}, bf16[64,1536]{1,0:T(8,128)(2,1)S(1)}, u32[]{:S(2)}, u32[]{:S(2)}) collective-permute-start(bf16[64,1536]{1,0:T(8,128)(2,1)S(1)} %collective-permute-done.10), channel_id=1, source_target_pairs={{0,2},{1,0},{2,1},{3,5},{4,3},{5,4},{6,8},{7,6},{8,7},{9,11},{10,9... | collective-permute-start | bytes 589832 | tf_op jit(solution)/shard_map/ppermute | solution.py:36
  166.7 3.5 %collective-permute-start.15 = (bf16[384,384]{1,0:T(8,128)(2,1)S(1)}, bf16[384,384]{1,0:T(8,128)(2,1)S(1)}, u32[]{:S(2)}, u32[]{:S(2)}) collective-permute-start(bf16[384,384]{1,0:T(8,128)(2,1)S(1)} %slice.130), channel_id=1, source_target_pairs={{0,6},{6,0},{12,18},{18,12},{24,30},{30,24},{36,42},{42,36},{48,54... | collective-permute-start | bytes 884744 | tf_op jit(solution)/shard_map/ppermute | solution.py:21
  170.7 7.0 %copy-start.2 = (bf16[384,640]{1,0:T(8,128)(2,1)S(1)}, bf16[384,640]{1,0:T(8,128)(2,1)}, u32[]{:S(2)}) copy-start(bf16[384,640]{1,0:T(8,128)(2,1)} %copy-done.1) | copy-start | bytes 1474564
  170.7 41.9 %collective-permute-start.17 = (bf16[384,640]{1,0:T(8,128)(2,1)S(1)}, bf16[384,640]{1,0:T(8,128)(2,1)S(1)}, u32[]{:S(2)}, u32[]{:S(2)}) collective-permute-start(bf16[384,640]{1,0:T(8,128)(2,1)S(1)} %add_convert_fusion), channel_id=1, source_target_pairs={{0,756},{6,762},{12,0},{18,6},{24,12},{30,18},{36,24},{42,30},{48,... | collective-permute-start | bytes 1474568 | tf_op jit(solution)/shard_map/ppermute | solution.py:16
  172.8 39.9 %collective-permute-start.19 = (bf16[384,640]{1,0:T(8,128)(2,1)S(1)}, bf16[384,640]{1,0:T(8,128)(2,1)S(1)}, u32[]{:S(2)}, u32[]{:S(2)}) collective-permute-start(bf16[384,640]{1,0:T(8,128)(2,1)S(1)} %convolution_convert_fusion), channel_id=1, source_target_pairs={{6,0},{24,6},{18,12},{36,18},{30,24},{48,30},{42,36},{60,42},{54,4... | collective-permute-start | bytes 1474568 | tf_op jit(solution)/shard_map/ppermute | solution.py:31
  175.5 37.2 %collective-permute-start.18 = (bf16[384,640]{1,0:T(8,128)(2,1)S(1)}, bf16[384,640]{1,0:T(8,128)(2,1)S(1)}, u32[]{:S(2)}, u32[]{:S(2)}) collective-permute-start(bf16[384,640]{1,0:T(8,128)(2,1)S(1)} %convolution_convert_fusion.1), channel_id=1, source_target_pairs={{0,744},{6,750},{12,756},{18,762},{24,0},{30,6},{36,12},{42,18},{4... | collective-permute-start | bytes 1474568 | tf_op jit(solution)/shard_map/ppermute | solution.py:16

commit v6 on v5

--- a/solution.py
+++ b/solution.py
@@ -36,12 +36,26 @@
     return lax.ppermute(value, "tensor", pairs)
 
 
+def pair_swap(value):
+    return lax.ppermute(value, "tensor", [(r, r ^ 1) for r in range(6)])
+
+
+def stride_shift(value, steps):
+    pairs = [(2 * n + w, 2 * ((n + steps) % 3) + w) for n in range(3) for w in range(2)]
+    return lax.ppermute(value, "tensor", pairs)
+
+
 def triple_swap(value):
     return lax.ppermute(value, "tensor", [(r, (r + 3) % 6) for r in range(6)])
 
 
 def rows_of(value, start, size):
     return lax.dynamic_slice_in_dim(value, start, size, 0)
+
+
+def parity_rows(value, w):
+    starts = [((w + 2 * n) % 3) * 128 + ((w + 2 * n) // 3) * 64 for n in range(3)]
+    return jnp.concatenate([rows_of(value, start, 64) for start in starts], axis=0)
 
 
 def partial_of(queries, keys):
@@ -102,32 +116,34 @@
     core = lax.axis_index("dp") % 2
     r = lax.axis_index("tensor")
     u, v = r // 3, r % 3
+    n, w = r // 2, r % 2
     weight = cotangent * padding.astype(F32)
     payload = with_codes(hidden, targets, padding)
 
     far = dp_shift(payload, 2)
     near = dp_shift(payload, 4)
     odd = odd_keys(payload)
-    pair_hidden = core_swap(after(hidden, odd))
+    far_code = codes_of(far)
+    near, odd = lax.optimization_barrier((near, odd, far_code))[:2]
+    pair_hidden = core_swap(hidden)
     own_rows = rows_of(hidden, v * 128, 128)
 
     near_keys = jnp.concatenate([near[:SEG], odd[:SEG]], axis=0)
     near_codes = jnp.concatenate([codes_of(near), codes_of(odd)])
-    near_out = outgoing(hidden, near_keys, v)
-    near_out = lax.optimization_barrier(near_out + (far,))[:2]
-    near_group = partial_of(own_rows, near_keys)
-    near_in = (triple_shift(near_out[0], 1), triple_shift(near_out[1], 2))
+    near_out = partial_of(parity_rows(hidden, 1 - w), near_keys)
+    near_in = pair_swap(near_out)
 
     far_pair = core_swap(far)
     far_keys = jnp.concatenate([far[:SEG], far_pair[:SEG]], axis=0)
-    far_codes = jnp.concatenate([codes_of(far), codes_of(far_pair)])
+    far_codes = jnp.concatenate([far_code, codes_of(far_pair)])
     far_out = outgoing(hidden, far_keys, v)
-    near_group = near_group + after(near_in[0], *far_out) + near_in[1]
-    near_other = triple_swap(rows_of(near_group, (1 - u) * 64, 64))
+    near_group = partial_of(parity_rows(hidden, w), near_keys) + after(near_in, *far_out)
+    near_one = stride_shift(rows_of(near_group, ((n + 1) % 3) * 64, 64), 1)
+    near_two = stride_shift(rows_of(near_group, ((n + 2) % 3) * 64, 64), 2)
     far_group = partial_of(own_rows, far_keys)
     far_group = far_group + triple_shift(far_out[0], 1) + triple_shift(far_out[1], 2)
     far_other = triple_swap(rows_of(far_group, (1 - u) * 64, 64))
-    near_scores = (rows_of(near_group, u * 64, 64) + near_other) * score_scale
+    near_scores = (rows_of(near_group, n * 64, 64) + near_one + near_two) * score_scale
     far_scores = (rows_of(far_group, u * 64, 64) + far_other) * score_scale
 
     base = v * 128 + u * 64

time: 215 us -> 206 us (0.958)
  the two profiles are of different devices: /device:TPU:224 before, /device:TPU:1 now
where the time goes in v6:
time: 206 us; the launch traced here: 203 us
  starting transfers between devices  110 us (53%)
  waiting for transfers between devices  77.9 us (38%)
  matrix products  7.17 us (3%)
  other arithmetic  5.57 us (3%)
  local copies, waits for them, and re-layouts  2.52 us (1%)
    ppermute x4, waiting for transfers between devices, dp_shift(): lax.ppermute(value, 'dp', [(i, (i + steps) % count) for i in range(count)])  41.6 us
    ppermute x6, starting transfers between devices, triple_shift(): return lax.ppermute(value, 'tensor', pairs)  34.4 us
    ppermute x4, starting transfers between devices, dp_shift(): lax.ppermute(value, 'dp', [(i, (i + steps) % count) for i in range(count)])  31.1 us
    ppermute x2, waiting for transfers between devices, stride_shift(): return lax.ppermute(value, 'tensor', pairs)  14.6 us
    ppermute x1, starting transfers between devices, pair_swap(): return lax.ppermute(value, 'tensor', [(r, r ^ 1) for r in range(6)])  13.3 us
    ppermute x6, waiting for transfers between devices, triple_shift(): return lax.ppermute(value, 'tensor', pairs)  11.8 us
    ppermute x2, starting transfers between devices, stride_shift(): return lax.ppermute(value, 'tensor', pairs)  9.19 us
    ppermute x3, starting transfers between devices, core_swap(): return lax.ppermute(value, 'dp', [(i, i ^ 1) for i in range(count)])  8.99 us
  transfers between devices with their start and end apart: 20, of which 11 were waited for; matrix products, arithmetic and copies ran while one was open for 4% of the time, Pallas kernels for 0%

profile of v6, /device:TPU:1, one launch (start us, length us, event | category | flops | bytes accessed | tf_op | source)
XLA Modules:
  0.0 203.3 jit_solution(123728332525666700)
XLA Ops:
  0.8 1.1 pad_maximum_fusion.2
  1.9 15.7 %collective-permute-start.2 = (bf16[400,640]{1,0:T(8,128)(2,1)S(1)}, bf16[400,640]{1,0:T(8,128)(2,1)S(1)}, u32[]{:S(2)}, u32[]{:S(2)}) collective-permute-start(bf16[400,640]{1,0:T(8,128)(2,1)S(1)} %pad_maximum_fusion.2), channel_id=1, source_target_pairs={{0,12},{6,18},{12,24},{18,30},{24,36},{30,42},{36,48},{42,54},{48,... | collective-permute-start | bytes 1536008 | tf_op jit(solution)/shard_map/ppermute | solution.py:16
  17.6 3.1 %collective-permute-start = (bf16[400,640]{1,0:T(8,128)(2,1)S(1)}, bf16[400,640]{1,0:T(8,128)(2,1)S(1)}, u32[]{:S(2)}, u32[]{:S(2)}) collective-permute-start(bf16[400,640]{1,0:T(8,128)(2,1)S(1)} %pad_maximum_fusion.2), channel_id=1, source_target_pairs={{0,24},{6,30},{12,36},{18,42},{24,48},{30,54},{36,60},{42,66},{48,... | collective-permute-start | bytes 1536008 | tf_op jit(solution)/shard_map/ppermute | solution.py:16
  20.7 4.2 %collective-permute-start.1 = (bf16[400,640]{1,0:T(8,128)(2,1)S(1)}, bf16[400,640]{1,0:T(8,128)(2,1)S(1)}, u32[]{:S(2)}, u32[]{:S(2)}) collective-permute-start(bf16[400,640]{1,0:T(8,128)(2,1)S(1)} %pad_maximum_fusion.2), channel_id=1, source_target_pairs={{0,6},{6,24},{12,18},{18,36},{24,30},{30,48},{36,42},{42,60},{48,5... | collective-permute-start | bytes 1536008 | tf_op jit(solution)/shard_map/ppermute | solution.py:26
  26.6 4.1 %collective-permute-done.2 = bf16[400,640]{1,0:T(8,128)(2,1)S(1)} collective-permute-done((bf16[400,640]{1,0:T(8,128)(2,1)S(1)}, bf16[400,640]{1,0:T(8,128)(2,1)S(1)}, u32[]{:S(2)}, u32[]{:S(2)}) %collective-permute-start.2) | collective-permute-done | bytes 512032 | tf_op jit(solution)/shard_map/ppermute | solution.py:16
  30.8 15.2 %collective-permute-done = bf16[400,640]{1,0:T(8,128)(2,1)S(1)} collective-permute-done((bf16[400,640]{1,0:T(8,128)(2,1)S(1)}, bf16[400,640]{1,0:T(8,128)(2,1)S(1)}, u32[]{:S(2)}, u32[]{:S(2)}) %collective-permute-start) | collective-permute-done | bytes 512032 | tf_op jit(solution)/shard_map/ppermute | solution.py:16
  46.6 13.3 %collective-permute-start.3 = (f32[192,768]{1,0:T(8,128)S(1)}, f32[192,768]{1,0:T(8,128)S(1)}, u32[]{:S(2)}, u32[]{:S(2)}) collective-permute-start(f32[192,768]{1,0:T(8,128)S(1)} %fusion.8), channel_id=1, source_target_pairs={{0,1},{1,0},{2,3},{3,2},{4,5},{5,4},{6,7},{7,6},{8,9},{9,8},{10,11... | collective-permute-start | bytes 1769480 | tf_op jit(solution)/shard_map/ppermute | solution.py:40
  59.8 3.6 %collective-permute-start.4 = (bf16[400,640]{1,0:T(8,128)(2,1)S(1)}, bf16[400,640]{1,0:T(8,128)(2,1)S(1)}, u32[]{:S(2)}, u32[]{:S(2)}) collective-permute-start(bf16[400,640]{1,0:T(8,128)(2,1)S(1)} %collective-permute-done.2), channel_id=1, source_target_pairs={{0,6},{6,0},{12,18},{18,12},{24,30},{30,24},{36,42},{42,36},{48,54... | collective-permute-start | bytes 1536008 | tf_op jit(solution)/shard_map/ppermute | solution.py:21
  63.6 1.4 collective-permute-done.4
  65.5 1.9 collective-permute-start.7
  67.8 4.3 %collective-permute-start.8 = (f32[128,768]{1,0:T(8,128)S(1)}, f32[128,768]{1,0:T(8,128)S(1)}, u32[]{:S(2)}, u32[]{:S(2)}) collective-permute-start(f32[128,768]{1,0:T(8,128)S(1)} %fusion.22), channel_id=1, source_target_pairs={{0,2},{1,0},{2,1},{3,5},{4,3},{5,4},{6,8},{7,6},{8,7},{9,11},{10,9... | collective-permute-start | bytes 1179656 | tf_op jit(solution)/shard_map/ppermute | solution.py:36
  72.1 8.3 %collective-permute-done.3 = f32[192,768]{1,0:T(8,128)S(1)} collective-permute-done((f32[192,768]{1,0:T(8,128)S(1)}, f32[192,768]{1,0:T(8,128)S(1)}, u32[]{:S(2)}, u32[]{:S(2)}) %collective-permute-start.3) | collective-permute-done | bytes 589856 | tf_op jit(solution)/shard_map/ppermute | solution.py:40
  81.0 1.9 collective-permute-start.5
  82.9 7.3 %collective-permute-start.6 = (f32[64,768]{1,0:T(8,128)S(1)}, f32[64,768]{1,0:T(8,128)S(1)}, u32[]{:S(2)}, u32[]{:S(2)}) collective-permute-start(f32[64,768]{1,0:T(8,128)S(1)} %get-tuple-element.36), channel_id=1, source_target_pairs={{0,4},{1,5},{2,0},{3,1},{4,2},{5,3},{6,10},{7,11},{8,6},{9,7},{10,... | collective-permute-start | bytes 589832 | tf_op jit(solution)/shard_map/ppermute | solution.py:45
  90.7 4.0 %collective-permute-start.9 = (f32[64,768]{1,0:T(8,128)S(1)}, f32[64,768]{1,0:T(8,128)S(1)}, u32[]{:S(2)}, u32[]{:S(2)}) collective-permute-start(f32[64,768]{1,0:T(8,128)S(1)} %constant_dynamic-slice_fusion), channel_id=1, source_target_pairs={{0,3},{1,4},{2,5},{3,0},{4,1},{5,2},{6,9},{7,10},{8,11},{9,6},{10,... | collective-permute-start | bytes 589832 | tf_op jit(solution)/shard_map/ppermute | solution.py:49
  94.8 14.6 %collective-permute-done.5 = f32[64,768]{1,0:T(8,128)S(1)} collective-permute-done((f32[64,768]{1,0:T(8,128)S(1)}, f32[64,768]{1,0:T(8,128)S(1)}, u32[]{:S(2)}, u32[]{:S(2)}) %collective-permute-start.5) | collective-permute-done | bytes 196640 | tf_op jit(solution)/shard_map/ppermute | solution.py:45
  111.4 1.9 collective-permute-start.10
  113.3 11.8 %collective-permute-start.11 = (bf16[64,1536]{1,0:T(8,128)(2,1)}, bf16[64,1536]{1,0:T(8,128)(2,1)}, u32[]{:S(2)}, u32[]{:S(2)}) collective-permute-start(bf16[64,1536]{1,0:T(8,128)(2,1)} %get-tuple-element.43), channel_id=1, source_target_pairs={{0,1},{1,2},{2,0},{3,4},{4,5},{5,3},{6,7},{7,8},{8,6},{9,10},{10,1... | collective-permute-start | bytes 589832 | tf_op jit(solution)/shard_map/ppermute | solution.py:36
  125.1 10.2 %collective-permute-start.12 = (bf16[64,1536]{1,0:T(8,128)(2,1)}, bf16[64,1536]{1,0:T(8,128)(2,1)}, u32[]{:S(2)}, u32[]{:S(2)}) collective-permute-start(bf16[64,1536]{1,0:T(8,128)(2,1)} %get-tuple-element.43), channel_id=1, source_target_pairs={{0,2},{1,0},{2,1},{3,5},{4,3},{5,4},{6,8},{7,6},{8,7},{9,11},{10,9... | collective-permute-start | bytes 589832 | tf_op jit(solution)/shard_map/ppermute | solution.py:36
  135.4 3.0 %collective-permute-start.16 = (bf16[384,640]{1,0:T(8,128)(2,1)S(1)}, bf16[384,640]{1,0:T(8,128)(2,1)}, u32[]{:S(2)}, u32[]{:S(2)}) collective-permute-start(bf16[384,640]{1,0:T(8,128)(2,1)S(1)} %copy-done), channel_id=1, source_target_pairs={{0,6},{6,0},{12,18},{18,12},{24,30},{30,24},{36,42},{42,36},{48,54... | collective-permute-start | bytes 1474568 | tf_op jit(solution)/shard_map/ppermute | solution.py:21
  138.4 1.1 collective-permute-done.11
  139.5 5.0 %collective-permute-done.12 = bf16[64,1536]{1,0:T(8,128)(2,1)} collective-permute-done((bf16[64,1536]{1,0:T(8,128)(2,1)}, bf16[64,1536]{1,0:T(8,128)(2,1)}, u32[]{:S(2)}, u32[]{:S(2)}) %collective-permute-start.12) | collective-permute-done | bytes 196640 | tf_op jit(solution)/shard_map/ppermute | solution.py:36
  144.5 1.9 collective-permute-start.13
  146.4 4.3 %collective-permute-start.14 = (bf16[64,1536]{1,0:T(8,128)(2,1)S(1)}, bf16[64,1536]{1,0:T(8,128)(2,1)S(1)}, u32[]{:S(2)}, u32[]{:S(2)}) collective-permute-start(bf16[64,1536]{1,0:T(8,128)(2,1)S(1)} %collective-permute-done.10), channel_id=1, source_target_pairs={{0,2},{1,0},{2,1},{3,5},{4,3},{5,4},{6,8},{7,6},{8,7},{9,11},{10,9... | collective-permute-start | bytes 589832 | tf_op jit(solution)/shard_map/ppermute | solution.py:36
  153.3 5.0 %collective-permute-done.14 = bf16[64,1536]{1,0:T(8,128)(2,1)S(1)} collective-permute-done((bf16[64,1536]{1,0:T(8,128)(2,1)S(1)}, bf16[64,1536]{1,0:T(8,128)(2,1)S(1)}, u32[]{:S(2)}, u32[]{:S(2)}) %collective-permute-start.14) | collective-permute-done | bytes 196640 | tf_op jit(solution)/shard_map/ppermute | solution.py:36
  158.9 2.4 %collective-permute-start.15 = (bf16[384,384]{1,0:T(8,128)(2,1)S(1)}, bf16[384,384]{1,0:T(8,128)(2,1)S(1)}, u32[]{:S(2)}, u32[]{:S(2)}) collective-permute-start(bf16[384,384]{1,0:T(8,128)(2,1)S(1)} %slice.126), channel_id=1, source_target_pairs={{0,6},{6,0},{12,18},{18,12},{24,30},{30,24},{36,42},{42,36},{48,54... | collective-permute-start | bytes 884744 | tf_op jit(solution)/shard_map/ppermute | solution.py:21
  162.5 1.5 fusion.42
  164.1 10.3 %collective-permute-start.17 = (bf16[384,640]{1,0:T(8,128)(2,1)S(1)}, bf16[384,640]{1,0:T(8,128)(2,1)S(1)}, u32[]{:S(2)}, u32[]{:S(2)}) collective-permute-start(bf16[384,640]{1,0:T(8,128)(2,1)S(1)} %add_convert_fusion), channel_id=1, source_target_pairs={{0,756},{6,762},{12,0},{18,6},{24,12},{30,18},{36,24},{42,30},{48,... | collective-permute-start | bytes 1474568 | tf_op jit(solution)/shard_map/ppermute | solution.py:16
  174.4 1.9 collective-permute-start.18
  176.4 2.6 %collective-permute-start.19 = (bf16[384,640]{1,0:T(8,128)(2,1)S(1)}, bf16[384,640]{1,0:T(8,128)(2,1)S(1)}, u32[]{:S(2)}, u32[]{:S(2)}) collective-permute-start(bf16[384,640]{1,0:T(8,128)(2,1)S(1)} %convolution_convert_fusion), channel_id=1, source_target_pairs={{6,0},{24,6},{18,12},{36,18},{30,24},{48,30},{42,36},{60,42},{54,4... | collective-permute-start | bytes 1474568 | tf_op jit(solution)/shard_map/ppermute | solution.py:31
  179.6 22.3 %collective-permute-done.17 = bf16[384,640]{1,0:T(8,128)(2,1)S(1)} collective-permute-done((bf16[384,640]{1,0:T(8,128)(2,1)S(1)}, bf16[384,640]{1,0:T(8,128)(2,1)S(1)}, u32[]{:S(2)}, u32[]{:S(2)}) %collective-permute-start.17) | collective-permute-done | bytes 491552 | tf_op jit(solution)/shard_map/ppermute | solution.py:16
  201.9 1.4 fusion.1
  (77 shorter events, 12.2 us)
Async XLA Ops:
  0.0 26.5 %copy-start = (bf16[384,640]{1,0:T(8,128)(2,1)S(1)}, bf16[384,640]{1,0:T(8,128)(2,1)}, u32[]{:S(2)}) copy-start(bf16[384,640]{1,0:T(8,128)(2,1)} %param.6) | copy-start | bytes 1474564
  1.9 28.9 %collective-permute-start.2 = (bf16[400,640]{1,0:T(8,128)(2,1)S(1)}, bf16[400,640]{1,0:T(8,128)(2,1)S(1)}, u32[]{:S(2)}, u32[]{:S(2)}) collective-permute-start(bf16[400,640]{1,0:T(8,128)(2,1)S(1)} %pad_maximum_fusion.2), channel_id=1, source_target_pairs={{0,12},{6,18},{12,24},{18,30},{24,36},{30,42},{36,48},{42,54},{48,... | collective-permute-start | bytes 1536008 | tf_op jit(solution)/shard_map/ppermute | solution.py:16
  17.6 28.4 %collective-permute-start = (bf16[400,640]{1,0:T(8,128)(2,1)S(1)}, bf16[400,640]{1,0:T(8,128)(2,1)S(1)}, u32[]{:S(2)}, u32[]{:S(2)}) collective-permute-start(bf16[400,640]{1,0:T(8,128)(2,1)S(1)} %pad_maximum_fusion.2), channel_id=1, source_target_pairs={{0,24},{6,30},{12,36},{18,42},{24,48},{30,54},{36,60},{42,66},{48,... | collective-permute-start | bytes 1536008 | tf_op jit(solution)/shard_map/ppermute | solution.py:16
  20.7 25.3 %collective-permute-start.1 = (bf16[400,640]{1,0:T(8,128)(2,1)S(1)}, bf16[400,640]{1,0:T(8,128)(2,1)S(1)}, u32[]{:S(2)}, u32[]{:S(2)}) collective-permute-start(bf16[400,640]{1,0:T(8,128)(2,1)S(1)} %pad_maximum_fusion.2), channel_id=1, source_target_pairs={{0,6},{6,24},{12,18},{18,36},{24,30},{30,48},{36,42},{42,60},{48,5... | collective-permute-start | bytes 1536008 | tf_op jit(solution)/shard_map/ppermute | solution.py:26
  46.6 33.9 %collective-permute-start.3 = (f32[192,768]{1,0:T(8,128)S(1)}, f32[192,768]{1,0:T(8,128)S(1)}, u32[]{:S(2)}, u32[]{:S(2)}) collective-permute-start(f32[192,768]{1,0:T(8,128)S(1)} %fusion.8), channel_id=1, source_target_pairs={{0,1},{1,0},{2,3},{3,2},{4,5},{5,4},{6,7},{7,6},{8,9},{9,8},{10,11... | collective-permute-start | bytes 1769480 | tf_op jit(solution)/shard_map/ppermute | solution.py:40
  59.8 5.1 %collective-permute-start.4 = (bf16[400,640]{1,0:T(8,128)(2,1)S(1)}, bf16[400,640]{1,0:T(8,128)(2,1)S(1)}, u32[]{:S(2)}, u32[]{:S(2)}) collective-permute-start(bf16[400,640]{1,0:T(8,128)(2,1)S(1)} %collective-permute-done.2), channel_id=1, source_target_pairs={{0,6},{6,0},{12,18},{18,12},{24,30},{30,24},{36,42},{42,36},{48,54... | collective-permute-start | bytes 1536008 | tf_op jit(solution)/shard_map/ppermute | solution.py:21
  65.0 25.2 %copy-start.1 = (bf16[384,640]{1,0:T(8,128)(2,1)}, bf16[384,640]{1,0:T(8,128)(2,1)S(1)}, u32[]{:S(2)}) copy-start(bf16[384,640]{1,0:T(8,128)(2,1)S(1)} %slice.119) | copy-start | bytes 1474564
  65.5 24.7 %collective-permute-start.7 = (f32[128,768]{1,0:T(8,128)S(1)}, f32[128,768]{1,0:T(8,128)S(1)}, u32[]{:S(2)}, u32[]{:S(2)}) collective-permute-start(f32[128,768]{1,0:T(8,128)S(1)} %fusion.24), channel_id=1, source_target_pairs={{0,1},{1,2},{2,0},{3,4},{4,5},{5,3},{6,7},{7,8},{8,6},{9,10},{10,1... | collective-permute-start | bytes 1179656 | tf_op jit(solution)/shard_map/ppermute | solution.py:36
  67.8 22.8 %collective-permute-start.8 = (f32[128,768]{1,0:T(8,128)S(1)}, f32[128,768]{1,0:T(8,128)S(1)}, u32[]{:S(2)}, u32[]{:S(2)}) collective-permute-start(f32[128,768]{1,0:T(8,128)S(1)} %fusion.22), channel_id=1, source_target_pairs={{0,2},{1,0},{2,1},{3,5},{4,3},{5,4},{6,8},{7,6},{8,7},{9,11},{10,9... | collective-permute-start | bytes 1179656 | tf_op jit(solution)/shard_map/ppermute | solution.py:36
  81.0 28.3 %collective-permute-start.5 = (f32[64,768]{1,0:T(8,128)S(1)}, f32[64,768]{1,0:T(8,128)S(1)}, u32[]{:S(2)}, u32[]{:S(2)}) collective-permute-start(f32[64,768]{1,0:T(8,128)S(1)} %get-tuple-element.35), channel_id=1, source_target_pairs={{0,2},{1,3},{2,4},{3,5},{4,0},{5,1},{6,8},{7,9},{8,10},{9,11},{10,... | collective-permute-start | bytes 589832 | tf_op jit(solution)/shard_map/ppermute | solution.py:45
  82.9 26.4 %collective-permute-start.6 = (f32[64,768]{1,0:T(8,128)S(1)}, f32[64,768]{1,0:T(8,128)S(1)}, u32[]{:S(2)}, u32[]{:S(2)}) collective-permute-start(f32[64,768]{1,0:T(8,128)S(1)} %get-tuple-element.36), channel_id=1, source_target_pairs={{0,4},{1,5},{2,0},{3,1},{4,2},{5,3},{6,10},{7,11},{8,6},{9,7},{10,... | collective-permute-start | bytes 589832 | tf_op jit(solution)/shard_map/ppermute | solution.py:45
  90.7 18.9 %copy-start.3 = (f32[384]{0:T(512)S(1)}, f32[384]{0:T(512)}, u32[]{:S(2)}) copy-start(f32[384]{0:T(512)} %param.10) | copy-start | bytes 4612
  90.7 19.0 %copy-start.4 = (f32[384]{0:T(512)S(1)}, f32[384]{0:T(512)}, u32[]{:S(2)}) copy-start(f32[384]{0:T(512)} %param.9) | copy-start | bytes 4612
  90.7 18.6 %collective-permute-start.9 = (f32[64,768]{1,0:T(8,128)S(1)}, f32[64,768]{1,0:T(8,128)S(1)}, u32[]{:S(2)}, u32[]{:S(2)}) collective-permute-start(f32[64,768]{1,0:T(8,128)S(1)} %constant_dynamic-slice_fusion), channel_id=1, source_target_pairs={{0,3},{1,4},{2,5},{3,0},{4,1},{5,2},{6,9},{7,10},{8,11},{9,6},{10,... | collective-permute-start | bytes 589832 | tf_op jit(solution)/shard_map/ppermute | solution.py:49
  111.4 27.0 %collective-permute-start.10 = (bf16[64,1536]{1,0:T(8,128)(2,1)}, bf16[64,1536]{1,0:T(8,128)(2,1)S(1)}, u32[]{:S(2)}, u32[]{:S(2)}) collective-permute-start(bf16[64,1536]{1,0:T(8,128)(2,1)} %get-tuple-element.43), channel_id=1, source_target_pairs={{0,3},{1,4},{2,5},{3,0},{4,1},{5,2},{6,9},{7,10},{8,11},{9,6},{10,... | collective-permute-start | bytes 589832 | tf_op jit(solution)/shard_map/ppermute | solution.py:49
  113.3 26.1 %collective-permute-start.11 = (bf16[64,1536]{1,0:T(8,128)(2,1)}, bf16[64,1536]{1,0:T(8,128)(2,1)}, u32[]{:S(2)}, u32[]{:S(2)}) collective-permute-start(bf16[64,1536]{1,0:T(8,128)(2,1)} %get-tuple-element.43), channel_id=1, source_target_pairs={{0,1},{1,2},{2,0},{3,4},{4,5},{5,3},{6,7},{7,8},{8,6},{9,10},{10,1... | collective-permute-start | bytes 589832 | tf_op jit(solution)/shard_map/ppermute | solution.py:36
  125.1 19.4 %collective-permute-start.12 = (bf16[64,1536]{1,0:T(8,128)(2,1)}, bf16[64,1536]{1,0:T(8,128)(2,1)}, u32[]{:S(2)}, u32[]{:S(2)}) collective-permute-start(bf16[64,1536]{1,0:T(8,128)(2,1)} %get-tuple-element.43), channel_id=1, source_target_pairs={{0,2},{1,0},{2,1},{3,5},{4,3},{5,4},{6,8},{7,6},{8,7},{9,11},{10,9... | collective-permute-start | bytes 589832 | tf_op jit(solution)/shard_map/ppermute | solution.py:36
  135.4 26.9 %collective-permute-start.16 = (bf16[384,640]{1,0:T(8,128)(2,1)S(1)}, bf16[384,640]{1,0:T(8,128)(2,1)}, u32[]{:S(2)}, u32[]{:S(2)}) collective-permute-start(bf16[384,640]{1,0:T(8,128)(2,1)S(1)} %copy-done), channel_id=1, source_target_pairs={{0,6},{6,0},{12,18},{18,12},{24,30},{30,24},{36,42},{42,36},{48,54... | collective-permute-start | bytes 1474568 | tf_op jit(solution)/shard_map/ppermute | solution.py:21
  144.5 8.8 %collective-permute-start.13 = (bf16[64,1536]{1,0:T(8,128)(2,1)S(1)}, bf16[64,1536]{1,0:T(8,128)(2,1)S(1)}, u32[]{:S(2)}, u32[]{:S(2)}) collective-permute-start(bf16[64,1536]{1,0:T(8,128)(2,1)S(1)} %collective-permute-done.10), channel_id=1, source_target_pairs={{0,1},{1,2},{2,0},{3,4},{4,5},{5,3},{6,7},{7,8},{8,6},{9,10},{10,1... | collective-permute-start | bytes 589832 | tf_op jit(solution)/shard_map/ppermute | solution.py:36
  146.4 11.9 %collective-permute-start.14 = (bf16[64,1536]{1,0:T(8,128)(2,1)S(1)}, bf16[64,1536]{1,0:T(8,128)(2,1)S(1)}, u32[]{:S(2)}, u32[]{:S(2)}) collective-permute-start(bf16[64,1536]{1,0:T(8,128)(2,1)S(1)} %collective-permute-done.10), channel_id=1, source_target_pairs={{0,2},{1,0},{2,1},{3,5},{4,3},{5,4},{6,8},{7,6},{8,7},{9,11},{10,9... | collective-permute-start | bytes 589832 | tf_op jit(solution)/shard_map/ppermute | solution.py:36
  158.9 3.6 %collective-permute-start.15 = (bf16[384,384]{1,0:T(8,128)(2,1)S(1)}, bf16[384,384]{1,0:T(8,128)(2,1)S(1)}, u32[]{:S(2)}, u32[]{:S(2)}) collective-permute-start(bf16[384,384]{1,0:T(8,128)(2,1)S(1)} %slice.126), channel_id=1, source_target_pairs={{0,6},{6,0},{12,18},{18,12},{24,30},{30,24},{36,42},{42,36},{48,54... | collective-permute-start | bytes 884744 | tf_op jit(solution)/shard_map/ppermute | solution.py:21
  164.1 14.9 %copy-start.2 = (bf16[384,640]{1,0:T(8,128)(2,1)S(1)}, bf16[384,640]{1,0:T(8,128)(2,1)}, u32[]{:S(2)}) copy-start(bf16[384,640]{1,0:T(8,128)(2,1)} %copy-done.1) | copy-start | bytes 1474564
  164.1 37.8 %collective-permute-start.17 = (bf16[384,640]{1,0:T(8,128)(2,1)S(1)}, bf16[384,640]{1,0:T(8,128)(2,1)S(1)}, u32[]{:S(2)}, u32[]{:S(2)}) collective-permute-start(bf16[384,640]{1,0:T(8,128)(2,1)S(1)} %add_convert_fusion), channel_id=1, source_target_pairs={{0,756},{6,762},{12,0},{18,6},{24,12},{30,18},{36,24},{42,30},{48,... | collective-permute-start | bytes 1474568 | tf_op jit(solution)/shard_map/ppermute | solution.py:16
  174.4 27.5 %collective-permute-start.18 = (bf16[384,640]{1,0:T(8,128)(2,1)S(1)}, bf16[384,640]{1,0:T(8,128)(2,1)S(1)}, u32[]{:S(2)}, u32[]{:S(2)}) collective-permute-start(bf16[384,640]{1,0:T(8,128)(2,1)S(1)} %convolution_convert_fusion.1), channel_id=1, source_target_pairs={{0,744},{6,750},{12,756},{18,762},{24,0},{30,6},{36,12},{42,18},{4... | collective-permute-start | bytes 1474568 | tf_op jit(solution)/shard_map/ppermute | solution.py:16
  176.4 25.5 %collective-permute-start.19 = (bf16[384,640]{1,0:T(8,128)(2,1)S(1)}, bf16[384,640]{1,0:T(8,128)(2,1)S(1)}, u32[]{:S(2)}, u32[]{:S(2)}) collective-permute-start(bf16[384,640]{1,0:T(8,128)(2,1)S(1)} %convolution_convert_fusion), channel_id=1, source_target_pairs={{6,0},{24,6},{18,12},{36,18},{30,24},{48,30},{42,36},{60,42},{54,4... | collective-permute-start | bytes 1474568 | tf_op jit(solution)/shard_map/ppermute | solution.py:31

commit v7 on v6

--- a/solution.py
+++ b/solution.py
@@ -124,7 +124,6 @@
     near = dp_shift(payload, 4)
     odd = odd_keys(payload)
     far_code = codes_of(far)
-    near, odd = lax.optimization_barrier((near, odd, far_code))[:2]
     pair_hidden = core_swap(hidden)
     own_rows = rows_of(hidden, v * 128, 128)
 
@@ -133,11 +132,12 @@
     near_out = partial_of(parity_rows(hidden, 1 - w), near_keys)
     near_in = pair_swap(near_out)
 
+    near_group = partial_of(parity_rows(hidden, w), near_keys) + near_in
     far_pair = core_swap(far)
     far_keys = jnp.concatenate([far[:SEG], far_pair[:SEG]], axis=0)
     far_codes = jnp.concatenate([far_code, codes_of(far_pair)])
+    far_keys, near_group = lax.optimization_barrier((far_keys, near_group))
     far_out = outgoing(hidden, far_keys, v)
-    near_group = partial_of(parity_rows(hidden, w), near_keys) + after(near_in, *far_out)
     near_one = stride_shift(rows_of(near_group, ((n + 1) % 3) * 64, 64), 1)
     near_two = stride_shift(rows_of(near_group, ((n + 2) % 3) * 64, 64), 2)
     far_group = partial_of(own_rows, far_keys)

time: 206 us -> 211 us (1.024)
  waiting for transfers between devices: 77.9 us -> 94.1 us
  starting transfers between devices: 110 us -> 97.1 us
    ppermute x1, starting transfers between devices: 13.3 us -> 3.1 us  [pair_swap(): return lax.ppermute(value, 'tensor', [(r, r ^ 1) for r in range(6)])]
    ppermute x4, waiting for transfers between devices: 41.6 us -> 50.3 us  [dp_shift(): lax.ppermute(value, 'dp', [(i, (i + steps) % count) for i in range(count)])]
    ppermute x6, waiting for transfers between devices: 11.8 us -> 19 us  [triple_shift(): return lax.ppermute(value, 'tensor', pairs)]
    ppermute x1, waiting for transfers between devices: 8.32 us -> 10.4 us  [pair_swap(): return lax.ppermute(value, 'tensor', [(r, r ^ 1) for r in range(6)])]
  transfers between devices with their start and end apart: 20 -> 20, of which waited for: 11 -> 12; matrix products, arithmetic and copies ran while one was open for 4% -> 3% of each run, Pallas kernels for 0% -> 0%
where the time goes in v7:
time: 211 us; the launch traced here: 207 us
  starting transfers between devices  97.1 us (46%)
  waiting for transfers between devices  94.1 us (45%)
  matrix products  7.13 us (3%)
  other arithmetic  4.89 us (2%)
  local copies, waits for them, and re-layouts  3.17 us (2%)
    ppermute x4, waiting for transfers between devices, dp_shift(): lax.ppermute(value, 'dp', [(i, (i + steps) % count) for i in range(count)])  50.3 us
    ppermute x6, starting transfers between devices, triple_shift(): return lax.ppermute(value, 'tensor', pairs)  33.2 us
    ppermute x4, starting transfers between devices, dp_shift(): lax.ppermute(value, 'dp', [(i, (i + steps) % count) for i in range(count)])  30 us
    ppermute x6, waiting for transfers between devices, triple_shift(): return lax.ppermute(value, 'tensor', pairs)  19 us
    ppermute x2, waiting for transfers between devices, stride_shift(): return lax.ppermute(value, 'tensor', pairs)  12.5 us
    ppermute x1, waiting for transfers between devices, pair_swap(): return lax.ppermute(value, 'tensor', [(r, r ^ 1) for r in range(6)])  10.4 us
    ppermute x2, starting transfers between devices, stride_shift(): return lax.ppermute(value, 'tensor', pairs)  9.19 us
    ppermute x2, starting transfers between devices, triple_swap(): return lax.ppermute(value, 'tensor', [(r, (r + 3) % 6) for r in range(6)])  7.51 us
  transfers between devices with their start and end apart: 20, of which 12 were waited for; matrix products, arithmetic and copies ran while one was open for 3% of the time, Pallas kernels for 0%

profile of v7, /device:TPU:1, one launch (start us, length us, event | category | flops | bytes accessed | tf_op | source)
XLA Modules:
  0.0 207.4 jit_solution(4434799632983500445)
XLA Ops:
  1.9 3.9 %collective-permute-start = (bf16[400,640]{1,0:T(8,128)(2,1)S(1)}, bf16[400,640]{1,0:T(8,128)(2,1)S(1)}, u32[]{:S(2)}, u32[]{:S(2)}) collective-permute-start(bf16[400,640]{1,0:T(8,128)(2,1)S(1)} %pad_maximum_fusion.2), channel_id=1, source_target_pairs={{0,24},{6,30},{12,36},{18,42},{24,48},{30,54},{36,60},{42,66},{48,... | collective-permute-start | bytes 1536008 | tf_op jit(solution)/shard_map/ppermute | solution.py:16
  5.8 4.0 %collective-permute-start.1 = (bf16[400,640]{1,0:T(8,128)(2,1)S(1)}, bf16[400,640]{1,0:T(8,128)(2,1)S(1)}, u32[]{:S(2)}, u32[]{:S(2)}) collective-permute-start(bf16[400,640]{1,0:T(8,128)(2,1)S(1)} %pad_maximum_fusion.2), channel_id=1, source_target_pairs={{0,6},{6,24},{12,18},{18,36},{24,30},{30,48},{36,42},{42,60},{48,5... | collective-permute-start | bytes 1536008 | tf_op jit(solution)/shard_map/ppermute | solution.py:26
  9.8 14.9 %collective-permute-start.2 = (bf16[400,640]{1,0:T(8,128)(2,1)S(1)}, bf16[400,640]{1,0:T(8,128)(2,1)S(1)}, u32[]{:S(2)}, u32[]{:S(2)}) collective-permute-start(bf16[400,640]{1,0:T(8,128)(2,1)S(1)} %pad_maximum_fusion.2), channel_id=1, source_target_pairs={{0,12},{6,18},{12,24},{18,30},{24,36},{30,42},{36,48},{42,54},{48,... | collective-permute-start | bytes 1536008 | tf_op jit(solution)/shard_map/ppermute | solution.py:16
  26.6 3.1 %collective-permute-start.4 = (f32[192,768]{1,0:T(8,128)S(1)}, f32[192,768]{1,0:T(8,128)S(1)}, u32[]{:S(2)}, u32[]{:S(2)}) collective-permute-start(f32[192,768]{1,0:T(8,128)S(1)} %fusion.9), channel_id=1, source_target_pairs={{0,1},{1,0},{2,3},{3,2},{4,5},{5,4},{6,7},{7,6},{8,9},{9,8},{10,11... | collective-permute-start | bytes 1769480 | tf_op jit(solution)/shard_map/ppermute | solution.py:40
  29.8 27.1 %collective-permute-done.2 = bf16[400,640]{1,0:T(8,128)(2,1)S(1)} collective-permute-done((bf16[400,640]{1,0:T(8,128)(2,1)S(1)}, bf16[400,640]{1,0:T(8,128)(2,1)S(1)}, u32[]{:S(2)}, u32[]{:S(2)}) %collective-permute-start.2) | collective-permute-done | bytes 512032 | tf_op jit(solution)/shard_map/ppermute | solution.py:16
  56.9 1.9 collective-permute-start.3
  58.9 1.7 collective-permute-done.3
  61.4 10.4 %collective-permute-done.4 = f32[192,768]{1,0:T(8,128)S(1)} collective-permute-done((f32[192,768]{1,0:T(8,128)S(1)}, f32[192,768]{1,0:T(8,128)S(1)}, u32[]{:S(2)}, u32[]{:S(2)}) %collective-permute-start.4) | collective-permute-done | bytes 589856 | tf_op jit(solution)/shard_map/ppermute | solution.py:40
  72.8 1.9 collective-permute-start.7
  75.1 4.3 %collective-permute-start.8 = (f32[128,768]{1,0:T(8,128)S(1)}, f32[128,768]{1,0:T(8,128)S(1)}, u32[]{:S(2)}, u32[]{:S(2)}) collective-permute-start(f32[128,768]{1,0:T(8,128)S(1)} %fusion.20), channel_id=1, source_target_pairs={{0,2},{1,0},{2,1},{3,5},{4,3},{5,4},{6,8},{7,6},{8,7},{9,11},{10,9... | collective-permute-start | bytes 1179656 | tf_op jit(solution)/shard_map/ppermute | solution.py:36
  79.5 1.9 collective-permute-start.5
  81.4 7.3 %collective-permute-start.6 = (f32[64,768]{1,0:T(8,128)S(1)}, f32[64,768]{1,0:T(8,128)S(1)}, u32[]{:S(2)}, u32[]{:S(2)}) collective-permute-start(f32[64,768]{1,0:T(8,128)S(1)} %get-tuple-element.34), channel_id=1, source_target_pairs={{0,4},{1,5},{2,0},{3,1},{4,2},{5,3},{6,10},{7,11},{8,6},{9,7},{10,... | collective-permute-start | bytes 589832 | tf_op jit(solution)/shard_map/ppermute | solution.py:45
  88.7 6.4 %collective-permute-done.8 = f32[128,768]{1,0:T(8,128)S(1)} collective-permute-done((f32[128,768]{1,0:T(8,128)S(1)}, f32[128,768]{1,0:T(8,128)S(1)}, u32[]{:S(2)}, u32[]{:S(2)}) %collective-permute-start.8) | collective-permute-done | bytes 393248 | tf_op jit(solution)/shard_map/ppermute | solution.py:36
  95.6 5.6 %collective-permute-start.9 = (f32[64,768]{1,0:T(8,128)S(1)}, f32[64,768]{1,0:T(8,128)S(1)}, u32[]{:S(2)}, u32[]{:S(2)}) collective-permute-start(f32[64,768]{1,0:T(8,128)S(1)} %constant_dynamic-slice_fusion), channel_id=1, source_target_pairs={{0,3},{1,4},{2,5},{3,0},{4,1},{5,2},{6,9},{7,10},{8,11},{9,6},{10,... | collective-permute-start | bytes 589832 | tf_op jit(solution)/shard_map/ppermute | solution.py:49
  101.2 8.8 %collective-permute-done.5 = f32[64,768]{1,0:T(8,128)S(1)} collective-permute-done((f32[64,768]{1,0:T(8,128)S(1)}, f32[64,768]{1,0:T(8,128)S(1)}, u32[]{:S(2)}, u32[]{:S(2)}) %collective-permute-start.5) | collective-permute-done | bytes 196640 | tf_op jit(solution)/shard_map/ppermute | solution.py:45
  109.9 3.7 %collective-permute-done.6 = f32[64,768]{1,0:T(8,128)S(1)} collective-permute-done((f32[64,768]{1,0:T(8,128)S(1)}, f32[64,768]{1,0:T(8,128)S(1)}, u32[]{:S(2)}, u32[]{:S(2)}) %collective-permute-start.6) | collective-permute-done | bytes 196640 | tf_op jit(solution)/shard_map/ppermute | solution.py:45
  115.8 1.9 collective-permute-start.10
  117.7 11.6 %collective-permute-start.11 = (bf16[64,1536]{1,0:T(8,128)(2,1)}, bf16[64,1536]{1,0:T(8,128)(2,1)}, u32[]{:S(2)}, u32[]{:S(2)}) collective-permute-start(bf16[64,1536]{1,0:T(8,128)(2,1)} %get-tuple-element.41), channel_id=1, source_target_pairs={{0,1},{1,2},{2,0},{3,4},{4,5},{5,3},{6,7},{7,8},{8,6},{9,10},{10,1... | collective-permute-start | bytes 589832 | tf_op jit(solution)/shard_map/ppermute | solution.py:36
  129.3 9.3 %collective-permute-start.12 = (bf16[64,1536]{1,0:T(8,128)(2,1)}, bf16[64,1536]{1,0:T(8,128)(2,1)}, u32[]{:S(2)}, u32[]{:S(2)}) collective-permute-start(bf16[64,1536]{1,0:T(8,128)(2,1)} %get-tuple-element.41), channel_id=1, source_target_pairs={{0,2},{1,0},{2,1},{3,5},{4,3},{5,4},{6,8},{7,6},{8,7},{9,11},{10,9... | collective-permute-start | bytes 589832 | tf_op jit(solution)/shard_map/ppermute | solution.py:36
  138.5 3.0 %collective-permute-start.16 = (bf16[384,640]{1,0:T(8,128)(2,1)S(1)}, bf16[384,640]{1,0:T(8,128)(2,1)}, u32[]{:S(2)}, u32[]{:S(2)}) collective-permute-start(bf16[384,640]{1,0:T(8,128)(2,1)S(1)} %copy-done), channel_id=1, source_target_pairs={{0,6},{6,0},{12,18},{18,12},{24,30},{30,24},{36,42},{42,36},{48,54... | collective-permute-start | bytes 1474568 | tf_op jit(solution)/shard_map/ppermute | solution.py:21
  141.6 1.9 collective-permute-done.11
  143.5 5.0 %collective-permute-done.12 = bf16[64,1536]{1,0:T(8,128)(2,1)} collective-permute-done((bf16[64,1536]{1,0:T(8,128)(2,1)}, bf16[64,1536]{1,0:T(8,128)(2,1)}, u32[]{:S(2)}, u32[]{:S(2)}) %collective-permute-start.12) | collective-permute-done | bytes 196640 | tf_op jit(solution)/shard_map/ppermute | solution.py:36
  148.5 1.9 collective-permute-start.13
  150.4 4.3 %collective-permute-start.14 = (bf16[64,1536]{1,0:T(8,128)(2,1)S(1)}, bf16[64,1536]{1,0:T(8,128)(2,1)S(1)}, u32[]{:S(2)}, u32[]{:S(2)}) collective-permute-start(bf16[64,1536]{1,0:T(8,128)(2,1)S(1)} %collective-permute-done.10), channel_id=1, source_target_pairs={{0,2},{1,0},{2,1},{3,5},{4,3},{5,4},{6,8},{7,6},{8,7},{9,11},{10,9... | collective-permute-start | bytes 589832 | tf_op jit(solution)/shard_map/ppermute | solution.py:36
  157.3 5.0 %collective-permute-done.14 = bf16[64,1536]{1,0:T(8,128)(2,1)S(1)} collective-permute-done((bf16[64,1536]{1,0:T(8,128)(2,1)S(1)}, bf16[64,1536]{1,0:T(8,128)(2,1)S(1)}, u32[]{:S(2)}, u32[]{:S(2)}) %collective-permute-start.14) | collective-permute-done | bytes 196640 | tf_op jit(solution)/shard_map/ppermute | solution.py:36
  162.9 2.4 %collective-permute-start.15 = (bf16[384,384]{1,0:T(8,128)(2,1)S(1)}, bf16[384,384]{1,0:T(8,128)(2,1)S(1)}, u32[]{:S(2)}, u32[]{:S(2)}) collective-permute-start(bf16[384,384]{1,0:T(8,128)(2,1)S(1)} %slice.130), channel_id=1, source_target_pairs={{0,6},{6,0},{12,18},{18,12},{24,30},{30,24},{36,42},{42,36},{48,54... | collective-permute-start | bytes 884744 | tf_op jit(solution)/shard_map/ppermute | solution.py:21
  166.4 1.5 fusion.41
  168.1 8.7 %collective-permute-start.17 = (bf16[384,640]{1,0:T(8,128)(2,1)S(1)}, bf16[384,640]{1,0:T(8,128)(2,1)S(1)}, u32[]{:S(2)}, u32[]{:S(2)}) collective-permute-start(bf16[384,640]{1,0:T(8,128)(2,1)S(1)} %add_convert_fusion), channel_id=1, source_target_pairs={{0,756},{6,762},{12,0},{18,6},{24,12},{30,18},{36,24},{42,30},{48,... | collective-permute-start | bytes 1474568 | tf_op jit(solution)/shard_map/ppermute | solution.py:16
  176.7 2.6 %collective-permute-start.18 = (bf16[384,640]{1,0:T(8,128)(2,1)S(1)}, bf16[384,640]{1,0:T(8,128)(2,1)S(1)}, u32[]{:S(2)}, u32[]{:S(2)}) collective-permute-start(bf16[384,640]{1,0:T(8,128)(2,1)S(1)} %convolution_convert_fusion.1), channel_id=1, source_target_pairs={{0,744},{6,750},{12,756},{18,762},{24,0},{30,6},{36,12},{42,18},{4... | collective-permute-start | bytes 1474568 | tf_op jit(solution)/shard_map/ppermute | solution.py:16
  179.3 2.8 %collective-permute-start.19 = (bf16[384,640]{1,0:T(8,128)(2,1)S(1)}, bf16[384,640]{1,0:T(8,128)(2,1)S(1)}, u32[]{:S(2)}, u32[]{:S(2)}) collective-permute-start(bf16[384,640]{1,0:T(8,128)(2,1)S(1)} %convolution_convert_fusion), channel_id=1, source_target_pairs={{6,0},{24,6},{18,12},{36,18},{30,24},{48,30},{42,36},{60,42},{54,4... | collective-permute-start | bytes 1474568 | tf_op jit(solution)/shard_map/ppermute | solution.py:31
  182.8 23.2 %collective-permute-done.17 = bf16[384,640]{1,0:T(8,128)(2,1)S(1)} collective-permute-done((bf16[384,640]{1,0:T(8,128)(2,1)S(1)}, bf16[384,640]{1,0:T(8,128)(2,1)S(1)}, u32[]{:S(2)}, u32[]{:S(2)}) %collective-permute-start.17) | collective-permute-done | bytes 491552 | tf_op jit(solution)/shard_map/ppermute | solution.py:16
  206.0 1.4 fusion.1
  (83 shorter events, 13.2 us)
Async XLA Ops:
  0.0 25.1 %copy-start.4 = (s32[384]{0:T(512)S(1)}, s32[384]{0:T(512)}, u32[]{:S(2)}) copy-start(s32[384]{0:T(512)} %param.8) | copy-start | bytes 4612
  0.0 25.9 %copy-start = (bf16[384,640]{1,0:T(8,128)(2,1)S(1)}, bf16[384,640]{1,0:T(8,128)(2,1)}, u32[]{:S(2)}) copy-start(bf16[384,640]{1,0:T(8,128)(2,1)} %param.6) | copy-start | bytes 1474564
  0.0 25.1 %copy-start.5 = (f32[384]{0:T(512)S(1)}, f32[384]{0:T(512)}, u32[]{:S(2)}) copy-start(f32[384]{0:T(512)} %param.11) | copy-start | bytes 4612
  1.9 24.1 %collective-permute-start = (bf16[400,640]{1,0:T(8,128)(2,1)S(1)}, bf16[400,640]{1,0:T(8,128)(2,1)S(1)}, u32[]{:S(2)}, u32[]{:S(2)}) collective-permute-start(bf16[400,640]{1,0:T(8,128)(2,1)S(1)} %pad_maximum_fusion.2), channel_id=1, source_target_pairs={{0,24},{6,30},{12,36},{18,42},{24,48},{30,54},{36,60},{42,66},{48,... | collective-permute-start | bytes 1536008 | tf_op jit(solution)/shard_map/ppermute | solution.py:16
  5.8 20.2 %collective-permute-start.1 = (bf16[400,640]{1,0:T(8,128)(2,1)S(1)}, bf16[400,640]{1,0:T(8,128)(2,1)S(1)}, u32[]{:S(2)}, u32[]{:S(2)}) collective-permute-start(bf16[400,640]{1,0:T(8,128)(2,1)S(1)} %pad_maximum_fusion.2), channel_id=1, source_target_pairs={{0,6},{6,24},{12,18},{18,36},{24,30},{30,48},{36,42},{42,60},{48,5... | collective-permute-start | bytes 1536008 | tf_op jit(solution)/shard_map/ppermute | solution.py:26
  9.8 47.0 %collective-permute-start.2 = (bf16[400,640]{1,0:T(8,128)(2,1)S(1)}, bf16[400,640]{1,0:T(8,128)(2,1)S(1)}, u32[]{:S(2)}, u32[]{:S(2)}) collective-permute-start(bf16[400,640]{1,0:T(8,128)(2,1)S(1)} %pad_maximum_fusion.2), channel_id=1, source_target_pairs={{0,12},{6,18},{12,24},{18,30},{24,36},{30,42},{36,48},{42,54},{48,... | collective-permute-start | bytes 1536008 | tf_op jit(solution)/shard_map/ppermute | solution.py:16
  26.1 45.8 %copy-start.2 = (bf16[384,640]{1,0:T(8,128)(2,1)}, bf16[384,640]{1,0:T(8,128)(2,1)S(1)}, u32[]{:S(2)}) copy-start(bf16[384,640]{1,0:T(8,128)(2,1)S(1)} %slice.119) | copy-start | bytes 1474564
  26.6 45.3 %collective-permute-start.4 = (f32[192,768]{1,0:T(8,128)S(1)}, f32[192,768]{1,0:T(8,128)S(1)}, u32[]{:S(2)}, u32[]{:S(2)}) collective-permute-start(f32[192,768]{1,0:T(8,128)S(1)} %fusion.9), channel_id=1, source_target_pairs={{0,1},{1,0},{2,3},{3,2},{4,5},{5,4},{6,7},{7,6},{8,9},{9,8},{10,11... | collective-permute-start | bytes 1769480 | tf_op jit(solution)/shard_map/ppermute | solution.py:40
  56.9 3.8 %collective-permute-start.3 = (bf16[400,640]{1,0:T(8,128)(2,1)S(1)}, bf16[400,640]{1,0:T(8,128)(2,1)S(1)}, u32[]{:S(2)}, u32[]{:S(2)}) collective-permute-start(bf16[400,640]{1,0:T(8,128)(2,1)S(1)} %collective-permute-done.2), channel_id=1, source_target_pairs={{0,6},{6,0},{12,18},{18,12},{24,30},{30,24},{36,42},{42,36},{48,54... | collective-permute-start | bytes 1536008 | tf_op jit(solution)/shard_map/ppermute | solution.py:21
  60.6 0.8 copy-start.1
  72.3 7.1 %slice-start = ((bf16[400,640]{1,0:T(8,128)(2,1)}), bf16[16,640]{1,0:T(8,128)(2,1)S(1)}, s32[]{:S(2)}) async-start(bf16[400,640]{1,0:T(8,128)(2,1)} %copy-done.1), calls=%async_computation | async-start | bytes 40960 | tf_op jit(solution)/shard_map/slice | solution.py:73
  72.8 15.9 %collective-permute-start.7 = (f32[128,768]{1,0:T(8,128)S(1)}, f32[128,768]{1,0:T(8,128)S(1)}, u32[]{:S(2)}, u32[]{:S(2)}) collective-permute-start(f32[128,768]{1,0:T(8,128)S(1)} %fusion.22), channel_id=1, source_target_pairs={{0,1},{1,2},{2,0},{3,4},{4,5},{5,3},{6,7},{7,8},{8,6},{9,10},{10,1... | collective-permute-start | bytes 1179656 | tf_op jit(solution)/shard_map/ppermute | solution.py:36
  75.1 19.9 %collective-permute-start.8 = (f32[128,768]{1,0:T(8,128)S(1)}, f32[128,768]{1,0:T(8,128)S(1)}, u32[]{:S(2)}, u32[]{:S(2)}) collective-permute-start(f32[128,768]{1,0:T(8,128)S(1)} %fusion.20), channel_id=1, source_target_pairs={{0,2},{1,0},{2,1},{3,5},{4,3},{5,4},{6,8},{7,6},{8,7},{9,11},{10,9... | collective-permute-start | bytes 1179656 | tf_op jit(solution)/shard_map/ppermute | solution.py:36
  79.5 30.5 %collective-permute-start.5 = (f32[64,768]{1,0:T(8,128)S(1)}, f32[64,768]{1,0:T(8,128)S(1)}, u32[]{:S(2)}, u32[]{:S(2)}) collective-permute-start(f32[64,768]{1,0:T(8,128)S(1)} %get-tuple-element.33), channel_id=1, source_target_pairs={{0,2},{1,3},{2,4},{3,5},{4,0},{5,1},{6,8},{7,9},{8,10},{9,11},{10,... | collective-permute-start | bytes 589832 | tf_op jit(solution)/shard_map/ppermute | solution.py:45
  81.4 32.3 %collective-permute-start.6 = (f32[64,768]{1,0:T(8,128)S(1)}, f32[64,768]{1,0:T(8,128)S(1)}, u32[]{:S(2)}, u32[]{:S(2)}) collective-permute-start(f32[64,768]{1,0:T(8,128)S(1)} %get-tuple-element.34), channel_id=1, source_target_pairs={{0,4},{1,5},{2,0},{3,1},{4,2},{5,3},{6,10},{7,11},{8,6},{9,7},{10,... | collective-permute-start | bytes 589832 | tf_op jit(solution)/shard_map/ppermute | solution.py:45
  95.5 18.5 %copy-start.6 = (f32[384]{0:T(512)S(1)}, f32[384]{0:T(512)}, u32[]{:S(2)}) copy-start(f32[384]{0:T(512)} %param.10) | copy-start | bytes 4612
  95.5 18.5 %copy-start.7 = (f32[384]{0:T(512)S(1)}, f32[384]{0:T(512)}, u32[]{:S(2)}) copy-start(f32[384]{0:T(512)} %param.9) | copy-start | bytes 4612
  95.6 18.1 %collective-permute-start.9 = (f32[64,768]{1,0:T(8,128)S(1)}, f32[64,768]{1,0:T(8,128)S(1)}, u32[]{:S(2)}, u32[]{:S(2)}) collective-permute-start(f32[64,768]{1,0:T(8,128)S(1)} %constant_dynamic-slice_fusion), channel_id=1, source_target_pairs={{0,3},{1,4},{2,5},{3,0},{4,1},{5,2},{6,9},{7,10},{8,11},{9,6},{10,... | collective-permute-start | bytes 589832 | tf_op jit(solution)/shard_map/ppermute | solution.py:49
  115.8 25.8 %collective-permute-start.10 = (bf16[64,1536]{1,0:T(8,128)(2,1)}, bf16[64,1536]{1,0:T(8,128)(2,1)S(1)}, u32[]{:S(2)}, u32[]{:S(2)}) collective-permute-start(bf16[64,1536]{1,0:T(8,128)(2,1)} %get-tuple-element.41), channel_id=1, source_target_pairs={{0,3},{1,4},{2,5},{3,0},{4,1},{5,2},{6,9},{7,10},{8,11},{9,6},{10,... | collective-permute-start | bytes 589832 | tf_op jit(solution)/shard_map/ppermute | solution.py:49
  117.7 25.8 %collective-permute-start.11 = (bf16[64,1536]{1,0:T(8,128)(2,1)}, bf16[64,1536]{1,0:T(8,128)(2,1)}, u32[]{:S(2)}, u32[]{:S(2)}) collective-permute-start(bf16[64,1536]{1,0:T(8,128)(2,1)} %get-tuple-element.41), channel_id=1, source_target_pairs={{0,1},{1,2},{2,0},{3,4},{4,5},{5,3},{6,7},{7,8},{8,6},{9,10},{10,1... | collective-permute-start | bytes 589832 | tf_op jit(solution)/shard_map/ppermute | solution.py:36
  129.3 19.2 %collective-permute-start.12 = (bf16[64,1536]{1,0:T(8,128)(2,1)}, bf16[64,1536]{1,0:T(8,128)(2,1)}, u32[]{:S(2)}, u32[]{:S(2)}) collective-permute-start(bf16[64,1536]{1,0:T(8,128)(2,1)} %get-tuple-element.41), channel_id=1, source_target_pairs={{0,2},{1,0},{2,1},{3,5},{4,3},{5,4},{6,8},{7,6},{8,7},{9,11},{10,9... | collective-permute-start | bytes 589832 | tf_op jit(solution)/shard_map/ppermute | solution.py:36
  138.5 27.7 %collective-permute-start.16 = (bf16[384,640]{1,0:T(8,128)(2,1)S(1)}, bf16[384,640]{1,0:T(8,128)(2,1)}, u32[]{:S(2)}, u32[]{:S(2)}) collective-permute-start(bf16[384,640]{1,0:T(8,128)(2,1)S(1)} %copy-done), channel_id=1, source_target_pairs={{0,6},{6,0},{12,18},{18,12},{24,30},{30,24},{36,42},{42,36},{48,54... | collective-permute-start | bytes 1474568 | tf_op jit(solution)/shard_map/ppermute | solution.py:21
  148.5 8.8 %collective-permute-start.13 = (bf16[64,1536]{1,0:T(8,128)(2,1)S(1)}, bf16[64,1536]{1,0:T(8,128)(2,1)S(1)}, u32[]{:S(2)}, u32[]{:S(2)}) collective-permute-start(bf16[64,1536]{1,0:T(8,128)(2,1)S(1)} %collective-permute-done.10), channel_id=1, source_target_pairs={{0,1},{1,2},{2,0},{3,4},{4,5},{5,3},{6,7},{7,8},{8,6},{9,10},{10,1... | collective-permute-start | bytes 589832 | tf_op jit(solution)/shard_map/ppermute | solution.py:36
  150.4 11.9 %collective-permute-start.14 = (bf16[64,1536]{1,0:T(8,128)(2,1)S(1)}, bf16[64,1536]{1,0:T(8,128)(2,1)S(1)}, u32[]{:S(2)}, u32[]{:S(2)}) collective-permute-start(bf16[64,1536]{1,0:T(8,128)(2,1)S(1)} %collective-permute-done.10), channel_id=1, source_target_pairs={{0,2},{1,0},{2,1},{3,5},{4,3},{5,4},{6,8},{7,6},{8,7},{9,11},{10,9... | collective-permute-start | bytes 589832 | tf_op jit(solution)/shard_map/ppermute | solution.py:36
  162.9 3.6 %collective-permute-start.15 = (bf16[384,384]{1,0:T(8,128)(2,1)S(1)}, bf16[384,384]{1,0:T(8,128)(2,1)S(1)}, u32[]{:S(2)}, u32[]{:S(2)}) collective-permute-start(bf16[384,384]{1,0:T(8,128)(2,1)S(1)} %slice.130), channel_id=1, source_target_pairs={{0,6},{6,0},{12,18},{18,12},{24,30},{30,24},{36,42},{42,36},{48,54... | collective-permute-start | bytes 884744 | tf_op jit(solution)/shard_map/ppermute | solution.py:21
  168.1 37.9 %collective-permute-start.17 = (bf16[384,640]{1,0:T(8,128)(2,1)S(1)}, bf16[384,640]{1,0:T(8,128)(2,1)S(1)}, u32[]{:S(2)}, u32[]{:S(2)}) collective-permute-start(bf16[384,640]{1,0:T(8,128)(2,1)S(1)} %add_convert_fusion), channel_id=1, source_target_pairs={{0,756},{6,762},{12,0},{18,6},{24,12},{30,18},{36,24},{42,30},{48,... | collective-permute-start | bytes 1474568 | tf_op jit(solution)/shard_map/ppermute | solution.py:16
  176.7 29.3 %collective-permute-start.18 = (bf16[384,640]{1,0:T(8,128)(2,1)S(1)}, bf16[384,640]{1,0:T(8,128)(2,1)S(1)}, u32[]{:S(2)}, u32[]{:S(2)}) collective-permute-start(bf16[384,640]{1,0:T(8,128)(2,1)S(1)} %convolution_convert_fusion.1), channel_id=1, source_target_pairs={{0,744},{6,750},{12,756},{18,762},{24,0},{30,6},{36,12},{42,18},{4... | collective-permute-start | bytes 1474568 | tf_op jit(solution)/shard_map/ppermute | solution.py:16
  179.3 26.7 %collective-permute-start.19 = (bf16[384,640]{1,0:T(8,128)(2,1)S(1)}, bf16[384,640]{1,0:T(8,128)(2,1)S(1)}, u32[]{:S(2)}, u32[]{:S(2)}) collective-permute-start(bf16[384,640]{1,0:T(8,128)(2,1)S(1)} %convolution_convert_fusion), channel_id=1, source_target_pairs={{6,0},{24,6},{18,12},{36,18},{30,24},{48,30},{42,36},{60,42},{54,4... | collective-permute-start | bytes 1474568 | tf_op jit(solution)/shard_map/ppermute | solution.py:31
  182.2 23.8 %copy-start.3 = (bf16[384,640]{1,0:T(8,128)(2,1)S(1)}, bf16[384,640]{1,0:T(8,128)(2,1)}, u32[]{:S(2)}) copy-start(bf16[384,640]{1,0:T(8,128)(2,1)} %copy-done.2) | copy-start | bytes 1474564

commit v8 on v0

v8 whole, which is shorter than its diff:
```python
import math

import jax
import jax.numpy as jnp
from jax import lax
from jax.sharding import PartitionSpec as P

KW = 3840
SEG = 384
BF = jnp.bfloat16
F32 = jnp.float32


def dp_permute(value, pairs):
    return lax.ppermute(value, "dp", pairs)


def core_swap(value):
    return dp_permute(value, [(i, i ^ 1) for i in range(lax.axis_size("dp"))])


def first_keys():
    count = lax.axis_size("dp")
    return [(i, (i + (4 if i % 2 == 0 else 2)) % count) for i in range(count)]


def second_keys():
    count = lax.axis_size("dp")
    return [(i, (i + 3) % count) for i in range(count)]


def reverse(pairs):
    return [(target, source) for source, target in pairs]


def triple_shift(value, steps):
    pairs = [(3 * u + v, 3 * u + (v + steps) % 3) for u in range(2) for v in range(3)]
    return lax.ppermute(value, "tensor", pairs)


def triple_swap(value):
    return lax.ppermute(value, "tensor", [(r, (r + 3) % 6) for r in range(6)])


def rows_of(value, start, size, axis=0):
    return lax.dynamic_slice_in_dim(value, start, size, axis)


def partial_of(queries, keys):
    return lax.dot_general(queries, keys, (((1,), (1,)), ((), ())), preferred_element_type=F32)


def key_grad(slopes, hidden):
    return lax.dot_general(slopes, hidden, (((0,), (0,)), ((), ())), preferred_element_type=F32)


def with_codes(hidden, targets, padding):
    code = jnp.where(padding == 1, targets + 1, 0)
    digits = jnp.stack([code >> 8, code & 255]).astype(BF)
    tail = jnp.pad(digits, ((0, 14), (0, hidden.shape[1] - SEG)))
    return jnp.concatenate([hidden, tail], axis=0)


def codes_of(payload):
    digits = lax.optimization_barrier(payload[SEG:])[:2, :SEG].astype(F32)
    return digits[0] * 256.0 + digits[1]


def summed_part(scores, allowed, outside):
    peak = jnp.maximum(outside, jnp.max(jnp.where(allowed, scores, -1e30), axis=2))
    return peak, jnp.sum(jnp.where(allowed, jnp.exp(scores - peak[..., None]), 0.0), axis=2)


def joined_lse(outside, mine, other):
    peak = jnp.maximum(mine[0], other[0])
    total = mine[1] * jnp.exp(mine[0] - peak) + other[1] * jnp.exp(other[0] - peak)
    return peak + jnp.log(jnp.exp(outside - peak) + total)


def gathered(mine, u, v):
    partner = triple_swap(mine)
    own = (triple_shift(mine, 1), triple_shift(mine, 2))
    partner, *own = lax.optimization_barrier((partner,) + own)
    passed = (triple_shift(partner, 1), triple_shift(partner, 2))
    full = jnp.zeros((2, SEG, mine.shape[2]), BF)
    for half, pieces in ((u, (mine, *own)), (1 - u, (partner, *passed))):
        for steps, piece in enumerate(pieces):
            start = ((v + 3 - steps) % 3) * 128 + half * 64
            full = lax.dynamic_update_slice_in_dim(full, piece, start, 1)
    return full


def per_device(hidden, targets, padding, gold_logit, vocab_lse, cotangent):
    score_scale = 1.0 / math.sqrt(KW)
    core = lax.axis_index("dp") % 2
    r = lax.axis_index("tensor")
    u, v = r // 3, r % 3
    payload = with_codes(hidden, targets, padding)

    key_one = dp_permute(payload, first_keys())
    key_two = dp_permute(payload, second_keys())
    pair_hidden = core_swap(payload)[:SEG]
    weight = cotangent * padding.astype(F32)
    row_data = jnp.stack([targets.astype(F32) + 1.0, gold_logit, vocab_lse, weight])
    row_data = rows_of(row_data, v * 128 + u * 64, 64, 1)
    row_data = jnp.stack([row_data, core_swap(row_data)])
    row_codes, gold, vocab, weight = (row_data[:, i] for i in range(4))

    key_own = jnp.where(core == 0, payload, key_one)
    keys = [
        jnp.concatenate([key_one[:SEG], key_two[:SEG]], axis=0),
        jnp.concatenate([key_own[:SEG], key_two[:SEG]], axis=0),
    ]
    code_two = codes_of(key_two)
    codes = jnp.stack(
        [
            jnp.concatenate([codes_of(key_one), code_two]),
            jnp.concatenate([codes_of(key_own), code_two]),
        ]
    )

    def partial(steps):
        start = ((v + steps) % 3) * 128
        return jnp.stack(
            [
                partial_of(rows_of(queries, start, 128), read)
                for queries, read in zip((hidden, pair_hidden), keys)
            ]
        )

    first = triple_shift(partial(1), 1)
    second = triple_shift(partial(2), 2)
    group = partial(0) + first + second
    other_half = triple_swap(rows_of(group, (1 - u) * 64, 64, 1))
    scores = (rows_of(group, u * 64, 64, 1) + other_half) * score_scale

    usable = jnp.broadcast_to((codes > 0.0)[:, None], scores.shape)
    matches = usable & (codes[:, None] == row_codes[:, :, None])
    total_part = summed_part(scores, usable, vocab)
    pos_part = summed_part(scores, matches, gold)
    stats = jnp.stack([*total_part, *pos_part], axis=1)
    other = core_swap(stats)
    other = jnp.concatenate([other[1:], other[:1]], axis=0)
    total_lse = joined_lse(vocab, total_part, (other[:, 0], other[:, 1]))
    pos_lse = joined_lse(gold, pos_part, (other[:, 2], other[:, 3]))
    spread = jnp.where(usable, jnp.exp(scores - total_lse[..., None]), 0.0) - jnp.where(
        matches, jnp.exp(scores - pos_lse[..., None]), 0.0
    )
    slopes = gathered((weight[..., None] * spread * score_scale).astype(BF), u, v)

    both_hidden = jnp.concatenate([hidden, pair_hidden], axis=0)
    flat = slopes.reshape(2 * SEG, 2 * SEG)
    grad_two = key_grad(flat[:, SEG:], both_hidden).astype(BF)
    home_two = dp_permute(grad_two, reverse(second_keys()))
    pair_one = key_grad(slopes[1, :, :SEG], pair_hidden)
    grad_one = key_grad(slopes[0, :, :SEG], hidden) + jnp.where(core == 1, pair_one, 0.0)
    home_one = dp_permute(grad_one.astype(BF), reverse(first_keys()))
    pair_grad = core_swap(jnp.dot(slopes[1], keys[1], preferred_element_type=F32).astype(BF))
    own_grad = jnp.dot(slopes[0], keys[0], preferred_element_type=F32)
    own_grad = own_grad + jnp.where(core == 0, pair_one, 0.0)
    home = home_one.astype(F32) + home_two.astype(F32) + pair_grad.astype(F32)
    return (own_grad + home).astype(BF)


def solution(mesh):
    placed = (P("dp", "tensor"), P("dp"), P("dp"), P("dp"), P("dp"), P("dp"))
    return jax.shard_map(
        per_device, mesh=mesh, in_specs=placed, out_specs=P("dp", "tensor"), check_vma=False
    )
```

time: 443 us -> 208 us (0.47)
  the two profiles are of different devices: /device:TPU:78 before, /device:TPU:1 now
where the time goes in v8:
time: 208 us; the launch traced here: 207 us
  waiting for transfers between devices  105 us (50%)
  starting transfers between devices  86.1 us (41%)
  matrix products  6.22 us (3%)
  other arithmetic  5.42 us (3%)
  local copies, waits for them, and re-layouts  4.06 us (2%)
    ppermute x8, waiting for transfers between devices, dp_permute(): return lax.ppermute(value, 'dp', pairs)  50.4 us
    ppermute x8, starting transfers between devices, dp_permute(): return lax.ppermute(value, 'dp', pairs)  43.9 us
    ppermute x6, waiting for transfers between devices, triple_shift(): return lax.ppermute(value, 'tensor', pairs)  32.9 us
    ppermute x6, starting transfers between devices, triple_shift(): return lax.ppermute(value, 'tensor', pairs)  30.2 us
    ppermute x2, waiting for transfers between devices, triple_swap(): return lax.ppermute(value, 'tensor', [(r, (r + 3) % 6) for r in range(6)])  21.5 us
    ppermute x2, starting transfers between devices, triple_swap(): return lax.ppermute(value, 'tensor', [(r, (r + 3) % 6) for r in range(6)])  12 us
  transfers between devices with their start and end apart: 16, of which 11 were waited for; matrix products, arithmetic and copies ran while one was open for 3% of the time, Pallas kernels for 0%

profile of v8, /device:TPU:1, one launch (start us, length us, event | category | flops | bytes accessed | tf_op | source)
XLA Modules:
  0.0 207.2 jit_solution(4221743609719744312)
XLA Ops:
  0.0 0.8 shift-right-arithmetic_convert_fusion
  0.8 1.1 pad_maximum_fusion.4
  1.9 12.4 %collective-permute-start.3 = (bf16[400,640]{1,0:T(8,128)(2,1)S(1)}, bf16[400,640]{1,0:T(8,128)(2,1)S(1)}, u32[]{:S(2)}, u32[]{:S(2)}) collective-permute-start(bf16[400,640]{1,0:T(8,128)(2,1)S(1)} %pad_maximum_fusion.4), channel_id=1, source_target_pairs={{0,6},{6,0},{12,18},{18,12},{24,30},{30,24},{36,42},{42,36},{48,54... | collective-permute-start | bytes 1536008 | tf_op jit(solution)/shard_map/ppermute | solution.py:15
  14.3 1.9 collective-permute-start.2
  16.2 6.9 %collective-permute-start.1 = (bf16[400,640]{1,0:T(8,128)(2,1)S(1)}, bf16[400,640]{1,0:T(8,128)(2,1)S(1)}, u32[]{:S(2)}, u32[]{:S(2)}) collective-permute-start(bf16[400,640]{1,0:T(8,128)(2,1)S(1)} %pad_maximum_fusion.4), channel_id=1, source_target_pairs={{0,24},{6,18},{12,36},{18,30},{24,48},{30,42},{36,60},{42,54},{48,... | collective-permute-start | bytes 1536008 | tf_op jit(solution)/shard_map/ppermute | solution.py:15
  26.0 2.7 %collective-permute-start = (f32[4,64]{1,0:T(4,128)S(1)}, f32[4,64]{1,0:T(4,128)S(1)}, u32[]{:S(2)}, u32[]{:S(2)}) collective-permute-start(f32[4,64]{1,0:T(4,128)S(1)} %fusion.29), channel_id=1, source_target_pairs={{0,6},{6,0},{12,18},{18,12},{24,30},{30,24},{36,42},{42,36},{48,54... | collective-permute-start | bytes 3080 | tf_op jit(solution)/shard_map/ppermute | solution.py:15
  29.5 24.1 %collective-permute-done.1 = bf16[400,640]{1,0:T(8,128)(2,1)S(1)} collective-permute-done((bf16[400,640]{1,0:T(8,128)(2,1)S(1)}, bf16[400,640]{1,0:T(8,128)(2,1)S(1)}, u32[]{:S(2)}, u32[]{:S(2)}) %collective-permute-start.1) | collective-permute-done | bytes 512032 | tf_op jit(solution)/shard_map/ppermute | solution.py:15
  56.2 1.9 collective-permute-start.5
  58.2 9.4 %collective-permute-start.4 = (f32[2,128,768]{2,1,0:T(8,128)S(1)}, f32[2,128,768]{2,1,0:T(8,128)S(1)}, u32[]{:S(2)}, u32[]{:S(2)}) collective-permute-start(f32[2,128,768]{2,1,0:T(8,128)S(1)} %pad_maximum_fusion.2), channel_id=1, source_target_pairs={{0,1},{1,2},{2,0},{3,4},{4,5},{5,3},{6,7},{7,8},{8,6},{9,10},{10,1... | collective-permute-start | bytes 2359304 | tf_op jit(solution)/shard_map/ppermute | solution.py:38
  68.1 14.7 %collective-permute-done.5 = f32[2,128,768]{2,1,0:T(8,128)S(1)} collective-permute-done((f32[2,128,768]{2,1,0:T(8,128)S(1)}, f32[2,128,768]{2,1,0:T(8,128)S(1)}, u32[]{:S(2)}, u32[]{:S(2)}) %collective-permute-start.5) | collective-permute-done | bytes 786464 | tf_op jit(solution)/shard_map/ppermute | solution.py:38
  82.8 8.4 %collective-permute-done.4 = f32[2,128,768]{2,1,0:T(8,128)S(1)} collective-permute-done((f32[2,128,768]{2,1,0:T(8,128)S(1)}, f32[2,128,768]{2,1,0:T(8,128)S(1)}, u32[]{:S(2)}, u32[]{:S(2)}) %collective-permute-start.4) | collective-permute-done | bytes 786464 | tf_op jit(solution)/shard_map/ppermute | solution.py:38
  91.5 10.1 %collective-permute-start.6 = (f32[2,64,768]{2,1,0:T(8,128)S(1)}, f32[2,64,768]{2,1,0:T(8,128)S(1)}, u32[]{:S(2)}, u32[]{:S(2)}) collective-permute-start(f32[2,64,768]{2,1,0:T(8,128)S(1)} %constant_dynamic-slice_fusion), channel_id=1, source_target_pairs={{0,3},{1,4},{2,5},{3,0},{4,1},{5,2},{6,9},{7,10},{8,11},{9,6},{10,... | collective-permute-start | bytes 1179656 | tf_op jit(solution)/shard_map/ppermute | solution.py:42
  101.7 21.5 %collective-permute-done.6 = f32[2,64,768]{2,1,0:T(8,128)S(1)} collective-permute-done((f32[2,64,768]{2,1,0:T(8,128)S(1)}, f32[2,64,768]{2,1,0:T(8,128)S(1)}, u32[]{:S(2)}, u32[]{:S(2)}) %collective-permute-start.6) | collective-permute-done | bytes 393248 | tf_op jit(solution)/shard_map/ppermute | solution.py:42
  123.8 1.9 collective-permute-start.7
  125.7 1.1 collective-permute-done.7
  126.9 1.0 constant_dynamic-update-slice_fusion.5
  127.9 2.0 collective-permute-start.9
  130.0 1.9 collective-permute-start.8
  131.9 8.4 %collective-permute-start.10 = (bf16[2,64,768]{2,1,0:T(8,128)(2,1)}, bf16[2,64,768]{2,1,0:T(8,128)(2,1)}, u32[]{:S(2)}, u32[]{:S(2)}) collective-permute-start(bf16[2,64,768]{2,1,0:T(8,128)(2,1)} %get-tuple-element.16), channel_id=1, source_target_pairs={{0,2},{1,0},{2,1},{3,5},{4,3},{5,4},{6,8},{7,6},{8,7},{9,11},{10,9... | collective-permute-start | bytes 589832 | tf_op jit(solution)/shard_map/ppermute | solution.py:38
  140.3 1.5 collective-permute-done.9
  141.8 4.0 %collective-permute-done.10 = bf16[2,64,768]{2,1,0:T(8,128)(2,1)} collective-permute-done((bf16[2,64,768]{2,1,0:T(8,128)(2,1)}, bf16[2,64,768]{2,1,0:T(8,128)(2,1)}, u32[]{:S(2)}, u32[]{:S(2)}) %collective-permute-start.10) | collective-permute-done | bytes 196640 | tf_op jit(solution)/shard_map/ppermute | solution.py:38
  145.8 3.5 %collective-permute-start.12 = (bf16[2,64,768]{2,1,0:T(8,128)(2,1)S(1)}, bf16[2,64,768]{2,1,0:T(8,128)(2,1)S(1)}, u32[]{:S(2)}, u32[]{:S(2)}) collective-permute-start(bf16[2,64,768]{2,1,0:T(8,128)(2,1)S(1)} %collective-permute-done.8), channel_id=1, source_target_pairs={{0,2},{1,0},{2,1},{3,5},{4,3},{5,4},{6,8},{7,6},{8,7},{9,11},{10,9... | collective-permute-start | bytes 589832 | tf_op jit(solution)/shard_map/ppermute | solution.py:38
  149.3 5.0 %collective-permute-start.11 = (bf16[2,64,768]{2,1,0:T(8,128)(2,1)S(1)}, bf16[2,64,768]{2,1,0:T(8,128)(2,1)S(1)}, u32[]{:S(2)}, u32[]{:S(2)}) collective-permute-start(bf16[2,64,768]{2,1,0:T(8,128)(2,1)S(1)} %collective-permute-done.8), channel_id=1, source_target_pairs={{0,1},{1,2},{2,0},{3,4},{4,5},{5,3},{6,7},{7,8},{8,6},{9,10},{10,1... | collective-permute-start | bytes 589832 | tf_op jit(solution)/shard_map/ppermute | solution.py:38
  154.3 0.9 constant_dynamic-update-slice_fusion.4
  155.2 0.9 constant_dynamic-update-slice_fusion.3
  156.2 4.3 %collective-permute-done.11 = bf16[2,64,768]{2,1,0:T(8,128)(2,1)S(1)} collective-permute-done((bf16[2,64,768]{2,1,0:T(8,128)(2,1)S(1)}, bf16[2,64,768]{2,1,0:T(8,128)(2,1)S(1)}, u32[]{:S(2)}, u32[]{:S(2)}) %collective-permute-start.11) | collective-permute-done | bytes 196640 | tf_op jit(solution)/shard_map/ppermute | solution.py:38
  163.3 10.7 %collective-permute-start.13 = (bf16[384,640]{1,0:T(8,128)(2,1)S(1)}, bf16[384,640]{1,0:T(8,128)(2,1)S(1)}, u32[]{:S(2)}, u32[]{:S(2)}) collective-permute-start(bf16[384,640]{1,0:T(8,128)(2,1)S(1)} %fusion.2), channel_id=1, source_target_pairs={{24,0},{18,6},{36,12},{30,18},{48,24},{42,30},{60,36},{54,42},{72,... | collective-permute-start | bytes 1474568 | tf_op jit(solution)/shard_map/ppermute | solution.py:15
  174.0 5.4 %collective-permute-start.14 = (bf16[384,640]{1,0:T(8,128)(2,1)S(1)}, bf16[384,640]{1,0:T(8,128)(2,1)S(1)}, u32[]{:S(2)}, u32[]{:S(2)}) collective-permute-start(bf16[384,640]{1,0:T(8,128)(2,1)S(1)} %convolution_convert_fusion.1), channel_id=1, source_target_pairs={{18,0},{24,6},{30,12},{36,18},{42,24},{48,30},{54,36},{60,42},{66,... | collective-permute-start | bytes 1474568 | tf_op jit(solution)/shard_map/ppermute | solution.py:15
  179.4 1.9 collective-permute-start.15
  181.3 5.2 %collective-permute-done.13 = bf16[384,640]{1,0:T(8,128)(2,1)S(1)} collective-permute-done((bf16[384,640]{1,0:T(8,128)(2,1)S(1)}, bf16[384,640]{1,0:T(8,128)(2,1)S(1)}, u32[]{:S(2)}, u32[]{:S(2)}) %collective-permute-start.13) | collective-permute-done | bytes 491552 | tf_op jit(solution)/shard_map/ppermute | solution.py:15
  186.5 19.3 %collective-permute-done.14 = bf16[384,640]{1,0:T(8,128)(2,1)S(1)} collective-permute-done((bf16[384,640]{1,0:T(8,128)(2,1)S(1)}, bf16[384,640]{1,0:T(8,128)(2,1)S(1)}, u32[]{:S(2)}, u32[]{:S(2)}) %collective-permute-start.14) | collective-permute-done | bytes 491552 | tf_op jit(solution)/shard_map/ppermute | solution.py:15
  205.8 1.5 fusion.1
  (75 shorter events, 10.2 us)
Async XLA Ops:
  0.0 53.6 %copy-start = (bf16[384,640]{1,0:T(8,128)(2,1)S(1)}, bf16[384,640]{1,0:T(8,128)(2,1)}, u32[]{:S(2)}) copy-start(bf16[384,640]{1,0:T(8,128)(2,1)} %param.6) | copy-start | bytes 1474564
  1.9 52.5 %collective-permute-start.3 = (bf16[400,640]{1,0:T(8,128)(2,1)S(1)}, bf16[400,640]{1,0:T(8,128)(2,1)S(1)}, u32[]{:S(2)}, u32[]{:S(2)}) collective-permute-start(bf16[400,640]{1,0:T(8,128)(2,1)S(1)} %pad_maximum_fusion.4), channel_id=1, source_target_pairs={{0,6},{6,0},{12,18},{18,12},{24,30},{30,24},{36,42},{42,36},{48,54... | collective-permute-start | bytes 1536008 | tf_op jit(solution)/shard_map/ppermute | solution.py:15
  14.3 39.6 %collective-permute-start.2 = (bf16[400,640]{1,0:T(8,128)(2,1)S(1)}, bf16[400,640]{1,0:T(8,128)(2,1)S(1)}, u32[]{:S(2)}, u32[]{:S(2)}) collective-permute-start(bf16[400,640]{1,0:T(8,128)(2,1)S(1)} %pad_maximum_fusion.4), channel_id=1, source_target_pairs={{0,18},{6,24},{12,30},{18,36},{24,42},{30,48},{36,54},{42,60},{48,... | collective-permute-start | bytes 1536008 | tf_op jit(solution)/shard_map/ppermute | solution.py:15
  16.2 37.4 %collective-permute-start.1 = (bf16[400,640]{1,0:T(8,128)(2,1)S(1)}, bf16[400,640]{1,0:T(8,128)(2,1)S(1)}, u32[]{:S(2)}, u32[]{:S(2)}) collective-permute-start(bf16[400,640]{1,0:T(8,128)(2,1)S(1)} %pad_maximum_fusion.4), channel_id=1, source_target_pairs={{0,24},{6,18},{12,36},{18,30},{24,48},{30,42},{36,60},{42,54},{48,... | collective-permute-start | bytes 1536008 | tf_op jit(solution)/shard_map/ppermute | solution.py:15
  26.0 3.5 %collective-permute-start = (f32[4,64]{1,0:T(4,128)S(1)}, f32[4,64]{1,0:T(4,128)S(1)}, u32[]{:S(2)}, u32[]{:S(2)}) collective-permute-start(f32[4,64]{1,0:T(4,128)S(1)} %fusion.29), channel_id=1, source_target_pairs={{0,6},{6,0},{12,18},{18,12},{24,30},{30,24},{36,42},{42,36},{48,54... | collective-permute-start | bytes 3080 | tf_op jit(solution)/shard_map/ppermute | solution.py:15
  53.9 13.7 %copy-start.1 = (bf16[384,640]{1,0:T(8,128)(2,1)}, bf16[384,640]{1,0:T(8,128)(2,1)S(1)}, u32[]{:S(2)}) copy-start(bf16[384,640]{1,0:T(8,128)(2,1)S(1)} %slice.139) | copy-start | bytes 1474564
  53.9 13.7 %copy-start.3 = (bf16[384,640]{1,0:T(8,128)(2,1)}, bf16[384,640]{1,0:T(8,128)(2,1)S(1)}, u32[]{:S(2)}) copy-start(bf16[384,640]{1,0:T(8,128)(2,1)S(1)} %slice.140) | copy-start | bytes 1474564
  54.4 1.3 copy-start.5
  56.2 26.6 %collective-permute-start.5 = (f32[2,128,768]{2,1,0:T(8,128)S(1)}, f32[2,128,768]{2,1,0:T(8,128)S(1)}, u32[]{:S(2)}, u32[]{:S(2)}) collective-permute-start(f32[2,128,768]{2,1,0:T(8,128)S(1)} %pad_maximum_fusion.3), channel_id=1, source_target_pairs={{0,2},{1,0},{2,1},{3,5},{4,3},{5,4},{6,8},{7,6},{8,7},{9,11},{10,9... | collective-permute-start | bytes 2359304 | tf_op jit(solution)/shard_map/ppermute | solution.py:38
  58.2 33.1 %collective-permute-start.4 = (f32[2,128,768]{2,1,0:T(8,128)S(1)}, f32[2,128,768]{2,1,0:T(8,128)S(1)}, u32[]{:S(2)}, u32[]{:S(2)}) collective-permute-start(f32[2,128,768]{2,1,0:T(8,128)S(1)} %pad_maximum_fusion.2), channel_id=1, source_target_pairs={{0,1},{1,2},{2,0},{3,4},{4,5},{5,3},{6,7},{7,8},{8,6},{9,10},{10,1... | collective-permute-start | bytes 2359304 | tf_op jit(solution)/shard_map/ppermute | solution.py:38
  91.5 31.7 %collective-permute-start.6 = (f32[2,64,768]{2,1,0:T(8,128)S(1)}, f32[2,64,768]{2,1,0:T(8,128)S(1)}, u32[]{:S(2)}, u32[]{:S(2)}) collective-permute-start(f32[2,64,768]{2,1,0:T(8,128)S(1)} %constant_dynamic-slice_fusion), channel_id=1, source_target_pairs={{0,3},{1,4},{2,5},{3,0},{4,1},{5,2},{6,9},{7,10},{8,11},{9,6},{10,... | collective-permute-start | bytes 1179656 | tf_op jit(solution)/shard_map/ppermute | solution.py:42
  123.8 3.1 %collective-permute-start.7 = (f32[2,4,64]{2,0,1:T(2,128)S(1)}, f32[2,4,64]{2,0,1:T(2,128)S(1)}, u32[]{:S(2)}, u32[]{:S(2)}) collective-permute-start(f32[2,4,64]{2,0,1:T(2,128)S(1)} %pad_maximum_fusion.8), channel_id=1, source_target_pairs={{0,6},{6,0},{12,18},{18,12},{24,30},{30,24},{36,42},{42,36},{48,54... | collective-permute-start | bytes 6152 | tf_op jit(solution)/shard_map/ppermute | solution.py:15
  127.9 32.7 %copy-start.4 = (bf16[384,640]{1,0:T(8,128)(2,1)S(1)}, bf16[384,640]{1,0:T(8,128)(2,1)}, u32[]{:S(2)}) copy-start(bf16[384,640]{1,0:T(8,128)(2,1)} %copy-done.3) | copy-start | bytes 1474564
  127.9 13.9 %collective-permute-start.9 = (bf16[2,64,768]{2,1,0:T(8,128)(2,1)}, bf16[2,64,768]{2,1,0:T(8,128)(2,1)}, u32[]{:S(2)}, u32[]{:S(2)}) collective-permute-start(bf16[2,64,768]{2,1,0:T(8,128)(2,1)} %get-tuple-element.16), channel_id=1, source_target_pairs={{0,1},{1,2},{2,0},{3,4},{4,5},{5,3},{6,7},{7,8},{8,6},{9,10},{10,1... | collective-permute-start | bytes 589832 | tf_op jit(solution)/shard_map/ppermute | solution.py:38
  130.0 11.8 %collective-permute-start.8 = (bf16[2,64,768]{2,1,0:T(8,128)(2,1)}, bf16[2,64,768]{2,1,0:T(8,128)(2,1)S(1)}, u32[]{:S(2)}, u32[]{:S(2)}) collective-permute-start(bf16[2,64,768]{2,1,0:T(8,128)(2,1)} %get-tuple-element.16), channel_id=1, source_target_pairs={{0,3},{1,4},{2,5},{3,0},{4,1},{5,2},{6,9},{7,10},{8,11},{9,6},{10,... | collective-permute-start | bytes 589832 | tf_op jit(solution)/shard_map/ppermute | solution.py:42
  131.9 13.9 %collective-permute-start.10 = (bf16[2,64,768]{2,1,0:T(8,128)(2,1)}, bf16[2,64,768]{2,1,0:T(8,128)(2,1)}, u32[]{:S(2)}, u32[]{:S(2)}) collective-permute-start(bf16[2,64,768]{2,1,0:T(8,128)(2,1)} %get-tuple-element.16), channel_id=1, source_target_pairs={{0,2},{1,0},{2,1},{3,5},{4,3},{5,4},{6,8},{7,6},{8,7},{9,11},{10,9... | collective-permute-start | bytes 589832 | tf_op jit(solution)/shard_map/ppermute | solution.py:38
  145.8 14.8 %collective-permute-start.12 = (bf16[2,64,768]{2,1,0:T(8,128)(2,1)S(1)}, bf16[2,64,768]{2,1,0:T(8,128)(2,1)S(1)}, u32[]{:S(2)}, u32[]{:S(2)}) collective-permute-start(bf16[2,64,768]{2,1,0:T(8,128)(2,1)S(1)} %collective-permute-done.8), channel_id=1, source_target_pairs={{0,2},{1,0},{2,1},{3,5},{4,3},{5,4},{6,8},{7,6},{8,7},{9,11},{10,9... | collective-permute-start | bytes 589832 | tf_op jit(solution)/shard_map/ppermute | solution.py:38
  149.3 11.2 %collective-permute-start.11 = (bf16[2,64,768]{2,1,0:T(8,128)(2,1)S(1)}, bf16[2,64,768]{2,1,0:T(8,128)(2,1)S(1)}, u32[]{:S(2)}, u32[]{:S(2)}) collective-permute-start(bf16[2,64,768]{2,1,0:T(8,128)(2,1)S(1)} %collective-permute-done.8), channel_id=1, source_target_pairs={{0,1},{1,2},{2,0},{3,4},{4,5},{5,3},{6,7},{7,8},{8,6},{9,10},{10,1... | collective-permute-start | bytes 589832 | tf_op jit(solution)/shard_map/ppermute | solution.py:38
  160.6 1.0 copy-start.6
  162.8 43.0 %copy-start.2 = (bf16[384,640]{1,0:T(8,128)(2,1)S(1)}, bf16[384,640]{1,0:T(8,128)(2,1)}, u32[]{:S(2)}) copy-start(bf16[384,640]{1,0:T(8,128)(2,1)} %copy-done.1) | copy-start | bytes 1474564
  163.3 23.2 %collective-permute-start.13 = (bf16[384,640]{1,0:T(8,128)(2,1)S(1)}, bf16[384,640]{1,0:T(8,128)(2,1)S(1)}, u32[]{:S(2)}, u32[]{:S(2)}) collective-permute-start(bf16[384,640]{1,0:T(8,128)(2,1)S(1)} %fusion.2), channel_id=1, source_target_pairs={{24,0},{18,6},{36,12},{30,18},{48,24},{42,30},{60,36},{54,42},{72,... | collective-permute-start | bytes 1474568 | tf_op jit(solution)/shard_map/ppermute | solution.py:15
  174.0 31.8 %collective-permute-start.14 = (bf16[384,640]{1,0:T(8,128)(2,1)S(1)}, bf16[384,640]{1,0:T(8,128)(2,1)S(1)}, u32[]{:S(2)}, u32[]{:S(2)}) collective-permute-start(bf16[384,640]{1,0:T(8,128)(2,1)S(1)} %convolution_convert_fusion.1), channel_id=1, source_target_pairs={{18,0},{24,6},{30,12},{36,18},{42,24},{48,30},{54,36},{60,42},{66,... | collective-permute-start | bytes 1474568 | tf_op jit(solution)/shard_map/ppermute | solution.py:15
  179.4 26.4 %collective-permute-start.15 = (bf16[384,640]{1,0:T(8,128)(2,1)S(1)}, bf16[384,640]{1,0:T(8,128)(2,1)S(1)}, u32[]{:S(2)}, u32[]{:S(2)}) collective-permute-start(bf16[384,640]{1,0:T(8,128)(2,1)S(1)} %convolution_convert_fusion), channel_id=1, source_target_pairs={{0,6},{6,0},{12,18},{18,12},{24,30},{30,24},{36,42},{42,36},{48,54... | collective-permute-start | bytes 1474568 | tf_op jit(solution)/shard_map/ppermute | solution.py:15

commit v9 on v8

--- a/solution.py
+++ b/solution.py
@@ -119,20 +119,21 @@
         ]
     )
 
-    def partial(steps):
-        start = ((v + steps) % 3) * 128
-        return jnp.stack(
-            [
-                partial_of(rows_of(queries, start, 128), read)
-                for queries, read in zip((hidden, pair_hidden), keys)
-            ]
-        )
+    def partial(queries, steps, half):
+        start = ((v + steps) % 3) * 128 + half * 64
+        parts = [partial_of(rows_of(q, start, 64), read) for q, read in zip(queries, keys)]
+        return jnp.stack(parts)
 
-    first = triple_shift(partial(1), 1)
-    second = triple_shift(partial(2), 2)
-    group = partial(0) + first + second
-    other_half = triple_swap(rows_of(group, (1 - u) * 64, 64, 1))
-    scores = (rows_of(group, u * 64, 64, 1) + other_half) * score_scale
+    queries = (hidden, pair_hidden)
+    sent = tuple(partial(queries, steps, 1 - u) for steps in (1, 2))
+    *sent, own, pair = lax.optimization_barrier(sent + queries)
+    queries = (own, pair)
+    passing = partial(queries, 0, 1 - u) + triple_shift(sent[0], 1) + triple_shift(sent[1], 2)
+    late = tuple(partial(queries, steps, u) for steps in (1, 2))
+    passing, *late = lax.optimization_barrier((passing,) + late)
+    from_partner = triple_swap(passing)
+    scores = partial(queries, 0, u) + triple_shift(late[0], 1) + triple_shift(late[1], 2)
+    scores = (scores + from_partner) * score_scale
 
     usable = jnp.broadcast_to((codes > 0.0)[:, None], scores.shape)
     matches = usable & (codes[:, None] == row_codes[:, :, None])

time: 208 us -> 207 us (level)
  starting transfers between devices: 86.1 us -> 81 us
  matrix products: 6.22 us -> 9.8 us
    ppermute x2, starting transfers between devices: 12 us -> 3.84 us  [triple_swap(): return lax.ppermute(value, 'tensor', [(r, (r + 3) % 6) for r in range(6)])]
    ppermute x6 -> x8, starting transfers between devices: 30.2 us -> 34.5 us  [triple_shift(): return lax.ppermute(value, 'tensor', pairs)]
    dot_general x6 -> x12, matrix products: 2.51 us -> 5.01 us  [partial_of(): lax.dot_general(queries, keys, (((1,), (1,)), ((), ())), preferred_elemen...]
    ppermute x6 -> x8, waiting for transfers between devices: 32.9 us -> 34.7 us  [triple_shift(): return lax.ppermute(value, 'tensor', pairs)]
  transfers between devices with their start and end apart: 16 -> 18, of which waited for: 11 -> 13; matrix products, arithmetic and copies ran while one was open for 3% -> 2% of each run, Pallas kernels for 0% -> 0%
where the time goes in v9:
time: 207 us; the launch traced here: 206 us
  waiting for transfers between devices  107 us (52%)
  starting transfers between devices  81 us (39%)
  matrix products  9.8 us (5%)
  other arithmetic  4.7 us (2%)
  local copies, waits for them, and re-layouts  2.61 us (1%)
    ppermute x8, waiting for transfers between devices, dp_permute(): return lax.ppermute(value, 'dp', pairs)  49.9 us
    ppermute x8, starting transfers between devices, dp_permute(): return lax.ppermute(value, 'dp', pairs)  42.6 us
    ppermute x8, waiting for transfers between devices, triple_shift(): return lax.ppermute(value, 'tensor', pairs)  34.7 us
    ppermute x8, starting transfers between devices, triple_shift(): return lax.ppermute(value, 'tensor', pairs)  34.5 us
    ppermute x2, waiting for transfers between devices, triple_swap(): return lax.ppermute(value, 'tensor', [(r, (r + 3) % 6) for r in range(6)])  22.2 us
    dot_general x12, matrix products, partial_of(): lax.dot_general(queries, keys, (((1,), (1,)), ((), ())), preferred_elemen...  5.01 us
  transfers between devices with their start and end apart: 18, of which 13 were waited for; matrix products, arithmetic and copies ran while one was open for 2% of the time, Pallas kernels for 0%

profile of v9, /device:TPU:1, one launch (start us, length us, event | category | flops | bytes accessed | tf_op | source)
XLA Modules:
  0.0 205.5 jit_solution(13855240132462438444)
XLA Ops:
  1.9 12.4 %collective-permute-start.3 = (bf16[400,640]{1,0:T(8,128)(2,1)S(1)}, bf16[400,640]{1,0:T(8,128)(2,1)S(1)}, u32[]{:S(2)}, u32[]{:S(2)}) collective-permute-start(bf16[400,640]{1,0:T(8,128)(2,1)S(1)} %pad_maximum_fusion.2), channel_id=1, source_target_pairs={{0,6},{6,0},{12,18},{18,12},{24,30},{30,24},{36,42},{42,36},{48,54... | collective-permute-start | bytes 1536008 | tf_op jit(solution)/shard_map/ppermute | solution.py:15
  14.3 1.9 collective-permute-start.2
  16.2 6.9 %collective-permute-start.1 = (bf16[400,640]{1,0:T(8,128)(2,1)S(1)}, bf16[400,640]{1,0:T(8,128)(2,1)S(1)}, u32[]{:S(2)}, u32[]{:S(2)}) collective-permute-start(bf16[400,640]{1,0:T(8,128)(2,1)S(1)} %pad_maximum_fusion.2), channel_id=1, source_target_pairs={{0,24},{6,18},{12,36},{18,30},{24,48},{30,42},{36,60},{42,54},{48,... | collective-permute-start | bytes 1536008 | tf_op jit(solution)/shard_map/ppermute | solution.py:15
  26.0 2.7 %collective-permute-start = (f32[4,64]{1,0:T(4,128)S(1)}, f32[4,64]{1,0:T(4,128)S(1)}, u32[]{:S(2)}, u32[]{:S(2)}) collective-permute-start(f32[4,64]{1,0:T(4,128)S(1)} %fusion.44), channel_id=1, source_target_pairs={{0,6},{6,0},{12,18},{18,12},{24,30},{30,24},{36,42},{42,36},{48,54... | collective-permute-start | bytes 3080 | tf_op jit(solution)/shard_map/ppermute | solution.py:15
  29.5 23.9 %collective-permute-done.1 = bf16[400,640]{1,0:T(8,128)(2,1)S(1)} collective-permute-done((bf16[400,640]{1,0:T(8,128)(2,1)S(1)}, bf16[400,640]{1,0:T(8,128)(2,1)S(1)}, u32[]{:S(2)}, u32[]{:S(2)}) %collective-permute-start.1) | collective-permute-done | bytes 512032 | tf_op jit(solution)/shard_map/ppermute | solution.py:15
  58.6 13.4 %collective-permute-start.4 = (f32[2,64,768]{2,1,0:T(8,128)S(1)}, f32[2,64,768]{2,1,0:T(8,128)S(1)}, u32[]{:S(2)}, u32[]{:S(2)}) collective-permute-start(f32[2,64,768]{2,1,0:T(8,128)S(1)} %get-tuple-element.17), channel_id=1, source_target_pairs={{0,1},{1,2},{2,0},{3,4},{4,5},{5,3},{6,7},{7,8},{8,6},{9,10},{10,1... | collective-permute-start | bytes 1179656 | tf_op jit(solution)/shard_map/ppermute | solution.py:38
  72.0 1.9 collective-permute-start.5
  74.5 5.1 %collective-permute-done.4 = f32[2,64,768]{2,1,0:T(8,128)S(1)} collective-permute-done((f32[2,64,768]{2,1,0:T(8,128)S(1)}, f32[2,64,768]{2,1,0:T(8,128)S(1)}, u32[]{:S(2)}, u32[]{:S(2)}) %collective-permute-start.4) | collective-permute-done | bytes 393248 | tf_op jit(solution)/shard_map/ppermute | solution.py:38
  79.6 8.6 %collective-permute-done.5 = f32[2,64,768]{2,1,0:T(8,128)S(1)} collective-permute-done((f32[2,64,768]{2,1,0:T(8,128)S(1)}, f32[2,64,768]{2,1,0:T(8,128)S(1)}, u32[]{:S(2)}, u32[]{:S(2)}) %collective-permute-start.5) | collective-permute-done | bytes 393248 | tf_op jit(solution)/shard_map/ppermute | solution.py:38
  88.2 1.9 collective-permute-start.6
  90.1 4.9 %collective-permute-start.7 = (f32[2,64,768]{2,1,0:T(8,128)S(1)}, f32[2,64,768]{2,1,0:T(8,128)S(1)}, u32[]{:S(2)}, u32[]{:S(2)}) collective-permute-start(f32[2,64,768]{2,1,0:T(8,128)S(1)} %pad_maximum_fusion.6), channel_id=1, source_target_pairs={{0,2},{1,0},{2,1},{3,5},{4,3},{5,4},{6,8},{7,6},{8,7},{9,11},{10,9... | collective-permute-start | bytes 1179656 | tf_op jit(solution)/shard_map/ppermute | solution.py:38
  95.0 1.9 collective-permute-start.8
  97.9 2.6 %collective-permute-done.6 = f32[2,64,768]{2,1,0:T(8,128)S(1)} collective-permute-done((f32[2,64,768]{2,1,0:T(8,128)S(1)}, f32[2,64,768]{2,1,0:T(8,128)S(1)}, u32[]{:S(2)}, u32[]{:S(2)}) %collective-permute-start.6) | collective-permute-done | bytes 393248 | tf_op jit(solution)/shard_map/ppermute | solution.py:38
  100.5 7.4 %collective-permute-done.7 = f32[2,64,768]{2,1,0:T(8,128)S(1)} collective-permute-done((f32[2,64,768]{2,1,0:T(8,128)S(1)}, f32[2,64,768]{2,1,0:T(8,128)S(1)}, u32[]{:S(2)}, u32[]{:S(2)}) %collective-permute-start.7) | collective-permute-done | bytes 393248 | tf_op jit(solution)/shard_map/ppermute | solution.py:38
  107.9 14.3 %collective-permute-done.8 = f32[2,64,768]{2,1,0:T(8,128)S(1)} collective-permute-done((f32[2,64,768]{2,1,0:T(8,128)S(1)}, f32[2,64,768]{2,1,0:T(8,128)S(1)}, u32[]{:S(2)}, u32[]{:S(2)}) %collective-permute-start.8) | collective-permute-done | bytes 393248 | tf_op jit(solution)/shard_map/ppermute | solution.py:42
  122.9 1.9 collective-permute-start.9
  124.9 1.1 collective-permute-done.9
  126.4 1.9 collective-permute-start.11
  128.3 1.9 collective-permute-start.10
  130.2 5.0 %collective-permute-start.12 = (bf16[2,64,768]{2,1,0:T(8,128)(2,1)S(1)}, bf16[2,64,768]{2,1,0:T(8,128)(2,1)S(1)}, u32[]{:S(2)}, u32[]{:S(2)}) collective-permute-start(bf16[2,64,768]{2,1,0:T(8,128)(2,1)S(1)} %get-tuple-element.30), channel_id=1, source_target_pairs={{0,2},{1,0},{2,1},{3,5},{4,3},{5,4},{6,8},{7,6},{8,7},{9,11},{10,9... | collective-permute-start | bytes 589832 | tf_op jit(solution)/shard_map/ppermute | solution.py:38
  135.3 3.7 %collective-permute-done.11 = bf16[2,64,768]{2,1,0:T(8,128)(2,1)S(1)} collective-permute-done((bf16[2,64,768]{2,1,0:T(8,128)(2,1)S(1)}, bf16[2,64,768]{2,1,0:T(8,128)(2,1)S(1)}, u32[]{:S(2)}, u32[]{:S(2)}) %collective-permute-start.11) | collective-permute-done | bytes 196640 | tf_op jit(solution)/shard_map/ppermute | solution.py:38
  139.0 7.9 %collective-permute-done.10 = bf16[2,64,768]{2,1,0:T(8,128)(2,1)S(1)} collective-permute-done((bf16[2,64,768]{2,1,0:T(8,128)(2,1)S(1)}, bf16[2,64,768]{2,1,0:T(8,128)(2,1)S(1)}, u32[]{:S(2)}, u32[]{:S(2)}) %collective-permute-start.10) | collective-permute-done | bytes 196640 | tf_op jit(solution)/shard_map/ppermute | solution.py:42
  146.8 2.3 %collective-permute-start.14 = (bf16[2,64,768]{2,1,0:T(8,128)(2,1)S(1)}, bf16[2,64,768]{2,1,0:T(8,128)(2,1)S(1)}, u32[]{:S(2)}, u32[]{:S(2)}) collective-permute-start(bf16[2,64,768]{2,1,0:T(8,128)(2,1)S(1)} %collective-permute-done.10), channel_id=1, source_target_pairs={{0,2},{1,0},{2,1},{3,5},{4,3},{5,4},{6,8},{7,6},{8,7},{9,11},{10,9... | collective-permute-start | bytes 589832 | tf_op jit(solution)/shard_map/ppermute | solution.py:38
  149.2 3.1 %collective-permute-start.13 = (bf16[2,64,768]{2,1,0:T(8,128)(2,1)S(1)}, bf16[2,64,768]{2,1,0:T(8,128)(2,1)S(1)}, u32[]{:S(2)}, u32[]{:S(2)}) collective-permute-start(bf16[2,64,768]{2,1,0:T(8,128)(2,1)S(1)} %collective-permute-done.10), channel_id=1, source_target_pairs={{0,1},{1,2},{2,0},{3,4},{4,5},{5,3},{6,7},{7,8},{8,6},{9,10},{10,1... | collective-permute-start | bytes 589832 | tf_op jit(solution)/shard_map/ppermute | solution.py:38
  152.4 7.3 %collective-permute-done.13 = bf16[2,64,768]{2,1,0:T(8,128)(2,1)S(1)} collective-permute-done((bf16[2,64,768]{2,1,0:T(8,128)(2,1)S(1)}, bf16[2,64,768]{2,1,0:T(8,128)(2,1)S(1)}, u32[]{:S(2)}, u32[]{:S(2)}) %collective-permute-start.13) | collective-permute-done | bytes 196640 | tf_op jit(solution)/shard_map/ppermute | solution.py:38
  159.8 1.7 convolution_convert_fusion
  163.1 10.2 %collective-permute-start.15 = (bf16[384,640]{1,0:T(8,128)(2,1)S(1)}, bf16[384,640]{1,0:T(8,128)(2,1)S(1)}, u32[]{:S(2)}, u32[]{:S(2)}) collective-permute-start(bf16[384,640]{1,0:T(8,128)(2,1)S(1)} %fusion.2), channel_id=1, source_target_pairs={{24,0},{18,6},{36,12},{30,18},{48,24},{42,30},{60,36},{54,42},{72,... | collective-permute-start | bytes 1474568 | tf_op jit(solution)/shard_map/ppermute | solution.py:15
  173.4 4.6 %collective-permute-start.16 = (bf16[384,640]{1,0:T(8,128)(2,1)S(1)}, bf16[384,640]{1,0:T(8,128)(2,1)S(1)}, u32[]{:S(2)}, u32[]{:S(2)}) collective-permute-start(bf16[384,640]{1,0:T(8,128)(2,1)S(1)} %convolution_convert_fusion.1), channel_id=1, source_target_pairs={{18,0},{24,6},{30,12},{36,18},{42,24},{48,30},{54,36},{60,42},{66,... | collective-permute-start | bytes 1474568 | tf_op jit(solution)/shard_map/ppermute | solution.py:15
  178.0 1.9 collective-permute-start.17
  179.9 10.7 %collective-permute-done.15 = bf16[384,640]{1,0:T(8,128)(2,1)S(1)} collective-permute-done((bf16[384,640]{1,0:T(8,128)(2,1)S(1)}, bf16[384,640]{1,0:T(8,128)(2,1)S(1)}, u32[]{:S(2)}, u32[]{:S(2)}) %collective-permute-start.15) | collective-permute-done | bytes 491552 | tf_op jit(solution)/shard_map/ppermute | solution.py:15
  190.6 13.4 %collective-permute-done.16 = bf16[384,640]{1,0:T(8,128)(2,1)S(1)} collective-permute-done((bf16[384,640]{1,0:T(8,128)(2,1)S(1)}, bf16[384,640]{1,0:T(8,128)(2,1)S(1)}, u32[]{:S(2)}, u32[]{:S(2)}) %collective-permute-start.16) | collective-permute-done | bytes 491552 | tf_op jit(solution)/shard_map/ppermute | solution.py:15
  204.1 1.5 fusion.1
  (86 shorter events, 14.6 us)
Async XLA Ops:
  0.0 53.4 %copy-start = (bf16[384,640]{1,0:T(8,128)(2,1)S(1)}, bf16[384,640]{1,0:T(8,128)(2,1)}, u32[]{:S(2)}) copy-start(bf16[384,640]{1,0:T(8,128)(2,1)} %param.6) | copy-start | bytes 1474564
  1.9 51.7 %collective-permute-start.3 = (bf16[400,640]{1,0:T(8,128)(2,1)S(1)}, bf16[400,640]{1,0:T(8,128)(2,1)S(1)}, u32[]{:S(2)}, u32[]{:S(2)}) collective-permute-start(bf16[400,640]{1,0:T(8,128)(2,1)S(1)} %pad_maximum_fusion.2), channel_id=1, source_target_pairs={{0,6},{6,0},{12,18},{18,12},{24,30},{30,24},{36,42},{42,36},{48,54... | collective-permute-start | bytes 1536008 | tf_op jit(solution)/shard_map/ppermute | solution.py:15
  14.3 39.4 %collective-permute-start.2 = (bf16[400,640]{1,0:T(8,128)(2,1)S(1)}, bf16[400,640]{1,0:T(8,128)(2,1)S(1)}, u32[]{:S(2)}, u32[]{:S(2)}) collective-permute-start(bf16[400,640]{1,0:T(8,128)(2,1)S(1)} %pad_maximum_fusion.2), channel_id=1, source_target_pairs={{0,18},{6,24},{12,30},{18,36},{24,42},{30,48},{36,54},{42,60},{48,... | collective-permute-start | bytes 1536008 | tf_op jit(solution)/shard_map/ppermute | solution.py:15
  16.2 37.2 %collective-permute-start.1 = (bf16[400,640]{1,0:T(8,128)(2,1)S(1)}, bf16[400,640]{1,0:T(8,128)(2,1)S(1)}, u32[]{:S(2)}, u32[]{:S(2)}) collective-permute-start(bf16[400,640]{1,0:T(8,128)(2,1)S(1)} %pad_maximum_fusion.2), channel_id=1, source_target_pairs={{0,24},{6,18},{12,36},{18,30},{24,48},{30,42},{36,60},{42,54},{48,... | collective-permute-start | bytes 1536008 | tf_op jit(solution)/shard_map/ppermute | solution.py:15
  26.0 3.5 %collective-permute-start = (f32[4,64]{1,0:T(4,128)S(1)}, f32[4,64]{1,0:T(4,128)S(1)}, u32[]{:S(2)}, u32[]{:S(2)}) collective-permute-start(f32[4,64]{1,0:T(4,128)S(1)} %fusion.44), channel_id=1, source_target_pairs={{0,6},{6,0},{12,18},{18,12},{24,30},{30,24},{36,42},{42,36},{48,54... | collective-permute-start | bytes 3080 | tf_op jit(solution)/shard_map/ppermute | solution.py:15
  53.5 0.8 copy-start.1
  53.6 43.8 %copy-start.4 = (bf16[384,640]{1,0:T(8,128)(2,1)}, bf16[384,640]{1,0:T(8,128)(2,1)S(1)}, u32[]{:S(2)}) copy-start(bf16[384,640]{1,0:T(8,128)(2,1)S(1)} %slice.142) | copy-start | bytes 1474564
  53.7 43.7 %copy-start.5 = (bf16[384,640]{1,0:T(8,128)(2,1)}, bf16[384,640]{1,0:T(8,128)(2,1)S(1)}, u32[]{:S(2)}) copy-start(bf16[384,640]{1,0:T(8,128)(2,1)S(1)} %slice.141) | copy-start | bytes 1474564
  55.2 41.8 %copy-start.2 = (bf16[384,640]{1,0:T(8,128)(2,1)}, bf16[384,640]{1,0:T(8,128)(2,1)S(1)}, u32[]{:S(2)}) copy-start(bf16[384,640]{1,0:T(8,128)(2,1)S(1)} %slice.139) | copy-start | bytes 1474564
  57.4 0.7 slice-start
  58.6 21.0 %collective-permute-start.4 = (f32[2,64,768]{2,1,0:T(8,128)S(1)}, f32[2,64,768]{2,1,0:T(8,128)S(1)}, u32[]{:S(2)}, u32[]{:S(2)}) collective-permute-start(f32[2,64,768]{2,1,0:T(8,128)S(1)} %get-tuple-element.17), channel_id=1, source_target_pairs={{0,1},{1,2},{2,0},{3,4},{4,5},{5,3},{6,7},{7,8},{8,6},{9,10},{10,1... | collective-permute-start | bytes 1179656 | tf_op jit(solution)/shard_map/ppermute | solution.py:38
  72.0 16.1 %collective-permute-start.5 = (f32[2,64,768]{2,1,0:T(8,128)S(1)}, f32[2,64,768]{2,1,0:T(8,128)S(1)}, u32[]{:S(2)}, u32[]{:S(2)}) collective-permute-start(f32[2,64,768]{2,1,0:T(8,128)S(1)} %get-tuple-element.18), channel_id=1, source_target_pairs={{0,2},{1,0},{2,1},{3,5},{4,3},{5,4},{6,8},{7,6},{8,7},{9,11},{10,9... | collective-permute-start | bytes 1179656 | tf_op jit(solution)/shard_map/ppermute | solution.py:38
  88.2 12.3 %collective-permute-start.6 = (f32[2,64,768]{2,1,0:T(8,128)S(1)}, f32[2,64,768]{2,1,0:T(8,128)S(1)}, u32[]{:S(2)}, u32[]{:S(2)}) collective-permute-start(f32[2,64,768]{2,1,0:T(8,128)S(1)} %pad_maximum_fusion.5), channel_id=1, source_target_pairs={{0,1},{1,2},{2,0},{3,4},{4,5},{5,3},{6,7},{7,8},{8,6},{9,10},{10,1... | collective-permute-start | bytes 1179656 | tf_op jit(solution)/shard_map/ppermute | solution.py:38
  90.1 17.8 %collective-permute-start.7 = (f32[2,64,768]{2,1,0:T(8,128)S(1)}, f32[2,64,768]{2,1,0:T(8,128)S(1)}, u32[]{:S(2)}, u32[]{:S(2)}) collective-permute-start(f32[2,64,768]{2,1,0:T(8,128)S(1)} %pad_maximum_fusion.6), channel_id=1, source_target_pairs={{0,2},{1,0},{2,1},{3,5},{4,3},{5,4},{6,8},{7,6},{8,7},{9,11},{10,9... | collective-permute-start | bytes 1179656 | tf_op jit(solution)/shard_map/ppermute | solution.py:38
  95.0 27.2 %collective-permute-start.8 = (f32[2,64,768]{2,1,0:T(8,128)S(1)}, f32[2,64,768]{2,1,0:T(8,128)S(1)}, u32[]{:S(2)}, u32[]{:S(2)}) collective-permute-start(f32[2,64,768]{2,1,0:T(8,128)S(1)} %fusion.10), channel_id=1, source_target_pairs={{0,3},{1,4},{2,5},{3,0},{4,1},{5,2},{6,9},{7,10},{8,11},{9,6},{10,... | collective-permute-start | bytes 1179656 | tf_op jit(solution)/shard_map/ppermute | solution.py:42
  122.9 3.1 %collective-permute-start.9 = (f32[2,4,64]{2,0,1:T(2,128)S(1)}, f32[2,4,64]{2,0,1:T(2,128)S(1)}, u32[]{:S(2)}, u32[]{:S(2)}) collective-permute-start(f32[2,4,64]{2,0,1:T(2,128)S(1)} %pad_maximum_fusion.10), channel_id=1, source_target_pairs={{0,6},{6,0},{12,18},{18,12},{24,30},{30,24},{36,42},{42,36},{48,54... | collective-permute-start | bytes 6152 | tf_op jit(solution)/shard_map/ppermute | solution.py:15
  126.4 12.6 %collective-permute-start.11 = (bf16[2,64,768]{2,1,0:T(8,128)(2,1)S(1)}, bf16[2,64,768]{2,1,0:T(8,128)(2,1)S(1)}, u32[]{:S(2)}, u32[]{:S(2)}) collective-permute-start(bf16[2,64,768]{2,1,0:T(8,128)(2,1)S(1)} %get-tuple-element.30), channel_id=1, source_target_pairs={{0,1},{1,2},{2,0},{3,4},{4,5},{5,3},{6,7},{7,8},{8,6},{9,10},{10,1... | collective-permute-start | bytes 589832 | tf_op jit(solution)/shard_map/ppermute | solution.py:38
  128.3 18.5 %collective-permute-start.10 = (bf16[2,64,768]{2,1,0:T(8,128)(2,1)S(1)}, bf16[2,64,768]{2,1,0:T(8,128)(2,1)S(1)}, u32[]{:S(2)}, u32[]{:S(2)}) collective-permute-start(bf16[2,64,768]{2,1,0:T(8,128)(2,1)S(1)} %get-tuple-element.30), channel_id=1, source_target_pairs={{0,3},{1,4},{2,5},{3,0},{4,1},{5,2},{6,9},{7,10},{8,11},{9,6},{10,... | collective-permute-start | bytes 589832 | tf_op jit(solution)/shard_map/ppermute | solution.py:42
  130.2 16.6 %collective-permute-start.12 = (bf16[2,64,768]{2,1,0:T(8,128)(2,1)S(1)}, bf16[2,64,768]{2,1,0:T(8,128)(2,1)S(1)}, u32[]{:S(2)}, u32[]{:S(2)}) collective-permute-start(bf16[2,64,768]{2,1,0:T(8,128)(2,1)S(1)} %get-tuple-element.30), channel_id=1, source_target_pairs={{0,2},{1,0},{2,1},{3,5},{4,3},{5,4},{6,8},{7,6},{8,7},{9,11},{10,9... | collective-permute-start | bytes 589832 | tf_op jit(solution)/shard_map/ppermute | solution.py:38
  146.8 12.9 %collective-permute-start.14 = (bf16[2,64,768]{2,1,0:T(8,128)(2,1)S(1)}, bf16[2,64,768]{2,1,0:T(8,128)(2,1)S(1)}, u32[]{:S(2)}, u32[]{:S(2)}) collective-permute-start(bf16[2,64,768]{2,1,0:T(8,128)(2,1)S(1)} %collective-permute-done.10), channel_id=1, source_target_pairs={{0,2},{1,0},{2,1},{3,5},{4,3},{5,4},{6,8},{7,6},{8,7},{9,11},{10,9... | collective-permute-start | bytes 589832 | tf_op jit(solution)/shard_map/ppermute | solution.py:38
  149.2 10.5 %collective-permute-start.13 = (bf16[2,64,768]{2,1,0:T(8,128)(2,1)S(1)}, bf16[2,64,768]{2,1,0:T(8,128)(2,1)S(1)}, u32[]{:S(2)}, u32[]{:S(2)}) collective-permute-start(bf16[2,64,768]{2,1,0:T(8,128)(2,1)S(1)} %collective-permute-done.10), channel_id=1, source_target_pairs={{0,1},{1,2},{2,0},{3,4},{4,5},{5,3},{6,7},{7,8},{8,6},{9,10},{10,1... | collective-permute-start | bytes 589832 | tf_op jit(solution)/shard_map/ppermute | solution.py:38
  159.8 1.7 copy-start.6
  162.6 41.4 %copy-start.3 = (bf16[384,640]{1,0:T(8,128)(2,1)S(1)}, bf16[384,640]{1,0:T(8,128)(2,1)}, u32[]{:S(2)}) copy-start(bf16[384,640]{1,0:T(8,128)(2,1)} %copy-done.2) | copy-start | bytes 1474564
  163.1 27.5 %collective-permute-start.15 = (bf16[384,640]{1,0:T(8,128)(2,1)S(1)}, bf16[384,640]{1,0:T(8,128)(2,1)S(1)}, u32[]{:S(2)}, u32[]{:S(2)}) collective-permute-start(bf16[384,640]{1,0:T(8,128)(2,1)S(1)} %fusion.2), channel_id=1, source_target_pairs={{24,0},{18,6},{36,12},{30,18},{48,24},{42,30},{60,36},{54,42},{72,... | collective-permute-start | bytes 1474568 | tf_op jit(solution)/shard_map/ppermute | solution.py:15
  173.4 30.7 %collective-permute-start.16 = (bf16[384,640]{1,0:T(8,128)(2,1)S(1)}, bf16[384,640]{1,0:T(8,128)(2,1)S(1)}, u32[]{:S(2)}, u32[]{:S(2)}) collective-permute-start(bf16[384,640]{1,0:T(8,128)(2,1)S(1)} %convolution_convert_fusion.1), channel_id=1, source_target_pairs={{18,0},{24,6},{30,12},{36,18},{42,24},{48,30},{54,36},{60,42},{66,... | collective-permute-start | bytes 1474568 | tf_op jit(solution)/shard_map/ppermute | solution.py:15
  178.0 26.1 %collective-permute-start.17 = (bf16[384,640]{1,0:T(8,128)(2,1)S(1)}, bf16[384,640]{1,0:T(8,128)(2,1)S(1)}, u32[]{:S(2)}, u32[]{:S(2)}) collective-permute-start(bf16[384,640]{1,0:T(8,128)(2,1)S(1)} %convolution_convert_fusion), channel_id=1, source_target_pairs={{0,6},{6,0},{12,18},{18,12},{24,30},{30,24},{36,42},{42,36},{48,54... | collective-permute-start | bytes 1474568 | tf_op jit(solution)/shard_map/ppermute | solution.py:15

commit v10 on v9

--- a/solution.py
+++ b/solution.py
@@ -99,14 +99,16 @@
 
     key_one = dp_permute(payload, first_keys())
     key_two = dp_permute(payload, second_keys())
-    pair_hidden = core_swap(payload)[:SEG]
     weight = cotangent * padding.astype(F32)
     row_data = jnp.stack([targets.astype(F32) + 1.0, gold_logit, vocab_lse, weight])
     row_data = rows_of(row_data, v * 128 + u * 64, 64, 1)
+    row_data, late_payload = lax.optimization_barrier((row_data, payload))
+    pair_hidden = core_swap(late_payload)[:SEG]
     row_data = jnp.stack([row_data, core_swap(row_data)])
     row_codes, gold, vocab, weight = (row_data[:, i] for i in range(4))
 
     key_own = jnp.where(core == 0, payload, key_one)
+    key_own, key_two = lax.optimization_barrier((key_own, key_two))
     keys = [
         jnp.concatenate([key_one[:SEG], key_two[:SEG]], axis=0),
         jnp.concatenate([key_own[:SEG], key_two[:SEG]], axis=0),
@@ -124,9 +126,14 @@
         parts = [partial_of(rows_of(q, start, 64), read) for q, read in zip(queries, keys)]
         return jnp.stack(parts)
 
-    queries = (hidden, pair_hidden)
-    sent = tuple(partial(queries, steps, 1 - u) for steps in (1, 2))
-    *sent, own, pair = lax.optimization_barrier(sent + queries)
+    read_rows = [rows_of(hidden, ((v + steps) % 3) * 128 + (1 - u) * 64, 64) for steps in (1, 2)]
+    own_sent = tuple(partial_of(rows, keys[0]) for rows in read_rows)
+    *own_sent, pair_hidden = lax.optimization_barrier(own_sent + (pair_hidden,))
+    sent = tuple(
+        jnp.stack([mine, partial_of(rows_of(pair_hidden, start, 64), keys[1])])
+        for mine, start in zip(own_sent, [((v + steps) % 3) * 128 + (1 - u) * 64 for steps in (1, 2)])
+    )
+    *sent, own, pair = lax.optimization_barrier(sent + (hidden, pair_hidden))
     queries = (own, pair)
     passing = partial(queries, 0, 1 - u) + triple_shift(sent[0], 1) + triple_shift(sent[1], 2)
     late = tuple(partial(queries, steps, u) for steps in (1, 2))
@@ -151,16 +158,19 @@
 
     both_hidden = jnp.concatenate([hidden, pair_hidden], axis=0)
     flat = slopes.reshape(2 * SEG, 2 * SEG)
-    grad_two = key_grad(flat[:, SEG:], both_hidden).astype(BF)
-    home_two = dp_permute(grad_two, reverse(second_keys()))
     pair_one = key_grad(slopes[1, :, :SEG], pair_hidden)
     grad_one = key_grad(slopes[0, :, :SEG], hidden) + jnp.where(core == 1, pair_one, 0.0)
-    home_one = dp_permute(grad_one.astype(BF), reverse(first_keys()))
-    pair_grad = core_swap(jnp.dot(slopes[1], keys[1], preferred_element_type=F32).astype(BF))
-    own_grad = jnp.dot(slopes[0], keys[0], preferred_element_type=F32)
-    own_grad = own_grad + jnp.where(core == 0, pair_one, 0.0)
-    home = home_one.astype(F32) + home_two.astype(F32) + pair_grad.astype(F32)
-    return (own_grad + home).astype(BF)
+    grad_one, flat = lax.optimization_barrier((grad_one.astype(BF), flat))
+    home_one = dp_permute(grad_one, reverse(first_keys()))
+    grad_two = key_grad(flat[:, SEG:], both_hidden).astype(BF)
+    grad_two, flat = lax.optimization_barrier((grad_two, flat))
+    home_two = dp_permute(grad_two, reverse(second_keys()))
+    pair_grad = core_swap(jnp.dot(flat[SEG:], keys[1], preferred_element_type=F32).astype(BF))
+    own_grad = jnp.dot(flat[:SEG], keys[0], preferred_element_type=F32)
+    own_grad = lax.optimization_barrier(own_grad + jnp.where(core == 0, pair_one, 0.0))
+    own_grad = lax.optimization_barrier(own_grad + home_one.astype(F32))
+    own_grad = lax.optimization_barrier(own_grad + home_two.astype(F32))
+    return (own_grad + pair_grad.astype(F32)).astype(BF)
 
 
 def solution(mesh):

time: 207 us -> 205 us (level)
  the two profiles are of different devices: /device:TPU:1 before, /device:TPU:86 now
where the time goes in v10:
time: 205 us; the launch traced here: 204 us
  waiting for transfers between devices  108 us (53%)
  starting transfers between devices  75.6 us (37%)
  matrix products  7.86 us (4%)
  other arithmetic  6.95 us (3%)
  local copies, waits for them, and re-layouts  4.66 us (2%)
    ppermute x8, waiting for transfers between devices, dp_permute(): return lax.ppermute(value, 'dp', pairs)  53 us
    ppermute x2, waiting for transfers between devices, triple_swap(): return lax.ppermute(value, 'tensor', [(r, (r + 3) % 6) for r in range(6)])  39.4 us
    ppermute x8, starting transfers between devices, dp_permute(): return lax.ppermute(value, 'dp', pairs)  29.9 us
    ppermute x2, starting transfers between devices, triple_swap(): return lax.ppermute(value, 'tensor', [(r, (r + 3) % 6) for r in range(6)])  23.4 us
    ppermute x8, starting transfers between devices, triple_shift(): return lax.ppermute(value, 'tensor', pairs)  22.3 us
    ppermute x8, waiting for transfers between devices, triple_shift(): return lax.ppermute(value, 'tensor', pairs)  15.6 us
    dot_general x12, matrix products, partial_of(): lax.dot_general(queries, keys, (((1,), (1,)), ((), ())), preferred_elemen...  5.02 us
  transfers between devices with their start and end apart: 18, of which 12 were waited for; matrix products, arithmetic and copies ran while one was open for 4% of the time, Pallas kernels for 0%

profile of v10, /device:TPU:86, one launch (start us, length us, event | category | flops | bytes accessed | tf_op | source)
XLA Modules:
  0.0 203.7 jit_solution(5420428302849857206)
XLA Ops:
  0.8 1.1 pad_maximum_fusion.2
  1.9 13.7 %collective-permute-start.2 = (bf16[400,640]{1,0:T(8,128)(2,1)S(1)}, bf16[400,640]{1,0:T(8,128)(2,1)S(1)}, u32[]{:S(2)}, u32[]{:S(2)}) collective-permute-start(bf16[400,640]{1,0:T(8,128)(2,1)S(1)} %pad_maximum_fusion.2), channel_id=1, source_target_pairs={{0,18},{6,24},{12,30},{18,36},{24,42},{30,48},{36,54},{42,60},{48,... | collective-permute-start | bytes 1536008 | tf_op jit(solution)/shard_map/ppermute | solution.py:15
  15.6 3.4 %collective-permute-start.1 = (bf16[400,640]{1,0:T(8,128)(2,1)S(1)}, bf16[400,640]{1,0:T(8,128)(2,1)S(1)}, u32[]{:S(2)}, u32[]{:S(2)}) collective-permute-start(bf16[400,640]{1,0:T(8,128)(2,1)S(1)} %pad_maximum_fusion.2), channel_id=1, source_target_pairs={{0,24},{6,18},{12,36},{18,30},{24,48},{30,42},{36,60},{42,54},{48,... | collective-permute-start | bytes 1536008 | tf_op jit(solution)/shard_map/ppermute | solution.py:15
  21.8 2.3 %collective-permute-start = (f32[4,64]{1,0:T(4,128)S(1)}, f32[4,64]{1,0:T(4,128)S(1)}, u32[]{:S(2)}, u32[]{:S(2)}) collective-permute-start(f32[4,64]{1,0:T(4,128)S(1)} %fusion.46), channel_id=1, source_target_pairs={{0,6},{6,0},{12,18},{18,12},{24,30},{30,24},{36,42},{42,36},{48,54... | collective-permute-start | bytes 3080 | tf_op jit(solution)/shard_map/ppermute | solution.py:15
  24.1 2.0 collective-permute-start.3
  26.3 2.2 %collective-permute-done.1 = bf16[400,640]{1,0:T(8,128)(2,1)S(1)} collective-permute-done((bf16[400,640]{1,0:T(8,128)(2,1)S(1)}, bf16[400,640]{1,0:T(8,128)(2,1)S(1)}, u32[]{:S(2)}, u32[]{:S(2)}) %collective-permute-start.1) | collective-permute-done | bytes 512032 | tf_op jit(solution)/shard_map/ppermute | solution.py:15
  28.6 15.9 %collective-permute-done.2 = bf16[400,640]{1,0:T(8,128)(2,1)S(1)} collective-permute-done((bf16[400,640]{1,0:T(8,128)(2,1)S(1)}, bf16[400,640]{1,0:T(8,128)(2,1)S(1)}, u32[]{:S(2)}, u32[]{:S(2)}) %collective-permute-start.2) | collective-permute-done | bytes 512032 | tf_op jit(solution)/shard_map/ppermute | solution.py:15
  46.2 1.1 slice.138
  50.6 1.9 collective-permute-start.4
  52.6 3.9 %collective-permute-start.5 = (f32[2,64,768]{2,1,0:T(8,128)S(1)}, f32[2,64,768]{2,1,0:T(8,128)S(1)}, u32[]{:S(2)}, u32[]{:S(2)}) collective-permute-start(f32[2,64,768]{2,1,0:T(8,128)S(1)} %get-tuple-element.36), channel_id=1, source_target_pairs={{0,2},{1,0},{2,1},{3,5},{4,3},{5,4},{6,8},{7,6},{8,7},{9,11},{10,9... | collective-permute-start | bytes 1179656 | tf_op jit(solution)/shard_map/ppermute | solution.py:38
  57.0 3.3 %collective-permute-done.4 = f32[2,64,768]{2,1,0:T(8,128)S(1)} collective-permute-done((f32[2,64,768]{2,1,0:T(8,128)S(1)}, f32[2,64,768]{2,1,0:T(8,128)S(1)}, u32[]{:S(2)}, u32[]{:S(2)}) %collective-permute-start.4) | collective-permute-done | bytes 393248 | tf_op jit(solution)/shard_map/ppermute | solution.py:38
  60.3 3.0 %collective-permute-done.5 = f32[2,64,768]{2,1,0:T(8,128)S(1)} collective-permute-done((f32[2,64,768]{2,1,0:T(8,128)S(1)}, f32[2,64,768]{2,1,0:T(8,128)S(1)}, u32[]{:S(2)}, u32[]{:S(2)}) %collective-permute-start.5) | collective-permute-done | bytes 393248 | tf_op jit(solution)/shard_map/ppermute | solution.py:38
  63.4 4.8 %collective-permute-start.6 = (f32[2,64,768]{2,1,0:T(8,128)S(1)}, f32[2,64,768]{2,1,0:T(8,128)S(1)}, u32[]{:S(2)}, u32[]{:S(2)}) collective-permute-start(f32[2,64,768]{2,1,0:T(8,128)S(1)} %pad_maximum_fusion.5), channel_id=1, source_target_pairs={{0,1},{1,2},{2,0},{3,4},{4,5},{5,3},{6,7},{7,8},{8,6},{9,10},{10,1... | collective-permute-start | bytes 1179656 | tf_op jit(solution)/shard_map/ppermute | solution.py:38
  68.2 1.9 collective-permute-start.7
  70.1 19.5 %collective-permute-start.8 = (f32[2,64,768]{2,1,0:T(8,128)S(1)}, f32[2,64,768]{2,1,0:T(8,128)S(1)}, u32[]{:S(2)}, u32[]{:S(2)}) collective-permute-start(f32[2,64,768]{2,1,0:T(8,128)S(1)} %fusion.10), channel_id=1, source_target_pairs={{0,3},{1,4},{2,5},{3,0},{4,1},{5,2},{6,9},{7,10},{8,11},{9,6},{10,... | collective-permute-start | bytes 1179656 | tf_op jit(solution)/shard_map/ppermute | solution.py:42
  90.6 29.6 %collective-permute-done.8 = f32[2,64,768]{2,1,0:T(8,128)S(1)} collective-permute-done((f32[2,64,768]{2,1,0:T(8,128)S(1)}, f32[2,64,768]{2,1,0:T(8,128)S(1)}, u32[]{:S(2)}, u32[]{:S(2)}) %collective-permute-start.8) | collective-permute-done | bytes 393248 | tf_op jit(solution)/shard_map/ppermute | solution.py:42
  121.4 2.0 collective-permute-start.9
  123.4 1.0 collective-permute-done.9
  125.5 1.9 collective-permute-start.11
  127.5 3.9 %collective-permute-start.10 = (bf16[2,64,768]{2,1,0:T(8,128)(2,1)}, bf16[2,64,768]{2,1,0:T(8,128)(2,1)S(1)}, u32[]{:S(2)}, u32[]{:S(2)}) collective-permute-start(bf16[2,64,768]{2,1,0:T(8,128)(2,1)} %get-tuple-element.52), channel_id=1, source_target_pairs={{0,3},{1,4},{2,5},{3,0},{4,1},{5,2},{6,9},{7,10},{8,11},{9,6},{10,... | collective-permute-start | bytes 589832 | tf_op jit(solution)/shard_map/ppermute | solution.py:42
  131.3 2.0 collective-permute-start.12
  133.3 2.0 %collective-permute-done.11 = bf16[2,64,768]{2,1,0:T(8,128)(2,1)S(1)} collective-permute-done((bf16[2,64,768]{2,1,0:T(8,128)(2,1)}, bf16[2,64,768]{2,1,0:T(8,128)(2,1)S(1)}, u32[]{:S(2)}, u32[]{:S(2)}) %collective-permute-start.11) | collective-permute-done | bytes 196640 | tf_op jit(solution)/shard_map/ppermute | solution.py:38
  135.4 9.8 %collective-permute-done.10 = bf16[2,64,768]{2,1,0:T(8,128)(2,1)S(1)} collective-permute-done((bf16[2,64,768]{2,1,0:T(8,128)(2,1)}, bf16[2,64,768]{2,1,0:T(8,128)(2,1)S(1)}, u32[]{:S(2)}, u32[]{:S(2)}) %collective-permute-start.10) | collective-permute-done | bytes 196640 | tf_op jit(solution)/shard_map/ppermute | solution.py:42
  145.2 2.9 %collective-permute-done.12 = bf16[2,64,768]{2,1,0:T(8,128)(2,1)} collective-permute-done((bf16[2,64,768]{2,1,0:T(8,128)(2,1)}, bf16[2,64,768]{2,1,0:T(8,128)(2,1)}, u32[]{:S(2)}, u32[]{:S(2)}) %collective-permute-start.12) | collective-permute-done | bytes 196640 | tf_op jit(solution)/shard_map/ppermute | solution.py:38
  148.1 2.1 %collective-permute-start.14 = (bf16[2,64,768]{2,1,0:T(8,128)(2,1)S(1)}, bf16[2,64,768]{2,1,0:T(8,128)(2,1)S(1)}, u32[]{:S(2)}, u32[]{:S(2)}) collective-permute-start(bf16[2,64,768]{2,1,0:T(8,128)(2,1)S(1)} %collective-permute-done.10), channel_id=1, source_target_pairs={{0,2},{1,0},{2,1},{3,5},{4,3},{5,4},{6,8},{7,6},{8,7},{9,11},{10,9... | collective-permute-start | bytes 589832 | tf_op jit(solution)/shard_map/ppermute | solution.py:38
  150.2 3.7 %collective-permute-start.13 = (bf16[2,64,768]{2,1,0:T(8,128)(2,1)S(1)}, bf16[2,64,768]{2,1,0:T(8,128)(2,1)S(1)}, u32[]{:S(2)}, u32[]{:S(2)}) collective-permute-start(bf16[2,64,768]{2,1,0:T(8,128)(2,1)S(1)} %collective-permute-done.10), channel_id=1, source_target_pairs={{0,1},{1,2},{2,0},{3,4},{4,5},{5,3},{6,7},{7,8},{8,6},{9,10},{10,1... | collective-permute-start | bytes 589832 | tf_op jit(solution)/shard_map/ppermute | solution.py:38
  154.9 4.3 %collective-permute-done.13 = bf16[2,64,768]{2,1,0:T(8,128)(2,1)S(1)} collective-permute-done((bf16[2,64,768]{2,1,0:T(8,128)(2,1)S(1)}, bf16[2,64,768]{2,1,0:T(8,128)(2,1)S(1)}, u32[]{:S(2)}, u32[]{:S(2)}) %collective-permute-start.13) | collective-permute-done | bytes 196640 | tf_op jit(solution)/shard_map/ppermute | solution.py:38
  161.0 2.7 %collective-permute-start.15 = (bf16[384,640]{1,0:T(8,128)(2,1)S(1)}, bf16[384,640]{1,0:T(8,128)(2,1)S(1)}, u32[]{:S(2)}, u32[]{:S(2)}) collective-permute-start(bf16[384,640]{1,0:T(8,128)(2,1)S(1)} %fusion), channel_id=1, source_target_pairs={{24,0},{18,6},{36,12},{30,18},{48,24},{42,30},{60,36},{54,42},{72,... | collective-permute-start | bytes 1474568 | tf_op jit(solution)/shard_map/ppermute | solution.py:15
  164.3 1.9 collective-permute-start.16
  166.9 1.9 collective-permute-start.17
  168.8 5.0 %collective-permute-done.15 = bf16[384,640]{1,0:T(8,128)(2,1)S(1)} collective-permute-done((bf16[384,640]{1,0:T(8,128)(2,1)S(1)}, bf16[384,640]{1,0:T(8,128)(2,1)S(1)}, u32[]{:S(2)}, u32[]{:S(2)}) %collective-permute-start.15) | collective-permute-done | bytes 491552 | tf_op jit(solution)/shard_map/ppermute | solution.py:15
  173.9 28.9 %collective-permute-done.16 = bf16[384,640]{1,0:T(8,128)(2,1)S(1)} collective-permute-done((bf16[384,640]{1,0:T(8,128)(2,1)S(1)}, bf16[384,640]{1,0:T(8,128)(2,1)S(1)}, u32[]{:S(2)}, u32[]{:S(2)}) %collective-permute-start.16) | collective-permute-done | bytes 491552 | tf_op jit(solution)/shard_map/ppermute | solution.py:15
  (96 shorter events, 17.3 us)
Async XLA Ops:
  0.0 28.5 %copy-start = (bf16[384,640]{1,0:T(8,128)(2,1)S(1)}, bf16[384,640]{1,0:T(8,128)(2,1)}, u32[]{:S(2)}) copy-start(bf16[384,640]{1,0:T(8,128)(2,1)} %param.6) | copy-start | bytes 1474564
  1.9 42.7 %collective-permute-start.2 = (bf16[400,640]{1,0:T(8,128)(2,1)S(1)}, bf16[400,640]{1,0:T(8,128)(2,1)S(1)}, u32[]{:S(2)}, u32[]{:S(2)}) collective-permute-start(bf16[400,640]{1,0:T(8,128)(2,1)S(1)} %pad_maximum_fusion.2), channel_id=1, source_target_pairs={{0,18},{6,24},{12,30},{18,36},{24,42},{30,48},{36,54},{42,60},{48,... | collective-permute-start | bytes 1536008 | tf_op jit(solution)/shard_map/ppermute | solution.py:15
  15.6 12.9 %collective-permute-start.1 = (bf16[400,640]{1,0:T(8,128)(2,1)S(1)}, bf16[400,640]{1,0:T(8,128)(2,1)S(1)}, u32[]{:S(2)}, u32[]{:S(2)}) collective-permute-start(bf16[400,640]{1,0:T(8,128)(2,1)S(1)} %pad_maximum_fusion.2), channel_id=1, source_target_pairs={{0,24},{6,18},{12,36},{18,30},{24,48},{30,42},{36,60},{42,54},{48,... | collective-permute-start | bytes 1536008 | tf_op jit(solution)/shard_map/ppermute | solution.py:15
  21.8 4.4 %collective-permute-start = (f32[4,64]{1,0:T(4,128)S(1)}, f32[4,64]{1,0:T(4,128)S(1)}, u32[]{:S(2)}, u32[]{:S(2)}) collective-permute-start(f32[4,64]{1,0:T(4,128)S(1)} %fusion.46), channel_id=1, source_target_pairs={{0,6},{6,0},{12,18},{18,12},{24,30},{30,24},{36,42},{42,36},{48,54... | collective-permute-start | bytes 3080 | tf_op jit(solution)/shard_map/ppermute | solution.py:15
  24.1 22.1 %collective-permute-start.3 = (bf16[400,640]{1,0:T(8,128)(2,1)S(1)}, bf16[400,640]{1,0:T(8,128)(2,1)}, u32[]{:S(2)}, u32[]{:S(2)}) collective-permute-start(bf16[400,640]{1,0:T(8,128)(2,1)S(1)} %pad_maximum_fusion.2), channel_id=1, source_target_pairs={{0,6},{6,0},{12,18},{18,12},{24,30},{30,24},{36,42},{42,36},{48,54... | collective-permute-start | bytes 1536008 | tf_op jit(solution)/shard_map/ppermute | solution.py:15
  26.3 18.3 %copy-start.7 = (f32[4,64]{1,0:T(4,128)}, f32[4,64]{1,0:T(4,128)S(1)}, u32[]{:S(2)}) copy-start(f32[4,64]{1,0:T(4,128)S(1)} %collective-permute-done) | copy-start | bytes 3076
  26.3 94.7 %copy-start.5 = (f32[2,64]{1,0:T(2,128)}, f32[2,64]{1,0:T(2,128)S(1)}, u32[]{:S(2)}) copy-start(f32[2,64]{1,0:T(2,128)S(1)} %fusion.60) | copy-start | bytes 1540
  28.6 16.1 %copy-start.1 = (bf16[400,640]{1,0:T(8,128)(2,1)}, bf16[400,640]{1,0:T(8,128)(2,1)S(1)}, u32[]{:S(2)}) copy-start(bf16[400,640]{1,0:T(8,128)(2,1)S(1)} %broadcast_select_fusion) | copy-start | bytes 1536004
  44.5 0.8 copy-start.2
  45.3 44.3 %copy-start.3 = (bf16[384,640]{1,0:T(8,128)(2,1)}, bf16[384,640]{1,0:T(8,128)(2,1)S(1)}, u32[]{:S(2)}) copy-start(bf16[384,640]{1,0:T(8,128)(2,1)S(1)} %slice.137) | copy-start | bytes 1474564
  49.5 0.7 slice-start.1
  49.5 0.8 slice-start
  50.6 9.7 %collective-permute-start.4 = (f32[2,64,768]{2,1,0:T(8,128)S(1)}, f32[2,64,768]{2,1,0:T(8,128)S(1)}, u32[]{:S(2)}, u32[]{:S(2)}) collective-permute-start(f32[2,64,768]{2,1,0:T(8,128)S(1)} %get-tuple-element.35), channel_id=1, source_target_pairs={{0,1},{1,2},{2,0},{3,4},{4,5},{5,3},{6,7},{7,8},{8,6},{9,10},{10,1... | collective-permute-start | bytes 1179656 | tf_op jit(solution)/shard_map/ppermute | solution.py:38
  52.6 10.8 %collective-permute-start.5 = (f32[2,64,768]{2,1,0:T(8,128)S(1)}, f32[2,64,768]{2,1,0:T(8,128)S(1)}, u32[]{:S(2)}, u32[]{:S(2)}) collective-permute-start(f32[2,64,768]{2,1,0:T(8,128)S(1)} %get-tuple-element.36), channel_id=1, source_target_pairs={{0,2},{1,0},{2,1},{3,5},{4,3},{5,4},{6,8},{7,6},{8,7},{9,11},{10,9... | collective-permute-start | bytes 1179656 | tf_op jit(solution)/shard_map/ppermute | solution.py:38
  63.4 27.2 %collective-permute-start.6 = (f32[2,64,768]{2,1,0:T(8,128)S(1)}, f32[2,64,768]{2,1,0:T(8,128)S(1)}, u32[]{:S(2)}, u32[]{:S(2)}) collective-permute-start(f32[2,64,768]{2,1,0:T(8,128)S(1)} %pad_maximum_fusion.5), channel_id=1, source_target_pairs={{0,1},{1,2},{2,0},{3,4},{4,5},{5,3},{6,7},{7,8},{8,6},{9,10},{10,1... | collective-permute-start | bytes 1179656 | tf_op jit(solution)/shard_map/ppermute | solution.py:38
  68.2 22.4 %collective-permute-start.7 = (f32[2,64,768]{2,1,0:T(8,128)S(1)}, f32[2,64,768]{2,1,0:T(8,128)S(1)}, u32[]{:S(2)}, u32[]{:S(2)}) collective-permute-start(f32[2,64,768]{2,1,0:T(8,128)S(1)} %pad_maximum_fusion.6), channel_id=1, source_target_pairs={{0,2},{1,0},{2,1},{3,5},{4,3},{5,4},{6,8},{7,6},{8,7},{9,11},{10,9... | collective-permute-start | bytes 1179656 | tf_op jit(solution)/shard_map/ppermute | solution.py:38
  70.1 50.0 %collective-permute-start.8 = (f32[2,64,768]{2,1,0:T(8,128)S(1)}, f32[2,64,768]{2,1,0:T(8,128)S(1)}, u32[]{:S(2)}, u32[]{:S(2)}) collective-permute-start(f32[2,64,768]{2,1,0:T(8,128)S(1)} %fusion.10), channel_id=1, source_target_pairs={{0,3},{1,4},{2,5},{3,0},{4,1},{5,2},{6,9},{7,10},{8,11},{9,6},{10,... | collective-permute-start | bytes 1179656 | tf_op jit(solution)/shard_map/ppermute | solution.py:42
  90.5 29.9 %copy-start.8 = (f32[4,64]{1,0:T(4,128)S(1)}, f32[4,64]{1,0:T(4,128)}, u32[]{:S(2)}) copy-start(f32[4,64]{1,0:T(4,128)} %copy-done.7) | copy-start | bytes 3076
  121.4 3.2 %copy-start.6 = (f32[2,64]{1,0:T(2,128)S(1)}, f32[2,64]{1,0:T(2,128)}, u32[]{:S(2)}) copy-start(f32[2,64]{1,0:T(2,128)} %copy-done.5) | copy-start | bytes 1540
  121.4 3.1 %collective-permute-start.9 = (f32[2,4,64]{2,0,1:T(2,128)S(1)}, f32[2,4,64]{2,0,1:T(2,128)S(1)}, u32[]{:S(2)}, u32[]{:S(2)}) collective-permute-start(f32[2,4,64]{2,0,1:T(2,128)S(1)} %pad_maximum_fusion.10), channel_id=1, source_target_pairs={{0,6},{6,0},{12,18},{18,12},{24,30},{30,24},{36,42},{42,36},{48,54... | collective-permute-start | bytes 6152 | tf_op jit(solution)/shard_map/ppermute | solution.py:15
  123.4 1.2 copy-start.9
  125.5 9.8 %collective-permute-start.11 = (bf16[2,64,768]{2,1,0:T(8,128)(2,1)}, bf16[2,64,768]{2,1,0:T(8,128)(2,1)S(1)}, u32[]{:S(2)}, u32[]{:S(2)}) collective-permute-start(bf16[2,64,768]{2,1,0:T(8,128)(2,1)} %get-tuple-element.52), channel_id=1, source_target_pairs={{0,1},{1,2},{2,0},{3,4},{4,5},{5,3},{6,7},{7,8},{8,6},{9,10},{10,1... | collective-permute-start | bytes 589832 | tf_op jit(solution)/shard_map/ppermute | solution.py:38
  127.5 17.7 %collective-permute-start.10 = (bf16[2,64,768]{2,1,0:T(8,128)(2,1)}, bf16[2,64,768]{2,1,0:T(8,128)(2,1)S(1)}, u32[]{:S(2)}, u32[]{:S(2)}) collective-permute-start(bf16[2,64,768]{2,1,0:T(8,128)(2,1)} %get-tuple-element.52), channel_id=1, source_target_pairs={{0,3},{1,4},{2,5},{3,0},{4,1},{5,2},{6,9},{7,10},{8,11},{9,6},{10,... | collective-permute-start | bytes 589832 | tf_op jit(solution)/shard_map/ppermute | solution.py:42
  131.3 16.8 %collective-permute-start.12 = (bf16[2,64,768]{2,1,0:T(8,128)(2,1)}, bf16[2,64,768]{2,1,0:T(8,128)(2,1)}, u32[]{:S(2)}, u32[]{:S(2)}) collective-permute-start(bf16[2,64,768]{2,1,0:T(8,128)(2,1)} %get-tuple-element.52), channel_id=1, source_target_pairs={{0,2},{1,0},{2,1},{3,5},{4,3},{5,4},{6,8},{7,6},{8,7},{9,11},{10,9... | collective-permute-start | bytes 589832 | tf_op jit(solution)/shard_map/ppermute | solution.py:38
  148.1 11.2 %collective-permute-start.14 = (bf16[2,64,768]{2,1,0:T(8,128)(2,1)S(1)}, bf16[2,64,768]{2,1,0:T(8,128)(2,1)S(1)}, u32[]{:S(2)}, u32[]{:S(2)}) collective-permute-start(bf16[2,64,768]{2,1,0:T(8,128)(2,1)S(1)} %collective-permute-done.10), channel_id=1, source_target_pairs={{0,2},{1,0},{2,1},{3,5},{4,3},{5,4},{6,8},{7,6},{8,7},{9,11},{10,9... | collective-permute-start | bytes 589832 | tf_op jit(solution)/shard_map/ppermute | solution.py:38
  150.2 9.0 %collective-permute-start.13 = (bf16[2,64,768]{2,1,0:T(8,128)(2,1)S(1)}, bf16[2,64,768]{2,1,0:T(8,128)(2,1)S(1)}, u32[]{:S(2)}, u32[]{:S(2)}) collective-permute-start(bf16[2,64,768]{2,1,0:T(8,128)(2,1)S(1)} %collective-permute-done.10), channel_id=1, source_target_pairs={{0,1},{1,2},{2,0},{3,4},{4,5},{5,3},{6,7},{7,8},{8,6},{9,10},{10,1... | collective-permute-start | bytes 589832 | tf_op jit(solution)/shard_map/ppermute | solution.py:38
  160.3 3.4 %copy-start.4 = (bf16[384,640]{1,0:T(8,128)(2,1)S(1)}, bf16[384,640]{1,0:T(8,128)(2,1)}, u32[]{:S(2)}) copy-start(bf16[384,640]{1,0:T(8,128)(2,1)} %copy-done.3) | copy-start | bytes 1474564
  161.0 12.8 %collective-permute-start.15 = (bf16[384,640]{1,0:T(8,128)(2,1)S(1)}, bf16[384,640]{1,0:T(8,128)(2,1)S(1)}, u32[]{:S(2)}, u32[]{:S(2)}) collective-permute-start(bf16[384,640]{1,0:T(8,128)(2,1)S(1)} %fusion), channel_id=1, source_target_pairs={{24,0},{18,6},{36,12},{30,18},{48,24},{42,30},{60,36},{54,42},{72,... | collective-permute-start | bytes 1474568 | tf_op jit(solution)/shard_map/ppermute | solution.py:15
  164.3 38.4 %collective-permute-start.16 = (bf16[384,640]{1,0:T(8,128)(2,1)S(1)}, bf16[384,640]{1,0:T(8,128)(2,1)S(1)}, u32[]{:S(2)}, u32[]{:S(2)}) collective-permute-start(bf16[384,640]{1,0:T(8,128)(2,1)S(1)} %convolution_convert_fusion.1), channel_id=1, source_target_pairs={{18,0},{24,6},{30,12},{36,18},{42,24},{48,30},{54,36},{60,42},{66,... | collective-permute-start | bytes 1474568 | tf_op jit(solution)/shard_map/ppermute | solution.py:15
  166.9 35.9 %collective-permute-start.17 = (bf16[384,640]{1,0:T(8,128)(2,1)S(1)}, bf16[384,640]{1,0:T(8,128)(2,1)S(1)}, u32[]{:S(2)}, u32[]{:S(2)}) collective-permute-start(bf16[384,640]{1,0:T(8,128)(2,1)S(1)} %convolution_convert_fusion), channel_id=1, source_target_pairs={{0,6},{6,0},{12,18},{18,12},{24,30},{30,24},{36,42},{42,36},{48,54... | collective-permute-start | bytes 1474568 | tf_op jit(solution)/shard_map/ppermute | solution.py:15

commit v11 on v10

--- a/solution.py
+++ b/solution.py
@@ -80,6 +80,7 @@
 def gathered(mine, u, v):
     partner = triple_swap(mine)
     own = (triple_shift(mine, 1), triple_shift(mine, 2))
+    partner = jnp.where(u + v < 6, partner, mine)
     partner, *own = lax.optimization_barrier((partner,) + own)
     passed = (triple_shift(partner, 1), triple_shift(partner, 2))
     full = jnp.zeros((2, SEG, mine.shape[2]), BF)
@@ -139,8 +140,8 @@
     late = tuple(partial(queries, steps, u) for steps in (1, 2))
     passing, *late = lax.optimization_barrier((passing,) + late)
     from_partner = triple_swap(passing)
-    scores = partial(queries, 0, u) + triple_shift(late[0], 1) + triple_shift(late[1], 2)
-    scores = (scores + from_partner) * score_scale
+    scores = lax.optimization_barrier(partial(queries, 0, u) + from_partner)
+    scores = (scores + triple_shift(late[0], 1) + triple_shift(late[1], 2)) * score_scale
 
     usable = jnp.broadcast_to((codes > 0.0)[:, None], scores.shape)
     matches = usable & (codes[:, None] == row_codes[:, :, None])

time: 205 us -> 205 us (level)
  the two profiles are of different devices: /device:TPU:86 before, /device:TPU:194 now
where the time goes in v11:
time: 205 us
  waiting for transfers between devices  106 us (52%)
  starting transfers between devices  80.4 us (39%)
  matrix products  7.87 us (4%)
  other arithmetic  5.8 us (3%)
  local copies, waits for them, and re-layouts  3.74 us (2%)
    ppermute x8, waiting for transfers between devices, triple_shift(): return lax.ppermute(value, 'tensor', pairs)  67.5 us
    ppermute x8, starting transfers between devices, triple_shift(): return lax.ppermute(value, 'tensor', pairs)  46.2 us
    ppermute x8, starting transfers between devices, dp_permute(): return lax.ppermute(value, 'dp', pairs)  27.5 us
    ppermute x8, waiting for transfers between devices, dp_permute(): return lax.ppermute(value, 'dp', pairs)  25.2 us
    ppermute x2, waiting for transfers between devices, triple_swap(): return lax.ppermute(value, 'tensor', [(r, (r + 3) % 6) for r in range(6)])  13.3 us
    ppermute x2, starting transfers between devices, triple_swap(): return lax.ppermute(value, 'tensor', [(r, (r + 3) % 6) for r in range(6)])  6.78 us
    dot_general x12, matrix products, partial_of(): lax.dot_general(queries, keys, (((1,), (1,)), ((), ())), preferred_elemen...  5.02 us
  transfers between devices with their start and end apart: 18, of which 14 were waited for; matrix products, arithmetic and copies ran while one was open for 3% of the time, Pallas kernels for 0%

profile of v11, /device:TPU:194, one launch (start us, length us, event | category | flops | bytes accessed | tf_op | source)
XLA Modules:
  0.0 204.6 jit_solution(9774302058913942099)
XLA Ops:
  0.8 1.1 pad_maximum_fusion.2
  1.9 11.9 %collective-permute-start.2 = (bf16[400,640]{1,0:T(8,128)(2,1)S(1)}, bf16[400,640]{1,0:T(8,128)(2,1)S(1)}, u32[]{:S(2)}, u32[]{:S(2)}) collective-permute-start(bf16[400,640]{1,0:T(8,128)(2,1)S(1)} %pad_maximum_fusion.2), channel_id=1, source_target_pairs={{0,18},{6,24},{12,30},{18,36},{24,42},{30,48},{36,54},{42,60},{48,... | collective-permute-start | bytes 1536008 | tf_op jit(solution)/shard_map/ppermute | solution.py:15
  13.8 3.4 %collective-permute-start.1 = (bf16[400,640]{1,0:T(8,128)(2,1)S(1)}, bf16[400,640]{1,0:T(8,128)(2,1)S(1)}, u32[]{:S(2)}, u32[]{:S(2)}) collective-permute-start(bf16[400,640]{1,0:T(8,128)(2,1)S(1)} %pad_maximum_fusion.2), channel_id=1, source_target_pairs={{0,24},{6,18},{12,36},{18,30},{24,48},{30,42},{36,60},{42,54},{48,... | collective-permute-start | bytes 1536008 | tf_op jit(solution)/shard_map/ppermute | solution.py:15
  20.0 2.3 %collective-permute-start = (f32[4,64]{1,0:T(4,128)S(1)}, f32[4,64]{1,0:T(4,128)S(1)}, u32[]{:S(2)}, u32[]{:S(2)}) collective-permute-start(f32[4,64]{1,0:T(4,128)S(1)} %fusion.43), channel_id=1, source_target_pairs={{0,6},{6,0},{12,18},{18,12},{24,30},{30,24},{36,42},{42,36},{48,54... | collective-permute-start | bytes 3080 | tf_op jit(solution)/shard_map/ppermute | solution.py:15
  22.3 2.0 collective-permute-start.3
  24.5 3.4 %collective-permute-done.1 = bf16[400,640]{1,0:T(8,128)(2,1)S(1)} collective-permute-done((bf16[400,640]{1,0:T(8,128)(2,1)S(1)}, bf16[400,640]{1,0:T(8,128)(2,1)S(1)}, u32[]{:S(2)}, u32[]{:S(2)}) %collective-permute-start.1) | collective-permute-done | bytes 512032 | tf_op jit(solution)/shard_map/ppermute | solution.py:15
  28.0 4.1 %collective-permute-done.2 = bf16[400,640]{1,0:T(8,128)(2,1)S(1)} collective-permute-done((bf16[400,640]{1,0:T(8,128)(2,1)S(1)}, bf16[400,640]{1,0:T(8,128)(2,1)S(1)}, u32[]{:S(2)}, u32[]{:S(2)}) %collective-permute-start.2) | collective-permute-done | bytes 512032 | tf_op jit(solution)/shard_map/ppermute | solution.py:15
  33.8 1.1 slice.138
  38.2 19.5 %collective-permute-start.4 = (f32[2,64,768]{2,1,0:T(8,128)S(1)}, f32[2,64,768]{2,1,0:T(8,128)S(1)}, u32[]{:S(2)}, u32[]{:S(2)}) collective-permute-start(f32[2,64,768]{2,1,0:T(8,128)S(1)} %get-tuple-element.35), channel_id=1, source_target_pairs={{0,1},{1,2},{2,0},{3,4},{4,5},{5,3},{6,7},{7,8},{8,6},{9,10},{10,1... | collective-permute-start | bytes 1179656 | tf_op jit(solution)/shard_map/ppermute | solution.py:38
  57.7 1.9 collective-permute-start.5
  60.2 6.7 %collective-permute-done.4 = f32[2,64,768]{2,1,0:T(8,128)S(1)} collective-permute-done((f32[2,64,768]{2,1,0:T(8,128)S(1)}, f32[2,64,768]{2,1,0:T(8,128)S(1)}, u32[]{:S(2)}, u32[]{:S(2)}) %collective-permute-start.4) | collective-permute-done | bytes 393248 | tf_op jit(solution)/shard_map/ppermute | solution.py:38
  66.9 8.4 %collective-permute-done.5 = f32[2,64,768]{2,1,0:T(8,128)S(1)} collective-permute-done((f32[2,64,768]{2,1,0:T(8,128)S(1)}, f32[2,64,768]{2,1,0:T(8,128)S(1)}, u32[]{:S(2)}, u32[]{:S(2)}) %collective-permute-start.5) | collective-permute-done | bytes 393248 | tf_op jit(solution)/shard_map/ppermute | solution.py:38
  75.4 1.9 collective-permute-start.6
  77.8 1.9 collective-permute-start.7
  79.7 6.5 %collective-permute-start.8 = (f32[2,64,768]{2,1,0:T(8,128)S(1)}, f32[2,64,768]{2,1,0:T(8,128)S(1)}, u32[]{:S(2)}, u32[]{:S(2)}) collective-permute-start(f32[2,64,768]{2,1,0:T(8,128)S(1)} %pad_maximum_fusion.6), channel_id=1, source_target_pairs={{0,2},{1,0},{2,1},{3,5},{4,3},{5,4},{6,8},{7,6},{8,7},{9,11},{10,9... | collective-permute-start | bytes 1179656 | tf_op jit(solution)/shard_map/ppermute | solution.py:38
  86.7 12.4 %collective-permute-done.6 = f32[2,64,768]{2,1,0:T(8,128)S(1)} collective-permute-done((f32[2,64,768]{2,1,0:T(8,128)S(1)}, f32[2,64,768]{2,1,0:T(8,128)S(1)}, u32[]{:S(2)}, u32[]{:S(2)}) %collective-permute-start.6) | collective-permute-done | bytes 393248 | tf_op jit(solution)/shard_map/ppermute | solution.py:42
  99.2 1.1 collective-permute-done.7
  100.3 10.8 %collective-permute-done.8 = f32[2,64,768]{2,1,0:T(8,128)S(1)} collective-permute-done((f32[2,64,768]{2,1,0:T(8,128)S(1)}, f32[2,64,768]{2,1,0:T(8,128)S(1)}, u32[]{:S(2)}, u32[]{:S(2)}) %collective-permute-start.8) | collective-permute-done | bytes 393248 | tf_op jit(solution)/shard_map/ppermute | solution.py:38
  111.7 2.0 collective-permute-start.9
  115.2 4.9 %collective-permute-start.10 = (bf16[2,64,768]{2,1,0:T(8,128)(2,1)S(1)}, bf16[2,64,768]{2,1,0:T(8,128)(2,1)S(1)}, u32[]{:S(2)}, u32[]{:S(2)}) collective-permute-start(bf16[2,64,768]{2,1,0:T(8,128)(2,1)S(1)} %get-tuple-element.52), channel_id=1, source_target_pairs={{0,3},{1,4},{2,5},{3,0},{4,1},{5,2},{6,9},{7,10},{8,11},{9,6},{10,... | collective-permute-start | bytes 589832 | tf_op jit(solution)/shard_map/ppermute | solution.py:42
  120.1 5.5 %collective-permute-start.11 = (bf16[2,64,768]{2,1,0:T(8,128)(2,1)S(1)}, bf16[2,64,768]{2,1,0:T(8,128)(2,1)S(1)}, u32[]{:S(2)}, u32[]{:S(2)}) collective-permute-start(bf16[2,64,768]{2,1,0:T(8,128)(2,1)S(1)} %get-tuple-element.52), channel_id=1, source_target_pairs={{0,1},{1,2},{2,0},{3,4},{4,5},{5,3},{6,7},{7,8},{8,6},{9,10},{10,1... | collective-permute-start | bytes 589832 | tf_op jit(solution)/shard_map/ppermute | solution.py:38
  125.6 2.4 %collective-permute-start.12 = (bf16[2,64,768]{2,1,0:T(8,128)(2,1)S(1)}, bf16[2,64,768]{2,1,0:T(8,128)(2,1)S(1)}, u32[]{:S(2)}, u32[]{:S(2)}) collective-permute-start(bf16[2,64,768]{2,1,0:T(8,128)(2,1)S(1)} %get-tuple-element.52), channel_id=1, source_target_pairs={{0,2},{1,0},{2,1},{3,5},{4,3},{5,4},{6,8},{7,6},{8,7},{9,11},{10,9... | collective-permute-start | bytes 589832 | tf_op jit(solution)/shard_map/ppermute | solution.py:38
  128.9 8.6 %collective-permute-done.11 = bf16[2,64,768]{2,1,0:T(8,128)(2,1)S(1)} collective-permute-done((bf16[2,64,768]{2,1,0:T(8,128)(2,1)S(1)}, bf16[2,64,768]{2,1,0:T(8,128)(2,1)S(1)}, u32[]{:S(2)}, u32[]{:S(2)}) %collective-permute-start.11) | collective-permute-done | bytes 196640 | tf_op jit(solution)/shard_map/ppermute | solution.py:38
  137.6 4.1 %collective-permute-done.12 = bf16[2,64,768]{2,1,0:T(8,128)(2,1)S(1)} collective-permute-done((bf16[2,64,768]{2,1,0:T(8,128)(2,1)S(1)}, bf16[2,64,768]{2,1,0:T(8,128)(2,1)S(1)}, u32[]{:S(2)}, u32[]{:S(2)}) %collective-permute-start.12) | collective-permute-done | bytes 196640 | tf_op jit(solution)/shard_map/ppermute | solution.py:38
  141.7 6.5 %collective-permute-start.14 = (bf16[2,64,768]{2,1,0:T(8,128)(2,1)S(1)}, bf16[2,64,768]{2,1,0:T(8,128)(2,1)S(1)}, u32[]{:S(2)}, u32[]{:S(2)}) collective-permute-start(bf16[2,64,768]{2,1,0:T(8,128)(2,1)S(1)} %broadcast_select_fusion.1), channel_id=1, source_target_pairs={{0,2},{1,0},{2,1},{3,5},{4,3},{5,4},{6,8},{7,6},{8,7},{9,11},{10,9... | collective-permute-start | bytes 589832 | tf_op jit(solution)/shard_map/ppermute | solution.py:38
  148.2 1.9 collective-permute-start.13
  150.2 27.8 %collective-permute-done.13 = bf16[2,64,768]{2,1,0:T(8,128)(2,1)S(1)} collective-permute-done((bf16[2,64,768]{2,1,0:T(8,128)(2,1)S(1)}, bf16[2,64,768]{2,1,0:T(8,128)(2,1)S(1)}, u32[]{:S(2)}, u32[]{:S(2)}) %collective-permute-start.13) | collective-permute-done | bytes 196640 | tf_op jit(solution)/shard_map/ppermute | solution.py:38
  179.6 2.1 %collective-permute-start.15 = (bf16[384,640]{1,0:T(8,128)(2,1)S(1)}, bf16[384,640]{1,0:T(8,128)(2,1)S(1)}, u32[]{:S(2)}, u32[]{:S(2)}) collective-permute-start(bf16[384,640]{1,0:T(8,128)(2,1)S(1)} %fusion), channel_id=1, source_target_pairs={{24,0},{18,6},{36,12},{30,18},{48,24},{42,30},{60,36},{54,42},{72,... | collective-permute-start | bytes 1474568 | tf_op jit(solution)/shard_map/ppermute | solution.py:15
  182.4 1.9 collective-permute-start.16
  184.9 1.9 collective-permute-start.17
  186.9 3.6 %collective-permute-done.15 = bf16[384,640]{1,0:T(8,128)(2,1)S(1)} collective-permute-done((bf16[384,640]{1,0:T(8,128)(2,1)S(1)}, bf16[384,640]{1,0:T(8,128)(2,1)S(1)}, u32[]{:S(2)}, u32[]{:S(2)}) %collective-permute-start.15) | collective-permute-done | bytes 491552 | tf_op jit(solution)/shard_map/ppermute | solution.py:15
  190.6 13.0 %collective-permute-done.16 = bf16[384,640]{1,0:T(8,128)(2,1)S(1)} collective-permute-done((bf16[384,640]{1,0:T(8,128)(2,1)S(1)}, bf16[384,640]{1,0:T(8,128)(2,1)S(1)}, u32[]{:S(2)}, u32[]{:S(2)}) %collective-permute-start.16) | collective-permute-done | bytes 491552 | tf_op jit(solution)/shard_map/ppermute | solution.py:15
  (92 shorter events, 17.2 us)
Async XLA Ops:
  0.0 27.8 %copy-start = (bf16[384,640]{1,0:T(8,128)(2,1)S(1)}, bf16[384,640]{1,0:T(8,128)(2,1)}, u32[]{:S(2)}) copy-start(bf16[384,640]{1,0:T(8,128)(2,1)} %param.6) | copy-start | bytes 1474564
  1.9 30.3 %collective-permute-start.2 = (bf16[400,640]{1,0:T(8,128)(2,1)S(1)}, bf16[400,640]{1,0:T(8,128)(2,1)S(1)}, u32[]{:S(2)}, u32[]{:S(2)}) collective-permute-start(bf16[400,640]{1,0:T(8,128)(2,1)S(1)} %pad_maximum_fusion.2), channel_id=1, source_target_pairs={{0,18},{6,24},{12,30},{18,36},{24,42},{30,48},{36,54},{42,60},{48,... | collective-permute-start | bytes 1536008 | tf_op jit(solution)/shard_map/ppermute | solution.py:15
  13.8 14.1 %collective-permute-start.1 = (bf16[400,640]{1,0:T(8,128)(2,1)S(1)}, bf16[400,640]{1,0:T(8,128)(2,1)S(1)}, u32[]{:S(2)}, u32[]{:S(2)}) collective-permute-start(bf16[400,640]{1,0:T(8,128)(2,1)S(1)} %pad_maximum_fusion.2), channel_id=1, source_target_pairs={{0,24},{6,18},{12,36},{18,30},{24,48},{30,42},{36,60},{42,54},{48,... | collective-permute-start | bytes 1536008 | tf_op jit(solution)/shard_map/ppermute | solution.py:15
  20.0 4.4 %collective-permute-start = (f32[4,64]{1,0:T(4,128)S(1)}, f32[4,64]{1,0:T(4,128)S(1)}, u32[]{:S(2)}, u32[]{:S(2)}) collective-permute-start(f32[4,64]{1,0:T(4,128)S(1)} %fusion.43), channel_id=1, source_target_pairs={{0,6},{6,0},{12,18},{18,12},{24,30},{30,24},{36,42},{42,36},{48,54... | collective-permute-start | bytes 3080 | tf_op jit(solution)/shard_map/ppermute | solution.py:15
  22.3 11.5 %collective-permute-start.3 = (bf16[400,640]{1,0:T(8,128)(2,1)S(1)}, bf16[400,640]{1,0:T(8,128)(2,1)}, u32[]{:S(2)}, u32[]{:S(2)}) collective-permute-start(bf16[400,640]{1,0:T(8,128)(2,1)S(1)} %pad_maximum_fusion.2), channel_id=1, source_target_pairs={{0,6},{6,0},{12,18},{18,12},{24,30},{30,24},{36,42},{42,36},{48,54... | collective-permute-start | bytes 1536008 | tf_op jit(solution)/shard_map/ppermute | solution.py:15
  28.0 4.3 %copy-start.1 = (bf16[400,640]{1,0:T(8,128)(2,1)}, bf16[400,640]{1,0:T(8,128)(2,1)S(1)}, u32[]{:S(2)}) copy-start(bf16[400,640]{1,0:T(8,128)(2,1)S(1)} %broadcast_select_fusion) | copy-start | bytes 1536004
  32.1 0.8 copy-start.2
  32.2 54.0 %copy-start.3 = (bf16[384,640]{1,0:T(8,128)(2,1)}, bf16[384,640]{1,0:T(8,128)(2,1)S(1)}, u32[]{:S(2)}) copy-start(bf16[384,640]{1,0:T(8,128)(2,1)S(1)} %slice.110) | copy-start | bytes 1474564
  33.0 44.4 %copy-start.5 = (bf16[384,640]{1,0:T(8,128)(2,1)}, bf16[384,640]{1,0:T(8,128)(2,1)S(1)}, u32[]{:S(2)}) copy-start(bf16[384,640]{1,0:T(8,128)(2,1)S(1)} %slice.137) | copy-start | bytes 1474564
  37.1 0.7 slice-start.1
  37.1 0.8 slice-start
  38.2 28.7 %collective-permute-start.4 = (f32[2,64,768]{2,1,0:T(8,128)S(1)}, f32[2,64,768]{2,1,0:T(8,128)S(1)}, u32[]{:S(2)}, u32[]{:S(2)}) collective-permute-start(f32[2,64,768]{2,1,0:T(8,128)S(1)} %get-tuple-element.35), channel_id=1, source_target_pairs={{0,1},{1,2},{2,0},{3,4},{4,5},{5,3},{6,7},{7,8},{8,6},{9,10},{10,1... | collective-permute-start | bytes 1179656 | tf_op jit(solution)/shard_map/ppermute | solution.py:38
  57.7 17.6 %collective-permute-start.5 = (f32[2,64,768]{2,1,0:T(8,128)S(1)}, f32[2,64,768]{2,1,0:T(8,128)S(1)}, u32[]{:S(2)}, u32[]{:S(2)}) collective-permute-start(f32[2,64,768]{2,1,0:T(8,128)S(1)} %get-tuple-element.36), channel_id=1, source_target_pairs={{0,2},{1,0},{2,1},{3,5},{4,3},{5,4},{6,8},{7,6},{8,7},{9,11},{10,9... | collective-permute-start | bytes 1179656 | tf_op jit(solution)/shard_map/ppermute | solution.py:38
  75.4 23.7 %collective-permute-start.6 = (f32[2,64,768]{2,1,0:T(8,128)S(1)}, f32[2,64,768]{2,1,0:T(8,128)S(1)}, u32[]{:S(2)}, u32[]{:S(2)}) collective-permute-start(f32[2,64,768]{2,1,0:T(8,128)S(1)} %fusion.7), channel_id=1, source_target_pairs={{0,3},{1,4},{2,5},{3,0},{4,1},{5,2},{6,9},{7,10},{8,11},{9,6},{10,... | collective-permute-start | bytes 1179656 | tf_op jit(solution)/shard_map/ppermute | solution.py:42
  77.8 22.4 %collective-permute-start.7 = (f32[2,64,768]{2,1,0:T(8,128)S(1)}, f32[2,64,768]{2,1,0:T(8,128)S(1)}, u32[]{:S(2)}, u32[]{:S(2)}) collective-permute-start(f32[2,64,768]{2,1,0:T(8,128)S(1)} %pad_maximum_fusion.5), channel_id=1, source_target_pairs={{0,1},{1,2},{2,0},{3,4},{4,5},{5,3},{6,7},{7,8},{8,6},{9,10},{10,1... | collective-permute-start | bytes 1179656 | tf_op jit(solution)/shard_map/ppermute | solution.py:38
  79.7 31.3 %collective-permute-start.8 = (f32[2,64,768]{2,1,0:T(8,128)S(1)}, f32[2,64,768]{2,1,0:T(8,128)S(1)}, u32[]{:S(2)}, u32[]{:S(2)}) collective-permute-start(f32[2,64,768]{2,1,0:T(8,128)S(1)} %pad_maximum_fusion.6), channel_id=1, source_target_pairs={{0,2},{1,0},{2,1},{3,5},{4,3},{5,4},{6,8},{7,6},{8,7},{9,11},{10,9... | collective-permute-start | bytes 1179656 | tf_op jit(solution)/shard_map/ppermute | solution.py:38
  111.7 3.1 %collective-permute-start.9 = (f32[2,4,64]{2,0,1:T(2,128)S(1)}, f32[2,4,64]{2,0,1:T(2,128)S(1)}, u32[]{:S(2)}, u32[]{:S(2)}) collective-permute-start(f32[2,4,64]{2,0,1:T(2,128)S(1)} %pad_maximum_fusion.10), channel_id=1, source_target_pairs={{0,6},{6,0},{12,18},{18,12},{24,30},{30,24},{36,42},{42,36},{48,54... | collective-permute-start | bytes 6152 | tf_op jit(solution)/shard_map/ppermute | solution.py:15
  115.2 13.7 %collective-permute-start.10 = (bf16[2,64,768]{2,1,0:T(8,128)(2,1)S(1)}, bf16[2,64,768]{2,1,0:T(8,128)(2,1)S(1)}, u32[]{:S(2)}, u32[]{:S(2)}) collective-permute-start(bf16[2,64,768]{2,1,0:T(8,128)(2,1)S(1)} %get-tuple-element.52), channel_id=1, source_target_pairs={{0,3},{1,4},{2,5},{3,0},{4,1},{5,2},{6,9},{7,10},{8,11},{9,6},{10,... | collective-permute-start | bytes 589832 | tf_op jit(solution)/shard_map/ppermute | solution.py:42
  120.1 17.5 %collective-permute-start.11 = (bf16[2,64,768]{2,1,0:T(8,128)(2,1)S(1)}, bf16[2,64,768]{2,1,0:T(8,128)(2,1)S(1)}, u32[]{:S(2)}, u32[]{:S(2)}) collective-permute-start(bf16[2,64,768]{2,1,0:T(8,128)(2,1)S(1)} %get-tuple-element.52), channel_id=1, source_target_pairs={{0,1},{1,2},{2,0},{3,4},{4,5},{5,3},{6,7},{7,8},{8,6},{9,10},{10,1... | collective-permute-start | bytes 589832 | tf_op jit(solution)/shard_map/ppermute | solution.py:38
  125.6 16.1 %collective-permute-start.12 = (bf16[2,64,768]{2,1,0:T(8,128)(2,1)S(1)}, bf16[2,64,768]{2,1,0:T(8,128)(2,1)S(1)}, u32[]{:S(2)}, u32[]{:S(2)}) collective-permute-start(bf16[2,64,768]{2,1,0:T(8,128)(2,1)S(1)} %get-tuple-element.52), channel_id=1, source_target_pairs={{0,2},{1,0},{2,1},{3,5},{4,3},{5,4},{6,8},{7,6},{8,7},{9,11},{10,9... | collective-permute-start | bytes 589832 | tf_op jit(solution)/shard_map/ppermute | solution.py:38
  141.7 36.3 %collective-permute-start.14 = (bf16[2,64,768]{2,1,0:T(8,128)(2,1)S(1)}, bf16[2,64,768]{2,1,0:T(8,128)(2,1)S(1)}, u32[]{:S(2)}, u32[]{:S(2)}) collective-permute-start(bf16[2,64,768]{2,1,0:T(8,128)(2,1)S(1)} %broadcast_select_fusion.1), channel_id=1, source_target_pairs={{0,2},{1,0},{2,1},{3,5},{4,3},{5,4},{6,8},{7,6},{8,7},{9,11},{10,9... | collective-permute-start | bytes 589832 | tf_op jit(solution)/shard_map/ppermute | solution.py:38
  148.2 29.8 %collective-permute-start.13 = (bf16[2,64,768]{2,1,0:T(8,128)(2,1)S(1)}, bf16[2,64,768]{2,1,0:T(8,128)(2,1)S(1)}, u32[]{:S(2)}, u32[]{:S(2)}) collective-permute-start(bf16[2,64,768]{2,1,0:T(8,128)(2,1)S(1)} %broadcast_select_fusion.1), channel_id=1, source_target_pairs={{0,1},{1,2},{2,0},{3,4},{4,5},{5,3},{6,7},{7,8},{8,6},{9,10},{10,1... | collective-permute-start | bytes 589832 | tf_op jit(solution)/shard_map/ppermute | solution.py:38
  178.9 2.8 %copy-start.6 = (bf16[384,640]{1,0:T(8,128)(2,1)S(1)}, bf16[384,640]{1,0:T(8,128)(2,1)}, u32[]{:S(2)}) copy-start(bf16[384,640]{1,0:T(8,128)(2,1)} %copy-done.5) | copy-start | bytes 1474564
  179.6 4.7 %copy-start.4 = (bf16[384,640]{1,0:T(8,128)(2,1)S(1)}, bf16[384,640]{1,0:T(8,128)(2,1)}, u32[]{:S(2)}) copy-start(bf16[384,640]{1,0:T(8,128)(2,1)} %copy-done.3) | copy-start | bytes 1474564
  179.6 10.9 %collective-permute-start.15 = (bf16[384,640]{1,0:T(8,128)(2,1)S(1)}, bf16[384,640]{1,0:T(8,128)(2,1)S(1)}, u32[]{:S(2)}, u32[]{:S(2)}) collective-permute-start(bf16[384,640]{1,0:T(8,128)(2,1)S(1)} %fusion), channel_id=1, source_target_pairs={{24,0},{18,6},{36,12},{30,18},{48,24},{42,30},{60,36},{54,42},{72,... | collective-permute-start | bytes 1474568 | tf_op jit(solution)/shard_map/ppermute | solution.py:15
  182.4 21.3 %collective-permute-start.16 = (bf16[384,640]{1,0:T(8,128)(2,1)S(1)}, bf16[384,640]{1,0:T(8,128)(2,1)S(1)}, u32[]{:S(2)}, u32[]{:S(2)}) collective-permute-start(bf16[384,640]{1,0:T(8,128)(2,1)S(1)} %convolution_convert_fusion.1), channel_id=1, source_target_pairs={{18,0},{24,6},{30,12},{36,18},{42,24},{48,30},{54,36},{60,42},{66,... | collective-permute-start | bytes 1474568 | tf_op jit(solution)/shard_map/ppermute | solution.py:15
  184.9 18.8 %collective-permute-start.17 = (bf16[384,640]{1,0:T(8,128)(2,1)S(1)}, bf16[384,640]{1,0:T(8,128)(2,1)S(1)}, u32[]{:S(2)}, u32[]{:S(2)}) collective-permute-start(bf16[384,640]{1,0:T(8,128)(2,1)S(1)} %convolution_convert_fusion), channel_id=1, source_target_pairs={{0,6},{6,0},{12,18},{18,12},{24,30},{30,24},{36,42},{42,36},{48,54... | collective-permute-start | bytes 1474568 | tf_op jit(solution)/shard_map/ppermute | solution.py:15

commit v12 on v11

--- a/solution.py
+++ b/solution.py
@@ -19,14 +19,9 @@
     return dp_permute(value, [(i, i ^ 1) for i in range(lax.axis_size("dp"))])
 
 
-def first_keys():
+def key_pairs():
     count = lax.axis_size("dp")
     return [(i, (i + (4 if i % 2 == 0 else 2)) % count) for i in range(count)]
-
-
-def second_keys():
-    count = lax.axis_size("dp")
-    return [(i, (i + 3) % count) for i in range(count)]
 
 
 def reverse(pairs):
@@ -98,18 +93,17 @@
     u, v = r // 3, r % 3
     payload = with_codes(hidden, targets, padding)
 
-    key_one = dp_permute(payload, first_keys())
-    key_two = dp_permute(payload, second_keys())
+    pair_payload = core_swap(payload)
+    pair_hidden = pair_payload[:SEG]
+    both = dp_permute(jnp.concatenate([payload, pair_payload], axis=0), key_pairs())
+    key_one, key_two = both[: SEG + 16], both[SEG + 16 :]
     weight = cotangent * padding.astype(F32)
     row_data = jnp.stack([targets.astype(F32) + 1.0, gold_logit, vocab_lse, weight])
     row_data = rows_of(row_data, v * 128 + u * 64, 64, 1)
-    row_data, late_payload = lax.optimization_barrier((row_data, payload))
-    pair_hidden = core_swap(late_payload)[:SEG]
     row_data = jnp.stack([row_data, core_swap(row_data)])
     row_codes, gold, vocab, weight = (row_data[:, i] for i in range(4))
 
     key_own = jnp.where(core == 0, payload, key_one)
-    key_own, key_two = lax.optimization_barrier((key_own, key_two))
     keys = [
         jnp.concatenate([key_one[:SEG], key_two[:SEG]], axis=0),
         jnp.concatenate([key_own[:SEG], key_two[:SEG]], axis=0),
@@ -159,18 +153,19 @@
 
     both_hidden = jnp.concatenate([hidden, pair_hidden], axis=0)
     flat = slopes.reshape(2 * SEG, 2 * SEG)
-    pair_one = key_grad(slopes[1, :, :SEG], pair_hidden)
-    grad_one = key_grad(slopes[0, :, :SEG], hidden) + jnp.where(core == 1, pair_one, 0.0)
-    grad_one, flat = lax.optimization_barrier((grad_one.astype(BF), flat))
-    home_one = dp_permute(grad_one, reverse(first_keys()))
     grad_two = key_grad(flat[:, SEG:], both_hidden).astype(BF)
     grad_two, flat = lax.optimization_barrier((grad_two, flat))
-    home_two = dp_permute(grad_two, reverse(second_keys()))
-    pair_grad = core_swap(jnp.dot(flat[SEG:], keys[1], preferred_element_type=F32).astype(BF))
+    home_two = dp_permute(grad_two, reverse(key_pairs()))
+    pair_one = key_grad(flat[SEG:, :SEG], pair_hidden)
+    grad_one = key_grad(flat[:SEG, :SEG], hidden) + jnp.where(core == 1, pair_one, 0.0)
+    grad_one, flat = lax.optimization_barrier((grad_one.astype(BF), flat))
+    home_one = dp_permute(grad_one, reverse(key_pairs()))
+    pair_grad = jnp.dot(flat[SEG:], keys[1], preferred_element_type=F32)
+    pair_grad = lax.optimization_barrier(pair_grad) + home_two.astype(F32)
+    pair_grad = core_swap(pair_grad.astype(BF))
     own_grad = jnp.dot(flat[:SEG], keys[0], preferred_element_type=F32)
     own_grad = lax.optimization_barrier(own_grad + jnp.where(core == 0, pair_one, 0.0))
     own_grad = lax.optimization_barrier(own_grad + home_one.astype(F32))
-    own_grad = lax.optimization_barrier(own_grad + home_two.astype(F32))
     return (own_grad + pair_grad.astype(F32)).astype(BF)
 
 

time: 205 us -> 208 us (1.015)
  the two profiles are of different devices: /device:TPU:194 before, /device:TPU:105 now
where the time goes in v12:
time: 208 us
  waiting for transfers between devices  113 us (54%)
  starting transfers between devices  78.8 us (38%)
  matrix products  7.87 us (4%)
  other arithmetic  5.49 us (3%)
    ppermute x7, waiting for transfers between devices, dp_permute(): return lax.ppermute(value, 'dp', pairs)  71 us
    ppermute x7, starting transfers between devices, dp_permute(): return lax.ppermute(value, 'dp', pairs)  35 us
    ppermute x8, waiting for transfers between devices, triple_shift(): return lax.ppermute(value, 'tensor', pairs)  34.2 us
    ppermute x8, starting transfers between devices, triple_shift(): return lax.ppermute(value, 'tensor', pairs)  33.9 us
    ppermute x2, starting transfers between devices, triple_swap(): return lax.ppermute(value, 'tensor', [(r, (r + 3) % 6) for r in range(6)])  9.9 us
    ppermute x2, waiting for transfers between devices, triple_swap(): return lax.ppermute(value, 'tensor', [(r, (r + 3) % 6) for r in range(6)])  8.3 us
    dot_general x12, matrix products, partial_of(): lax.dot_general(queries, keys, (((1,), (1,)), ((), ())), preferred_elemen...  5.02 us
  transfers between devices with their start and end apart: 17, of which 14 were waited for; matrix products, arithmetic and copies ran while one was open for 2% of the time, Pallas kernels for 0%

profile of v12, /device:TPU:105, one launch (start us, length us, event | category | flops | bytes accessed | tf_op | source)
XLA Modules:
  0.0 207.8 jit_solution(17529735868429878169)
XLA Ops:
  0.8 1.1 pad_maximum_fusion.3
  1.9 2.7 %collective-permute-start.1 = (bf16[400,640]{1,0:T(8,128)(2,1)S(1)}, bf16[400,640]{1,0:T(8,128)(2,1)S(1)}, u32[]{:S(2)}, u32[]{:S(2)}) collective-permute-start(bf16[400,640]{1,0:T(8,128)(2,1)S(1)} %pad_maximum_fusion.3), channel_id=1, source_target_pairs={{0,6},{6,0},{12,18},{18,12},{24,30},{30,24},{36,42},{42,36},{48,54... | collective-permute-start | bytes 1536008 | tf_op jit(solution)/shard_map/ppermute | solution.py:15
  4.7 1.5 collective-permute-done.1
  6.2 1.1 pad_maximum_fusion.2
  7.2 13.9 %collective-permute-start.2 = (bf16[800,640]{1,0:T(8,128)(2,1)}, bf16[800,640]{1,0:T(8,128)(2,1)S(1)}, u32[]{:S(2)}, u32[]{:S(2)}) collective-permute-start(bf16[800,640]{1,0:T(8,128)(2,1)} %pad_maximum_fusion.2), channel_id=1, source_target_pairs={{0,24},{6,18},{12,36},{18,30},{24,48},{30,42},{36,60},{42,54},{48,... | collective-permute-start | bytes 3072008 | tf_op jit(solution)/shard_map/ppermute | solution.py:15
  21.4 1.9 collective-permute-start
  23.5 1.0 collective-permute-done
  24.5 43.1 %collective-permute-done.2 = bf16[800,640]{1,0:T(8,128)(2,1)S(1)} collective-permute-done((bf16[800,640]{1,0:T(8,128)(2,1)}, bf16[800,640]{1,0:T(8,128)(2,1)S(1)}, u32[]{:S(2)}, u32[]{:S(2)}) %collective-permute-start.2) | collective-permute-done | bytes 1024032 | tf_op jit(solution)/shard_map/ppermute | solution.py:15
  72.8 1.9 collective-permute-start.3
  74.7 3.4 %collective-permute-start.4 = (f32[2,64,768]{2,1,0:T(8,128)S(1)}, f32[2,64,768]{2,1,0:T(8,128)S(1)}, u32[]{:S(2)}, u32[]{:S(2)}) collective-permute-start(f32[2,64,768]{2,1,0:T(8,128)S(1)} %get-tuple-element.28), channel_id=1, source_target_pairs={{0,2},{1,0},{2,1},{3,5},{4,3},{5,4},{6,8},{7,6},{8,7},{9,11},{10,9... | collective-permute-start | bytes 1179656 | tf_op jit(solution)/shard_map/ppermute | solution.py:33
  78.6 7.3 %collective-permute-done.3 = f32[2,64,768]{2,1,0:T(8,128)S(1)} collective-permute-done((f32[2,64,768]{2,1,0:T(8,128)S(1)}, f32[2,64,768]{2,1,0:T(8,128)S(1)}, u32[]{:S(2)}, u32[]{:S(2)}) %collective-permute-start.3) | collective-permute-done | bytes 393248 | tf_op jit(solution)/shard_map/ppermute | solution.py:33
  85.8 9.2 %collective-permute-done.4 = f32[2,64,768]{2,1,0:T(8,128)S(1)} collective-permute-done((f32[2,64,768]{2,1,0:T(8,128)S(1)}, f32[2,64,768]{2,1,0:T(8,128)S(1)}, u32[]{:S(2)}, u32[]{:S(2)}) %collective-permute-start.4) | collective-permute-done | bytes 393248 | tf_op jit(solution)/shard_map/ppermute | solution.py:33
  95.1 4.3 %collective-permute-start.5 = (f32[2,64,768]{2,1,0:T(8,128)S(1)}, f32[2,64,768]{2,1,0:T(8,128)S(1)}, u32[]{:S(2)}, u32[]{:S(2)}) collective-permute-start(f32[2,64,768]{2,1,0:T(8,128)S(1)} %fusion.8), channel_id=1, source_target_pairs={{0,3},{1,4},{2,5},{3,0},{4,1},{5,2},{6,9},{7,10},{8,11},{9,6},{10,... | collective-permute-start | bytes 1179656 | tf_op jit(solution)/shard_map/ppermute | solution.py:37
  99.8 15.7 %collective-permute-start.6 = (f32[2,64,768]{2,1,0:T(8,128)S(1)}, f32[2,64,768]{2,1,0:T(8,128)S(1)}, u32[]{:S(2)}, u32[]{:S(2)}) collective-permute-start(f32[2,64,768]{2,1,0:T(8,128)S(1)} %pad_maximum_fusion.6), channel_id=1, source_target_pairs={{0,1},{1,2},{2,0},{3,4},{4,5},{5,3},{6,7},{7,8},{8,6},{9,10},{10,1... | collective-permute-start | bytes 1179656 | tf_op jit(solution)/shard_map/ppermute | solution.py:33
  115.6 1.9 collective-permute-start.7
  118.0 6.5 %collective-permute-done.6 = f32[2,64,768]{2,1,0:T(8,128)S(1)} collective-permute-done((f32[2,64,768]{2,1,0:T(8,128)S(1)}, f32[2,64,768]{2,1,0:T(8,128)S(1)}, u32[]{:S(2)}, u32[]{:S(2)}) %collective-permute-start.6) | collective-permute-done | bytes 393248 | tf_op jit(solution)/shard_map/ppermute | solution.py:33
  125.6 1.9 collective-permute-start.8
  127.6 1.1 collective-permute-done.8
  129.1 5.6 %collective-permute-start.9 = (bf16[2,64,768]{2,1,0:T(8,128)(2,1)S(1)}, bf16[2,64,768]{2,1,0:T(8,128)(2,1)S(1)}, u32[]{:S(2)}, u32[]{:S(2)}) collective-permute-start(bf16[2,64,768]{2,1,0:T(8,128)(2,1)S(1)} %get-tuple-element.44), channel_id=1, source_target_pairs={{0,3},{1,4},{2,5},{3,0},{4,1},{5,2},{6,9},{7,10},{8,11},{9,6},{10,... | collective-permute-start | bytes 589832 | tf_op jit(solution)/shard_map/ppermute | solution.py:37
  134.8 3.8 %collective-permute-start.10 = (bf16[2,64,768]{2,1,0:T(8,128)(2,1)S(1)}, bf16[2,64,768]{2,1,0:T(8,128)(2,1)S(1)}, u32[]{:S(2)}, u32[]{:S(2)}) collective-permute-start(bf16[2,64,768]{2,1,0:T(8,128)(2,1)S(1)} %get-tuple-element.44), channel_id=1, source_target_pairs={{0,1},{1,2},{2,0},{3,4},{4,5},{5,3},{6,7},{7,8},{8,6},{9,10},{10,1... | collective-permute-start | bytes 589832 | tf_op jit(solution)/shard_map/ppermute | solution.py:33
  138.6 1.9 collective-permute-start.11
  140.5 8.3 %collective-permute-done.9 = bf16[2,64,768]{2,1,0:T(8,128)(2,1)S(1)} collective-permute-done((bf16[2,64,768]{2,1,0:T(8,128)(2,1)S(1)}, bf16[2,64,768]{2,1,0:T(8,128)(2,1)S(1)}, u32[]{:S(2)}, u32[]{:S(2)}) %collective-permute-start.9) | collective-permute-done | bytes 196640 | tf_op jit(solution)/shard_map/ppermute | solution.py:37
  148.8 2.2 %collective-permute-done.10 = bf16[2,64,768]{2,1,0:T(8,128)(2,1)S(1)} collective-permute-done((bf16[2,64,768]{2,1,0:T(8,128)(2,1)S(1)}, bf16[2,64,768]{2,1,0:T(8,128)(2,1)S(1)}, u32[]{:S(2)}, u32[]{:S(2)}) %collective-permute-start.10) | collective-permute-done | bytes 196640 | tf_op jit(solution)/shard_map/ppermute | solution.py:33
  151.0 2.5 %collective-permute-done.11 = bf16[2,64,768]{2,1,0:T(8,128)(2,1)S(1)} collective-permute-done((bf16[2,64,768]{2,1,0:T(8,128)(2,1)S(1)}, bf16[2,64,768]{2,1,0:T(8,128)(2,1)S(1)}, u32[]{:S(2)}, u32[]{:S(2)}) %collective-permute-start.11) | collective-permute-done | bytes 196640 | tf_op jit(solution)/shard_map/ppermute | solution.py:33
  153.5 1.9 collective-permute-start.13
  155.5 3.4 %collective-permute-start.12 = (bf16[2,64,768]{2,1,0:T(8,128)(2,1)S(1)}, bf16[2,64,768]{2,1,0:T(8,128)(2,1)S(1)}, u32[]{:S(2)}, u32[]{:S(2)}) collective-permute-start(bf16[2,64,768]{2,1,0:T(8,128)(2,1)S(1)} %broadcast_select_fusion), channel_id=1, source_target_pairs={{0,1},{1,2},{2,0},{3,4},{4,5},{5,3},{6,7},{7,8},{8,6},{9,10},{10,1... | collective-permute-start | bytes 589832 | tf_op jit(solution)/shard_map/ppermute | solution.py:33
  158.9 6.1 %collective-permute-done.12 = bf16[2,64,768]{2,1,0:T(8,128)(2,1)S(1)} collective-permute-done((bf16[2,64,768]{2,1,0:T(8,128)(2,1)S(1)}, bf16[2,64,768]{2,1,0:T(8,128)(2,1)S(1)}, u32[]{:S(2)}, u32[]{:S(2)}) %collective-permute-start.12) | collective-permute-done | bytes 196640 | tf_op jit(solution)/shard_map/ppermute | solution.py:33
  166.2 2.1 %collective-permute-start.15 = (bf16[384,640]{1,0:T(8,128)(2,1)S(1)}, bf16[384,640]{1,0:T(8,128)(2,1)S(1)}, u32[]{:S(2)}, u32[]{:S(2)}) collective-permute-start(bf16[384,640]{1,0:T(8,128)(2,1)S(1)} %convolution_convert_fusion), channel_id=1, source_target_pairs={{24,0},{18,6},{36,12},{30,18},{48,24},{42,30},{60,36},{54,42},{72,... | collective-permute-start | bytes 1474568 | tf_op jit(solution)/shard_map/ppermute | solution.py:15
  169.4 10.4 %collective-permute-start.14 = (bf16[384,640]{1,0:T(8,128)(2,1)S(1)}, bf16[384,640]{1,0:T(8,128)(2,1)S(1)}, u32[]{:S(2)}, u32[]{:S(2)}) collective-permute-start(bf16[384,640]{1,0:T(8,128)(2,1)S(1)} %fusion), channel_id=1, source_target_pairs={{24,0},{18,6},{36,12},{30,18},{48,24},{42,30},{60,36},{54,42},{72,... | collective-permute-start | bytes 1474568 | tf_op jit(solution)/shard_map/ppermute | solution.py:15
  179.9 6.1 %collective-permute-done.15 = bf16[384,640]{1,0:T(8,128)(2,1)S(1)} collective-permute-done((bf16[384,640]{1,0:T(8,128)(2,1)S(1)}, bf16[384,640]{1,0:T(8,128)(2,1)S(1)}, u32[]{:S(2)}, u32[]{:S(2)}) %collective-permute-start.15) | collective-permute-done | bytes 491552 | tf_op jit(solution)/shard_map/ppermute | solution.py:15
  186.0 1.9 collective-permute-start.16
  188.6 18.2 %collective-permute-done.14 = bf16[384,640]{1,0:T(8,128)(2,1)S(1)} collective-permute-done((bf16[384,640]{1,0:T(8,128)(2,1)S(1)}, bf16[384,640]{1,0:T(8,128)(2,1)S(1)}, u32[]{:S(2)}, u32[]{:S(2)}) %collective-permute-start.14) | collective-permute-done | bytes 491552 | tf_op jit(solution)/shard_map/ppermute | solution.py:15
  (96 shorter events, 13.1 us)
Async XLA Ops:
  0.0 6.2 %copy-start = (bf16[384,640]{1,0:T(8,128)(2,1)S(1)}, bf16[384,640]{1,0:T(8,128)(2,1)}, u32[]{:S(2)}) copy-start(bf16[384,640]{1,0:T(8,128)(2,1)} %param.6) | copy-start | bytes 1474564
  1.9 19.4 %copy-start.9 = (f32[384]{0:T(512)S(1)}, f32[384]{0:T(512)}, u32[]{:S(2)}) copy-start(f32[384]{0:T(512)} %param.9) | copy-start | bytes 4612
  1.9 19.4 %copy-start.10 = (f32[384]{0:T(512)S(1)}, f32[384]{0:T(512)}, u32[]{:S(2)}) copy-start(f32[384]{0:T(512)} %param.10) | copy-start | bytes 4612
  1.9 19.4 %copy-start.6 = (s32[384]{0:T(512)S(1)}, s32[384]{0:T(512)}, u32[]{:S(2)}) copy-start(s32[384]{0:T(512)} %param.8) | copy-start | bytes 4612
  1.9 19.4 %copy-start.8 = (f32[384]{0:T(512)S(1)}, f32[384]{0:T(512)}, u32[]{:S(2)}) copy-start(f32[384]{0:T(512)} %param.11) | copy-start | bytes 4612
  1.9 19.4 %copy-start.7 = (s32[384]{0:T(512)S(1)}, s32[384]{0:T(512)}, u32[]{:S(2)}) copy-start(s32[384]{0:T(512)} %param.7) | copy-start | bytes 4612
  1.9 4.2 %collective-permute-start.1 = (bf16[400,640]{1,0:T(8,128)(2,1)S(1)}, bf16[400,640]{1,0:T(8,128)(2,1)S(1)}, u32[]{:S(2)}, u32[]{:S(2)}) collective-permute-start(bf16[400,640]{1,0:T(8,128)(2,1)S(1)} %pad_maximum_fusion.3), channel_id=1, source_target_pairs={{0,6},{6,0},{12,18},{18,12},{24,30},{30,24},{36,42},{42,36},{48,54... | collective-permute-start | bytes 1536008 | tf_op jit(solution)/shard_map/ppermute | solution.py:15
  7.2 60.4 %collective-permute-start.2 = (bf16[800,640]{1,0:T(8,128)(2,1)}, bf16[800,640]{1,0:T(8,128)(2,1)S(1)}, u32[]{:S(2)}, u32[]{:S(2)}) collective-permute-start(bf16[800,640]{1,0:T(8,128)(2,1)} %pad_maximum_fusion.2), channel_id=1, source_target_pairs={{0,24},{6,18},{12,36},{18,30},{24,48},{30,42},{36,60},{42,54},{48,... | collective-permute-start | bytes 3072008 | tf_op jit(solution)/shard_map/ppermute | solution.py:15
  21.4 3.0 %collective-permute-start = (f32[4,64]{1,0:T(4,128)S(1)}, f32[4,64]{1,0:T(4,128)S(1)}, u32[]{:S(2)}, u32[]{:S(2)}) collective-permute-start(f32[4,64]{1,0:T(4,128)S(1)} %fusion.46), channel_id=1, source_target_pairs={{0,6},{6,0},{12,18},{18,12},{24,30},{30,24},{36,42},{42,36},{48,54... | collective-permute-start | bytes 3080 | tf_op jit(solution)/shard_map/ppermute | solution.py:15
  67.8 0.8 copy-start.1
  68.6 30.8 %copy-start.2 = (bf16[384,640]{1,0:T(8,128)(2,1)}, bf16[384,640]{1,0:T(8,128)(2,1)S(1)}, u32[]{:S(2)}) copy-start(bf16[384,640]{1,0:T(8,128)(2,1)S(1)} %get-tuple-element.52) | copy-start | bytes 1474564
  68.6 48.9 %copy-start.4 = (bf16[384,640]{1,0:T(8,128)(2,1)}, bf16[384,640]{1,0:T(8,128)(2,1)S(1)}, u32[]{:S(2)}) copy-start(bf16[384,640]{1,0:T(8,128)(2,1)S(1)} %get-tuple-element.53) | copy-start | bytes 1474564
  71.6 0.7 slice-start
  72.8 13.1 %collective-permute-start.3 = (f32[2,64,768]{2,1,0:T(8,128)S(1)}, f32[2,64,768]{2,1,0:T(8,128)S(1)}, u32[]{:S(2)}, u32[]{:S(2)}) collective-permute-start(f32[2,64,768]{2,1,0:T(8,128)S(1)} %get-tuple-element.27), channel_id=1, source_target_pairs={{0,1},{1,2},{2,0},{3,4},{4,5},{5,3},{6,7},{7,8},{8,6},{9,10},{10,1... | collective-permute-start | bytes 1179656 | tf_op jit(solution)/shard_map/ppermute | solution.py:33
  74.7 20.3 %collective-permute-start.4 = (f32[2,64,768]{2,1,0:T(8,128)S(1)}, f32[2,64,768]{2,1,0:T(8,128)S(1)}, u32[]{:S(2)}, u32[]{:S(2)}) collective-permute-start(f32[2,64,768]{2,1,0:T(8,128)S(1)} %get-tuple-element.28), channel_id=1, source_target_pairs={{0,2},{1,0},{2,1},{3,5},{4,3},{5,4},{6,8},{7,6},{8,7},{9,11},{10,9... | collective-permute-start | bytes 1179656 | tf_op jit(solution)/shard_map/ppermute | solution.py:33
  95.1 22.9 %collective-permute-start.5 = (f32[2,64,768]{2,1,0:T(8,128)S(1)}, f32[2,64,768]{2,1,0:T(8,128)S(1)}, u32[]{:S(2)}, u32[]{:S(2)}) collective-permute-start(f32[2,64,768]{2,1,0:T(8,128)S(1)} %fusion.8), channel_id=1, source_target_pairs={{0,3},{1,4},{2,5},{3,0},{4,1},{5,2},{6,9},{7,10},{8,11},{9,6},{10,... | collective-permute-start | bytes 1179656 | tf_op jit(solution)/shard_map/ppermute | solution.py:37
  99.8 24.6 %collective-permute-start.6 = (f32[2,64,768]{2,1,0:T(8,128)S(1)}, f32[2,64,768]{2,1,0:T(8,128)S(1)}, u32[]{:S(2)}, u32[]{:S(2)}) collective-permute-start(f32[2,64,768]{2,1,0:T(8,128)S(1)} %pad_maximum_fusion.6), channel_id=1, source_target_pairs={{0,1},{1,2},{2,0},{3,4},{4,5},{5,3},{6,7},{7,8},{8,6},{9,10},{10,1... | collective-permute-start | bytes 1179656 | tf_op jit(solution)/shard_map/ppermute | solution.py:33
  115.6 9.4 %collective-permute-start.7 = (f32[2,64,768]{2,1,0:T(8,128)S(1)}, f32[2,64,768]{2,1,0:T(8,128)S(1)}, u32[]{:S(2)}, u32[]{:S(2)}) collective-permute-start(f32[2,64,768]{2,1,0:T(8,128)S(1)} %pad_maximum_fusion.7), channel_id=1, source_target_pairs={{0,2},{1,0},{2,1},{3,5},{4,3},{5,4},{6,8},{7,6},{8,7},{9,11},{10,9... | collective-permute-start | bytes 1179656 | tf_op jit(solution)/shard_map/ppermute | solution.py:33
  125.6 3.1 %collective-permute-start.8 = (f32[2,4,64]{2,0,1:T(2,128)S(1)}, f32[2,4,64]{2,0,1:T(2,128)S(1)}, u32[]{:S(2)}, u32[]{:S(2)}) collective-permute-start(f32[2,4,64]{2,0,1:T(2,128)S(1)} %pad_maximum_fusion.11), channel_id=1, source_target_pairs={{0,6},{6,0},{12,18},{18,12},{24,30},{30,24},{36,42},{42,36},{48,54... | collective-permute-start | bytes 6152 | tf_op jit(solution)/shard_map/ppermute | solution.py:15
  129.1 19.7 %collective-permute-start.9 = (bf16[2,64,768]{2,1,0:T(8,128)(2,1)S(1)}, bf16[2,64,768]{2,1,0:T(8,128)(2,1)S(1)}, u32[]{:S(2)}, u32[]{:S(2)}) collective-permute-start(bf16[2,64,768]{2,1,0:T(8,128)(2,1)S(1)} %get-tuple-element.44), channel_id=1, source_target_pairs={{0,3},{1,4},{2,5},{3,0},{4,1},{5,2},{6,9},{7,10},{8,11},{9,6},{10,... | collective-permute-start | bytes 589832 | tf_op jit(solution)/shard_map/ppermute | solution.py:37
  134.8 16.3 %collective-permute-start.10 = (bf16[2,64,768]{2,1,0:T(8,128)(2,1)S(1)}, bf16[2,64,768]{2,1,0:T(8,128)(2,1)S(1)}, u32[]{:S(2)}, u32[]{:S(2)}) collective-permute-start(bf16[2,64,768]{2,1,0:T(8,128)(2,1)S(1)} %get-tuple-element.44), channel_id=1, source_target_pairs={{0,1},{1,2},{2,0},{3,4},{4,5},{5,3},{6,7},{7,8},{8,6},{9,10},{10,1... | collective-permute-start | bytes 589832 | tf_op jit(solution)/shard_map/ppermute | solution.py:33
  138.6 15.0 %collective-permute-start.11 = (bf16[2,64,768]{2,1,0:T(8,128)(2,1)S(1)}, bf16[2,64,768]{2,1,0:T(8,128)(2,1)S(1)}, u32[]{:S(2)}, u32[]{:S(2)}) collective-permute-start(bf16[2,64,768]{2,1,0:T(8,128)(2,1)S(1)} %get-tuple-element.44), channel_id=1, source_target_pairs={{0,2},{1,0},{2,1},{3,5},{4,3},{5,4},{6,8},{7,6},{8,7},{9,11},{10,9... | collective-permute-start | bytes 589832 | tf_op jit(solution)/shard_map/ppermute | solution.py:33
  153.5 11.4 %collective-permute-start.13 = (bf16[2,64,768]{2,1,0:T(8,128)(2,1)S(1)}, bf16[2,64,768]{2,1,0:T(8,128)(2,1)S(1)}, u32[]{:S(2)}, u32[]{:S(2)}) collective-permute-start(bf16[2,64,768]{2,1,0:T(8,128)(2,1)S(1)} %broadcast_select_fusion), channel_id=1, source_target_pairs={{0,2},{1,0},{2,1},{3,5},{4,3},{5,4},{6,8},{7,6},{8,7},{9,11},{10,9... | collective-permute-start | bytes 589832 | tf_op jit(solution)/shard_map/ppermute | solution.py:33
  155.5 9.5 %collective-permute-start.12 = (bf16[2,64,768]{2,1,0:T(8,128)(2,1)S(1)}, bf16[2,64,768]{2,1,0:T(8,128)(2,1)S(1)}, u32[]{:S(2)}, u32[]{:S(2)}) collective-permute-start(bf16[2,64,768]{2,1,0:T(8,128)(2,1)S(1)} %broadcast_select_fusion), channel_id=1, source_target_pairs={{0,1},{1,2},{2,0},{3,4},{4,5},{5,3},{6,7},{7,8},{8,6},{9,10},{10,1... | collective-permute-start | bytes 589832 | tf_op jit(solution)/shard_map/ppermute | solution.py:33
  166.2 2.6 %copy-start.5 = (bf16[384,640]{1,0:T(8,128)(2,1)S(1)}, bf16[384,640]{1,0:T(8,128)(2,1)}, u32[]{:S(2)}) copy-start(bf16[384,640]{1,0:T(8,128)(2,1)} %copy-done.4) | copy-start | bytes 1474564
  166.2 19.8 %collective-permute-start.15 = (bf16[384,640]{1,0:T(8,128)(2,1)S(1)}, bf16[384,640]{1,0:T(8,128)(2,1)S(1)}, u32[]{:S(2)}, u32[]{:S(2)}) collective-permute-start(bf16[384,640]{1,0:T(8,128)(2,1)S(1)} %convolution_convert_fusion), channel_id=1, source_target_pairs={{24,0},{18,6},{36,12},{30,18},{48,24},{42,30},{60,36},{54,42},{72,... | collective-permute-start | bytes 1474568 | tf_op jit(solution)/shard_map/ppermute | solution.py:15
  169.4 18.5 %copy-start.3 = (bf16[384,640]{1,0:T(8,128)(2,1)S(1)}, bf16[384,640]{1,0:T(8,128)(2,1)}, u32[]{:S(2)}) copy-start(bf16[384,640]{1,0:T(8,128)(2,1)} %copy-done.2) | copy-start | bytes 1474564
  169.4 37.4 %collective-permute-start.14 = (bf16[384,640]{1,0:T(8,128)(2,1)S(1)}, bf16[384,640]{1,0:T(8,128)(2,1)S(1)}, u32[]{:S(2)}, u32[]{:S(2)}) collective-permute-start(bf16[384,640]{1,0:T(8,128)(2,1)S(1)} %fusion), channel_id=1, source_target_pairs={{24,0},{18,6},{36,12},{30,18},{48,24},{42,30},{60,36},{54,42},{72,... | collective-permute-start | bytes 1474568 | tf_op jit(solution)/shard_map/ppermute | solution.py:15
  186.0 20.8 %collective-permute-start.16 = (bf16[384,640]{1,0:T(8,128)(2,1)S(1)}, bf16[384,640]{1,0:T(8,128)(2,1)S(1)}, u32[]{:S(2)}, u32[]{:S(2)}) collective-permute-start(bf16[384,640]{1,0:T(8,128)(2,1)S(1)} %add_convert_fusion.1), channel_id=1, source_target_pairs={{0,6},{6,0},{12,18},{18,12},{24,30},{30,24},{36,42},{42,36},{48,54... | collective-permute-start | bytes 1474568 | tf_op jit(solution)/shard_map/ppermute | solution.py:15

commit v13 on v12

--- a/solution.py
+++ b/solution.py
@@ -22,6 +22,11 @@
 def key_pairs():
     count = lax.axis_size("dp")
     return [(i, (i + (4 if i % 2 == 0 else 2)) % count) for i in range(count)]
+
+
+def crossed_pairs():
+    count = lax.axis_size("dp")
+    return [(i, (i + 3) % count) for i in range(count)]
 
 
 def reverse(pairs):
@@ -93,17 +98,18 @@
     u, v = r // 3, r % 3
     payload = with_codes(hidden, targets, padding)
 
-    pair_payload = core_swap(payload)
-    pair_hidden = pair_payload[:SEG]
-    both = dp_permute(jnp.concatenate([payload, pair_payload], axis=0), key_pairs())
-    key_one, key_two = both[: SEG + 16], both[SEG + 16 :]
+    key_one = dp_permute(payload, key_pairs())
+    key_two = dp_permute(payload, crossed_pairs())
     weight = cotangent * padding.astype(F32)
     row_data = jnp.stack([targets.astype(F32) + 1.0, gold_logit, vocab_lse, weight])
     row_data = rows_of(row_data, v * 128 + u * 64, 64, 1)
+    row_data, late_payload = lax.optimization_barrier((row_data, payload))
+    pair_hidden = core_swap(late_payload)[:SEG]
     row_data = jnp.stack([row_data, core_swap(row_data)])
     row_codes, gold, vocab, weight = (row_data[:, i] for i in range(4))
 
     key_own = jnp.where(core == 0, payload, key_one)
+    key_own, key_two = lax.optimization_barrier((key_own, key_two))
     keys = [
         jnp.concatenate([key_one[:SEG], key_two[:SEG]], axis=0),
         jnp.concatenate([key_own[:SEG], key_two[:SEG]], axis=0),

time: 208 us -> 203 us (0.976)
  the two profiles are of different devices: /device:TPU:105 before, /device:TPU:1 now
where the time goes in v13:
time: 203 us; the launch traced here: 202 us
  starting transfers between devices  110 us (54%)
  waiting for transfers between devices  73.7 us (36%)
  matrix products  7.86 us (4%)
  other arithmetic  5.82 us (3%)
  local copies, waits for them, and re-layouts  3.87 us (2%)
    ppermute x8, starting transfers between devices, triple_shift(): return lax.ppermute(value, 'tensor', pairs)  50.6 us
    ppermute x8, starting transfers between devices, dp_permute(): return lax.ppermute(value, 'dp', pairs)  45.2 us
    ppermute x8, waiting for transfers between devices, triple_shift(): return lax.ppermute(value, 'tensor', pairs)  30.8 us
    ppermute x8, waiting for transfers between devices, dp_permute(): return lax.ppermute(value, 'dp', pairs)  30.6 us
    ppermute x2, starting transfers between devices, triple_swap(): return lax.ppermute(value, 'tensor', [(r, (r + 3) % 6) for r in range(6)])  13.8 us
    ppermute x2, waiting for transfers between devices, triple_swap(): return lax.ppermute(value, 'tensor', [(r, (r + 3) % 6) for r in range(6)])  12.4 us
    dot_general x12, matrix products, partial_of(): lax.dot_general(queries, keys, (((1,), (1,)), ((), ())), preferred_elemen...  5.01 us
  transfers between devices with their start and end apart: 18, of which 11 were waited for; matrix products, arithmetic and copies ran while one was open for 4% of the time, Pallas kernels for 0%

profile of v13, /device:TPU:1, one launch (start us, length us, event | category | flops | bytes accessed | tf_op | source)
XLA Modules:
  0.0 201.7 jit_solution(13602748427506539318)
XLA Ops:
  0.8 1.1 pad_maximum_fusion.2
  1.9 4.5 %collective-permute-start.2 = (bf16[400,640]{1,0:T(8,128)(2,1)S(1)}, bf16[400,640]{1,0:T(8,128)(2,1)S(1)}, u32[]{:S(2)}, u32[]{:S(2)}) collective-permute-start(bf16[400,640]{1,0:T(8,128)(2,1)S(1)} %pad_maximum_fusion.2), channel_id=1, source_target_pairs={{0,18},{6,24},{12,30},{18,36},{24,42},{30,48},{36,54},{42,60},{48,... | collective-permute-start | bytes 1536008 | tf_op jit(solution)/shard_map/ppermute | solution.py:15
  6.4 14.9 %collective-permute-start.1 = (bf16[400,640]{1,0:T(8,128)(2,1)S(1)}, bf16[400,640]{1,0:T(8,128)(2,1)S(1)}, u32[]{:S(2)}, u32[]{:S(2)}) collective-permute-start(bf16[400,640]{1,0:T(8,128)(2,1)S(1)} %pad_maximum_fusion.2), channel_id=1, source_target_pairs={{0,24},{6,18},{12,36},{18,30},{24,48},{30,42},{36,60},{42,54},{48,... | collective-permute-start | bytes 1536008 | tf_op jit(solution)/shard_map/ppermute | solution.py:15
  24.1 2.0 collective-permute-start
  26.1 2.3 %collective-permute-start.3 = (bf16[400,640]{1,0:T(8,128)(2,1)S(1)}, bf16[400,640]{1,0:T(8,128)(2,1)}, u32[]{:S(2)}, u32[]{:S(2)}) collective-permute-start(bf16[400,640]{1,0:T(8,128)(2,1)S(1)} %pad_maximum_fusion.2), channel_id=1, source_target_pairs={{0,6},{6,0},{12,18},{18,12},{24,30},{30,24},{36,42},{42,36},{48,54... | collective-permute-start | bytes 1536008 | tf_op jit(solution)/shard_map/ppermute | solution.py:15
  28.6 7.8 %collective-permute-done.1 = bf16[400,640]{1,0:T(8,128)(2,1)S(1)} collective-permute-done((bf16[400,640]{1,0:T(8,128)(2,1)S(1)}, bf16[400,640]{1,0:T(8,128)(2,1)S(1)}, u32[]{:S(2)}, u32[]{:S(2)}) %collective-permute-start.1) | collective-permute-done | bytes 512032 | tf_op jit(solution)/shard_map/ppermute | solution.py:15
  38.3 1.1 slice.138
  42.7 24.4 %collective-permute-start.4 = (f32[2,64,768]{2,1,0:T(8,128)S(1)}, f32[2,64,768]{2,1,0:T(8,128)S(1)}, u32[]{:S(2)}, u32[]{:S(2)}) collective-permute-start(f32[2,64,768]{2,1,0:T(8,128)S(1)} %get-tuple-element.35), channel_id=1, source_target_pairs={{0,1},{1,2},{2,0},{3,4},{4,5},{5,3},{6,7},{7,8},{8,6},{9,10},{10,1... | collective-permute-start | bytes 1179656 | tf_op jit(solution)/shard_map/ppermute | solution.py:38
  67.1 1.9 collective-permute-start.5
  69.5 2.3 %collective-permute-done.4 = f32[2,64,768]{2,1,0:T(8,128)S(1)} collective-permute-done((f32[2,64,768]{2,1,0:T(8,128)S(1)}, f32[2,64,768]{2,1,0:T(8,128)S(1)}, u32[]{:S(2)}, u32[]{:S(2)}) %collective-permute-start.4) | collective-permute-done | bytes 393248 | tf_op jit(solution)/shard_map/ppermute | solution.py:38
  71.8 4.2 %collective-permute-done.5 = f32[2,64,768]{2,1,0:T(8,128)S(1)} collective-permute-done((f32[2,64,768]{2,1,0:T(8,128)S(1)}, f32[2,64,768]{2,1,0:T(8,128)S(1)}, u32[]{:S(2)}, u32[]{:S(2)}) %collective-permute-start.5) | collective-permute-done | bytes 393248 | tf_op jit(solution)/shard_map/ppermute | solution.py:38
  76.1 8.3 %collective-permute-start.6 = (f32[2,64,768]{2,1,0:T(8,128)S(1)}, f32[2,64,768]{2,1,0:T(8,128)S(1)}, u32[]{:S(2)}, u32[]{:S(2)}) collective-permute-start(f32[2,64,768]{2,1,0:T(8,128)S(1)} %fusion.8), channel_id=1, source_target_pairs={{0,3},{1,4},{2,5},{3,0},{4,1},{5,2},{6,9},{7,10},{8,11},{9,6},{10,... | collective-permute-start | bytes 1179656 | tf_op jit(solution)/shard_map/ppermute | solution.py:42
  84.9 1.9 collective-permute-start.7
  86.9 5.9 %collective-permute-start.8 = (f32[2,64,768]{2,1,0:T(8,128)S(1)}, f32[2,64,768]{2,1,0:T(8,128)S(1)}, u32[]{:S(2)}, u32[]{:S(2)}) collective-permute-start(f32[2,64,768]{2,1,0:T(8,128)S(1)} %pad_maximum_fusion.6), channel_id=1, source_target_pairs={{0,2},{1,0},{2,1},{3,5},{4,3},{5,4},{6,8},{7,6},{8,7},{9,11},{10,9... | collective-permute-start | bytes 1179656 | tf_op jit(solution)/shard_map/ppermute | solution.py:38
  93.2 12.3 %collective-permute-done.6 = f32[2,64,768]{2,1,0:T(8,128)S(1)} collective-permute-done((f32[2,64,768]{2,1,0:T(8,128)S(1)}, f32[2,64,768]{2,1,0:T(8,128)S(1)}, u32[]{:S(2)}, u32[]{:S(2)}) %collective-permute-start.6) | collective-permute-done | bytes 393248 | tf_op jit(solution)/shard_map/ppermute | solution.py:42
  105.6 8.0 %collective-permute-done.7 = f32[2,64,768]{2,1,0:T(8,128)S(1)} collective-permute-done((f32[2,64,768]{2,1,0:T(8,128)S(1)}, f32[2,64,768]{2,1,0:T(8,128)S(1)}, u32[]{:S(2)}, u32[]{:S(2)}) %collective-permute-start.7) | collective-permute-done | bytes 393248 | tf_op jit(solution)/shard_map/ppermute | solution.py:38
  113.7 0.9 collective-permute-done.8
  115.2 2.3 %collective-permute-start.9 = (f32[2,4,64]{2,0,1:T(2,128)S(1)}, f32[2,4,64]{2,0,1:T(2,128)S(1)}, u32[]{:S(2)}, u32[]{:S(2)}) collective-permute-start(f32[2,4,64]{2,0,1:T(2,128)S(1)} %pad_maximum_fusion.10), channel_id=1, source_target_pairs={{0,6},{6,0},{12,18},{18,12},{24,30},{30,24},{36,42},{42,36},{48,54... | collective-permute-start | bytes 6152 | tf_op jit(solution)/shard_map/ppermute | solution.py:15
  117.5 0.8 collective-permute-done.9
  118.7 5.5 %collective-permute-start.10 = (bf16[2,64,768]{2,1,0:T(8,128)(2,1)S(1)}, bf16[2,64,768]{2,1,0:T(8,128)(2,1)S(1)}, u32[]{:S(2)}, u32[]{:S(2)}) collective-permute-start(bf16[2,64,768]{2,1,0:T(8,128)(2,1)S(1)} %get-tuple-element.52), channel_id=1, source_target_pairs={{0,3},{1,4},{2,5},{3,0},{4,1},{5,2},{6,9},{7,10},{8,11},{9,6},{10,... | collective-permute-start | bytes 589832 | tf_op jit(solution)/shard_map/ppermute | solution.py:42
  124.2 4.5 %collective-permute-start.11 = (bf16[2,64,768]{2,1,0:T(8,128)(2,1)S(1)}, bf16[2,64,768]{2,1,0:T(8,128)(2,1)S(1)}, u32[]{:S(2)}, u32[]{:S(2)}) collective-permute-start(bf16[2,64,768]{2,1,0:T(8,128)(2,1)S(1)} %get-tuple-element.52), channel_id=1, source_target_pairs={{0,1},{1,2},{2,0},{3,4},{4,5},{5,3},{6,7},{7,8},{8,6},{9,10},{10,1... | collective-permute-start | bytes 589832 | tf_op jit(solution)/shard_map/ppermute | solution.py:38
  128.8 3.3 %collective-permute-start.12 = (bf16[2,64,768]{2,1,0:T(8,128)(2,1)S(1)}, bf16[2,64,768]{2,1,0:T(8,128)(2,1)S(1)}, u32[]{:S(2)}, u32[]{:S(2)}) collective-permute-start(bf16[2,64,768]{2,1,0:T(8,128)(2,1)S(1)} %get-tuple-element.52), channel_id=1, source_target_pairs={{0,2},{1,0},{2,1},{3,5},{4,3},{5,4},{6,8},{7,6},{8,7},{9,11},{10,9... | collective-permute-start | bytes 589832 | tf_op jit(solution)/shard_map/ppermute | solution.py:38
  132.2 3.0 %collective-permute-done.11 = bf16[2,64,768]{2,1,0:T(8,128)(2,1)S(1)} collective-permute-done((bf16[2,64,768]{2,1,0:T(8,128)(2,1)S(1)}, bf16[2,64,768]{2,1,0:T(8,128)(2,1)S(1)}, u32[]{:S(2)}, u32[]{:S(2)}) %collective-permute-start.11) | collective-permute-done | bytes 196640 | tf_op jit(solution)/shard_map/ppermute | solution.py:38
  135.2 4.7 %collective-permute-done.12 = bf16[2,64,768]{2,1,0:T(8,128)(2,1)S(1)} collective-permute-done((bf16[2,64,768]{2,1,0:T(8,128)(2,1)S(1)}, bf16[2,64,768]{2,1,0:T(8,128)(2,1)S(1)}, u32[]{:S(2)}, u32[]{:S(2)}) %collective-permute-start.12) | collective-permute-done | bytes 196640 | tf_op jit(solution)/shard_map/ppermute | solution.py:38
  139.8 6.7 %collective-permute-start.14 = (bf16[2,64,768]{2,1,0:T(8,128)(2,1)S(1)}, bf16[2,64,768]{2,1,0:T(8,128)(2,1)S(1)}, u32[]{:S(2)}, u32[]{:S(2)}) collective-permute-start(bf16[2,64,768]{2,1,0:T(8,128)(2,1)S(1)} %broadcast_select_fusion.1), channel_id=1, source_target_pairs={{0,2},{1,0},{2,1},{3,5},{4,3},{5,4},{6,8},{7,6},{8,7},{9,11},{10,9... | collective-permute-start | bytes 589832 | tf_op jit(solution)/shard_map/ppermute | solution.py:38
  146.6 1.9 collective-permute-start.13
  148.6 7.8 %collective-permute-done.13 = bf16[2,64,768]{2,1,0:T(8,128)(2,1)S(1)} collective-permute-done((bf16[2,64,768]{2,1,0:T(8,128)(2,1)S(1)}, bf16[2,64,768]{2,1,0:T(8,128)(2,1)S(1)}, u32[]{:S(2)}, u32[]{:S(2)}) %collective-permute-start.13) | collective-permute-done | bytes 196640 | tf_op jit(solution)/shard_map/ppermute | solution.py:38
  157.6 6.6 %collective-permute-start.16 = (bf16[384,640]{1,0:T(8,128)(2,1)S(1)}, bf16[384,640]{1,0:T(8,128)(2,1)S(1)}, u32[]{:S(2)}, u32[]{:S(2)}) collective-permute-start(bf16[384,640]{1,0:T(8,128)(2,1)S(1)} %convolution_convert_fusion), channel_id=1, source_target_pairs={{24,0},{18,6},{36,12},{30,18},{48,24},{42,30},{60,36},{54,42},{72,... | collective-permute-start | bytes 1474568 | tf_op jit(solution)/shard_map/ppermute | solution.py:15
  165.3 10.7 %collective-permute-start.15 = (bf16[384,640]{1,0:T(8,128)(2,1)S(1)}, bf16[384,640]{1,0:T(8,128)(2,1)S(1)}, u32[]{:S(2)}, u32[]{:S(2)}) collective-permute-start(bf16[384,640]{1,0:T(8,128)(2,1)S(1)} %fusion), channel_id=1, source_target_pairs={{24,0},{18,6},{36,12},{30,18},{48,24},{42,30},{60,36},{54,42},{72,... | collective-permute-start | bytes 1474568 | tf_op jit(solution)/shard_map/ppermute | solution.py:15
  176.1 1.9 collective-permute-start.17
  178.7 22.0 %collective-permute-done.15 = bf16[384,640]{1,0:T(8,128)(2,1)S(1)} collective-permute-done((bf16[384,640]{1,0:T(8,128)(2,1)S(1)}, bf16[384,640]{1,0:T(8,128)(2,1)S(1)}, u32[]{:S(2)}, u32[]{:S(2)}) %collective-permute-start.15) | collective-permute-done | bytes 491552 | tf_op jit(solution)/shard_map/ppermute | solution.py:15
  200.8 0.9 add_convert_fusion
  (92 shorter events, 14.5 us)
Async XLA Ops:
  0.0 36.3 %copy-start = (bf16[384,640]{1,0:T(8,128)(2,1)S(1)}, bf16[384,640]{1,0:T(8,128)(2,1)}, u32[]{:S(2)}) copy-start(bf16[384,640]{1,0:T(8,128)(2,1)} %param.6) | copy-start | bytes 1474564
  1.9 34.6 %collective-permute-start.2 = (bf16[400,640]{1,0:T(8,128)(2,1)S(1)}, bf16[400,640]{1,0:T(8,128)(2,1)S(1)}, u32[]{:S(2)}, u32[]{:S(2)}) collective-permute-start(bf16[400,640]{1,0:T(8,128)(2,1)S(1)} %pad_maximum_fusion.2), channel_id=1, source_target_pairs={{0,18},{6,24},{12,30},{18,36},{24,42},{30,48},{36,54},{42,60},{48,... | collective-permute-start | bytes 1536008 | tf_op jit(solution)/shard_map/ppermute | solution.py:15
  6.4 29.9 %collective-permute-start.1 = (bf16[400,640]{1,0:T(8,128)(2,1)S(1)}, bf16[400,640]{1,0:T(8,128)(2,1)S(1)}, u32[]{:S(2)}, u32[]{:S(2)}) collective-permute-start(bf16[400,640]{1,0:T(8,128)(2,1)S(1)} %pad_maximum_fusion.2), channel_id=1, source_target_pairs={{0,24},{6,18},{12,36},{18,30},{24,48},{30,42},{36,60},{42,54},{48,... | collective-permute-start | bytes 1536008 | tf_op jit(solution)/shard_map/ppermute | solution.py:15
  24.1 4.4 %collective-permute-start = (f32[4,64]{1,0:T(4,128)S(1)}, f32[4,64]{1,0:T(4,128)S(1)}, u32[]{:S(2)}, u32[]{:S(2)}) collective-permute-start(f32[4,64]{1,0:T(4,128)S(1)} %fusion.46), channel_id=1, source_target_pairs={{0,6},{6,0},{12,18},{18,12},{24,30},{30,24},{36,42},{42,36},{48,54... | collective-permute-start | bytes 3080 | tf_op jit(solution)/shard_map/ppermute | solution.py:15
  26.1 12.2 %collective-permute-start.3 = (bf16[400,640]{1,0:T(8,128)(2,1)S(1)}, bf16[400,640]{1,0:T(8,128)(2,1)}, u32[]{:S(2)}, u32[]{:S(2)}) collective-permute-start(bf16[400,640]{1,0:T(8,128)(2,1)S(1)} %pad_maximum_fusion.2), channel_id=1, source_target_pairs={{0,6},{6,0},{12,18},{18,12},{24,30},{30,24},{36,42},{42,36},{48,54... | collective-permute-start | bytes 1536008 | tf_op jit(solution)/shard_map/ppermute | solution.py:15
  36.5 0.8 copy-start.1
  36.5 1.0 copy-start.2
  36.6 56.2 %copy-start.5 = (bf16[384,640]{1,0:T(8,128)(2,1)}, bf16[384,640]{1,0:T(8,128)(2,1)S(1)}, u32[]{:S(2)}) copy-start(bf16[384,640]{1,0:T(8,128)(2,1)S(1)} %slice.110) | copy-start | bytes 1474564
  37.4 47.0 %copy-start.3 = (bf16[384,640]{1,0:T(8,128)(2,1)}, bf16[384,640]{1,0:T(8,128)(2,1)S(1)}, u32[]{:S(2)}) copy-start(bf16[384,640]{1,0:T(8,128)(2,1)S(1)} %slice.137) | copy-start | bytes 1474564
  41.5 0.7 slice-start.1
  41.5 0.8 slice-start
  42.7 29.1 %collective-permute-start.4 = (f32[2,64,768]{2,1,0:T(8,128)S(1)}, f32[2,64,768]{2,1,0:T(8,128)S(1)}, u32[]{:S(2)}, u32[]{:S(2)}) collective-permute-start(f32[2,64,768]{2,1,0:T(8,128)S(1)} %get-tuple-element.35), channel_id=1, source_target_pairs={{0,1},{1,2},{2,0},{3,4},{4,5},{5,3},{6,7},{7,8},{8,6},{9,10},{10,1... | collective-permute-start | bytes 1179656 | tf_op jit(solution)/shard_map/ppermute | solution.py:38
  67.1 8.9 %collective-permute-start.5 = (f32[2,64,768]{2,1,0:T(8,128)S(1)}, f32[2,64,768]{2,1,0:T(8,128)S(1)}, u32[]{:S(2)}, u32[]{:S(2)}) collective-permute-start(f32[2,64,768]{2,1,0:T(8,128)S(1)} %get-tuple-element.36), channel_id=1, source_target_pairs={{0,2},{1,0},{2,1},{3,5},{4,3},{5,4},{6,8},{7,6},{8,7},{9,11},{10,9... | collective-permute-start | bytes 1179656 | tf_op jit(solution)/shard_map/ppermute | solution.py:38
  76.1 29.5 %collective-permute-start.6 = (f32[2,64,768]{2,1,0:T(8,128)S(1)}, f32[2,64,768]{2,1,0:T(8,128)S(1)}, u32[]{:S(2)}, u32[]{:S(2)}) collective-permute-start(f32[2,64,768]{2,1,0:T(8,128)S(1)} %fusion.8), channel_id=1, source_target_pairs={{0,3},{1,4},{2,5},{3,0},{4,1},{5,2},{6,9},{7,10},{8,11},{9,6},{10,... | collective-permute-start | bytes 1179656 | tf_op jit(solution)/shard_map/ppermute | solution.py:42
  84.9 28.7 %collective-permute-start.7 = (f32[2,64,768]{2,1,0:T(8,128)S(1)}, f32[2,64,768]{2,1,0:T(8,128)S(1)}, u32[]{:S(2)}, u32[]{:S(2)}) collective-permute-start(f32[2,64,768]{2,1,0:T(8,128)S(1)} %pad_maximum_fusion.5), channel_id=1, source_target_pairs={{0,1},{1,2},{2,0},{3,4},{4,5},{5,3},{6,7},{7,8},{8,6},{9,10},{10,1... | collective-permute-start | bytes 1179656 | tf_op jit(solution)/shard_map/ppermute | solution.py:38
  86.9 27.7 %collective-permute-start.8 = (f32[2,64,768]{2,1,0:T(8,128)S(1)}, f32[2,64,768]{2,1,0:T(8,128)S(1)}, u32[]{:S(2)}, u32[]{:S(2)}) collective-permute-start(f32[2,64,768]{2,1,0:T(8,128)S(1)} %pad_maximum_fusion.6), channel_id=1, source_target_pairs={{0,2},{1,0},{2,1},{3,5},{4,3},{5,4},{6,8},{7,6},{8,7},{9,11},{10,9... | collective-permute-start | bytes 1179656 | tf_op jit(solution)/shard_map/ppermute | solution.py:38
  115.2 3.1 %collective-permute-start.9 = (f32[2,4,64]{2,0,1:T(2,128)S(1)}, f32[2,4,64]{2,0,1:T(2,128)S(1)}, u32[]{:S(2)}, u32[]{:S(2)}) collective-permute-start(f32[2,4,64]{2,0,1:T(2,128)S(1)} %pad_maximum_fusion.10), channel_id=1, source_target_pairs={{0,6},{6,0},{12,18},{18,12},{24,30},{30,24},{36,42},{42,36},{48,54... | collective-permute-start | bytes 6152 | tf_op jit(solution)/shard_map/ppermute | solution.py:15
  118.7 13.4 %collective-permute-start.10 = (bf16[2,64,768]{2,1,0:T(8,128)(2,1)S(1)}, bf16[2,64,768]{2,1,0:T(8,128)(2,1)S(1)}, u32[]{:S(2)}, u32[]{:S(2)}) collective-permute-start(bf16[2,64,768]{2,1,0:T(8,128)(2,1)S(1)} %get-tuple-element.52), channel_id=1, source_target_pairs={{0,3},{1,4},{2,5},{3,0},{4,1},{5,2},{6,9},{7,10},{8,11},{9,6},{10,... | collective-permute-start | bytes 589832 | tf_op jit(solution)/shard_map/ppermute | solution.py:42
  124.2 10.9 %collective-permute-start.11 = (bf16[2,64,768]{2,1,0:T(8,128)(2,1)S(1)}, bf16[2,64,768]{2,1,0:T(8,128)(2,1)S(1)}, u32[]{:S(2)}, u32[]{:S(2)}) collective-permute-start(bf16[2,64,768]{2,1,0:T(8,128)(2,1)S(1)} %get-tuple-element.52), channel_id=1, source_target_pairs={{0,1},{1,2},{2,0},{3,4},{4,5},{5,3},{6,7},{7,8},{8,6},{9,10},{10,1... | collective-permute-start | bytes 589832 | tf_op jit(solution)/shard_map/ppermute | solution.py:38
  128.8 11.0 %collective-permute-start.12 = (bf16[2,64,768]{2,1,0:T(8,128)(2,1)S(1)}, bf16[2,64,768]{2,1,0:T(8,128)(2,1)S(1)}, u32[]{:S(2)}, u32[]{:S(2)}) collective-permute-start(bf16[2,64,768]{2,1,0:T(8,128)(2,1)S(1)} %get-tuple-element.52), channel_id=1, source_target_pairs={{0,2},{1,0},{2,1},{3,5},{4,3},{5,4},{6,8},{7,6},{8,7},{9,11},{10,9... | collective-permute-start | bytes 589832 | tf_op jit(solution)/shard_map/ppermute | solution.py:38
  139.8 16.5 %collective-permute-start.14 = (bf16[2,64,768]{2,1,0:T(8,128)(2,1)S(1)}, bf16[2,64,768]{2,1,0:T(8,128)(2,1)S(1)}, u32[]{:S(2)}, u32[]{:S(2)}) collective-permute-start(bf16[2,64,768]{2,1,0:T(8,128)(2,1)S(1)} %broadcast_select_fusion.1), channel_id=1, source_target_pairs={{0,2},{1,0},{2,1},{3,5},{4,3},{5,4},{6,8},{7,6},{8,7},{9,11},{10,9... | collective-permute-start | bytes 589832 | tf_op jit(solution)/shard_map/ppermute | solution.py:38
  146.6 9.8 %collective-permute-start.13 = (bf16[2,64,768]{2,1,0:T(8,128)(2,1)S(1)}, bf16[2,64,768]{2,1,0:T(8,128)(2,1)S(1)}, u32[]{:S(2)}, u32[]{:S(2)}) collective-permute-start(bf16[2,64,768]{2,1,0:T(8,128)(2,1)S(1)} %broadcast_select_fusion.1), channel_id=1, source_target_pairs={{0,1},{1,2},{2,0},{3,4},{4,5},{5,3},{6,7},{7,8},{8,6},{9,10},{10,1... | collective-permute-start | bytes 589832 | tf_op jit(solution)/shard_map/ppermute | solution.py:38
  157.6 7.1 %copy-start.6 = (bf16[384,640]{1,0:T(8,128)(2,1)S(1)}, bf16[384,640]{1,0:T(8,128)(2,1)}, u32[]{:S(2)}) copy-start(bf16[384,640]{1,0:T(8,128)(2,1)} %copy-done.5) | copy-start | bytes 1474564
  157.6 18.4 %collective-permute-start.16 = (bf16[384,640]{1,0:T(8,128)(2,1)S(1)}, bf16[384,640]{1,0:T(8,128)(2,1)S(1)}, u32[]{:S(2)}, u32[]{:S(2)}) collective-permute-start(bf16[384,640]{1,0:T(8,128)(2,1)S(1)} %convolution_convert_fusion), channel_id=1, source_target_pairs={{24,0},{18,6},{36,12},{30,18},{48,24},{42,30},{60,36},{54,42},{72,... | collective-permute-start | bytes 1474568 | tf_op jit(solution)/shard_map/ppermute | solution.py:15
  165.3 12.7 %copy-start.4 = (bf16[384,640]{1,0:T(8,128)(2,1)S(1)}, bf16[384,640]{1,0:T(8,128)(2,1)}, u32[]{:S(2)}) copy-start(bf16[384,640]{1,0:T(8,128)(2,1)} %copy-done.3) | copy-start | bytes 1474564
  165.3 35.4 %collective-permute-start.15 = (bf16[384,640]{1,0:T(8,128)(2,1)S(1)}, bf16[384,640]{1,0:T(8,128)(2,1)S(1)}, u32[]{:S(2)}, u32[]{:S(2)}) collective-permute-start(bf16[384,640]{1,0:T(8,128)(2,1)S(1)} %fusion), channel_id=1, source_target_pairs={{24,0},{18,6},{36,12},{30,18},{48,24},{42,30},{60,36},{54,42},{72,... | collective-permute-start | bytes 1474568 | tf_op jit(solution)/shard_map/ppermute | solution.py:15
  176.1 24.7 %collective-permute-start.17 = (bf16[384,640]{1,0:T(8,128)(2,1)S(1)}, bf16[384,640]{1,0:T(8,128)(2,1)S(1)}, u32[]{:S(2)}, u32[]{:S(2)}) collective-permute-start(bf16[384,640]{1,0:T(8,128)(2,1)S(1)} %add_convert_fusion.1), channel_id=1, source_target_pairs={{0,6},{6,0},{12,18},{18,12},{24,30},{30,24},{36,42},{42,36},{48,54... | collective-permute-start | bytes 1474568 | tf_op jit(solution)/shard_map/ppermute | solution.py:15

commit v14 on v13

--- a/solution.py
+++ b/solution.py
@@ -33,13 +33,34 @@
     return [(target, source) for source, target in pairs]
 
 
-def triple_shift(value, steps):
-    pairs = [(3 * u + v, 3 * u + (v + steps) % 3) for u in range(2) for v in range(3)]
-    return lax.ppermute(value, "tensor", pairs)
-
-
-def triple_swap(value):
-    return lax.ppermute(value, "tensor", [(r, (r + 3) % 6) for r in range(6)])
+def triple(steps):
+    return lambda r: 3 * (r // 3) + (r + steps) % 3
+
+
+def stride(steps):
+    return lambda r: (r + 2 * steps) % 6
+
+
+def across(r):
+    return (r + 3) % 6
+
+
+def beside(r):
+    return r + 1 - 2 * (r % 2)
+
+
+def line_permute(value, even_to, odd_to):
+    size = lax.axis_size("tensor")
+    pairs = [
+        (i * size + r, i * size + (odd_to if i % 2 else even_to)(r))
+        for i in range(lax.axis_size("dp"))
+        for r in range(size)
+    ]
+    return lax.ppermute(value, ("dp", "tensor"), pairs)
+
+
+def row_start(device):
+    return (device % 3) * 128 + (device // 3) * 64
 
 
 def rows_of(value, start, size, axis=0):
@@ -77,17 +98,26 @@
     return peak + jnp.log(jnp.exp(outside - peak) + total)
 
 
-def gathered(mine, u, v):
-    partner = triple_swap(mine)
-    own = (triple_shift(mine, 1), triple_shift(mine, 2))
-    partner = jnp.where(u + v < 6, partner, mine)
-    partner, *own = lax.optimization_barrier((partner,) + own)
-    passed = (triple_shift(partner, 1), triple_shift(partner, 2))
+def gathered(mine, core, r):
+    def owner(even, odd):
+        return jnp.where(core == 0, even(r), odd(r))
+
+    paired = line_permute(mine, beside, across)
+    one = line_permute(mine, stride(1), triple(1))
+    two = line_permute(mine, stride(2), triple(2))
+    passed_one = line_permute(jnp.where(core == 0, one, paired), beside, triple(1))
+    passed_two = line_permute(jnp.where(core == 0, two, paired), beside, triple(2))
+    pieces = (
+        (mine, r),
+        (paired, owner(beside, across)),
+        (one, owner(stride(2), triple(2))),
+        (two, owner(stride(1), triple(1))),
+        (passed_one, owner(lambda q: beside(stride(2)(q)), lambda q: across(triple(2)(q)))),
+        (passed_two, owner(lambda q: beside(stride(1)(q)), lambda q: across(triple(1)(q)))),
+    )
     full = jnp.zeros((2, SEG, mine.shape[2]), BF)
-    for half, pieces in ((u, (mine, *own)), (1 - u, (partner, *passed))):
-        for steps, piece in enumerate(pieces):
-            start = ((v + 3 - steps) % 3) * 128 + half * 64
-            full = lax.dynamic_update_slice_in_dim(full, piece, start, 1)
+    for piece, device in pieces:
+        full = lax.dynamic_update_slice_in_dim(full, piece, row_start(device), 1)
     return full
 
 
@@ -95,14 +125,13 @@
     score_scale = 1.0 / math.sqrt(KW)
     core = lax.axis_index("dp") % 2
     r = lax.axis_index("tensor")
-    u, v = r // 3, r % 3
     payload = with_codes(hidden, targets, padding)
 
     key_one = dp_permute(payload, key_pairs())
     key_two = dp_permute(payload, crossed_pairs())
     weight = cotangent * padding.astype(F32)
     row_data = jnp.stack([targets.astype(F32) + 1.0, gold_logit, vocab_lse, weight])
-    row_data = rows_of(row_data, v * 128 + u * 64, 64, 1)
+    row_data = rows_of(row_data, row_start(r), 64, 1)
     row_data, late_payload = lax.optimization_barrier((row_data, payload))
     pair_hidden = core_swap(late_payload)[:SEG]
     row_data = jnp.stack([row_data, core_swap(row_data)])
@@ -122,26 +151,38 @@
         ]
     )
 
-    def partial(queries, steps, half):
-        start = ((v + steps) % 3) * 128 + half * 64
-        parts = [partial_of(rows_of(q, start, 64), read) for q, read in zip(queries, keys)]
+    def owner(even, odd):
+        return jnp.where(core == 0, even(r), odd(r))
+
+    def partial(queries, device):
+        parts = [
+            partial_of(rows_of(q, row_start(device), 64), read) for q, read in zip(queries, keys)
+        ]
         return jnp.stack(parts)
 
-    read_rows = [rows_of(hidden, ((v + steps) % 3) * 128 + (1 - u) * 64, 64) for steps in (1, 2)]
-    own_sent = tuple(partial_of(rows, keys[0]) for rows in read_rows)
+    ahead = [
+        owner(lambda q: beside(stride(1)(q)), lambda q: across(triple(1)(q))),
+        owner(lambda q: beside(stride(2)(q)), lambda q: across(triple(2)(q))),
+    ]
+    own_sent = tuple(partial_of(rows_of(hidden, row_start(d), 64), keys[0]) for d in ahead)
     *own_sent, pair_hidden = lax.optimization_barrier(own_sent + (pair_hidden,))
     sent = tuple(
-        jnp.stack([mine, partial_of(rows_of(pair_hidden, start, 64), keys[1])])
-        for mine, start in zip(own_sent, [((v + steps) % 3) * 128 + (1 - u) * 64 for steps in (1, 2)])
+        jnp.stack([mine, partial_of(rows_of(pair_hidden, row_start(d), 64), keys[1])])
+        for mine, d in zip(own_sent, ahead)
     )
     *sent, own, pair = lax.optimization_barrier(sent + (hidden, pair_hidden))
     queries = (own, pair)
-    passing = partial(queries, 0, 1 - u) + triple_shift(sent[0], 1) + triple_shift(sent[1], 2)
-    late = tuple(partial(queries, steps, u) for steps in (1, 2))
-    passing, *late = lax.optimization_barrier((passing,) + late)
-    from_partner = triple_swap(passing)
-    scores = lax.optimization_barrier(partial(queries, 0, u) + from_partner)
-    scores = (scores + triple_shift(late[0], 1) + triple_shift(late[1], 2)) * score_scale
+    in_one = line_permute(sent[0], beside, triple(1))
+    in_two = line_permute(sent[1], beside, triple(2))
+    paired = partial(queries, owner(beside, across)) + jnp.where(core == 1, in_one + in_two, 0.0)
+    one = partial(queries, owner(stride(1), triple(1))) + jnp.where(core == 0, in_one, 0.0)
+    two = partial(queries, owner(stride(2), triple(2))) + jnp.where(core == 0, in_two, 0.0)
+    paired, one, two = lax.optimization_barrier((paired, one, two))
+    paired = line_permute(paired, beside, across)
+    scores = lax.optimization_barrier(partial(queries, r) + paired)
+    one = line_permute(one, stride(1), triple(1))
+    two = line_permute(two, stride(2), triple(2))
+    scores = (scores + one + two) * score_scale
 
     usable = jnp.broadcast_to((codes > 0.0)[:, None], scores.shape)
     matches = usable & (codes[:, None] == row_codes[:, :, None])
@@ -155,7 +196,7 @@
     spread = jnp.where(usable, jnp.exp(scores - total_lse[..., None]), 0.0) - jnp.where(
         matches, jnp.exp(scores - pos_lse[..., None]), 0.0
     )
-    slopes = gathered((weight[..., None] * spread * score_scale).astype(BF), u, v)
+    slopes = gathered((weight[..., None] * spread * score_scale).astype(BF), core, r)
 
     both_hidden = jnp.concatenate([hidden, pair_hidden], axis=0)
     flat = slopes.reshape(2 * SEG, 2 * SEG)

time: 203 us -> 201 us (level)
  the two profiles are of different devices: /device:TPU:1 before, /device:TPU:129 now
where the time goes in v14:
time: 201 us; the launch traced here: 200 us
  waiting for transfers between devices  98.6 us (49%)
  starting transfers between devices  83.8 us (42%)
  matrix products  7.86 us (4%)
  other arithmetic  5.85 us (3%)
  local copies, waits for them, and re-layouts  2.97 us (1%)
    ppermute x10, waiting for transfers between devices, line_permute(): return lax.ppermute(value, ('dp', 'tensor'), pairs)  54.4 us
    ppermute x8, waiting for transfers between devices, dp_permute(): return lax.ppermute(value, 'dp', pairs)  44.2 us
    ppermute x10, starting transfers between devices, line_permute(): return lax.ppermute(value, ('dp', 'tensor'), pairs)  43.6 us
    ppermute x8, starting transfers between devices, dp_permute(): return lax.ppermute(value, 'dp', pairs)  40.1 us
    dot_general x12, matrix products, partial_of(): lax.dot_general(queries, keys, (((1,), (1,)), ((), ())), preferred_elemen...  5 us
  transfers between devices with their start and end apart: 18, of which 14 were waited for; matrix products, arithmetic and copies ran while one was open for 4% of the time, Pallas kernels for 0%

profile of v14, /device:TPU:129, one launch (start us, length us, event | category | flops | bytes accessed | tf_op | source)
XLA Modules:
  0.0 199.8 jit_solution(8562606749882994944)
XLA Ops:
  0.8 1.1 pad_maximum_fusion.2
  1.9 3.7 %collective-permute-start.2 = (bf16[400,640]{1,0:T(8,128)(2,1)S(1)}, bf16[400,640]{1,0:T(8,128)(2,1)S(1)}, u32[]{:S(2)}, u32[]{:S(2)}) collective-permute-start(bf16[400,640]{1,0:T(8,128)(2,1)S(1)} %pad_maximum_fusion.2), channel_id=1, source_target_pairs={{0,18},{6,24},{12,30},{18,36},{24,42},{30,48},{36,54},{42,60},{48,... | collective-permute-start | bytes 1536008 | tf_op jit(solution)/shard_map/ppermute | solution.py:15
  5.6 12.5 %collective-permute-start.1 = (bf16[400,640]{1,0:T(8,128)(2,1)S(1)}, bf16[400,640]{1,0:T(8,128)(2,1)S(1)}, u32[]{:S(2)}, u32[]{:S(2)}) collective-permute-start(bf16[400,640]{1,0:T(8,128)(2,1)S(1)} %pad_maximum_fusion.2), channel_id=1, source_target_pairs={{0,24},{6,18},{12,36},{18,30},{24,48},{30,42},{36,60},{42,54},{48,... | collective-permute-start | bytes 1536008 | tf_op jit(solution)/shard_map/ppermute | solution.py:15
  20.9 2.0 %collective-permute-start = (f32[4,64]{1,0:T(4,128)S(1)}, f32[4,64]{1,0:T(4,128)S(1)}, u32[]{:S(2)}, u32[]{:S(2)}) collective-permute-start(f32[4,64]{1,0:T(4,128)S(1)} %fusion.45), channel_id=1, source_target_pairs={{0,6},{6,0},{12,18},{18,12},{24,30},{30,24},{36,42},{42,36},{48,54... | collective-permute-start | bytes 3080 | tf_op jit(solution)/shard_map/ppermute | solution.py:15
  22.9 2.3 %collective-permute-start.3 = (bf16[400,640]{1,0:T(8,128)(2,1)S(1)}, bf16[400,640]{1,0:T(8,128)(2,1)S(1)}, u32[]{:S(2)}, u32[]{:S(2)}) collective-permute-start(bf16[400,640]{1,0:T(8,128)(2,1)S(1)} %pad_maximum_fusion.2), channel_id=1, source_target_pairs={{0,6},{6,0},{12,18},{18,12},{24,30},{30,24},{36,42},{42,36},{48,54... | collective-permute-start | bytes 1536008 | tf_op jit(solution)/shard_map/ppermute | solution.py:15
  25.6 17.8 %collective-permute-done.1 = bf16[400,640]{1,0:T(8,128)(2,1)S(1)} collective-permute-done((bf16[400,640]{1,0:T(8,128)(2,1)S(1)}, bf16[400,640]{1,0:T(8,128)(2,1)S(1)}, u32[]{:S(2)}, u32[]{:S(2)}) %collective-permute-start.1) | collective-permute-done | bytes 512032 | tf_op jit(solution)/shard_map/ppermute | solution.py:15
  48.2 1.9 collective-permute-start.4
  50.1 13.8 %collective-permute-start.5 = (f32[2,64,768]{2,1,0:T(8,128)S(1)}, f32[2,64,768]{2,1,0:T(8,128)S(1)}, u32[]{:S(2)}, u32[]{:S(2)}) collective-permute-start(f32[2,64,768]{2,1,0:T(8,128)S(1)} %get-tuple-element.33), channel_id=1, source_target_pairs={{0,1},{1,0},{2,3},{3,2},{4,5},{5,4},{6,8},{7,6},{8,7},{9,11},{10,9... | collective-permute-start | bytes 1179656 | tf_op jit(solution)/shard_map/ppermute | solution.py:59
  65.1 2.3 %collective-permute-done.4 = f32[2,64,768]{2,1,0:T(8,128)S(1)} collective-permute-done((f32[2,64,768]{2,1,0:T(8,128)S(1)}, f32[2,64,768]{2,1,0:T(8,128)S(1)}, u32[]{:S(2)}, u32[]{:S(2)}) %collective-permute-start.4) | collective-permute-done | bytes 393248 | tf_op jit(solution)/shard_map/ppermute | solution.py:59
  67.4 7.6 %collective-permute-done.5 = f32[2,64,768]{2,1,0:T(8,128)S(1)} collective-permute-done((f32[2,64,768]{2,1,0:T(8,128)S(1)}, f32[2,64,768]{2,1,0:T(8,128)S(1)}, u32[]{:S(2)}, u32[]{:S(2)}) %collective-permute-start.5) | collective-permute-done | bytes 393248 | tf_op jit(solution)/shard_map/ppermute | solution.py:59
  75.1 4.5 %collective-permute-start.6 = (f32[2,64,768]{2,1,0:T(8,128)S(1)}, f32[2,64,768]{2,1,0:T(8,128)S(1)}, u32[]{:S(2)}, u32[]{:S(2)}) collective-permute-start(f32[2,64,768]{2,1,0:T(8,128)S(1)} %get-tuple-element.34), channel_id=1, source_target_pairs={{0,1},{1,0},{2,3},{3,2},{4,5},{5,4},{6,9},{7,10},{8,11},{9,6},{10,... | collective-permute-start | bytes 1179656 | tf_op jit(solution)/shard_map/ppermute | solution.py:59
  80.1 1.9 collective-permute-start.7
  82.0 3.6 %collective-permute-start.8 = (f32[2,64,768]{2,1,0:T(8,128)S(1)}, f32[2,64,768]{2,1,0:T(8,128)S(1)}, u32[]{:S(2)}, u32[]{:S(2)}) collective-permute-start(f32[2,64,768]{2,1,0:T(8,128)S(1)} %get-tuple-element.36), channel_id=1, source_target_pairs={{0,4},{1,5},{2,0},{3,1},{4,2},{5,3},{6,8},{7,6},{8,7},{9,11},{10,9... | collective-permute-start | bytes 1179656 | tf_op jit(solution)/shard_map/ppermute | solution.py:59
  86.1 19.6 %collective-permute-done.6 = f32[2,64,768]{2,1,0:T(8,128)S(1)} collective-permute-done((f32[2,64,768]{2,1,0:T(8,128)S(1)}, f32[2,64,768]{2,1,0:T(8,128)S(1)}, u32[]{:S(2)}, u32[]{:S(2)}) %collective-permute-start.6) | collective-permute-done | bytes 393248 | tf_op jit(solution)/shard_map/ppermute | solution.py:59
  105.8 1.9 collective-permute-done.7
  107.7 4.3 %collective-permute-done.8 = f32[2,64,768]{2,1,0:T(8,128)S(1)} collective-permute-done((f32[2,64,768]{2,1,0:T(8,128)S(1)}, f32[2,64,768]{2,1,0:T(8,128)S(1)}, u32[]{:S(2)}, u32[]{:S(2)}) %collective-permute-start.8) | collective-permute-done | bytes 393248 | tf_op jit(solution)/shard_map/ppermute | solution.py:59
  112.7 5.4 %collective-permute-start.9 = (f32[2,4,64]{2,0,1:T(2,128)S(1)}, f32[2,4,64]{2,0,1:T(2,128)S(1)}, u32[]{:S(2)}, u32[]{:S(2)}) collective-permute-start(f32[2,4,64]{2,0,1:T(2,128)S(1)} %pad_maximum_fusion.8), channel_id=1, source_target_pairs={{0,6},{6,0},{12,18},{18,12},{24,30},{30,24},{36,42},{42,36},{48,54... | collective-permute-start | bytes 6152 | tf_op jit(solution)/shard_map/ppermute | solution.py:15
  119.3 6.9 %collective-permute-start.10 = (bf16[2,64,768]{2,1,0:T(8,128)(2,1)S(1)}, bf16[2,64,768]{2,1,0:T(8,128)(2,1)S(1)}, u32[]{:S(2)}, u32[]{:S(2)}) collective-permute-start(bf16[2,64,768]{2,1,0:T(8,128)(2,1)S(1)} %get-tuple-element.46), channel_id=1, source_target_pairs={{0,1},{1,0},{2,3},{3,2},{4,5},{5,4},{6,9},{7,10},{8,11},{9,6},{10,... | collective-permute-start | bytes 589832 | tf_op jit(solution)/shard_map/ppermute | solution.py:59
  126.2 1.9 collective-permute-start.11
  128.1 3.4 %collective-permute-start.12 = (bf16[2,64,768]{2,1,0:T(8,128)(2,1)S(1)}, bf16[2,64,768]{2,1,0:T(8,128)(2,1)S(1)}, u32[]{:S(2)}, u32[]{:S(2)}) collective-permute-start(bf16[2,64,768]{2,1,0:T(8,128)(2,1)S(1)} %get-tuple-element.46), channel_id=1, source_target_pairs={{0,4},{1,5},{2,0},{3,1},{4,2},{5,3},{6,8},{7,6},{8,7},{9,11},{10,9... | collective-permute-start | bytes 589832 | tf_op jit(solution)/shard_map/ppermute | solution.py:59
  131.5 2.1 %collective-permute-done.10 = bf16[2,64,768]{2,1,0:T(8,128)(2,1)S(1)} collective-permute-done((bf16[2,64,768]{2,1,0:T(8,128)(2,1)S(1)}, bf16[2,64,768]{2,1,0:T(8,128)(2,1)S(1)}, u32[]{:S(2)}, u32[]{:S(2)}) %collective-permute-start.10) | collective-permute-done | bytes 196640 | tf_op jit(solution)/shard_map/ppermute | solution.py:59
  133.7 5.9 %collective-permute-done.11 = bf16[2,64,768]{2,1,0:T(8,128)(2,1)S(1)} collective-permute-done((bf16[2,64,768]{2,1,0:T(8,128)(2,1)S(1)}, bf16[2,64,768]{2,1,0:T(8,128)(2,1)S(1)}, u32[]{:S(2)}, u32[]{:S(2)}) %collective-permute-start.11) | collective-permute-done | bytes 196640 | tf_op jit(solution)/shard_map/ppermute | solution.py:59
  139.6 2.0 %collective-permute-done.12 = bf16[2,64,768]{2,1,0:T(8,128)(2,1)S(1)} collective-permute-done((bf16[2,64,768]{2,1,0:T(8,128)(2,1)S(1)}, bf16[2,64,768]{2,1,0:T(8,128)(2,1)S(1)}, u32[]{:S(2)}, u32[]{:S(2)}) %collective-permute-start.12) | collective-permute-done | bytes 196640 | tf_op jit(solution)/shard_map/ppermute | solution.py:59
  141.7 1.9 collective-permute-start.13
  143.7 3.8 %collective-permute-start.14 = (bf16[2,64,768]{2,1,0:T(8,128)(2,1)S(1)}, bf16[2,64,768]{2,1,0:T(8,128)(2,1)S(1)}, u32[]{:S(2)}, u32[]{:S(2)}) collective-permute-start(bf16[2,64,768]{2,1,0:T(8,128)(2,1)S(1)} %get-tuple-element.55), channel_id=1, source_target_pairs={{0,1},{1,0},{2,3},{3,2},{4,5},{5,4},{6,8},{7,6},{8,7},{9,11},{10,9... | collective-permute-start | bytes 589832 | tf_op jit(solution)/shard_map/ppermute | solution.py:59
  147.5 1.1 collective-permute-done.13
  148.6 7.3 %collective-permute-done.14 = bf16[2,64,768]{2,1,0:T(8,128)(2,1)S(1)} collective-permute-done((bf16[2,64,768]{2,1,0:T(8,128)(2,1)S(1)}, bf16[2,64,768]{2,1,0:T(8,128)(2,1)S(1)}, u32[]{:S(2)}, u32[]{:S(2)}) %collective-permute-start.14) | collective-permute-done | bytes 196640 | tf_op jit(solution)/shard_map/ppermute | solution.py:59
  157.1 6.6 %collective-permute-start.16 = (bf16[384,640]{1,0:T(8,128)(2,1)S(1)}, bf16[384,640]{1,0:T(8,128)(2,1)S(1)}, u32[]{:S(2)}, u32[]{:S(2)}) collective-permute-start(bf16[384,640]{1,0:T(8,128)(2,1)S(1)} %convolution_convert_fusion), channel_id=1, source_target_pairs={{24,0},{18,6},{36,12},{30,18},{48,24},{42,30},{60,36},{54,42},{72,... | collective-permute-start | bytes 1474568 | tf_op jit(solution)/shard_map/ppermute | solution.py:15
  164.8 5.8 %collective-permute-start.15 = (bf16[384,640]{1,0:T(8,128)(2,1)S(1)}, bf16[384,640]{1,0:T(8,128)(2,1)S(1)}, u32[]{:S(2)}, u32[]{:S(2)}) collective-permute-start(bf16[384,640]{1,0:T(8,128)(2,1)S(1)} %fusion), channel_id=1, source_target_pairs={{24,0},{18,6},{36,12},{30,18},{48,24},{42,30},{60,36},{54,42},{72,... | collective-permute-start | bytes 1474568 | tf_op jit(solution)/shard_map/ppermute | solution.py:15
  170.6 23.0 %collective-permute-done.16 = bf16[384,640]{1,0:T(8,128)(2,1)S(1)} collective-permute-done((bf16[384,640]{1,0:T(8,128)(2,1)S(1)}, bf16[384,640]{1,0:T(8,128)(2,1)S(1)}, u32[]{:S(2)}, u32[]{:S(2)}) %collective-permute-start.16) | collective-permute-done | bytes 491552 | tf_op jit(solution)/shard_map/ppermute | solution.py:15
  193.7 1.9 collective-permute-start.17
  196.3 2.6 %collective-permute-done.15 = bf16[384,640]{1,0:T(8,128)(2,1)S(1)} collective-permute-done((bf16[384,640]{1,0:T(8,128)(2,1)S(1)}, bf16[384,640]{1,0:T(8,128)(2,1)S(1)}, u32[]{:S(2)}, u32[]{:S(2)}) %collective-permute-start.15) | collective-permute-done | bytes 491552 | tf_op jit(solution)/shard_map/ppermute | solution.py:15
  (81 shorter events, 16.4 us)
Async XLA Ops:
  0.0 43.4 %copy-start = (bf16[384,640]{1,0:T(8,128)(2,1)S(1)}, bf16[384,640]{1,0:T(8,128)(2,1)}, u32[]{:S(2)}) copy-start(bf16[384,640]{1,0:T(8,128)(2,1)} %param.6) | copy-start | bytes 1474564
  1.9 41.7 %collective-permute-start.2 = (bf16[400,640]{1,0:T(8,128)(2,1)S(1)}, bf16[400,640]{1,0:T(8,128)(2,1)S(1)}, u32[]{:S(2)}, u32[]{:S(2)}) collective-permute-start(bf16[400,640]{1,0:T(8,128)(2,1)S(1)} %pad_maximum_fusion.2), channel_id=1, source_target_pairs={{0,18},{6,24},{12,30},{18,36},{24,42},{30,48},{36,54},{42,60},{48,... | collective-permute-start | bytes 1536008 | tf_op jit(solution)/shard_map/ppermute | solution.py:15
  5.6 37.8 %collective-permute-start.1 = (bf16[400,640]{1,0:T(8,128)(2,1)S(1)}, bf16[400,640]{1,0:T(8,128)(2,1)S(1)}, u32[]{:S(2)}, u32[]{:S(2)}) collective-permute-start(bf16[400,640]{1,0:T(8,128)(2,1)S(1)} %pad_maximum_fusion.2), channel_id=1, source_target_pairs={{0,24},{6,18},{12,36},{18,30},{24,48},{30,42},{36,60},{42,54},{48,... | collective-permute-start | bytes 1536008 | tf_op jit(solution)/shard_map/ppermute | solution.py:15
  20.9 4.7 %collective-permute-start = (f32[4,64]{1,0:T(4,128)S(1)}, f32[4,64]{1,0:T(4,128)S(1)}, u32[]{:S(2)}, u32[]{:S(2)}) collective-permute-start(f32[4,64]{1,0:T(4,128)S(1)} %fusion.45), channel_id=1, source_target_pairs={{0,6},{6,0},{12,18},{18,12},{24,30},{30,24},{36,42},{42,36},{48,54... | collective-permute-start | bytes 3080 | tf_op jit(solution)/shard_map/ppermute | solution.py:15
  22.9 22.3 %collective-permute-start.3 = (bf16[400,640]{1,0:T(8,128)(2,1)S(1)}, bf16[400,640]{1,0:T(8,128)(2,1)S(1)}, u32[]{:S(2)}, u32[]{:S(2)}) collective-permute-start(bf16[400,640]{1,0:T(8,128)(2,1)S(1)} %pad_maximum_fusion.2), channel_id=1, source_target_pairs={{0,6},{6,0},{12,18},{18,12},{24,30},{30,24},{36,42},{42,36},{48,54... | collective-permute-start | bytes 1536008 | tf_op jit(solution)/shard_map/ppermute | solution.py:15
  43.5 20.8 %copy-start.1 = (bf16[400,640]{1,0:T(8,128)(2,1)}, bf16[400,640]{1,0:T(8,128)(2,1)S(1)}, u32[]{:S(2)}) copy-start(bf16[400,640]{1,0:T(8,128)(2,1)S(1)} %broadcast_select_fusion) | copy-start | bytes 1536004
  43.6 0.8 copy-start.2
  47.4 0.7 slice-start.1
  48.2 19.2 %collective-permute-start.4 = (f32[2,64,768]{2,1,0:T(8,128)S(1)}, f32[2,64,768]{2,1,0:T(8,128)S(1)}, u32[]{:S(2)}, u32[]{:S(2)}) collective-permute-start(f32[2,64,768]{2,1,0:T(8,128)S(1)} %get-tuple-element.32), channel_id=1, source_target_pairs={{0,1},{1,0},{2,3},{3,2},{4,5},{5,4},{6,7},{7,8},{8,6},{9,10},{10,1... | collective-permute-start | bytes 1179656 | tf_op jit(solution)/shard_map/ppermute | solution.py:59
  50.1 24.9 %collective-permute-start.5 = (f32[2,64,768]{2,1,0:T(8,128)S(1)}, f32[2,64,768]{2,1,0:T(8,128)S(1)}, u32[]{:S(2)}, u32[]{:S(2)}) collective-permute-start(f32[2,64,768]{2,1,0:T(8,128)S(1)} %get-tuple-element.33), channel_id=1, source_target_pairs={{0,1},{1,0},{2,3},{3,2},{4,5},{5,4},{6,8},{7,6},{8,7},{9,11},{10,9... | collective-permute-start | bytes 1179656 | tf_op jit(solution)/shard_map/ppermute | solution.py:59
  64.3 0.7 slice-start
  75.1 30.6 %collective-permute-start.6 = (f32[2,64,768]{2,1,0:T(8,128)S(1)}, f32[2,64,768]{2,1,0:T(8,128)S(1)}, u32[]{:S(2)}, u32[]{:S(2)}) collective-permute-start(f32[2,64,768]{2,1,0:T(8,128)S(1)} %get-tuple-element.34), channel_id=1, source_target_pairs={{0,1},{1,0},{2,3},{3,2},{4,5},{5,4},{6,9},{7,10},{8,11},{9,6},{10,... | collective-permute-start | bytes 1179656 | tf_op jit(solution)/shard_map/ppermute | solution.py:59
  80.1 27.6 %collective-permute-start.7 = (f32[2,64,768]{2,1,0:T(8,128)S(1)}, f32[2,64,768]{2,1,0:T(8,128)S(1)}, u32[]{:S(2)}, u32[]{:S(2)}) collective-permute-start(f32[2,64,768]{2,1,0:T(8,128)S(1)} %get-tuple-element.35), channel_id=1, source_target_pairs={{0,2},{1,3},{2,4},{3,5},{4,0},{5,1},{6,7},{7,8},{8,6},{9,10},{10,1... | collective-permute-start | bytes 1179656 | tf_op jit(solution)/shard_map/ppermute | solution.py:59
  82.0 30.0 %collective-permute-start.8 = (f32[2,64,768]{2,1,0:T(8,128)S(1)}, f32[2,64,768]{2,1,0:T(8,128)S(1)}, u32[]{:S(2)}, u32[]{:S(2)}) collective-permute-start(f32[2,64,768]{2,1,0:T(8,128)S(1)} %get-tuple-element.36), channel_id=1, source_target_pairs={{0,4},{1,5},{2,0},{3,1},{4,2},{5,3},{6,8},{7,6},{8,7},{9,11},{10,9... | collective-permute-start | bytes 1179656 | tf_op jit(solution)/shard_map/ppermute | solution.py:59
  112.7 6.2 %collective-permute-start.9 = (f32[2,4,64]{2,0,1:T(2,128)S(1)}, f32[2,4,64]{2,0,1:T(2,128)S(1)}, u32[]{:S(2)}, u32[]{:S(2)}) collective-permute-start(f32[2,4,64]{2,0,1:T(2,128)S(1)} %pad_maximum_fusion.8), channel_id=1, source_target_pairs={{0,6},{6,0},{12,18},{18,12},{24,30},{30,24},{36,42},{42,36},{48,54... | collective-permute-start | bytes 6152 | tf_op jit(solution)/shard_map/ppermute | solution.py:15
  119.3 14.3 %collective-permute-start.10 = (bf16[2,64,768]{2,1,0:T(8,128)(2,1)S(1)}, bf16[2,64,768]{2,1,0:T(8,128)(2,1)S(1)}, u32[]{:S(2)}, u32[]{:S(2)}) collective-permute-start(bf16[2,64,768]{2,1,0:T(8,128)(2,1)S(1)} %get-tuple-element.46), channel_id=1, source_target_pairs={{0,1},{1,0},{2,3},{3,2},{4,5},{5,4},{6,9},{7,10},{8,11},{9,6},{10,... | collective-permute-start | bytes 589832 | tf_op jit(solution)/shard_map/ppermute | solution.py:59
  126.2 13.4 %collective-permute-start.11 = (bf16[2,64,768]{2,1,0:T(8,128)(2,1)S(1)}, bf16[2,64,768]{2,1,0:T(8,128)(2,1)S(1)}, u32[]{:S(2)}, u32[]{:S(2)}) collective-permute-start(bf16[2,64,768]{2,1,0:T(8,128)(2,1)S(1)} %get-tuple-element.46), channel_id=1, source_target_pairs={{0,2},{1,3},{2,4},{3,5},{4,0},{5,1},{6,7},{7,8},{8,6},{9,10},{10,1... | collective-permute-start | bytes 589832 | tf_op jit(solution)/shard_map/ppermute | solution.py:59
  128.1 13.5 %collective-permute-start.12 = (bf16[2,64,768]{2,1,0:T(8,128)(2,1)S(1)}, bf16[2,64,768]{2,1,0:T(8,128)(2,1)S(1)}, u32[]{:S(2)}, u32[]{:S(2)}) collective-permute-start(bf16[2,64,768]{2,1,0:T(8,128)(2,1)S(1)} %get-tuple-element.46), channel_id=1, source_target_pairs={{0,4},{1,5},{2,0},{3,1},{4,2},{5,3},{6,8},{7,6},{8,7},{9,11},{10,9... | collective-permute-start | bytes 589832 | tf_op jit(solution)/shard_map/ppermute | solution.py:59
  141.7 6.9 %collective-permute-start.13 = (bf16[2,64,768]{2,1,0:T(8,128)(2,1)S(1)}, bf16[2,64,768]{2,1,0:T(8,128)(2,1)S(1)}, u32[]{:S(2)}, u32[]{:S(2)}) collective-permute-start(bf16[2,64,768]{2,1,0:T(8,128)(2,1)S(1)} %get-tuple-element.56), channel_id=1, source_target_pairs={{0,1},{1,0},{2,3},{3,2},{4,5},{5,4},{6,7},{7,8},{8,6},{9,10},{10,1... | collective-permute-start | bytes 589832 | tf_op jit(solution)/shard_map/ppermute | solution.py:59
  143.7 12.3 %collective-permute-start.14 = (bf16[2,64,768]{2,1,0:T(8,128)(2,1)S(1)}, bf16[2,64,768]{2,1,0:T(8,128)(2,1)S(1)}, u32[]{:S(2)}, u32[]{:S(2)}) collective-permute-start(bf16[2,64,768]{2,1,0:T(8,128)(2,1)S(1)} %get-tuple-element.55), channel_id=1, source_target_pairs={{0,1},{1,0},{2,3},{3,2},{4,5},{5,4},{6,8},{7,6},{8,7},{9,11},{10,9... | collective-permute-start | bytes 589832 | tf_op jit(solution)/shard_map/ppermute | solution.py:59
  157.1 36.5 %collective-permute-start.16 = (bf16[384,640]{1,0:T(8,128)(2,1)S(1)}, bf16[384,640]{1,0:T(8,128)(2,1)S(1)}, u32[]{:S(2)}, u32[]{:S(2)}) collective-permute-start(bf16[384,640]{1,0:T(8,128)(2,1)S(1)} %convolution_convert_fusion), channel_id=1, source_target_pairs={{24,0},{18,6},{36,12},{30,18},{48,24},{42,30},{60,36},{54,42},{72,... | collective-permute-start | bytes 1474568 | tf_op jit(solution)/shard_map/ppermute | solution.py:15
  164.8 34.1 %collective-permute-start.15 = (bf16[384,640]{1,0:T(8,128)(2,1)S(1)}, bf16[384,640]{1,0:T(8,128)(2,1)S(1)}, u32[]{:S(2)}, u32[]{:S(2)}) collective-permute-start(bf16[384,640]{1,0:T(8,128)(2,1)S(1)} %fusion), channel_id=1, source_target_pairs={{24,0},{18,6},{36,12},{30,18},{48,24},{42,30},{60,36},{54,42},{72,... | collective-permute-start | bytes 1474568 | tf_op jit(solution)/shard_map/ppermute | solution.py:15
  193.7 5.3 %collective-permute-start.17 = (bf16[384,640]{1,0:T(8,128)(2,1)S(1)}, bf16[384,640]{1,0:T(8,128)(2,1)S(1)}, u32[]{:S(2)}, u32[]{:S(2)}) collective-permute-start(bf16[384,640]{1,0:T(8,128)(2,1)S(1)} %add_convert_fusion.1), channel_id=1, source_target_pairs={{0,6},{6,0},{12,18},{18,12},{24,30},{30,24},{36,42},{42,36},{48,54... | collective-permute-start | bytes 1474568 | tf_op jit(solution)/shard_map/ppermute | solution.py:15

commit v15 on v14

--- a/solution.py
+++ b/solution.py
@@ -154,32 +154,24 @@
     def owner(even, odd):
         return jnp.where(core == 0, even(r), odd(r))
 
-    def partial(queries, device):
-        parts = [
-            partial_of(rows_of(q, row_start(device), 64), read) for q, read in zip(queries, keys)
-        ]
-        return jnp.stack(parts)
-
-    ahead = [
-        owner(lambda q: beside(stride(1)(q)), lambda q: across(triple(1)(q))),
-        owner(lambda q: beside(stride(2)(q)), lambda q: across(triple(2)(q))),
-    ]
-    own_sent = tuple(partial_of(rows_of(hidden, row_start(d), 64), keys[0]) for d in ahead)
-    *own_sent, pair_hidden = lax.optimization_barrier(own_sent + (pair_hidden,))
-    sent = tuple(
-        jnp.stack([mine, partial_of(rows_of(pair_hidden, row_start(d), 64), keys[1])])
-        for mine, d in zip(own_sent, ahead)
-    )
-    *sent, own, pair = lax.optimization_barrier(sent + (hidden, pair_hidden))
-    queries = (own, pair)
-    in_one = line_permute(sent[0], beside, triple(1))
-    in_two = line_permute(sent[1], beside, triple(2))
-    paired = partial(queries, owner(beside, across)) + jnp.where(core == 1, in_one + in_two, 0.0)
-    one = partial(queries, owner(stride(1), triple(1))) + jnp.where(core == 0, in_one, 0.0)
-    two = partial(queries, owner(stride(2), triple(2))) + jnp.where(core == 0, in_two, 0.0)
+    own_part = partial_of(hidden, keys[0])
+    own_part, pair_hidden = lax.optimization_barrier((own_part, pair_hidden))
+    pair_part = partial_of(pair_hidden, keys[1])
+
+    def partial(device):
+        start = row_start(device)
+        return jnp.stack([rows_of(own_part, start, 64), rows_of(pair_part, start, 64)])
+
+    ahead_one = partial(owner(lambda q: beside(stride(1)(q)), lambda q: across(triple(1)(q))))
+    ahead_two = partial(owner(lambda q: beside(stride(2)(q)), lambda q: across(triple(2)(q))))
+    in_one = line_permute(ahead_one, beside, triple(1))
+    in_two = line_permute(ahead_two, beside, triple(2))
+    paired = partial(owner(beside, across)) + jnp.where(core == 1, in_one + in_two, 0.0)
+    one = partial(owner(stride(1), triple(1))) + jnp.where(core == 0, in_one, 0.0)
+    two = partial(owner(stride(2), triple(2))) + jnp.where(core == 0, in_two, 0.0)
     paired, one, two = lax.optimization_barrier((paired, one, two))
     paired = line_permute(paired, beside, across)
-    scores = lax.optimization_barrier(partial(queries, r) + paired)
+    scores = lax.optimization_barrier(partial(r) + paired)
     one = line_permute(one, stride(1), triple(1))
     two = line_permute(two, stride(2), triple(2))
     scores = (scores + one + two) * score_scale

time: 201 us -> 208 us (1.035)
  other arithmetic: 5.85 us -> 11.6 us
  local copies, waits for them, and re-layouts: 2.97 us -> 8.38 us
  matrix products: 7.86 us -> 4.25 us
    dynamic_slice x0 -> x7, local copies, waits for them, and re-layouts: none -> 4.62 us  [rows_of(): return lax.dynamic_slice_in_dim(value, start, size, axis)]
    dot_general x12 -> x2, matrix products: 5 us -> 1.39 us  [partial_of(): lax.dot_general(queries, keys, (((1,), (1,)), ((), ())), preferred_elemen...]
    another operation x2 -> x3, other arithmetic: 0.83 us -> 4.41 us  [the longest x2 3.65 us: partial(): jnp.stack([rows_of(own_part, start, 64), rows_of(pair_part, start, 64)])]
    ppermute x10, starting transfers between devices: 43.6 us -> 46.8 us  [line_permute(): return lax.ppermute(value, ('dp', 'tensor'), pairs)]
    add x2, other arithmetic: 0.17 us -> 2.36 us  [the longest x1 2.32 us: per_device(): partial(owner(stride(2), triple(2))) + jnp.where(core == 0, in_two, 0.0)]
where the time goes in v15:
time: 208 us; the launch traced here: 207 us
  waiting for transfers between devices  97 us (47%)
  starting transfers between devices  85.1 us (41%)
  other arithmetic  11.6 us (6%)
  local copies, waits for them, and re-layouts  8.38 us (4%)
  matrix products  4.25 us (2%)
    ppermute x10, waiting for transfers between devices, line_permute(): return lax.ppermute(value, ('dp', 'tensor'), pairs)  52.7 us
    ppermute x10, starting transfers between devices, line_permute(): return lax.ppermute(value, ('dp', 'tensor'), pairs)  46.8 us
    ppermute x8, waiting for transfers between devices, dp_permute(): return lax.ppermute(value, 'dp', pairs)  44.2 us
    ppermute x8, starting transfers between devices, dp_permute(): return lax.ppermute(value, 'dp', pairs)  38.3 us
    dynamic_slice x7, local copies, waits for them, and re-layouts, rows_of(): return lax.dynamic_slice_in_dim(value, start, size, axis)  4.62 us
  transfers between devices with their start and end apart: 18, of which 14 were waited for; matrix products, arithmetic and copies ran while one was open for 4% of the time, Pallas kernels for 0%

profile of v15, /device:TPU:129, one launch (start us, length us, event | category | flops | bytes accessed | tf_op | source)
XLA Modules:
  0.0 207.3 jit_solution(9997143439833540984)
XLA Ops:
  1.9 3.7 %collective-permute-start.2 = (bf16[400,640]{1,0:T(8,128)(2,1)S(1)}, bf16[400,640]{1,0:T(8,128)(2,1)S(1)}, u32[]{:S(2)}, u32[]{:S(2)}) collective-permute-start(bf16[400,640]{1,0:T(8,128)(2,1)S(1)} %pad_maximum_fusion.6), channel_id=1, source_target_pairs={{0,18},{6,24},{12,30},{18,36},{24,42},{30,48},{36,54},{42,60},{48,... | collective-permute-start | bytes 1536008 | tf_op jit(solution)/shard_map/ppermute | solution.py:15
  5.6 12.5 %collective-permute-start.1 = (bf16[400,640]{1,0:T(8,128)(2,1)S(1)}, bf16[400,640]{1,0:T(8,128)(2,1)S(1)}, u32[]{:S(2)}, u32[]{:S(2)}) collective-permute-start(bf16[400,640]{1,0:T(8,128)(2,1)S(1)} %pad_maximum_fusion.6), channel_id=1, source_target_pairs={{0,24},{6,18},{12,36},{18,30},{24,48},{30,42},{36,60},{42,54},{48,... | collective-permute-start | bytes 1536008 | tf_op jit(solution)/shard_map/ppermute | solution.py:15
  20.9 2.0 collective-permute-start
  22.9 2.3 %collective-permute-start.3 = (bf16[400,640]{1,0:T(8,128)(2,1)S(1)}, bf16[400,640]{1,0:T(8,128)(2,1)S(1)}, u32[]{:S(2)}, u32[]{:S(2)}) collective-permute-start(bf16[400,640]{1,0:T(8,128)(2,1)S(1)} %pad_maximum_fusion.6), channel_id=1, source_target_pairs={{0,6},{6,0},{12,18},{18,12},{24,30},{30,24},{36,42},{42,36},{48,54... | collective-permute-start | bytes 1536008 | tf_op jit(solution)/shard_map/ppermute | solution.py:15
  25.6 17.8 %collective-permute-done.1 = bf16[400,640]{1,0:T(8,128)(2,1)S(1)} collective-permute-done((bf16[400,640]{1,0:T(8,128)(2,1)S(1)}, bf16[400,640]{1,0:T(8,128)(2,1)S(1)}, u32[]{:S(2)}, u32[]{:S(2)}) %collective-permute-start.1) | collective-permute-done | bytes 512032 | tf_op jit(solution)/shard_map/ppermute | solution.py:15
  47.0 1.4 constant_dynamic-slice_fusion.5
  48.4 1.8 copy.13
  51.0 1.8 pad_maximum_fusion.7
  52.8 1.9 collective-permute-start.4
  54.8 1.9 pad_maximum_fusion.8
  56.6 13.6 %collective-permute-start.5 = (f32[2,64,768]{2,1,0:T(8,128)}, f32[2,64,768]{2,1,0:T(8,128)}, u32[]{:S(2)}, u32[]{:S(2)}) collective-permute-start(f32[2,64,768]{2,1,0:T(8,128)} %pad_maximum_fusion.8), channel_id=1, source_target_pairs={{0,1},{1,0},{2,3},{3,2},{4,5},{5,4},{6,8},{7,6},{8,7},{9,11},{10,9... | collective-permute-start | bytes 1179656 | tf_op jit(solution)/shard_map/ppermute | solution.py:59
  71.9 5.8 %collective-permute-done.5 = f32[2,64,768]{2,1,0:T(8,128)} collective-permute-done((f32[2,64,768]{2,1,0:T(8,128)}, f32[2,64,768]{2,1,0:T(8,128)}, u32[]{:S(2)}, u32[]{:S(2)}) %collective-permute-start.5) | collective-permute-done | bytes 393248 | tf_op jit(solution)/shard_map/ppermute | solution.py:59
  77.7 2.3 %maximum_add_fusion.3 = (f32[2,64,768]{2,1,0:T(8,128)}, f32[2,64,768]{2,1,0:T(8,128)}, f32[2,64,768]{2,1,0:T(8,128)}) fusion(f32[1,64,768]{2,1,0:T(8,128)S(1)} %copy-done.4, f32[1,64,768]{2,1,0:T(8,128)S(1)} %bitcast.118, f32[2,64,768]{2,1,0:T(8,128)} %collective-permute-done.5, pred[]{:T(512)S(6)} %eq.84, f32[2,64,768]{2,1,0:T(8,128)} %collective-permute-done.4, ...), kind=kLoop, calls=%fused_computation.25 | loop fusion | flops 983040 | bytes 3145730 | tf_op jit(solution)/shard_map/add | solution.py:171
  80.0 7.9 %collective-permute-start.6 = (f32[2,64,768]{2,1,0:T(8,128)}, f32[2,64,768]{2,1,0:T(8,128)S(1)}, u32[]{:S(2)}, u32[]{:S(2)}) collective-permute-start(f32[2,64,768]{2,1,0:T(8,128)} %get-tuple-element.24), channel_id=1, source_target_pairs={{0,1},{1,0},{2,3},{3,2},{4,5},{5,4},{6,9},{7,10},{8,11},{9,6},{10,... | collective-permute-start | bytes 1179656 | tf_op jit(solution)/shard_map/ppermute | solution.py:59
  88.0 1.9 collective-permute-start.7
  89.9 3.4 %collective-permute-start.8 = (f32[2,64,768]{2,1,0:T(8,128)}, f32[2,64,768]{2,1,0:T(8,128)S(1)}, u32[]{:S(2)}, u32[]{:S(2)}) collective-permute-start(f32[2,64,768]{2,1,0:T(8,128)} %get-tuple-element.26), channel_id=1, source_target_pairs={{0,4},{1,5},{2,0},{3,1},{4,2},{5,3},{6,8},{7,6},{8,7},{9,11},{10,9... | collective-permute-start | bytes 1179656 | tf_op jit(solution)/shard_map/ppermute | solution.py:59
  93.5 19.6 %collective-permute-done.6 = f32[2,64,768]{2,1,0:T(8,128)S(1)} collective-permute-done((f32[2,64,768]{2,1,0:T(8,128)}, f32[2,64,768]{2,1,0:T(8,128)S(1)}, u32[]{:S(2)}, u32[]{:S(2)}) %collective-permute-start.6) | collective-permute-done | bytes 393248 | tf_op jit(solution)/shard_map/ppermute | solution.py:59
  114.2 6.6 %collective-permute-done.8 = f32[2,64,768]{2,1,0:T(8,128)S(1)} collective-permute-done((f32[2,64,768]{2,1,0:T(8,128)}, f32[2,64,768]{2,1,0:T(8,128)S(1)}, u32[]{:S(2)}, u32[]{:S(2)}) %collective-permute-start.8) | collective-permute-done | bytes 393248 | tf_op jit(solution)/shard_map/ppermute | solution.py:59
  121.5 3.5 %collective-permute-start.9 = (f32[2,4,64]{2,0,1:T(2,128)S(1)}, f32[2,4,64]{2,0,1:T(2,128)S(1)}, u32[]{:S(2)}, u32[]{:S(2)}) collective-permute-start(f32[2,4,64]{2,0,1:T(2,128)S(1)} %pad_maximum_fusion.12), channel_id=1, source_target_pairs={{0,6},{6,0},{12,18},{18,12},{24,30},{30,24},{36,42},{42,36},{48,54... | collective-permute-start | bytes 6152 | tf_op jit(solution)/shard_map/ppermute | solution.py:15
  126.2 7.1 %collective-permute-start.10 = (bf16[2,64,768]{2,1,0:T(8,128)(2,1)S(1)}, bf16[2,64,768]{2,1,0:T(8,128)(2,1)S(1)}, u32[]{:S(2)}, u32[]{:S(2)}) collective-permute-start(bf16[2,64,768]{2,1,0:T(8,128)(2,1)S(1)} %get-tuple-element.36), channel_id=1, source_target_pairs={{0,1},{1,0},{2,3},{3,2},{4,5},{5,4},{6,9},{7,10},{8,11},{9,6},{10,... | collective-permute-start | bytes 589832 | tf_op jit(solution)/shard_map/ppermute | solution.py:59
  133.2 1.9 collective-permute-start.11
  135.2 3.4 %collective-permute-start.12 = (bf16[2,64,768]{2,1,0:T(8,128)(2,1)S(1)}, bf16[2,64,768]{2,1,0:T(8,128)(2,1)S(1)}, u32[]{:S(2)}, u32[]{:S(2)}) collective-permute-start(bf16[2,64,768]{2,1,0:T(8,128)(2,1)S(1)} %get-tuple-element.36), channel_id=1, source_target_pairs={{0,4},{1,5},{2,0},{3,1},{4,2},{5,3},{6,8},{7,6},{8,7},{9,11},{10,9... | collective-permute-start | bytes 589832 | tf_op jit(solution)/shard_map/ppermute | solution.py:59
  138.5 2.1 %collective-permute-done.10 = bf16[2,64,768]{2,1,0:T(8,128)(2,1)S(1)} collective-permute-done((bf16[2,64,768]{2,1,0:T(8,128)(2,1)S(1)}, bf16[2,64,768]{2,1,0:T(8,128)(2,1)S(1)}, u32[]{:S(2)}, u32[]{:S(2)}) %collective-permute-start.10) | collective-permute-done | bytes 196640 | tf_op jit(solution)/shard_map/ppermute | solution.py:59
  140.7 6.9 %collective-permute-done.11 = bf16[2,64,768]{2,1,0:T(8,128)(2,1)S(1)} collective-permute-done((bf16[2,64,768]{2,1,0:T(8,128)(2,1)S(1)}, bf16[2,64,768]{2,1,0:T(8,128)(2,1)S(1)}, u32[]{:S(2)}, u32[]{:S(2)}) %collective-permute-start.11) | collective-permute-done | bytes 196640 | tf_op jit(solution)/shard_map/ppermute | solution.py:59
  148.9 1.9 collective-permute-start.13
  150.8 3.8 %collective-permute-start.14 = (bf16[2,64,768]{2,1,0:T(8,128)(2,1)S(1)}, bf16[2,64,768]{2,1,0:T(8,128)(2,1)S(1)}, u32[]{:S(2)}, u32[]{:S(2)}) collective-permute-start(bf16[2,64,768]{2,1,0:T(8,128)(2,1)S(1)} %get-tuple-element.57), channel_id=1, source_target_pairs={{0,1},{1,0},{2,3},{3,2},{4,5},{5,4},{6,8},{7,6},{8,7},{9,11},{10,9... | collective-permute-start | bytes 589832 | tf_op jit(solution)/shard_map/ppermute | solution.py:59
  156.1 7.1 %collective-permute-done.14 = bf16[2,64,768]{2,1,0:T(8,128)(2,1)S(1)} collective-permute-done((bf16[2,64,768]{2,1,0:T(8,128)(2,1)S(1)}, bf16[2,64,768]{2,1,0:T(8,128)(2,1)S(1)}, u32[]{:S(2)}, u32[]{:S(2)}) %collective-permute-start.14) | collective-permute-done | bytes 196640 | tf_op jit(solution)/shard_map/ppermute | solution.py:59
  164.4 6.3 %collective-permute-start.16 = (bf16[384,640]{1,0:T(8,128)(2,1)S(1)}, bf16[384,640]{1,0:T(8,128)(2,1)S(1)}, u32[]{:S(2)}, u32[]{:S(2)}) collective-permute-start(bf16[384,640]{1,0:T(8,128)(2,1)S(1)} %convolution_convert_fusion), channel_id=1, source_target_pairs={{24,0},{18,6},{36,12},{30,18},{48,24},{42,30},{60,36},{54,42},{72,... | collective-permute-start | bytes 1474568 | tf_op jit(solution)/shard_map/ppermute | solution.py:15
  171.8 6.2 %collective-permute-start.15 = (bf16[384,640]{1,0:T(8,128)(2,1)S(1)}, bf16[384,640]{1,0:T(8,128)(2,1)S(1)}, u32[]{:S(2)}, u32[]{:S(2)}) collective-permute-start(bf16[384,640]{1,0:T(8,128)(2,1)S(1)} %fusion), channel_id=1, source_target_pairs={{24,0},{18,6},{36,12},{30,18},{48,24},{42,30},{60,36},{54,42},{72,... | collective-permute-start | bytes 1474568 | tf_op jit(solution)/shard_map/ppermute | solution.py:15
  178.0 23.0 %collective-permute-done.16 = bf16[384,640]{1,0:T(8,128)(2,1)S(1)} collective-permute-done((bf16[384,640]{1,0:T(8,128)(2,1)S(1)}, bf16[384,640]{1,0:T(8,128)(2,1)S(1)}, u32[]{:S(2)}, u32[]{:S(2)}) %collective-permute-start.16) | collective-permute-done | bytes 491552 | tf_op jit(solution)/shard_map/ppermute | solution.py:15
  201.1 1.9 collective-permute-start.17
  203.7 2.6 %collective-permute-done.15 = bf16[384,640]{1,0:T(8,128)(2,1)S(1)} collective-permute-done((bf16[384,640]{1,0:T(8,128)(2,1)S(1)}, bf16[384,640]{1,0:T(8,128)(2,1)S(1)}, u32[]{:S(2)}, u32[]{:S(2)}) %collective-permute-start.15) | collective-permute-done | bytes 491552 | tf_op jit(solution)/shard_map/ppermute | solution.py:15
  (98 shorter events, 20.5 us)
Async XLA Ops:
  0.0 43.4 %copy-start = (bf16[384,640]{1,0:T(8,128)(2,1)S(1)}, bf16[384,640]{1,0:T(8,128)(2,1)}, u32[]{:S(2)}) copy-start(bf16[384,640]{1,0:T(8,128)(2,1)} %param.6) | copy-start | bytes 1474564
  1.9 41.7 %collective-permute-start.2 = (bf16[400,640]{1,0:T(8,128)(2,1)S(1)}, bf16[400,640]{1,0:T(8,128)(2,1)S(1)}, u32[]{:S(2)}, u32[]{:S(2)}) collective-permute-start(bf16[400,640]{1,0:T(8,128)(2,1)S(1)} %pad_maximum_fusion.6), channel_id=1, source_target_pairs={{0,18},{6,24},{12,30},{18,36},{24,42},{30,48},{36,54},{42,60},{48,... | collective-permute-start | bytes 1536008 | tf_op jit(solution)/shard_map/ppermute | solution.py:15
  5.6 37.8 %collective-permute-start.1 = (bf16[400,640]{1,0:T(8,128)(2,1)S(1)}, bf16[400,640]{1,0:T(8,128)(2,1)S(1)}, u32[]{:S(2)}, u32[]{:S(2)}) collective-permute-start(bf16[400,640]{1,0:T(8,128)(2,1)S(1)} %pad_maximum_fusion.6), channel_id=1, source_target_pairs={{0,24},{6,18},{12,36},{18,30},{24,48},{30,42},{36,60},{42,54},{48,... | collective-permute-start | bytes 1536008 | tf_op jit(solution)/shard_map/ppermute | solution.py:15
  20.9 4.7 %collective-permute-start = (f32[4,64]{1,0:T(4,128)S(1)}, f32[4,64]{1,0:T(4,128)S(1)}, u32[]{:S(2)}, u32[]{:S(2)}) collective-permute-start(f32[4,64]{1,0:T(4,128)S(1)} %fusion.20), channel_id=1, source_target_pairs={{0,6},{6,0},{12,18},{18,12},{24,30},{30,24},{36,42},{42,36},{48,54... | collective-permute-start | bytes 3080 | tf_op jit(solution)/shard_map/ppermute | solution.py:15
  22.9 22.3 %collective-permute-start.3 = (bf16[400,640]{1,0:T(8,128)(2,1)S(1)}, bf16[400,640]{1,0:T(8,128)(2,1)S(1)}, u32[]{:S(2)}, u32[]{:S(2)}) collective-permute-start(bf16[400,640]{1,0:T(8,128)(2,1)S(1)} %pad_maximum_fusion.6), channel_id=1, source_target_pairs={{0,6},{6,0},{12,18},{18,12},{24,30},{30,24},{36,42},{42,36},{48,54... | collective-permute-start | bytes 1536008 | tf_op jit(solution)/shard_map/ppermute | solution.py:15
  43.4 26.9 %copy-start.1 = (bf16[400,640]{1,0:T(8,128)(2,1)}, bf16[400,640]{1,0:T(8,128)(2,1)S(1)}, u32[]{:S(2)}) copy-start(bf16[400,640]{1,0:T(8,128)(2,1)S(1)} %collective-permute-done.1) | copy-start | bytes 1536004
  43.5 0.9 copy-start.2
  43.6 1.6 copy-start.6
  43.7 1.6 copy-start.10
  44.4 0.8 copy-start.8
  50.2 20.1 %slice-start.1 = ((bf16[400,640]{1,0:T(8,128)(2,1)}), bf16[16,640]{1,0:T(8,128)(2,1)S(1)}, s32[]{:S(2)}) async-start(bf16[400,640]{1,0:T(8,128)(2,1)} %copy-done.2), calls=%async_computation.1 | async-start | bytes 40960 | tf_op jit(solution)/shard_map/slice | solution.py:86
  52.8 19.1 %collective-permute-start.4 = (f32[2,64,768]{2,1,0:T(8,128)}, f32[2,64,768]{2,1,0:T(8,128)}, u32[]{:S(2)}, u32[]{:S(2)}) collective-permute-start(f32[2,64,768]{2,1,0:T(8,128)} %pad_maximum_fusion.7), channel_id=1, source_target_pairs={{0,1},{1,0},{2,3},{3,2},{4,5},{5,4},{6,7},{7,8},{8,6},{9,10},{10,1... | collective-permute-start | bytes 1179656 | tf_op jit(solution)/shard_map/ppermute | solution.py:59
  54.7 23.0 %copy-start.4 = (f32[1,64,768]{2,1,0:T(8,128)S(1)}, f32[1,64,768]{2,1,0:T(8,128)}, u32[]{:S(2)}) copy-start(f32[1,64,768]{2,1,0:T(8,128)} %get-tuple-element.49) | copy-start | bytes 589828
  54.7 23.0 %copy-start.5 = (f32[1,64,768]{2,1,0:T(8,128)S(1)}, f32[1,64,768]{2,1,0:T(8,128)}, u32[]{:S(2)}) copy-start(f32[1,64,768]{2,1,0:T(8,128)} %get-tuple-element.50) | copy-start | bytes 589828
  56.6 21.1 %collective-permute-start.5 = (f32[2,64,768]{2,1,0:T(8,128)}, f32[2,64,768]{2,1,0:T(8,128)}, u32[]{:S(2)}, u32[]{:S(2)}) collective-permute-start(f32[2,64,768]{2,1,0:T(8,128)} %pad_maximum_fusion.8), channel_id=1, source_target_pairs={{0,1},{1,0},{2,3},{3,2},{4,5},{5,4},{6,8},{7,6},{8,7},{9,11},{10,9... | collective-permute-start | bytes 1179656 | tf_op jit(solution)/shard_map/ppermute | solution.py:59
  70.3 0.7 slice-start
  77.7 35.4 %copy-start.3 = (f32[1,64,768]{2,1,0:T(8,128)S(1)}, f32[1,64,768]{2,1,0:T(8,128)}, u32[]{:S(2)}) copy-start(f32[1,64,768]{2,1,0:T(8,128)} %get-tuple-element.48) | copy-start | bytes 589828
  80.0 33.1 %collective-permute-start.6 = (f32[2,64,768]{2,1,0:T(8,128)}, f32[2,64,768]{2,1,0:T(8,128)S(1)}, u32[]{:S(2)}, u32[]{:S(2)}) collective-permute-start(f32[2,64,768]{2,1,0:T(8,128)} %get-tuple-element.24), channel_id=1, source_target_pairs={{0,1},{1,0},{2,3},{3,2},{4,5},{5,4},{6,9},{7,10},{8,11},{9,6},{10,... | collective-permute-start | bytes 1179656 | tf_op jit(solution)/shard_map/ppermute | solution.py:59
  88.0 26.3 %collective-permute-start.7 = (f32[2,64,768]{2,1,0:T(8,128)}, f32[2,64,768]{2,1,0:T(8,128)S(1)}, u32[]{:S(2)}, u32[]{:S(2)}) collective-permute-start(f32[2,64,768]{2,1,0:T(8,128)} %get-tuple-element.25), channel_id=1, source_target_pairs={{0,2},{1,3},{2,4},{3,5},{4,0},{5,1},{6,7},{7,8},{8,6},{9,10},{10,1... | collective-permute-start | bytes 1179656 | tf_op jit(solution)/shard_map/ppermute | solution.py:59
  89.9 31.0 %collective-permute-start.8 = (f32[2,64,768]{2,1,0:T(8,128)}, f32[2,64,768]{2,1,0:T(8,128)S(1)}, u32[]{:S(2)}, u32[]{:S(2)}) collective-permute-start(f32[2,64,768]{2,1,0:T(8,128)} %get-tuple-element.26), channel_id=1, source_target_pairs={{0,4},{1,5},{2,0},{3,1},{4,2},{5,3},{6,8},{7,6},{8,7},{9,11},{10,9... | collective-permute-start | bytes 1179656 | tf_op jit(solution)/shard_map/ppermute | solution.py:59
  121.5 4.3 %collective-permute-start.9 = (f32[2,4,64]{2,0,1:T(2,128)S(1)}, f32[2,4,64]{2,0,1:T(2,128)S(1)}, u32[]{:S(2)}, u32[]{:S(2)}) collective-permute-start(f32[2,4,64]{2,0,1:T(2,128)S(1)} %pad_maximum_fusion.12), channel_id=1, source_target_pairs={{0,6},{6,0},{12,18},{18,12},{24,30},{30,24},{36,42},{42,36},{48,54... | collective-permute-start | bytes 6152 | tf_op jit(solution)/shard_map/ppermute | solution.py:15
  126.2 14.4 %collective-permute-start.10 = (bf16[2,64,768]{2,1,0:T(8,128)(2,1)S(1)}, bf16[2,64,768]{2,1,0:T(8,128)(2,1)S(1)}, u32[]{:S(2)}, u32[]{:S(2)}) collective-permute-start(bf16[2,64,768]{2,1,0:T(8,128)(2,1)S(1)} %get-tuple-element.36), channel_id=1, source_target_pairs={{0,1},{1,0},{2,3},{3,2},{4,5},{5,4},{6,9},{7,10},{8,11},{9,6},{10,... | collective-permute-start | bytes 589832 | tf_op jit(solution)/shard_map/ppermute | solution.py:59
  133.2 14.3 %collective-permute-start.11 = (bf16[2,64,768]{2,1,0:T(8,128)(2,1)S(1)}, bf16[2,64,768]{2,1,0:T(8,128)(2,1)S(1)}, u32[]{:S(2)}, u32[]{:S(2)}) collective-permute-start(bf16[2,64,768]{2,1,0:T(8,128)(2,1)S(1)} %get-tuple-element.36), channel_id=1, source_target_pairs={{0,2},{1,3},{2,4},{3,5},{4,0},{5,1},{6,7},{7,8},{8,6},{9,10},{10,1... | collective-permute-start | bytes 589832 | tf_op jit(solution)/shard_map/ppermute | solution.py:59
  135.2 13.6 %collective-permute-start.12 = (bf16[2,64,768]{2,1,0:T(8,128)(2,1)S(1)}, bf16[2,64,768]{2,1,0:T(8,128)(2,1)S(1)}, u32[]{:S(2)}, u32[]{:S(2)}) collective-permute-start(bf16[2,64,768]{2,1,0:T(8,128)(2,1)S(1)} %get-tuple-element.36), channel_id=1, source_target_pairs={{0,4},{1,5},{2,0},{3,1},{4,2},{5,3},{6,8},{7,6},{8,7},{9,11},{10,9... | collective-permute-start | bytes 589832 | tf_op jit(solution)/shard_map/ppermute | solution.py:59
  148.9 7.2 %collective-permute-start.13 = (bf16[2,64,768]{2,1,0:T(8,128)(2,1)S(1)}, bf16[2,64,768]{2,1,0:T(8,128)(2,1)S(1)}, u32[]{:S(2)}, u32[]{:S(2)}) collective-permute-start(bf16[2,64,768]{2,1,0:T(8,128)(2,1)S(1)} %get-tuple-element.58), channel_id=1, source_target_pairs={{0,1},{1,0},{2,3},{3,2},{4,5},{5,4},{6,7},{7,8},{8,6},{9,10},{10,1... | collective-permute-start | bytes 589832 | tf_op jit(solution)/shard_map/ppermute | solution.py:59
  150.8 12.4 %collective-permute-start.14 = (bf16[2,64,768]{2,1,0:T(8,128)(2,1)S(1)}, bf16[2,64,768]{2,1,0:T(8,128)(2,1)S(1)}, u32[]{:S(2)}, u32[]{:S(2)}) collective-permute-start(bf16[2,64,768]{2,1,0:T(8,128)(2,1)S(1)} %get-tuple-element.57), channel_id=1, source_target_pairs={{0,1},{1,0},{2,3},{3,2},{4,5},{5,4},{6,8},{7,6},{8,7},{9,11},{10,9... | collective-permute-start | bytes 589832 | tf_op jit(solution)/shard_map/ppermute | solution.py:59
  164.4 6.8 %copy-start.7 = (bf16[384,640]{1,0:T(8,128)(2,1)S(1)}, bf16[384,640]{1,0:T(8,128)(2,1)}, u32[]{:S(2)}) copy-start(bf16[384,640]{1,0:T(8,128)(2,1)} %copy-done.6) | copy-start | bytes 1474564
  164.4 6.8 %copy-start.11 = (bf16[384,640]{1,0:T(8,128)(2,1)S(1)}, bf16[384,640]{1,0:T(8,128)(2,1)}, u32[]{:S(2)}) copy-start(bf16[384,640]{1,0:T(8,128)(2,1)} %copy-done.10) | copy-start | bytes 1474564
  164.4 36.7 %collective-permute-start.16 = (bf16[384,640]{1,0:T(8,128)(2,1)S(1)}, bf16[384,640]{1,0:T(8,128)(2,1)S(1)}, u32[]{:S(2)}, u32[]{:S(2)}) collective-permute-start(bf16[384,640]{1,0:T(8,128)(2,1)S(1)} %convolution_convert_fusion), channel_id=1, source_target_pairs={{24,0},{18,6},{36,12},{30,18},{48,24},{42,30},{60,36},{54,42},{72,... | collective-permute-start | bytes 1474568 | tf_op jit(solution)/shard_map/ppermute | solution.py:15
  171.8 31.2 %copy-start.9 = (bf16[384,640]{1,0:T(8,128)(2,1)S(1)}, bf16[384,640]{1,0:T(8,128)(2,1)}, u32[]{:S(2)}) copy-start(bf16[384,640]{1,0:T(8,128)(2,1)} %copy-done.8) | copy-start | bytes 1474564
  171.8 34.5 %collective-permute-start.15 = (bf16[384,640]{1,0:T(8,128)(2,1)S(1)}, bf16[384,640]{1,0:T(8,128)(2,1)S(1)}, u32[]{:S(2)}, u32[]{:S(2)}) collective-permute-start(bf16[384,640]{1,0:T(8,128)(2,1)S(1)} %fusion), channel_id=1, source_target_pairs={{24,0},{18,6},{36,12},{30,18},{48,24},{42,30},{60,36},{54,42},{72,... | collective-permute-start | bytes 1474568 | tf_op jit(solution)/shard_map/ppermute | solution.py:15
  201.1 5.3 %collective-permute-start.17 = (bf16[384,640]{1,0:T(8,128)(2,1)S(1)}, bf16[384,640]{1,0:T(8,128)(2,1)S(1)}, u32[]{:S(2)}, u32[]{:S(2)}) collective-permute-start(bf16[384,640]{1,0:T(8,128)(2,1)S(1)} %add_convert_fusion.1), channel_id=1, source_target_pairs={{0,6},{6,0},{12,18},{18,12},{24,30},{30,24},{36,42},{42,36},{48,54... | collective-permute-start | bytes 1474568 | tf_op jit(solution)/shard_map/ppermute | solution.py:15

commit v16 on v14

--- a/solution.py
+++ b/solution.py
@@ -154,32 +154,34 @@
     def owner(even, odd):
         return jnp.where(core == 0, even(r), odd(r))
 
-    def partial(queries, device):
-        parts = [
-            partial_of(rows_of(q, row_start(device), 64), read) for q, read in zip(queries, keys)
-        ]
-        return jnp.stack(parts)
+    def products(queries, read, one, two):
+        rows = [rows_of(queries, row_start(device), 64) for device in (one, two)]
+        return partial_of(jnp.concatenate(rows, axis=0), read)
+
+    def blocks(own, pair):
+        return jnp.stack([own[:64], pair[:64]]), jnp.stack([own[64:], pair[64:]])
 
     ahead = [
         owner(lambda q: beside(stride(1)(q)), lambda q: across(triple(1)(q))),
         owner(lambda q: beside(stride(2)(q)), lambda q: across(triple(2)(q))),
     ]
-    own_sent = tuple(partial_of(rows_of(hidden, row_start(d), 64), keys[0]) for d in ahead)
-    *own_sent, pair_hidden = lax.optimization_barrier(own_sent + (pair_hidden,))
-    sent = tuple(
-        jnp.stack([mine, partial_of(rows_of(pair_hidden, row_start(d), 64), keys[1])])
-        for mine, d in zip(own_sent, ahead)
-    )
-    *sent, own, pair = lax.optimization_barrier(sent + (hidden, pair_hidden))
-    queries = (own, pair)
+    own = payload[:SEG]
+    own_sent = products(own, keys[0], *ahead)
+    own_sent, pair_hidden = lax.optimization_barrier((own_sent, pair_hidden))
+    sent = blocks(own_sent, products(pair_hidden, keys[1], *ahead))
+    *sent, own, pair = lax.optimization_barrier(sent + (own, pair_hidden))
     in_one = line_permute(sent[0], beside, triple(1))
     in_two = line_permute(sent[1], beside, triple(2))
-    paired = partial(queries, owner(beside, across)) + jnp.where(core == 1, in_one + in_two, 0.0)
-    one = partial(queries, owner(stride(1), triple(1))) + jnp.where(core == 0, in_one, 0.0)
-    two = partial(queries, owner(stride(2), triple(2))) + jnp.where(core == 0, in_two, 0.0)
+    ends = (owner(stride(1), triple(1)), owner(stride(2), triple(2)))
+    one, two = blocks(products(own, keys[0], *ends), products(pair, keys[1], *ends))
+    ends = (owner(beside, across), r)
+    paired, kept = blocks(products(own, keys[0], *ends), products(pair, keys[1], *ends))
+    paired = paired + jnp.where(core == 1, in_one + in_two, 0.0)
+    one = one + jnp.where(core == 0, in_one, 0.0)
+    two = two + jnp.where(core == 0, in_two, 0.0)
     paired, one, two = lax.optimization_barrier((paired, one, two))
     paired = line_permute(paired, beside, across)
-    scores = lax.optimization_barrier(partial(queries, r) + paired)
+    scores = lax.optimization_barrier(kept + paired)
     one = line_permute(one, stride(1), triple(1))
     two = line_permute(two, stride(2), triple(2))
     scores = (scores + one + two) * score_scale

time: 201 us -> 198 us (0.985)
  matrix products: 7.86 us -> 5.35 us
    dot_general x12 -> x6, matrix products: 5 us -> 2.5 us  [partial_of(): lax.dot_general(queries, keys, (((1,), (1,)), ((), ())), preferred_elemen...]
where the time goes in v16:
time: 198 us; the launch traced here: 197 us
  waiting for transfers between devices  97.6 us (49%)
  starting transfers between devices  84.1 us (42%)
  other arithmetic  5.82 us (3%)
  matrix products  5.35 us (3%)
  local copies, waits for them, and re-layouts  3.13 us (2%)
    ppermute x10, waiting for transfers between devices, line_permute(): return lax.ppermute(value, ('dp', 'tensor'), pairs)  54 us
    ppermute x8, waiting for transfers between devices, dp_permute(): return lax.ppermute(value, 'dp', pairs)  43.6 us
    ppermute x10, starting transfers between devices, line_permute(): return lax.ppermute(value, ('dp', 'tensor'), pairs)  43 us
    ppermute x8, starting transfers between devices, dp_permute(): return lax.ppermute(value, 'dp', pairs)  41.1 us
  transfers between devices with their start and end apart: 18, of which 14 were waited for; matrix products, arithmetic and copies ran while one was open for 4% of the time, Pallas kernels for 0%

profile of v16, /device:TPU:129, one launch (start us, length us, event | category | flops | bytes accessed | tf_op | source)
XLA Modules:
  0.0 196.9 jit_solution(18312070971248920577)
XLA Ops:
  0.8 1.1 pad_maximum_fusion.2
  1.9 3.7 %collective-permute-start.2 = (bf16[400,640]{1,0:T(8,128)(2,1)S(1)}, bf16[400,640]{1,0:T(8,128)(2,1)S(1)}, u32[]{:S(2)}, u32[]{:S(2)}) collective-permute-start(bf16[400,640]{1,0:T(8,128)(2,1)S(1)} %pad_maximum_fusion.2), channel_id=1, source_target_pairs={{0,18},{6,24},{12,30},{18,36},{24,42},{30,48},{36,54},{42,60},{48,... | collective-permute-start | bytes 1536008 | tf_op jit(solution)/shard_map/ppermute | solution.py:15
  5.6 12.5 %collective-permute-start.1 = (bf16[400,640]{1,0:T(8,128)(2,1)S(1)}, bf16[400,640]{1,0:T(8,128)(2,1)S(1)}, u32[]{:S(2)}, u32[]{:S(2)}) collective-permute-start(bf16[400,640]{1,0:T(8,128)(2,1)S(1)} %pad_maximum_fusion.2), channel_id=1, source_target_pairs={{0,24},{6,18},{12,36},{18,30},{24,48},{30,42},{36,60},{42,54},{48,... | collective-permute-start | bytes 1536008 | tf_op jit(solution)/shard_map/ppermute | solution.py:15
  20.9 2.0 %collective-permute-start = (f32[4,64]{1,0:T(4,128)S(1)}, f32[4,64]{1,0:T(4,128)S(1)}, u32[]{:S(2)}, u32[]{:S(2)}) collective-permute-start(f32[4,64]{1,0:T(4,128)S(1)} %fusion.43), channel_id=1, source_target_pairs={{0,6},{6,0},{12,18},{18,12},{24,30},{30,24},{36,42},{42,36},{48,54... | collective-permute-start | bytes 3080 | tf_op jit(solution)/shard_map/ppermute | solution.py:15
  22.9 2.3 %collective-permute-start.3 = (bf16[400,640]{1,0:T(8,128)(2,1)S(1)}, bf16[400,640]{1,0:T(8,128)(2,1)S(1)}, u32[]{:S(2)}, u32[]{:S(2)}) collective-permute-start(bf16[400,640]{1,0:T(8,128)(2,1)S(1)} %pad_maximum_fusion.2), channel_id=1, source_target_pairs={{0,6},{6,0},{12,18},{18,12},{24,30},{30,24},{36,42},{42,36},{48,54... | collective-permute-start | bytes 1536008 | tf_op jit(solution)/shard_map/ppermute | solution.py:15
  25.7 17.7 %collective-permute-done.1 = bf16[400,640]{1,0:T(8,128)(2,1)S(1)} collective-permute-done((bf16[400,640]{1,0:T(8,128)(2,1)S(1)}, bf16[400,640]{1,0:T(8,128)(2,1)S(1)}, u32[]{:S(2)}, u32[]{:S(2)}) %collective-permute-start.1) | collective-permute-done | bytes 512032 | tf_op jit(solution)/shard_map/ppermute | solution.py:15
  45.9 1.9 collective-permute-start.4
  47.9 13.7 %collective-permute-start.5 = (f32[2,64,768]{2,1,0:T(8,128)S(1)}, f32[2,64,768]{2,1,0:T(8,128)S(1)}, u32[]{:S(2)}, u32[]{:S(2)}) collective-permute-start(f32[2,64,768]{2,1,0:T(8,128)S(1)} %pad_maximum_fusion.4), channel_id=1, source_target_pairs={{0,1},{1,0},{2,3},{3,2},{4,5},{5,4},{6,8},{7,6},{8,7},{9,11},{10,9... | collective-permute-start | bytes 1179656 | tf_op jit(solution)/shard_map/ppermute | solution.py:59
  63.5 1.6 collective-permute-done.4
  65.1 7.7 %collective-permute-done.5 = f32[2,64,768]{2,1,0:T(8,128)S(1)} collective-permute-done((f32[2,64,768]{2,1,0:T(8,128)S(1)}, f32[2,64,768]{2,1,0:T(8,128)S(1)}, u32[]{:S(2)}, u32[]{:S(2)}) %collective-permute-start.5) | collective-permute-done | bytes 393248 | tf_op jit(solution)/shard_map/ppermute | solution.py:59
  72.9 4.3 %collective-permute-start.6 = (f32[2,64,768]{2,1,0:T(8,128)S(1)}, f32[2,64,768]{2,1,0:T(8,128)S(1)}, u32[]{:S(2)}, u32[]{:S(2)}) collective-permute-start(f32[2,64,768]{2,1,0:T(8,128)S(1)} %get-tuple-element.32), channel_id=1, source_target_pairs={{0,1},{1,0},{2,3},{3,2},{4,5},{5,4},{6,9},{7,10},{8,11},{9,6},{10,... | collective-permute-start | bytes 1179656 | tf_op jit(solution)/shard_map/ppermute | solution.py:59
  77.3 1.9 collective-permute-start.7
  79.2 3.6 %collective-permute-start.8 = (f32[2,64,768]{2,1,0:T(8,128)S(1)}, f32[2,64,768]{2,1,0:T(8,128)S(1)}, u32[]{:S(2)}, u32[]{:S(2)}) collective-permute-start(f32[2,64,768]{2,1,0:T(8,128)S(1)} %get-tuple-element.34), channel_id=1, source_target_pairs={{0,4},{1,5},{2,0},{3,1},{4,2},{5,3},{6,8},{7,6},{8,7},{9,11},{10,9... | collective-permute-start | bytes 1179656 | tf_op jit(solution)/shard_map/ppermute | solution.py:59
  82.9 20.3 %collective-permute-done.6 = f32[2,64,768]{2,1,0:T(8,128)S(1)} collective-permute-done((f32[2,64,768]{2,1,0:T(8,128)S(1)}, f32[2,64,768]{2,1,0:T(8,128)S(1)}, u32[]{:S(2)}, u32[]{:S(2)}) %collective-permute-start.6) | collective-permute-done | bytes 393248 | tf_op jit(solution)/shard_map/ppermute | solution.py:59
  103.2 2.3 %collective-permute-done.7 = f32[2,64,768]{2,1,0:T(8,128)S(1)} collective-permute-done((f32[2,64,768]{2,1,0:T(8,128)S(1)}, f32[2,64,768]{2,1,0:T(8,128)S(1)}, u32[]{:S(2)}, u32[]{:S(2)}) %collective-permute-start.7) | collective-permute-done | bytes 393248 | tf_op jit(solution)/shard_map/ppermute | solution.py:59
  105.5 4.0 %collective-permute-done.8 = f32[2,64,768]{2,1,0:T(8,128)S(1)} collective-permute-done((f32[2,64,768]{2,1,0:T(8,128)S(1)}, f32[2,64,768]{2,1,0:T(8,128)S(1)}, u32[]{:S(2)}, u32[]{:S(2)}) %collective-permute-start.8) | collective-permute-done | bytes 393248 | tf_op jit(solution)/shard_map/ppermute | solution.py:59
  110.1 5.6 %collective-permute-start.9 = (f32[2,4,64]{2,0,1:T(2,128)S(1)}, f32[2,4,64]{2,0,1:T(2,128)S(1)}, u32[]{:S(2)}, u32[]{:S(2)}) collective-permute-start(f32[2,4,64]{2,0,1:T(2,128)S(1)} %pad_maximum_fusion.8), channel_id=1, source_target_pairs={{0,6},{6,0},{12,18},{18,12},{24,30},{30,24},{36,42},{42,36},{48,54... | collective-permute-start | bytes 6152 | tf_op jit(solution)/shard_map/ppermute | solution.py:15
  116.9 6.5 %collective-permute-start.10 = (bf16[2,64,768]{2,1,0:T(8,128)(2,1)S(1)}, bf16[2,64,768]{2,1,0:T(8,128)(2,1)S(1)}, u32[]{:S(2)}, u32[]{:S(2)}) collective-permute-start(bf16[2,64,768]{2,1,0:T(8,128)(2,1)S(1)} %get-tuple-element.44), channel_id=1, source_target_pairs={{0,1},{1,0},{2,3},{3,2},{4,5},{5,4},{6,9},{7,10},{8,11},{9,6},{10,... | collective-permute-start | bytes 589832 | tf_op jit(solution)/shard_map/ppermute | solution.py:59
  123.4 1.9 collective-permute-start.11
  125.3 3.4 %collective-permute-start.12 = (bf16[2,64,768]{2,1,0:T(8,128)(2,1)S(1)}, bf16[2,64,768]{2,1,0:T(8,128)(2,1)S(1)}, u32[]{:S(2)}, u32[]{:S(2)}) collective-permute-start(bf16[2,64,768]{2,1,0:T(8,128)(2,1)S(1)} %get-tuple-element.44), channel_id=1, source_target_pairs={{0,4},{1,5},{2,0},{3,1},{4,2},{5,3},{6,8},{7,6},{8,7},{9,11},{10,9... | collective-permute-start | bytes 589832 | tf_op jit(solution)/shard_map/ppermute | solution.py:59
  128.7 1.8 collective-permute-done.10
  130.5 6.9 %collective-permute-done.11 = bf16[2,64,768]{2,1,0:T(8,128)(2,1)S(1)} collective-permute-done((bf16[2,64,768]{2,1,0:T(8,128)(2,1)S(1)}, bf16[2,64,768]{2,1,0:T(8,128)(2,1)S(1)}, u32[]{:S(2)}, u32[]{:S(2)}) %collective-permute-start.11) | collective-permute-done | bytes 196640 | tf_op jit(solution)/shard_map/ppermute | solution.py:59
  137.4 1.3 collective-permute-done.12
  138.7 1.9 collective-permute-start.13
  140.7 3.8 %collective-permute-start.14 = (bf16[2,64,768]{2,1,0:T(8,128)(2,1)S(1)}, bf16[2,64,768]{2,1,0:T(8,128)(2,1)S(1)}, u32[]{:S(2)}, u32[]{:S(2)}) collective-permute-start(bf16[2,64,768]{2,1,0:T(8,128)(2,1)S(1)} %get-tuple-element.77), channel_id=1, source_target_pairs={{0,1},{1,0},{2,3},{3,2},{4,5},{5,4},{6,8},{7,6},{8,7},{9,11},{10,9... | collective-permute-start | bytes 589832 | tf_op jit(solution)/shard_map/ppermute | solution.py:59
  144.5 1.1 collective-permute-done.13
  145.6 7.2 %collective-permute-done.14 = bf16[2,64,768]{2,1,0:T(8,128)(2,1)S(1)} collective-permute-done((bf16[2,64,768]{2,1,0:T(8,128)(2,1)S(1)}, bf16[2,64,768]{2,1,0:T(8,128)(2,1)S(1)}, u32[]{:S(2)}, u32[]{:S(2)}) %collective-permute-start.14) | collective-permute-done | bytes 196640 | tf_op jit(solution)/shard_map/ppermute | solution.py:59
  154.0 7.2 %collective-permute-start.16 = (bf16[384,640]{1,0:T(8,128)(2,1)S(1)}, bf16[384,640]{1,0:T(8,128)(2,1)S(1)}, u32[]{:S(2)}, u32[]{:S(2)}) collective-permute-start(bf16[384,640]{1,0:T(8,128)(2,1)S(1)} %convolution_convert_fusion), channel_id=1, source_target_pairs={{24,0},{18,6},{36,12},{30,18},{48,24},{42,30},{60,36},{54,42},{72,... | collective-permute-start | bytes 1474568 | tf_op jit(solution)/shard_map/ppermute | solution.py:15
  162.3 6.0 %collective-permute-start.15 = (bf16[384,640]{1,0:T(8,128)(2,1)S(1)}, bf16[384,640]{1,0:T(8,128)(2,1)S(1)}, u32[]{:S(2)}, u32[]{:S(2)}) collective-permute-start(bf16[384,640]{1,0:T(8,128)(2,1)S(1)} %fusion), channel_id=1, source_target_pairs={{24,0},{18,6},{36,12},{30,18},{48,24},{42,30},{60,36},{54,42},{72,... | collective-permute-start | bytes 1474568 | tf_op jit(solution)/shard_map/ppermute | solution.py:15
  168.2 21.9 %collective-permute-done.16 = bf16[384,640]{1,0:T(8,128)(2,1)S(1)} collective-permute-done((bf16[384,640]{1,0:T(8,128)(2,1)S(1)}, bf16[384,640]{1,0:T(8,128)(2,1)S(1)}, u32[]{:S(2)}, u32[]{:S(2)}) %collective-permute-start.16) | collective-permute-done | bytes 491552 | tf_op jit(solution)/shard_map/ppermute | solution.py:15
  190.2 1.9 collective-permute-start.17
  192.8 3.2 %collective-permute-done.15 = bf16[384,640]{1,0:T(8,128)(2,1)S(1)} collective-permute-done((bf16[384,640]{1,0:T(8,128)(2,1)S(1)}, bf16[384,640]{1,0:T(8,128)(2,1)S(1)}, u32[]{:S(2)}, u32[]{:S(2)}) %collective-permute-start.15) | collective-permute-done | bytes 491552 | tf_op jit(solution)/shard_map/ppermute | solution.py:15
  (85 shorter events, 14.0 us)
Async XLA Ops:
  0.0 25.6 %copy-start = (bf16[384,640]{1,0:T(8,128)(2,1)S(1)}, bf16[384,640]{1,0:T(8,128)(2,1)}, u32[]{:S(2)}) copy-start(bf16[384,640]{1,0:T(8,128)(2,1)} %param.6) | copy-start | bytes 1474564
  1.9 41.7 %collective-permute-start.2 = (bf16[400,640]{1,0:T(8,128)(2,1)S(1)}, bf16[400,640]{1,0:T(8,128)(2,1)S(1)}, u32[]{:S(2)}, u32[]{:S(2)}) collective-permute-start(bf16[400,640]{1,0:T(8,128)(2,1)S(1)} %pad_maximum_fusion.2), channel_id=1, source_target_pairs={{0,18},{6,24},{12,30},{18,36},{24,42},{30,48},{36,54},{42,60},{48,... | collective-permute-start | bytes 1536008 | tf_op jit(solution)/shard_map/ppermute | solution.py:15
  5.6 37.8 %collective-permute-start.1 = (bf16[400,640]{1,0:T(8,128)(2,1)S(1)}, bf16[400,640]{1,0:T(8,128)(2,1)S(1)}, u32[]{:S(2)}, u32[]{:S(2)}) collective-permute-start(bf16[400,640]{1,0:T(8,128)(2,1)S(1)} %pad_maximum_fusion.2), channel_id=1, source_target_pairs={{0,24},{6,18},{12,36},{18,30},{24,48},{30,42},{36,60},{42,54},{48,... | collective-permute-start | bytes 1536008 | tf_op jit(solution)/shard_map/ppermute | solution.py:15
  20.9 4.8 %collective-permute-start = (f32[4,64]{1,0:T(4,128)S(1)}, f32[4,64]{1,0:T(4,128)S(1)}, u32[]{:S(2)}, u32[]{:S(2)}) collective-permute-start(f32[4,64]{1,0:T(4,128)S(1)} %fusion.43), channel_id=1, source_target_pairs={{0,6},{6,0},{12,18},{18,12},{24,30},{30,24},{36,42},{42,36},{48,54... | collective-permute-start | bytes 3080 | tf_op jit(solution)/shard_map/ppermute | solution.py:15
  22.9 22.3 %collective-permute-start.3 = (bf16[400,640]{1,0:T(8,128)(2,1)S(1)}, bf16[400,640]{1,0:T(8,128)(2,1)S(1)}, u32[]{:S(2)}, u32[]{:S(2)}) collective-permute-start(bf16[400,640]{1,0:T(8,128)(2,1)S(1)} %pad_maximum_fusion.2), channel_id=1, source_target_pairs={{0,6},{6,0},{12,18},{18,12},{24,30},{30,24},{36,42},{42,36},{48,54... | collective-permute-start | bytes 1536008 | tf_op jit(solution)/shard_map/ppermute | solution.py:15
  43.5 0.8 copy-start.1
  43.6 1.0 copy-start.2
  44.5 0.7 slice-start.1
  44.5 0.7 slice-start
  45.9 19.2 %collective-permute-start.4 = (f32[2,64,768]{2,1,0:T(8,128)S(1)}, f32[2,64,768]{2,1,0:T(8,128)S(1)}, u32[]{:S(2)}, u32[]{:S(2)}) collective-permute-start(f32[2,64,768]{2,1,0:T(8,128)S(1)} %pad_maximum_fusion.3), channel_id=1, source_target_pairs={{0,1},{1,0},{2,3},{3,2},{4,5},{5,4},{6,7},{7,8},{8,6},{9,10},{10,1... | collective-permute-start | bytes 1179656 | tf_op jit(solution)/shard_map/ppermute | solution.py:59
  47.9 24.9 %collective-permute-start.5 = (f32[2,64,768]{2,1,0:T(8,128)S(1)}, f32[2,64,768]{2,1,0:T(8,128)S(1)}, u32[]{:S(2)}, u32[]{:S(2)}) collective-permute-start(f32[2,64,768]{2,1,0:T(8,128)S(1)} %pad_maximum_fusion.4), channel_id=1, source_target_pairs={{0,1},{1,0},{2,3},{3,2},{4,5},{5,4},{6,8},{7,6},{8,7},{9,11},{10,9... | collective-permute-start | bytes 1179656 | tf_op jit(solution)/shard_map/ppermute | solution.py:59
  72.9 30.3 %collective-permute-start.6 = (f32[2,64,768]{2,1,0:T(8,128)S(1)}, f32[2,64,768]{2,1,0:T(8,128)S(1)}, u32[]{:S(2)}, u32[]{:S(2)}) collective-permute-start(f32[2,64,768]{2,1,0:T(8,128)S(1)} %get-tuple-element.32), channel_id=1, source_target_pairs={{0,1},{1,0},{2,3},{3,2},{4,5},{5,4},{6,9},{7,10},{8,11},{9,6},{10,... | collective-permute-start | bytes 1179656 | tf_op jit(solution)/shard_map/ppermute | solution.py:59
  77.3 28.2 %collective-permute-start.7 = (f32[2,64,768]{2,1,0:T(8,128)S(1)}, f32[2,64,768]{2,1,0:T(8,128)S(1)}, u32[]{:S(2)}, u32[]{:S(2)}) collective-permute-start(f32[2,64,768]{2,1,0:T(8,128)S(1)} %get-tuple-element.33), channel_id=1, source_target_pairs={{0,2},{1,3},{2,4},{3,5},{4,0},{5,1},{6,7},{7,8},{8,6},{9,10},{10,1... | collective-permute-start | bytes 1179656 | tf_op jit(solution)/shard_map/ppermute | solution.py:59
  79.2 30.3 %collective-permute-start.8 = (f32[2,64,768]{2,1,0:T(8,128)S(1)}, f32[2,64,768]{2,1,0:T(8,128)S(1)}, u32[]{:S(2)}, u32[]{:S(2)}) collective-permute-start(f32[2,64,768]{2,1,0:T(8,128)S(1)} %get-tuple-element.34), channel_id=1, source_target_pairs={{0,4},{1,5},{2,0},{3,1},{4,2},{5,3},{6,8},{7,6},{8,7},{9,11},{10,9... | collective-permute-start | bytes 1179656 | tf_op jit(solution)/shard_map/ppermute | solution.py:59
  110.1 6.4 %collective-permute-start.9 = (f32[2,4,64]{2,0,1:T(2,128)S(1)}, f32[2,4,64]{2,0,1:T(2,128)S(1)}, u32[]{:S(2)}, u32[]{:S(2)}) collective-permute-start(f32[2,4,64]{2,0,1:T(2,128)S(1)} %pad_maximum_fusion.8), channel_id=1, source_target_pairs={{0,6},{6,0},{12,18},{18,12},{24,30},{30,24},{36,42},{42,36},{48,54... | collective-permute-start | bytes 6152 | tf_op jit(solution)/shard_map/ppermute | solution.py:15
  116.9 13.6 %collective-permute-start.10 = (bf16[2,64,768]{2,1,0:T(8,128)(2,1)S(1)}, bf16[2,64,768]{2,1,0:T(8,128)(2,1)S(1)}, u32[]{:S(2)}, u32[]{:S(2)}) collective-permute-start(bf16[2,64,768]{2,1,0:T(8,128)(2,1)S(1)} %get-tuple-element.44), channel_id=1, source_target_pairs={{0,1},{1,0},{2,3},{3,2},{4,5},{5,4},{6,9},{7,10},{8,11},{9,6},{10,... | collective-permute-start | bytes 589832 | tf_op jit(solution)/shard_map/ppermute | solution.py:59
  123.4 14.0 %collective-permute-start.11 = (bf16[2,64,768]{2,1,0:T(8,128)(2,1)S(1)}, bf16[2,64,768]{2,1,0:T(8,128)(2,1)S(1)}, u32[]{:S(2)}, u32[]{:S(2)}) collective-permute-start(bf16[2,64,768]{2,1,0:T(8,128)(2,1)S(1)} %get-tuple-element.44), channel_id=1, source_target_pairs={{0,2},{1,3},{2,4},{3,5},{4,0},{5,1},{6,7},{7,8},{8,6},{9,10},{10,1... | collective-permute-start | bytes 589832 | tf_op jit(solution)/shard_map/ppermute | solution.py:59
  125.3 13.3 %collective-permute-start.12 = (bf16[2,64,768]{2,1,0:T(8,128)(2,1)S(1)}, bf16[2,64,768]{2,1,0:T(8,128)(2,1)S(1)}, u32[]{:S(2)}, u32[]{:S(2)}) collective-permute-start(bf16[2,64,768]{2,1,0:T(8,128)(2,1)S(1)} %get-tuple-element.44), channel_id=1, source_target_pairs={{0,4},{1,5},{2,0},{3,1},{4,2},{5,3},{6,8},{7,6},{8,7},{9,11},{10,9... | collective-permute-start | bytes 589832 | tf_op jit(solution)/shard_map/ppermute | solution.py:59
  138.7 6.9 %collective-permute-start.13 = (bf16[2,64,768]{2,1,0:T(8,128)(2,1)S(1)}, bf16[2,64,768]{2,1,0:T(8,128)(2,1)S(1)}, u32[]{:S(2)}, u32[]{:S(2)}) collective-permute-start(bf16[2,64,768]{2,1,0:T(8,128)(2,1)S(1)} %get-tuple-element.78), channel_id=1, source_target_pairs={{0,1},{1,0},{2,3},{3,2},{4,5},{5,4},{6,7},{7,8},{8,6},{9,10},{10,1... | collective-permute-start | bytes 589832 | tf_op jit(solution)/shard_map/ppermute | solution.py:59
  140.7 12.1 %collective-permute-start.14 = (bf16[2,64,768]{2,1,0:T(8,128)(2,1)S(1)}, bf16[2,64,768]{2,1,0:T(8,128)(2,1)S(1)}, u32[]{:S(2)}, u32[]{:S(2)}) collective-permute-start(bf16[2,64,768]{2,1,0:T(8,128)(2,1)S(1)} %get-tuple-element.77), channel_id=1, source_target_pairs={{0,1},{1,0},{2,3},{3,2},{4,5},{5,4},{6,8},{7,6},{8,7},{9,11},{10,9... | collective-permute-start | bytes 589832 | tf_op jit(solution)/shard_map/ppermute | solution.py:59
  154.0 36.1 %collective-permute-start.16 = (bf16[384,640]{1,0:T(8,128)(2,1)S(1)}, bf16[384,640]{1,0:T(8,128)(2,1)S(1)}, u32[]{:S(2)}, u32[]{:S(2)}) collective-permute-start(bf16[384,640]{1,0:T(8,128)(2,1)S(1)} %convolution_convert_fusion), channel_id=1, source_target_pairs={{24,0},{18,6},{36,12},{30,18},{48,24},{42,30},{60,36},{54,42},{72,... | collective-permute-start | bytes 1474568 | tf_op jit(solution)/shard_map/ppermute | solution.py:15
  162.3 33.7 %collective-permute-start.15 = (bf16[384,640]{1,0:T(8,128)(2,1)S(1)}, bf16[384,640]{1,0:T(8,128)(2,1)S(1)}, u32[]{:S(2)}, u32[]{:S(2)}) collective-permute-start(bf16[384,640]{1,0:T(8,128)(2,1)S(1)} %fusion), channel_id=1, source_target_pairs={{24,0},{18,6},{36,12},{30,18},{48,24},{42,30},{60,36},{54,42},{72,... | collective-permute-start | bytes 1474568 | tf_op jit(solution)/shard_map/ppermute | solution.py:15
  190.2 5.8 %collective-permute-start.17 = (bf16[384,640]{1,0:T(8,128)(2,1)S(1)}, bf16[384,640]{1,0:T(8,128)(2,1)S(1)}, u32[]{:S(2)}, u32[]{:S(2)}) collective-permute-start(bf16[384,640]{1,0:T(8,128)(2,1)S(1)} %add_convert_fusion.1), channel_id=1, source_target_pairs={{0,6},{6,0},{12,18},{18,12},{24,30},{30,24},{36,42},{42,36},{48,54... | collective-permute-start | bytes 1474568 | tf_op jit(solution)/shard_map/ppermute | solution.py:15

commit v17 on v16

--- a/solution.py
+++ b/solution.py
@@ -125,7 +125,7 @@
     score_scale = 1.0 / math.sqrt(KW)
     core = lax.axis_index("dp") % 2
     r = lax.axis_index("tensor")
-    payload = with_codes(hidden, targets, padding)
+    payload = lax.optimization_barrier(with_codes(hidden, targets, padding))
 
     key_one = dp_permute(payload, key_pairs())
     key_two = dp_permute(payload, crossed_pairs())
@@ -165,11 +165,10 @@
         owner(lambda q: beside(stride(1)(q)), lambda q: across(triple(1)(q))),
         owner(lambda q: beside(stride(2)(q)), lambda q: across(triple(2)(q))),
     ]
-    own = payload[:SEG]
-    own_sent = products(own, keys[0], *ahead)
+    own_sent = products(payload, keys[0], *ahead)
     own_sent, pair_hidden = lax.optimization_barrier((own_sent, pair_hidden))
     sent = blocks(own_sent, products(pair_hidden, keys[1], *ahead))
-    *sent, own, pair = lax.optimization_barrier(sent + (own, pair_hidden))
+    *sent, own, pair = lax.optimization_barrier(sent + (hidden, pair_hidden))
     in_one = line_permute(sent[0], beside, triple(1))
     in_two = line_permute(sent[1], beside, triple(2))
     ends = (owner(stride(1), triple(1)), owner(stride(2), triple(2)))

time: 198 us -> 198 us (level)
  the two profiles are of different devices: /device:TPU:129 before, /device:TPU:27 now
where the time goes in v17:
time: 198 us; the launch traced here: 197 us
  starting transfers between devices  110 us (56%)
  waiting for transfers between devices  72.1 us (36%)
  other arithmetic  5.71 us (3%)
  matrix products  5.34 us (3%)
  local copies, waits for them, and re-layouts  3.08 us (2%)
    ppermute x10, starting transfers between devices, line_permute(): return lax.ppermute(value, ('dp', 'tensor'), pairs)  65.1 us
    ppermute x8, starting transfers between devices, dp_permute(): return lax.ppermute(value, 'dp', pairs)  44.5 us
    ppermute x10, waiting for transfers between devices, line_permute(): return lax.ppermute(value, ('dp', 'tensor'), pairs)  44.2 us
    ppermute x8, waiting for transfers between devices, dp_permute(): return lax.ppermute(value, 'dp', pairs)  27.9 us
  transfers between devices with their start and end apart: 18, of which 11 were waited for; matrix products, arithmetic and copies ran while one was open for 4% of the time, Pallas kernels for 0%

profile of v17, /device:TPU:27, one launch (start us, length us, event | category | flops | bytes accessed | tf_op | source)
XLA Modules:
  0.0 196.9 jit_solution(17638376202216169703)
XLA Ops:
  0.0 0.7 shift-right-arithmetic_convert_fusion
  0.7 1.1 pad_maximum_fusion.2
  1.8 3.7 %collective-permute-start.2 = (bf16[400,640]{1,0:T(8,128)(2,1)S(1)}, bf16[400,640]{1,0:T(8,128)(2,1)S(1)}, u32[]{:S(2)}, u32[]{:S(2)}) collective-permute-start(bf16[400,640]{1,0:T(8,128)(2,1)S(1)} %pad_maximum_fusion.2), channel_id=1, source_target_pairs={{0,18},{6,24},{12,30},{18,36},{24,42},{30,48},{36,54},{42,60},{48,... | collective-permute-start | bytes 1536008 | tf_op jit(solution)/shard_map/ppermute | solution.py:15
  5.5 14.9 %collective-permute-start.1 = (bf16[400,640]{1,0:T(8,128)(2,1)S(1)}, bf16[400,640]{1,0:T(8,128)(2,1)S(1)}, u32[]{:S(2)}, u32[]{:S(2)}) collective-permute-start(bf16[400,640]{1,0:T(8,128)(2,1)S(1)} %pad_maximum_fusion.2), channel_id=1, source_target_pairs={{0,24},{6,18},{12,36},{18,30},{24,48},{30,42},{36,60},{42,54},{48,... | collective-permute-start | bytes 1536008 | tf_op jit(solution)/shard_map/ppermute | solution.py:15
  23.3 2.0 %collective-permute-start = (f32[4,64]{1,0:T(4,128)S(1)}, f32[4,64]{1,0:T(4,128)S(1)}, u32[]{:S(2)}, u32[]{:S(2)}) collective-permute-start(f32[4,64]{1,0:T(4,128)S(1)} %fusion.43), channel_id=1, source_target_pairs={{0,6},{6,0},{12,18},{18,12},{24,30},{30,24},{36,42},{42,36},{48,54... | collective-permute-start | bytes 3080 | tf_op jit(solution)/shard_map/ppermute | solution.py:15
  25.3 2.3 %collective-permute-start.3 = (bf16[400,640]{1,0:T(8,128)(2,1)S(1)}, bf16[400,640]{1,0:T(8,128)(2,1)S(1)}, u32[]{:S(2)}, u32[]{:S(2)}) collective-permute-start(bf16[400,640]{1,0:T(8,128)(2,1)S(1)} %pad_maximum_fusion.2), channel_id=1, source_target_pairs={{0,6},{6,0},{12,18},{18,12},{24,30},{30,24},{36,42},{42,36},{48,54... | collective-permute-start | bytes 1536008 | tf_op jit(solution)/shard_map/ppermute | solution.py:15
  28.1 2.4 %collective-permute-done.1 = bf16[400,640]{1,0:T(8,128)(2,1)S(1)} collective-permute-done((bf16[400,640]{1,0:T(8,128)(2,1)S(1)}, bf16[400,640]{1,0:T(8,128)(2,1)S(1)}, u32[]{:S(2)}, u32[]{:S(2)}) %collective-permute-start.1) | collective-permute-done | bytes 512032 | tf_op jit(solution)/shard_map/ppermute | solution.py:15
  32.9 24.2 %collective-permute-start.4 = (f32[2,64,768]{2,1,0:T(8,128)S(1)}, f32[2,64,768]{2,1,0:T(8,128)S(1)}, u32[]{:S(2)}, u32[]{:S(2)}) collective-permute-start(f32[2,64,768]{2,1,0:T(8,128)S(1)} %pad_maximum_fusion.3), channel_id=1, source_target_pairs={{0,1},{1,0},{2,3},{3,2},{4,5},{5,4},{6,7},{7,8},{8,6},{9,10},{10,1... | collective-permute-start | bytes 1179656 | tf_op jit(solution)/shard_map/ppermute | solution.py:59
  57.0 1.9 collective-permute-start.5
  60.9 3.6 %collective-permute-done.4 = f32[2,64,768]{2,1,0:T(8,128)S(1)} collective-permute-done((f32[2,64,768]{2,1,0:T(8,128)S(1)}, f32[2,64,768]{2,1,0:T(8,128)S(1)}, u32[]{:S(2)}, u32[]{:S(2)}) %collective-permute-start.4) | collective-permute-done | bytes 393248 | tf_op jit(solution)/shard_map/ppermute | solution.py:59
  64.5 4.7 %collective-permute-done.5 = f32[2,64,768]{2,1,0:T(8,128)S(1)} collective-permute-done((f32[2,64,768]{2,1,0:T(8,128)S(1)}, f32[2,64,768]{2,1,0:T(8,128)S(1)}, u32[]{:S(2)}, u32[]{:S(2)}) %collective-permute-start.5) | collective-permute-done | bytes 393248 | tf_op jit(solution)/shard_map/ppermute | solution.py:59
  69.3 5.5 %collective-permute-start.6 = (f32[2,64,768]{2,1,0:T(8,128)S(1)}, f32[2,64,768]{2,1,0:T(8,128)S(1)}, u32[]{:S(2)}, u32[]{:S(2)}) collective-permute-start(f32[2,64,768]{2,1,0:T(8,128)S(1)} %get-tuple-element.32), channel_id=1, source_target_pairs={{0,1},{1,0},{2,3},{3,2},{4,5},{5,4},{6,9},{7,10},{8,11},{9,6},{10,... | collective-permute-start | bytes 1179656 | tf_op jit(solution)/shard_map/ppermute | solution.py:59
  74.9 8.2 %collective-permute-start.7 = (f32[2,64,768]{2,1,0:T(8,128)S(1)}, f32[2,64,768]{2,1,0:T(8,128)S(1)}, u32[]{:S(2)}, u32[]{:S(2)}) collective-permute-start(f32[2,64,768]{2,1,0:T(8,128)S(1)} %get-tuple-element.33), channel_id=1, source_target_pairs={{0,2},{1,3},{2,4},{3,5},{4,0},{5,1},{6,7},{7,8},{8,6},{9,10},{10,1... | collective-permute-start | bytes 1179656 | tf_op jit(solution)/shard_map/ppermute | solution.py:59
  83.1 1.9 collective-permute-start.8
  85.2 21.2 %collective-permute-done.7 = f32[2,64,768]{2,1,0:T(8,128)S(1)} collective-permute-done((f32[2,64,768]{2,1,0:T(8,128)S(1)}, f32[2,64,768]{2,1,0:T(8,128)S(1)}, u32[]{:S(2)}, u32[]{:S(2)}) %collective-permute-start.7) | collective-permute-done | bytes 393248 | tf_op jit(solution)/shard_map/ppermute | solution.py:59
  107.0 7.0 %collective-permute-start.9 = (f32[2,4,64]{2,0,1:T(2,128)S(1)}, f32[2,4,64]{2,0,1:T(2,128)S(1)}, u32[]{:S(2)}, u32[]{:S(2)}) collective-permute-start(f32[2,4,64]{2,0,1:T(2,128)S(1)} %pad_maximum_fusion.8), channel_id=1, source_target_pairs={{0,6},{6,0},{12,18},{18,12},{24,30},{30,24},{36,42},{42,36},{48,54... | collective-permute-start | bytes 6152 | tf_op jit(solution)/shard_map/ppermute | solution.py:15
  114.0 0.8 collective-permute-done.9
  115.2 7.2 %collective-permute-start.10 = (bf16[2,64,768]{2,1,0:T(8,128)(2,1)S(1)}, bf16[2,64,768]{2,1,0:T(8,128)(2,1)S(1)}, u32[]{:S(2)}, u32[]{:S(2)}) collective-permute-start(bf16[2,64,768]{2,1,0:T(8,128)(2,1)S(1)} %get-tuple-element.44), channel_id=1, source_target_pairs={{0,1},{1,0},{2,3},{3,2},{4,5},{5,4},{6,9},{7,10},{8,11},{9,6},{10,... | collective-permute-start | bytes 589832 | tf_op jit(solution)/shard_map/ppermute | solution.py:59
  122.5 1.9 collective-permute-start.11
  124.4 5.9 %collective-permute-start.12 = (bf16[2,64,768]{2,1,0:T(8,128)(2,1)S(1)}, bf16[2,64,768]{2,1,0:T(8,128)(2,1)S(1)}, u32[]{:S(2)}, u32[]{:S(2)}) collective-permute-start(bf16[2,64,768]{2,1,0:T(8,128)(2,1)S(1)} %get-tuple-element.44), channel_id=1, source_target_pairs={{0,4},{1,5},{2,0},{3,1},{4,2},{5,3},{6,8},{7,6},{8,7},{9,11},{10,9... | collective-permute-start | bytes 589832 | tf_op jit(solution)/shard_map/ppermute | solution.py:59
  130.3 1.8 collective-permute-done.10
  132.1 6.1 %collective-permute-done.11 = bf16[2,64,768]{2,1,0:T(8,128)(2,1)S(1)} collective-permute-done((bf16[2,64,768]{2,1,0:T(8,128)(2,1)S(1)}, bf16[2,64,768]{2,1,0:T(8,128)(2,1)S(1)}, u32[]{:S(2)}, u32[]{:S(2)}) %collective-permute-start.11) | collective-permute-done | bytes 196640 | tf_op jit(solution)/shard_map/ppermute | solution.py:59
  138.3 6.3 %collective-permute-start.13 = (bf16[2,64,768]{2,1,0:T(8,128)(2,1)S(1)}, bf16[2,64,768]{2,1,0:T(8,128)(2,1)S(1)}, u32[]{:S(2)}, u32[]{:S(2)}) collective-permute-start(bf16[2,64,768]{2,1,0:T(8,128)(2,1)S(1)} %get-tuple-element.78), channel_id=1, source_target_pairs={{0,1},{1,0},{2,3},{3,2},{4,5},{5,4},{6,7},{7,8},{8,6},{9,10},{10,1... | collective-permute-start | bytes 589832 | tf_op jit(solution)/shard_map/ppermute | solution.py:59
  144.6 1.9 collective-permute-start.14
  146.6 2.6 %collective-permute-done.13 = bf16[2,64,768]{2,1,0:T(8,128)(2,1)S(1)} collective-permute-done((bf16[2,64,768]{2,1,0:T(8,128)(2,1)S(1)}, bf16[2,64,768]{2,1,0:T(8,128)(2,1)S(1)}, u32[]{:S(2)}, u32[]{:S(2)}) %collective-permute-start.13) | collective-permute-done | bytes 196640 | tf_op jit(solution)/shard_map/ppermute | solution.py:59
  149.2 4.3 %collective-permute-done.14 = bf16[2,64,768]{2,1,0:T(8,128)(2,1)S(1)} collective-permute-done((bf16[2,64,768]{2,1,0:T(8,128)(2,1)S(1)}, bf16[2,64,768]{2,1,0:T(8,128)(2,1)S(1)}, u32[]{:S(2)}, u32[]{:S(2)}) %collective-permute-start.14) | collective-permute-done | bytes 196640 | tf_op jit(solution)/shard_map/ppermute | solution.py:59
  154.7 1.9 collective-permute-start.16
  157.7 10.8 %collective-permute-start.15 = (bf16[384,640]{1,0:T(8,128)(2,1)S(1)}, bf16[384,640]{1,0:T(8,128)(2,1)S(1)}, u32[]{:S(2)}, u32[]{:S(2)}) collective-permute-start(bf16[384,640]{1,0:T(8,128)(2,1)S(1)} %fusion), channel_id=1, source_target_pairs={{24,0},{18,6},{36,12},{30,18},{48,24},{42,30},{60,36},{54,42},{72,... | collective-permute-start | bytes 1474568 | tf_op jit(solution)/shard_map/ppermute | solution.py:15
  168.5 8.8 %collective-permute-done.16 = bf16[384,640]{1,0:T(8,128)(2,1)S(1)} collective-permute-done((bf16[384,640]{1,0:T(8,128)(2,1)S(1)}, bf16[384,640]{1,0:T(8,128)(2,1)S(1)}, u32[]{:S(2)}, u32[]{:S(2)}) %collective-permute-start.16) | collective-permute-done | bytes 491552 | tf_op jit(solution)/shard_map/ppermute | solution.py:15
  177.4 1.9 collective-permute-start.17
  180.0 15.9 %collective-permute-done.15 = bf16[384,640]{1,0:T(8,128)(2,1)S(1)} collective-permute-done((bf16[384,640]{1,0:T(8,128)(2,1)S(1)}, bf16[384,640]{1,0:T(8,128)(2,1)S(1)}, u32[]{:S(2)}, u32[]{:S(2)}) %collective-permute-start.15) | collective-permute-done | bytes 491552 | tf_op jit(solution)/shard_map/ppermute | solution.py:15
  196.0 0.9 add_convert_fusion
  (85 shorter events, 11.5 us)
Async XLA Ops:
  1.8 28.7 %collective-permute-start.2 = (bf16[400,640]{1,0:T(8,128)(2,1)S(1)}, bf16[400,640]{1,0:T(8,128)(2,1)S(1)}, u32[]{:S(2)}, u32[]{:S(2)}) collective-permute-start(bf16[400,640]{1,0:T(8,128)(2,1)S(1)} %pad_maximum_fusion.2), channel_id=1, source_target_pairs={{0,18},{6,24},{12,30},{18,36},{24,42},{30,48},{36,54},{42,60},{48,... | collective-permute-start | bytes 1536008 | tf_op jit(solution)/shard_map/ppermute | solution.py:15
  5.5 24.9 %collective-permute-start.1 = (bf16[400,640]{1,0:T(8,128)(2,1)S(1)}, bf16[400,640]{1,0:T(8,128)(2,1)S(1)}, u32[]{:S(2)}, u32[]{:S(2)}) collective-permute-start(bf16[400,640]{1,0:T(8,128)(2,1)S(1)} %pad_maximum_fusion.2), channel_id=1, source_target_pairs={{0,24},{6,18},{12,36},{18,30},{24,48},{30,42},{36,60},{42,54},{48,... | collective-permute-start | bytes 1536008 | tf_op jit(solution)/shard_map/ppermute | solution.py:15
  23.3 4.8 %collective-permute-start = (f32[4,64]{1,0:T(4,128)S(1)}, f32[4,64]{1,0:T(4,128)S(1)}, u32[]{:S(2)}, u32[]{:S(2)}) collective-permute-start(f32[4,64]{1,0:T(4,128)S(1)} %fusion.43), channel_id=1, source_target_pairs={{0,6},{6,0},{12,18},{18,12},{24,30},{30,24},{36,42},{42,36},{48,54... | collective-permute-start | bytes 3080 | tf_op jit(solution)/shard_map/ppermute | solution.py:15
  25.3 6.9 %collective-permute-start.3 = (bf16[400,640]{1,0:T(8,128)(2,1)S(1)}, bf16[400,640]{1,0:T(8,128)(2,1)S(1)}, u32[]{:S(2)}, u32[]{:S(2)}) collective-permute-start(bf16[400,640]{1,0:T(8,128)(2,1)S(1)} %pad_maximum_fusion.2), channel_id=1, source_target_pairs={{0,6},{6,0},{12,18},{18,12},{24,30},{30,24},{36,42},{42,36},{48,54... | collective-permute-start | bytes 1536008 | tf_op jit(solution)/shard_map/ppermute | solution.py:15
  30.4 0.8 copy-start.1
  30.5 0.9 copy-start.2
  31.4 0.8 slice-start
  31.4 0.7 slice-start.1
  32.7 26.2 %copy-start = (bf16[384,640]{1,0:T(8,128)(2,1)S(1)}, bf16[384,640]{1,0:T(8,128)(2,1)}, u32[]{:S(2)}) copy-start(bf16[384,640]{1,0:T(8,128)(2,1)} %param.6) | copy-start | bytes 1474564
  32.9 31.7 %collective-permute-start.4 = (f32[2,64,768]{2,1,0:T(8,128)S(1)}, f32[2,64,768]{2,1,0:T(8,128)S(1)}, u32[]{:S(2)}, u32[]{:S(2)}) collective-permute-start(f32[2,64,768]{2,1,0:T(8,128)S(1)} %pad_maximum_fusion.3), channel_id=1, source_target_pairs={{0,1},{1,0},{2,3},{3,2},{4,5},{5,4},{6,7},{7,8},{8,6},{9,10},{10,1... | collective-permute-start | bytes 1179656 | tf_op jit(solution)/shard_map/ppermute | solution.py:59
  57.0 12.1 %collective-permute-start.5 = (f32[2,64,768]{2,1,0:T(8,128)S(1)}, f32[2,64,768]{2,1,0:T(8,128)S(1)}, u32[]{:S(2)}, u32[]{:S(2)}) collective-permute-start(f32[2,64,768]{2,1,0:T(8,128)S(1)} %pad_maximum_fusion.4), channel_id=1, source_target_pairs={{0,1},{1,0},{2,3},{3,2},{4,5},{5,4},{6,8},{7,6},{8,7},{9,11},{10,9... | collective-permute-start | bytes 1179656 | tf_op jit(solution)/shard_map/ppermute | solution.py:59
  69.3 15.8 %collective-permute-start.6 = (f32[2,64,768]{2,1,0:T(8,128)S(1)}, f32[2,64,768]{2,1,0:T(8,128)S(1)}, u32[]{:S(2)}, u32[]{:S(2)}) collective-permute-start(f32[2,64,768]{2,1,0:T(8,128)S(1)} %get-tuple-element.32), channel_id=1, source_target_pairs={{0,1},{1,0},{2,3},{3,2},{4,5},{5,4},{6,9},{7,10},{8,11},{9,6},{10,... | collective-permute-start | bytes 1179656 | tf_op jit(solution)/shard_map/ppermute | solution.py:59
  74.9 31.5 %collective-permute-start.7 = (f32[2,64,768]{2,1,0:T(8,128)S(1)}, f32[2,64,768]{2,1,0:T(8,128)S(1)}, u32[]{:S(2)}, u32[]{:S(2)}) collective-permute-start(f32[2,64,768]{2,1,0:T(8,128)S(1)} %get-tuple-element.33), channel_id=1, source_target_pairs={{0,2},{1,3},{2,4},{3,5},{4,0},{5,1},{6,7},{7,8},{8,6},{9,10},{10,1... | collective-permute-start | bytes 1179656 | tf_op jit(solution)/shard_map/ppermute | solution.py:59
  83.1 23.2 %collective-permute-start.8 = (f32[2,64,768]{2,1,0:T(8,128)S(1)}, f32[2,64,768]{2,1,0:T(8,128)S(1)}, u32[]{:S(2)}, u32[]{:S(2)}) collective-permute-start(f32[2,64,768]{2,1,0:T(8,128)S(1)} %get-tuple-element.34), channel_id=1, source_target_pairs={{0,4},{1,5},{2,0},{3,1},{4,2},{5,3},{6,8},{7,6},{8,7},{9,11},{10,9... | collective-permute-start | bytes 1179656 | tf_op jit(solution)/shard_map/ppermute | solution.py:59
  107.0 7.8 %collective-permute-start.9 = (f32[2,4,64]{2,0,1:T(2,128)S(1)}, f32[2,4,64]{2,0,1:T(2,128)S(1)}, u32[]{:S(2)}, u32[]{:S(2)}) collective-permute-start(f32[2,4,64]{2,0,1:T(2,128)S(1)} %pad_maximum_fusion.8), channel_id=1, source_target_pairs={{0,6},{6,0},{12,18},{18,12},{24,30},{30,24},{36,42},{42,36},{48,54... | collective-permute-start | bytes 6152 | tf_op jit(solution)/shard_map/ppermute | solution.py:15
  115.2 16.9 %collective-permute-start.10 = (bf16[2,64,768]{2,1,0:T(8,128)(2,1)S(1)}, bf16[2,64,768]{2,1,0:T(8,128)(2,1)S(1)}, u32[]{:S(2)}, u32[]{:S(2)}) collective-permute-start(bf16[2,64,768]{2,1,0:T(8,128)(2,1)S(1)} %get-tuple-element.44), channel_id=1, source_target_pairs={{0,1},{1,0},{2,3},{3,2},{4,5},{5,4},{6,9},{7,10},{8,11},{9,6},{10,... | collective-permute-start | bytes 589832 | tf_op jit(solution)/shard_map/ppermute | solution.py:59
  122.5 15.8 %collective-permute-start.11 = (bf16[2,64,768]{2,1,0:T(8,128)(2,1)S(1)}, bf16[2,64,768]{2,1,0:T(8,128)(2,1)S(1)}, u32[]{:S(2)}, u32[]{:S(2)}) collective-permute-start(bf16[2,64,768]{2,1,0:T(8,128)(2,1)S(1)} %get-tuple-element.44), channel_id=1, source_target_pairs={{0,2},{1,3},{2,4},{3,5},{4,0},{5,1},{6,7},{7,8},{8,6},{9,10},{10,1... | collective-permute-start | bytes 589832 | tf_op jit(solution)/shard_map/ppermute | solution.py:59
  124.4 13.8 %collective-permute-start.12 = (bf16[2,64,768]{2,1,0:T(8,128)(2,1)S(1)}, bf16[2,64,768]{2,1,0:T(8,128)(2,1)S(1)}, u32[]{:S(2)}, u32[]{:S(2)}) collective-permute-start(bf16[2,64,768]{2,1,0:T(8,128)(2,1)S(1)} %get-tuple-element.44), channel_id=1, source_target_pairs={{0,4},{1,5},{2,0},{3,1},{4,2},{5,3},{6,8},{7,6},{8,7},{9,11},{10,9... | collective-permute-start | bytes 589832 | tf_op jit(solution)/shard_map/ppermute | solution.py:59
  138.3 10.9 %collective-permute-start.13 = (bf16[2,64,768]{2,1,0:T(8,128)(2,1)S(1)}, bf16[2,64,768]{2,1,0:T(8,128)(2,1)S(1)}, u32[]{:S(2)}, u32[]{:S(2)}) collective-permute-start(bf16[2,64,768]{2,1,0:T(8,128)(2,1)S(1)} %get-tuple-element.78), channel_id=1, source_target_pairs={{0,1},{1,0},{2,3},{3,2},{4,5},{5,4},{6,7},{7,8},{8,6},{9,10},{10,1... | collective-permute-start | bytes 589832 | tf_op jit(solution)/shard_map/ppermute | solution.py:59
  144.6 8.9 %collective-permute-start.14 = (bf16[2,64,768]{2,1,0:T(8,128)(2,1)S(1)}, bf16[2,64,768]{2,1,0:T(8,128)(2,1)S(1)}, u32[]{:S(2)}, u32[]{:S(2)}) collective-permute-start(bf16[2,64,768]{2,1,0:T(8,128)(2,1)S(1)} %get-tuple-element.77), channel_id=1, source_target_pairs={{0,1},{1,0},{2,3},{3,2},{4,5},{5,4},{6,8},{7,6},{8,7},{9,11},{10,9... | collective-permute-start | bytes 589832 | tf_op jit(solution)/shard_map/ppermute | solution.py:59
  154.7 22.7 %collective-permute-start.16 = (bf16[384,640]{1,0:T(8,128)(2,1)S(1)}, bf16[384,640]{1,0:T(8,128)(2,1)S(1)}, u32[]{:S(2)}, u32[]{:S(2)}) collective-permute-start(bf16[384,640]{1,0:T(8,128)(2,1)S(1)} %convolution_convert_fusion), channel_id=1, source_target_pairs={{24,0},{18,6},{36,12},{30,18},{48,24},{42,30},{60,36},{54,42},{72,... | collective-permute-start | bytes 1474568 | tf_op jit(solution)/shard_map/ppermute | solution.py:15
  157.7 38.2 %collective-permute-start.15 = (bf16[384,640]{1,0:T(8,128)(2,1)S(1)}, bf16[384,640]{1,0:T(8,128)(2,1)S(1)}, u32[]{:S(2)}, u32[]{:S(2)}) collective-permute-start(bf16[384,640]{1,0:T(8,128)(2,1)S(1)} %fusion), channel_id=1, source_target_pairs={{24,0},{18,6},{36,12},{30,18},{48,24},{42,30},{60,36},{54,42},{72,... | collective-permute-start | bytes 1474568 | tf_op jit(solution)/shard_map/ppermute | solution.py:15
  177.4 18.5 %collective-permute-start.17 = (bf16[384,640]{1,0:T(8,128)(2,1)S(1)}, bf16[384,640]{1,0:T(8,128)(2,1)S(1)}, u32[]{:S(2)}, u32[]{:S(2)}) collective-permute-start(bf16[384,640]{1,0:T(8,128)(2,1)S(1)} %add_convert_fusion.1), channel_id=1, source_target_pairs={{0,6},{6,0},{12,18},{18,12},{24,30},{30,24},{36,42},{42,36},{48,54... | collective-permute-start | bytes 1474568 | tf_op jit(solution)/shard_map/ppermute | solution.py:15

commit v18 on v17

--- a/solution.py
+++ b/solution.py
@@ -128,11 +128,11 @@
     payload = lax.optimization_barrier(with_codes(hidden, targets, padding))
 
     key_one = dp_permute(payload, key_pairs())
-    key_two = dp_permute(payload, crossed_pairs())
     weight = cotangent * padding.astype(F32)
     row_data = jnp.stack([targets.astype(F32) + 1.0, gold_logit, vocab_lse, weight])
     row_data = rows_of(row_data, row_start(r), 64, 1)
     row_data, late_payload = lax.optimization_barrier((row_data, payload))
+    key_two = dp_permute(late_payload, crossed_pairs())
     pair_hidden = core_swap(late_payload)[:SEG]
     row_data = jnp.stack([row_data, core_swap(row_data)])
     row_codes, gold, vocab, weight = (row_data[:, i] for i in range(4))

time: 198 us -> 201 us (1.015)
  the two profiles are of different devices: /device:TPU:27 before, /device:TPU:1 now
where the time goes in v18:
time: 201 us; the launch traced here: 200 us
  waiting for transfers between devices  99.3 us (49%)
  starting transfers between devices  86.2 us (43%)
  other arithmetic  5.71 us (3%)
  matrix products  5.34 us (3%)
  local copies, waits for them, and re-layouts  2.35 us (1%)
    ppermute x8, waiting for transfers between devices, dp_permute(): return lax.ppermute(value, 'dp', pairs)  60.9 us
    ppermute x10, starting transfers between devices, line_permute(): return lax.ppermute(value, ('dp', 'tensor'), pairs)  45.1 us
    ppermute x8, starting transfers between devices, dp_permute(): return lax.ppermute(value, 'dp', pairs)  41.1 us
    ppermute x10, waiting for transfers between devices, line_permute(): return lax.ppermute(value, ('dp', 'tensor'), pairs)  38.4 us
  transfers between devices with their start and end apart: 18, of which 15 were waited for; matrix products, arithmetic and copies ran while one was open for 4% of the time, Pallas kernels for 0%

profile of v18, /device:TPU:1, one launch (start us, length us, event | category | flops | bytes accessed | tf_op | source)
XLA Modules:
  0.0 200.0 jit_solution(8398308457747045963)
XLA Ops:
  0.7 1.1 pad_maximum_fusion.2
  1.8 15.7 %collective-permute-start.1 = (bf16[400,640]{1,0:T(8,128)(2,1)S(1)}, bf16[400,640]{1,0:T(8,128)(2,1)S(1)}, u32[]{:S(2)}, u32[]{:S(2)}) collective-permute-start(bf16[400,640]{1,0:T(8,128)(2,1)S(1)} %pad_maximum_fusion.2), channel_id=1, source_target_pairs={{0,24},{6,18},{12,36},{18,30},{24,48},{30,42},{36,60},{42,54},{48,... | collective-permute-start | bytes 1536008 | tf_op jit(solution)/shard_map/ppermute | solution.py:15
  20.4 1.9 collective-permute-start.2
  22.3 2.3 %collective-permute-start.3 = (bf16[400,640]{1,0:T(8,128)(2,1)S(1)}, bf16[400,640]{1,0:T(8,128)(2,1)S(1)}, u32[]{:S(2)}, u32[]{:S(2)}) collective-permute-start(bf16[400,640]{1,0:T(8,128)(2,1)S(1)} %pad_maximum_fusion.2), channel_id=1, source_target_pairs={{0,6},{6,0},{12,18},{18,12},{24,30},{30,24},{36,42},{42,36},{48,54... | collective-permute-start | bytes 1536008 | tf_op jit(solution)/shard_map/ppermute | solution.py:15
  24.6 2.0 %collective-permute-start = (f32[4,64]{1,0:T(4,128)S(1)}, f32[4,64]{1,0:T(4,128)S(1)}, u32[]{:S(2)}, u32[]{:S(2)}) collective-permute-start(f32[4,64]{1,0:T(4,128)S(1)} %fusion.43), channel_id=1, source_target_pairs={{0,6},{6,0},{12,18},{18,12},{24,30},{30,24},{36,42},{42,36},{48,54... | collective-permute-start | bytes 3080 | tf_op jit(solution)/shard_map/ppermute | solution.py:15
  27.7 1.5 collective-permute-done.1
  29.3 33.3 %collective-permute-done.2 = bf16[400,640]{1,0:T(8,128)(2,1)S(1)} collective-permute-done((bf16[400,640]{1,0:T(8,128)(2,1)S(1)}, bf16[400,640]{1,0:T(8,128)(2,1)S(1)}, u32[]{:S(2)}, u32[]{:S(2)}) %collective-permute-start.2) | collective-permute-done | bytes 512032 | tf_op jit(solution)/shard_map/ppermute | solution.py:15
  64.2 2.1 %collective-permute-start.4 = (f32[2,64,768]{2,1,0:T(8,128)S(1)}, f32[2,64,768]{2,1,0:T(8,128)S(1)}, u32[]{:S(2)}, u32[]{:S(2)}) collective-permute-start(f32[2,64,768]{2,1,0:T(8,128)S(1)} %pad_maximum_fusion.3), channel_id=1, source_target_pairs={{0,1},{1,0},{2,3},{3,2},{4,5},{5,4},{6,7},{7,8},{8,6},{9,10},{10,1... | collective-permute-start | bytes 1179656 | tf_op jit(solution)/shard_map/ppermute | solution.py:59
  66.3 4.3 %collective-permute-start.5 = (f32[2,64,768]{2,1,0:T(8,128)S(1)}, f32[2,64,768]{2,1,0:T(8,128)S(1)}, u32[]{:S(2)}, u32[]{:S(2)}) collective-permute-start(f32[2,64,768]{2,1,0:T(8,128)S(1)} %pad_maximum_fusion.4), channel_id=1, source_target_pairs={{0,1},{1,0},{2,3},{3,2},{4,5},{5,4},{6,8},{7,6},{8,7},{9,11},{10,9... | collective-permute-start | bytes 1179656 | tf_op jit(solution)/shard_map/ppermute | solution.py:59
  72.5 1.4 collective-permute-done.4
  73.9 12.5 %collective-permute-done.5 = f32[2,64,768]{2,1,0:T(8,128)S(1)} collective-permute-done((f32[2,64,768]{2,1,0:T(8,128)S(1)}, f32[2,64,768]{2,1,0:T(8,128)S(1)}, u32[]{:S(2)}, u32[]{:S(2)}) %collective-permute-start.5) | collective-permute-done | bytes 393248 | tf_op jit(solution)/shard_map/ppermute | solution.py:59
  86.5 1.9 collective-permute-start.6
  88.5 7.3 %collective-permute-start.7 = (f32[2,64,768]{2,1,0:T(8,128)S(1)}, f32[2,64,768]{2,1,0:T(8,128)S(1)}, u32[]{:S(2)}, u32[]{:S(2)}) collective-permute-start(f32[2,64,768]{2,1,0:T(8,128)S(1)} %get-tuple-element.33), channel_id=1, source_target_pairs={{0,2},{1,3},{2,4},{3,5},{4,0},{5,1},{6,7},{7,8},{8,6},{9,10},{10,1... | collective-permute-start | bytes 1179656 | tf_op jit(solution)/shard_map/ppermute | solution.py:59
  95.8 1.9 collective-permute-start.8
  98.4 5.2 %collective-permute-done.7 = f32[2,64,768]{2,1,0:T(8,128)S(1)} collective-permute-done((f32[2,64,768]{2,1,0:T(8,128)S(1)}, f32[2,64,768]{2,1,0:T(8,128)S(1)}, u32[]{:S(2)}, u32[]{:S(2)}) %collective-permute-start.7) | collective-permute-done | bytes 393248 | tf_op jit(solution)/shard_map/ppermute | solution.py:59
  103.5 4.1 %collective-permute-done.8 = f32[2,64,768]{2,1,0:T(8,128)S(1)} collective-permute-done((f32[2,64,768]{2,1,0:T(8,128)S(1)}, f32[2,64,768]{2,1,0:T(8,128)S(1)}, u32[]{:S(2)}, u32[]{:S(2)}) %collective-permute-start.8) | collective-permute-done | bytes 393248 | tf_op jit(solution)/shard_map/ppermute | solution.py:59
  108.3 1.9 collective-permute-start.9
  110.2 1.1 collective-permute-done.9
  111.7 11.7 %collective-permute-start.10 = (bf16[2,64,768]{2,1,0:T(8,128)(2,1)S(1)}, bf16[2,64,768]{2,1,0:T(8,128)(2,1)S(1)}, u32[]{:S(2)}, u32[]{:S(2)}) collective-permute-start(bf16[2,64,768]{2,1,0:T(8,128)(2,1)S(1)} %get-tuple-element.44), channel_id=1, source_target_pairs={{0,1},{1,0},{2,3},{3,2},{4,5},{5,4},{6,9},{7,10},{8,11},{9,6},{10,... | collective-permute-start | bytes 589832 | tf_op jit(solution)/shard_map/ppermute | solution.py:59
  123.4 1.9 collective-permute-start.11
  125.4 5.9 %collective-permute-start.12 = (bf16[2,64,768]{2,1,0:T(8,128)(2,1)S(1)}, bf16[2,64,768]{2,1,0:T(8,128)(2,1)S(1)}, u32[]{:S(2)}, u32[]{:S(2)}) collective-permute-start(bf16[2,64,768]{2,1,0:T(8,128)(2,1)S(1)} %get-tuple-element.44), channel_id=1, source_target_pairs={{0,4},{1,5},{2,0},{3,1},{4,2},{5,3},{6,8},{7,6},{8,7},{9,11},{10,9... | collective-permute-start | bytes 589832 | tf_op jit(solution)/shard_map/ppermute | solution.py:59
  131.3 1.3 collective-permute-done.10
  132.6 6.5 %collective-permute-done.11 = bf16[2,64,768]{2,1,0:T(8,128)(2,1)S(1)} collective-permute-done((bf16[2,64,768]{2,1,0:T(8,128)(2,1)S(1)}, bf16[2,64,768]{2,1,0:T(8,128)(2,1)S(1)}, u32[]{:S(2)}, u32[]{:S(2)}) %collective-permute-start.11) | collective-permute-done | bytes 196640 | tf_op jit(solution)/shard_map/ppermute | solution.py:59
  139.2 6.2 %collective-permute-start.13 = (bf16[2,64,768]{2,1,0:T(8,128)(2,1)S(1)}, bf16[2,64,768]{2,1,0:T(8,128)(2,1)S(1)}, u32[]{:S(2)}, u32[]{:S(2)}) collective-permute-start(bf16[2,64,768]{2,1,0:T(8,128)(2,1)S(1)} %get-tuple-element.78), channel_id=1, source_target_pairs={{0,1},{1,0},{2,3},{3,2},{4,5},{5,4},{6,7},{7,8},{8,6},{9,10},{10,1... | collective-permute-start | bytes 589832 | tf_op jit(solution)/shard_map/ppermute | solution.py:59
  145.4 1.9 collective-permute-start.14
  147.4 2.7 %collective-permute-done.13 = bf16[2,64,768]{2,1,0:T(8,128)(2,1)S(1)} collective-permute-done((bf16[2,64,768]{2,1,0:T(8,128)(2,1)S(1)}, bf16[2,64,768]{2,1,0:T(8,128)(2,1)S(1)}, u32[]{:S(2)}, u32[]{:S(2)}) %collective-permute-start.13) | collective-permute-done | bytes 196640 | tf_op jit(solution)/shard_map/ppermute | solution.py:59
  150.2 4.2 %collective-permute-done.14 = bf16[2,64,768]{2,1,0:T(8,128)(2,1)S(1)} collective-permute-done((bf16[2,64,768]{2,1,0:T(8,128)(2,1)S(1)}, bf16[2,64,768]{2,1,0:T(8,128)(2,1)S(1)}, u32[]{:S(2)}, u32[]{:S(2)}) %collective-permute-start.14) | collective-permute-done | bytes 196640 | tf_op jit(solution)/shard_map/ppermute | solution.py:59
  155.5 12.5 %collective-permute-start.16 = (bf16[384,640]{1,0:T(8,128)(2,1)S(1)}, bf16[384,640]{1,0:T(8,128)(2,1)S(1)}, u32[]{:S(2)}, u32[]{:S(2)}) collective-permute-start(bf16[384,640]{1,0:T(8,128)(2,1)S(1)} %convolution_convert_fusion), channel_id=1, source_target_pairs={{24,0},{18,6},{36,12},{30,18},{48,24},{42,30},{60,36},{54,42},{72,... | collective-permute-start | bytes 1474568 | tf_op jit(solution)/shard_map/ppermute | solution.py:15
  169.1 2.8 %collective-permute-start.15 = (bf16[384,640]{1,0:T(8,128)(2,1)S(1)}, bf16[384,640]{1,0:T(8,128)(2,1)S(1)}, u32[]{:S(2)}, u32[]{:S(2)}) collective-permute-start(bf16[384,640]{1,0:T(8,128)(2,1)S(1)} %fusion), channel_id=1, source_target_pairs={{24,0},{18,6},{36,12},{30,18},{48,24},{42,30},{60,36},{54,42},{72,... | collective-permute-start | bytes 1474568 | tf_op jit(solution)/shard_map/ppermute | solution.py:15
  172.0 16.5 %collective-permute-done.16 = bf16[384,640]{1,0:T(8,128)(2,1)S(1)} collective-permute-done((bf16[384,640]{1,0:T(8,128)(2,1)S(1)}, bf16[384,640]{1,0:T(8,128)(2,1)S(1)}, u32[]{:S(2)}, u32[]{:S(2)}) %collective-permute-start.16) | collective-permute-done | bytes 491552 | tf_op jit(solution)/shard_map/ppermute | solution.py:15
  188.6 1.9 collective-permute-start.17
  191.2 7.8 %collective-permute-done.15 = bf16[384,640]{1,0:T(8,128)(2,1)S(1)} collective-permute-done((bf16[384,640]{1,0:T(8,128)(2,1)S(1)}, bf16[384,640]{1,0:T(8,128)(2,1)S(1)}, u32[]{:S(2)}, u32[]{:S(2)}) %collective-permute-start.15) | collective-permute-done | bytes 491552 | tf_op jit(solution)/shard_map/ppermute | solution.py:15
  (85 shorter events, 13.4 us)
Async XLA Ops:
  1.8 27.4 %collective-permute-start.1 = (bf16[400,640]{1,0:T(8,128)(2,1)S(1)}, bf16[400,640]{1,0:T(8,128)(2,1)S(1)}, u32[]{:S(2)}, u32[]{:S(2)}) collective-permute-start(bf16[400,640]{1,0:T(8,128)(2,1)S(1)} %pad_maximum_fusion.2), channel_id=1, source_target_pairs={{0,24},{6,18},{12,36},{18,30},{24,48},{30,42},{36,60},{42,54},{48,... | collective-permute-start | bytes 1536008 | tf_op jit(solution)/shard_map/ppermute | solution.py:15
  20.4 42.2 %collective-permute-start.2 = (bf16[400,640]{1,0:T(8,128)(2,1)S(1)}, bf16[400,640]{1,0:T(8,128)(2,1)S(1)}, u32[]{:S(2)}, u32[]{:S(2)}) collective-permute-start(bf16[400,640]{1,0:T(8,128)(2,1)S(1)} %pad_maximum_fusion.2), channel_id=1, source_target_pairs={{0,18},{6,24},{12,30},{18,36},{24,42},{30,48},{36,54},{42,60},{48,... | collective-permute-start | bytes 1536008 | tf_op jit(solution)/shard_map/ppermute | solution.py:15
  22.3 41.2 %collective-permute-start.3 = (bf16[400,640]{1,0:T(8,128)(2,1)S(1)}, bf16[400,640]{1,0:T(8,128)(2,1)S(1)}, u32[]{:S(2)}, u32[]{:S(2)}) collective-permute-start(bf16[400,640]{1,0:T(8,128)(2,1)S(1)} %pad_maximum_fusion.2), channel_id=1, source_target_pairs={{0,6},{6,0},{12,18},{18,12},{24,30},{30,24},{36,42},{42,36},{48,54... | collective-permute-start | bytes 1536008 | tf_op jit(solution)/shard_map/ppermute | solution.py:15
  24.6 3.1 %collective-permute-start = (f32[4,64]{1,0:T(4,128)S(1)}, f32[4,64]{1,0:T(4,128)S(1)}, u32[]{:S(2)}, u32[]{:S(2)}) collective-permute-start(f32[4,64]{1,0:T(4,128)S(1)} %fusion.43), channel_id=1, source_target_pairs={{0,6},{6,0},{12,18},{18,12},{24,30},{30,24},{36,42},{42,36},{48,54... | collective-permute-start | bytes 3080 | tf_op jit(solution)/shard_map/ppermute | solution.py:15
  29.2 33.5 %copy-start.1 = (bf16[400,640]{1,0:T(8,128)(2,1)}, bf16[400,640]{1,0:T(8,128)(2,1)S(1)}, u32[]{:S(2)}) copy-start(bf16[400,640]{1,0:T(8,128)(2,1)S(1)} %collective-permute-done.1) | copy-start | bytes 1536004
  29.3 33.5 %copy-start.2 = (bf16[400,640]{1,0:T(8,128)(2,1)}, bf16[400,640]{1,0:T(8,128)(2,1)S(1)}, u32[]{:S(2)}) copy-start(bf16[400,640]{1,0:T(8,128)(2,1)S(1)} %broadcast_select_fusion) | copy-start | bytes 1536004
  62.8 0.8 slice-start
  62.8 0.7 slice-start.1
  64.1 6.5 %copy-start = (bf16[384,640]{1,0:T(8,128)(2,1)S(1)}, bf16[384,640]{1,0:T(8,128)(2,1)}, u32[]{:S(2)}) copy-start(bf16[384,640]{1,0:T(8,128)(2,1)} %param.6) | copy-start | bytes 1474564
  64.2 9.7 %collective-permute-start.4 = (f32[2,64,768]{2,1,0:T(8,128)S(1)}, f32[2,64,768]{2,1,0:T(8,128)S(1)}, u32[]{:S(2)}, u32[]{:S(2)}) collective-permute-start(f32[2,64,768]{2,1,0:T(8,128)S(1)} %pad_maximum_fusion.3), channel_id=1, source_target_pairs={{0,1},{1,0},{2,3},{3,2},{4,5},{5,4},{6,7},{7,8},{8,6},{9,10},{10,1... | collective-permute-start | bytes 1179656 | tf_op jit(solution)/shard_map/ppermute | solution.py:59
  66.3 20.1 %collective-permute-start.5 = (f32[2,64,768]{2,1,0:T(8,128)S(1)}, f32[2,64,768]{2,1,0:T(8,128)S(1)}, u32[]{:S(2)}, u32[]{:S(2)}) collective-permute-start(f32[2,64,768]{2,1,0:T(8,128)S(1)} %pad_maximum_fusion.4), channel_id=1, source_target_pairs={{0,1},{1,0},{2,3},{3,2},{4,5},{5,4},{6,8},{7,6},{8,7},{9,11},{10,9... | collective-permute-start | bytes 1179656 | tf_op jit(solution)/shard_map/ppermute | solution.py:59
  86.5 11.8 %collective-permute-start.6 = (f32[2,64,768]{2,1,0:T(8,128)S(1)}, f32[2,64,768]{2,1,0:T(8,128)S(1)}, u32[]{:S(2)}, u32[]{:S(2)}) collective-permute-start(f32[2,64,768]{2,1,0:T(8,128)S(1)} %get-tuple-element.32), channel_id=1, source_target_pairs={{0,1},{1,0},{2,3},{3,2},{4,5},{5,4},{6,9},{7,10},{8,11},{9,6},{10,... | collective-permute-start | bytes 1179656 | tf_op jit(solution)/shard_map/ppermute | solution.py:59
  88.5 15.0 %collective-permute-start.7 = (f32[2,64,768]{2,1,0:T(8,128)S(1)}, f32[2,64,768]{2,1,0:T(8,128)S(1)}, u32[]{:S(2)}, u32[]{:S(2)}) collective-permute-start(f32[2,64,768]{2,1,0:T(8,128)S(1)} %get-tuple-element.33), channel_id=1, source_target_pairs={{0,2},{1,3},{2,4},{3,5},{4,0},{5,1},{6,7},{7,8},{8,6},{9,10},{10,1... | collective-permute-start | bytes 1179656 | tf_op jit(solution)/shard_map/ppermute | solution.py:59
  95.8 11.8 %collective-permute-start.8 = (f32[2,64,768]{2,1,0:T(8,128)S(1)}, f32[2,64,768]{2,1,0:T(8,128)S(1)}, u32[]{:S(2)}, u32[]{:S(2)}) collective-permute-start(f32[2,64,768]{2,1,0:T(8,128)S(1)} %get-tuple-element.34), channel_id=1, source_target_pairs={{0,4},{1,5},{2,0},{3,1},{4,2},{5,3},{6,8},{7,6},{8,7},{9,11},{10,9... | collective-permute-start | bytes 1179656 | tf_op jit(solution)/shard_map/ppermute | solution.py:59
  108.3 3.1 %collective-permute-start.9 = (f32[2,4,64]{2,0,1:T(2,128)S(1)}, f32[2,4,64]{2,0,1:T(2,128)S(1)}, u32[]{:S(2)}, u32[]{:S(2)}) collective-permute-start(f32[2,4,64]{2,0,1:T(2,128)S(1)} %pad_maximum_fusion.8), channel_id=1, source_target_pairs={{0,6},{6,0},{12,18},{18,12},{24,30},{30,24},{36,42},{42,36},{48,54... | collective-permute-start | bytes 6152 | tf_op jit(solution)/shard_map/ppermute | solution.py:15
  111.7 20.8 %collective-permute-start.10 = (bf16[2,64,768]{2,1,0:T(8,128)(2,1)S(1)}, bf16[2,64,768]{2,1,0:T(8,128)(2,1)S(1)}, u32[]{:S(2)}, u32[]{:S(2)}) collective-permute-start(bf16[2,64,768]{2,1,0:T(8,128)(2,1)S(1)} %get-tuple-element.44), channel_id=1, source_target_pairs={{0,1},{1,0},{2,3},{3,2},{4,5},{5,4},{6,9},{7,10},{8,11},{9,6},{10,... | collective-permute-start | bytes 589832 | tf_op jit(solution)/shard_map/ppermute | solution.py:59
  123.4 15.7 %collective-permute-start.11 = (bf16[2,64,768]{2,1,0:T(8,128)(2,1)S(1)}, bf16[2,64,768]{2,1,0:T(8,128)(2,1)S(1)}, u32[]{:S(2)}, u32[]{:S(2)}) collective-permute-start(bf16[2,64,768]{2,1,0:T(8,128)(2,1)S(1)} %get-tuple-element.44), channel_id=1, source_target_pairs={{0,2},{1,3},{2,4},{3,5},{4,0},{5,1},{6,7},{7,8},{8,6},{9,10},{10,1... | collective-permute-start | bytes 589832 | tf_op jit(solution)/shard_map/ppermute | solution.py:59
  125.4 13.8 %collective-permute-start.12 = (bf16[2,64,768]{2,1,0:T(8,128)(2,1)S(1)}, bf16[2,64,768]{2,1,0:T(8,128)(2,1)S(1)}, u32[]{:S(2)}, u32[]{:S(2)}) collective-permute-start(bf16[2,64,768]{2,1,0:T(8,128)(2,1)S(1)} %get-tuple-element.44), channel_id=1, source_target_pairs={{0,4},{1,5},{2,0},{3,1},{4,2},{5,3},{6,8},{7,6},{8,7},{9,11},{10,9... | collective-permute-start | bytes 589832 | tf_op jit(solution)/shard_map/ppermute | solution.py:59
  139.2 10.9 %collective-permute-start.13 = (bf16[2,64,768]{2,1,0:T(8,128)(2,1)S(1)}, bf16[2,64,768]{2,1,0:T(8,128)(2,1)S(1)}, u32[]{:S(2)}, u32[]{:S(2)}) collective-permute-start(bf16[2,64,768]{2,1,0:T(8,128)(2,1)S(1)} %get-tuple-element.78), channel_id=1, source_target_pairs={{0,1},{1,0},{2,3},{3,2},{4,5},{5,4},{6,7},{7,8},{8,6},{9,10},{10,1... | collective-permute-start | bytes 589832 | tf_op jit(solution)/shard_map/ppermute | solution.py:59
  145.4 8.9 %collective-permute-start.14 = (bf16[2,64,768]{2,1,0:T(8,128)(2,1)S(1)}, bf16[2,64,768]{2,1,0:T(8,128)(2,1)S(1)}, u32[]{:S(2)}, u32[]{:S(2)}) collective-permute-start(bf16[2,64,768]{2,1,0:T(8,128)(2,1)S(1)} %get-tuple-element.77), channel_id=1, source_target_pairs={{0,1},{1,0},{2,3},{3,2},{4,5},{5,4},{6,8},{7,6},{8,7},{9,11},{10,9... | collective-permute-start | bytes 589832 | tf_op jit(solution)/shard_map/ppermute | solution.py:59
  155.5 33.0 %collective-permute-start.16 = (bf16[384,640]{1,0:T(8,128)(2,1)S(1)}, bf16[384,640]{1,0:T(8,128)(2,1)S(1)}, u32[]{:S(2)}, u32[]{:S(2)}) collective-permute-start(bf16[384,640]{1,0:T(8,128)(2,1)S(1)} %convolution_convert_fusion), channel_id=1, source_target_pairs={{24,0},{18,6},{36,12},{30,18},{48,24},{42,30},{60,36},{54,42},{72,... | collective-permute-start | bytes 1474568 | tf_op jit(solution)/shard_map/ppermute | solution.py:15
  169.1 29.8 %collective-permute-start.15 = (bf16[384,640]{1,0:T(8,128)(2,1)S(1)}, bf16[384,640]{1,0:T(8,128)(2,1)S(1)}, u32[]{:S(2)}, u32[]{:S(2)}) collective-permute-start(bf16[384,640]{1,0:T(8,128)(2,1)S(1)} %fusion), channel_id=1, source_target_pairs={{24,0},{18,6},{36,12},{30,18},{48,24},{42,30},{60,36},{54,42},{72,... | collective-permute-start | bytes 1474568 | tf_op jit(solution)/shard_map/ppermute | solution.py:15
  188.6 10.5 %collective-permute-start.17 = (bf16[384,640]{1,0:T(8,128)(2,1)S(1)}, bf16[384,640]{1,0:T(8,128)(2,1)S(1)}, u32[]{:S(2)}, u32[]{:S(2)}) collective-permute-start(bf16[384,640]{1,0:T(8,128)(2,1)S(1)} %add_convert_fusion.1), channel_id=1, source_target_pairs={{0,6},{6,0},{12,18},{18,12},{24,30},{30,24},{36,42},{42,36},{48,54... | collective-permute-start | bytes 1474568 | tf_op jit(solution)/shard_map/ppermute | solution.py:15
